TPU v7x, 32 devices: a whole 2x2x4 slice. The times are simulated.
32 devices in a mesh: seq: 4 (over x, core), blk: 8 (over z, y).
Axes of the slice: x: 2, y: 2, z: 4, core: 2. Of those that a mesh axis runs over, the one named last changes fastest.
Arguments:
- tokens: bfloat16 [512, 8, 1024], P('blk', 'seq'), may hold values from -6 to 6
- segment_ids: int32 [512, 8], P('blk', 'seq'), may hold values from 0 to 7, as said below
- ln1_gain: float32 [1024], replicated, may hold values from 0.5 to 1.5
- ln1_bias: float32 [1024], replicated, may hold values from -1.5 to 1.5
- w_qkv: bfloat16 [1024, 3072], replicated, may hold values from -0.1875 to 0.1875
- w_out: bfloat16 [1024, 1024], replicated, may hold values from -0.75 to 0.75
- ln2_gain: float32 [1024], replicated, may hold values from 0.5 to 1.5
- ln2_bias: float32 [1024], replicated, may hold values from -1.5 to 1.5
- w_fc: bfloat16 [1024, 4096], replicated, may hold values from -0.1875 to 0.1875
- w_proj: bfloat16 [4096, 1024], replicated, may hold values from -0.09375 to 0.09375
- prefix_embed: float32 [10, 1024], replicated, may hold values from -5 to 5
- w_mlp1: float32 [1024, 512], replicated, may hold values from -0.1875 to 0.1875
- b_mlp1: float32 [512], replicated, may hold values from -3 to 3
- w_mlp2: float32 [512, 2048], replicated, may hold values from -0.5 to 0.5
- b_mlp2: float32 [2048], replicated, may hold values from -1.5 to 1.5
- cotangent: bfloat16 [512, 8, 1024], P('blk', 'seq'), may hold values from -6 to 6
Outputs:
- block_out: bfloat16 [512, 8, 1024], P('blk', 'seq')
- input_grad: float32 [512, 8, 1024], P('blk', 'seq')
- grad_prefix: float32 [10, 1024], replicated
- grad_mlp1: float32 [1024, 512], replicated
- grad_bias1: float32 [512], replicated
- grad_mlp2: float32 [512, 2048], replicated
- grad_bias2: float32 [2048], replicated
- softmax_lse: float32 [8, 16, 512], P('seq', None, 'blk')
Inputs may be any that keep to these rules, and one draw needn't show every extreme that they name: `segment_ids`: along each row the ids never fall. Of the 2 rows that one index of seq holds, one row, drawn, is a single segment; every other row has exactly 8 segments of drawn lengths.
All inputs are finite; a program needn't handle non-finite values.
Results may differ from a plain program's by a relative error of at most 0.012.
Values may be sent and summed in bfloat16 or wider, within the bound.
No kernel may reach another device: no remote copies, remote signals or barrier semaphores. Data moves between devices by JAX's collectives and lax.ppermute only.
A program may use at most 256 MiB of HBM per device.

v0:
```python
from functools import partial
import math

import jax
import jax.numpy as jnp
from jax import lax
from jax.sharding import PartitionSpec as P

HEADS = 16
HEAD = 64


EPS = 1e-05
NEG = -1e30
HIGH = lax.Precision.HIGHEST


def layer_norm(value_in, gain, bias):
    average = jnp.mean(value_in, axis=-1, keepdims=True)
    centered = value_in - average
    variance = jnp.mean(centered * centered, axis=-1, keepdims=True)
    return centered * lax.rsqrt(variance + EPS) * gain + bias


def adapter(prefix_embed, w_mlp1, b_mlp1, w_mlp2, b_mlp2):
    inner_act = jnp.tanh(jnp.dot(prefix_embed, w_mlp1, precision=HIGH) + b_mlp1)
    return jnp.dot(inner_act, w_mlp2, precision=HIGH) + b_mlp2


def gelu_tanh(pre_act):
    return jax.nn.gelu(pre_act, approximate=True)


def split_heads(block_in):
    return block_in.reshape(block_in.shape[0], block_in.shape[1], HEADS, HEAD)


def allowed(query_pos, query_seg, key_pos, key_seg):
    same_seg = query_seg.T[:, :, None] == key_seg.T[:, None, :]
    causal = key_pos[None, None, :] <= query_pos[None, :, None]
    return jnp.logical_and(same_seg, causal)[:, None]


def scores_of(query_heads, key_block, score_scale):
    return score_scale * jnp.einsum(
        "prhd,krhd->rhpk", query_heads, split_heads(key_block), preferred_element_type=jnp.float32
    )


def block_grads(
    query_heads,
    grad_heads,
    log_total,
    slope_base,
    query_pos,
    query_seg,
    key_block,
    value_block,
    key_pos,
    key_seg,
    score_scale,
):
    scores = scores_of(query_heads, key_block, score_scale)
    scores = jnp.where(allowed(query_pos, query_seg, key_pos, key_seg), scores, NEG)
    weights = jnp.exp(scores - log_total[..., None])
    grad_weights = jnp.einsum(
        "prhd,krhd->rhpk", grad_heads, split_heads(value_block), preferred_element_type=jnp.float32
    )
    slopes = (weights * (grad_weights - slope_base[..., None])).astype(jnp.bfloat16)
    return (weights.astype(jnp.bfloat16), slopes)


def body(
    tokens,
    segment_ids,
    ln1_gain,
    ln1_bias,
    w_qkv,
    w_out,
    ln2_gain,
    ln2_bias,
    w_fc,
    w_proj,
    prefix_embed,
    w_mlp1,
    b_mlp1,
    w_mlp2,
    b_mlp2,
    cotangent,
):
    pos_dev, row_count, width = tokens.shape
    score_scale = HEAD ** (-0.5)
    flat_rows = pos_dev * row_count
    own_pos = lax.axis_index("blk") * pos_dev + jnp.arange(pos_dev)
    inputs = tokens.astype(jnp.float32).reshape(flat_rows, width)
    normed_one = layer_norm(inputs, ln1_gain, ln1_bias).astype(jnp.bfloat16)
    projected = jnp.dot(normed_one, w_qkv, preferred_element_type=jnp.float32).astype(jnp.bfloat16)
    queries = projected[:, :width].reshape(pos_dev, row_count, width)
    keys = projected[:, width : 2 * width].reshape(pos_dev, row_count, width)
    values = projected[:, 2 * width :].reshape(pos_dev, row_count, width)
    query_heads = split_heads(queries)
    prefix_low = adapter(prefix_embed, w_mlp1, b_mlp1, w_mlp2, b_mlp2).astype(jnp.bfloat16)
    prefix_keys = prefix_low[:, :width].reshape(-1, HEADS, HEAD)
    prefix_values = prefix_low[:, width:].reshape(-1, HEADS, HEAD)
    prefix_scores = score_scale * jnp.einsum(
        "prhd,jhd->rhpj", query_heads, prefix_keys, preferred_element_type=jnp.float32
    )
    start_top = jnp.max(prefix_scores, -1)
    start_weights = jnp.exp(prefix_scores - start_top[..., None])
    start_denom = jnp.sum(start_weights, -1)
    start_numer = jnp.einsum(
        "rhpj,jhd->rhpd",
        start_weights.astype(jnp.bfloat16),
        prefix_values,
        preferred_element_type=jnp.float32,
    )
    start_state = (start_top, start_denom, start_numer)
    running = start_state
    key_shards = lax.all_gather(keys, "blk", axis=0, tiled=True)
    value_shards = lax.all_gather(values, "blk", axis=0, tiled=True)
    seg_shards = lax.all_gather(segment_ids, "blk", axis=0, tiled=True)
    num_rows = key_shards.shape[0]
    forward_stride = math.gcd(num_rows, 512)

    def inner(state, block_index):
        running_top, denominator, numerator = state
        offset = block_index * forward_stride
        key_block = lax.dynamic_slice_in_dim(key_shards, offset, forward_stride, 0)
        value_block = lax.dynamic_slice_in_dim(value_shards, offset, forward_stride, 0)
        seg_block = lax.dynamic_slice_in_dim(seg_shards, offset, forward_stride, 0)
        key_pos = offset + jnp.arange(forward_stride)
        scores = jnp.where(
            allowed(own_pos, segment_ids, key_pos, seg_block),
            scores_of(query_heads, key_block, score_scale),
            NEG,
        )
        new_top = jnp.maximum(running_top, jnp.max(scores, -1))
        fading = jnp.exp(running_top - new_top)
        weights = jnp.exp(scores - new_top[..., None])
        denominator = denominator * fading + jnp.sum(weights, -1)
        numerator = numerator * fading[..., None] + jnp.einsum(
            "rhpk,krhd->rhpd",
            weights.astype(jnp.bfloat16),
            split_heads(value_block),
            preferred_element_type=jnp.float32,
        )
        return ((new_top, denominator, numerator), None)

    running, _ = lax.scan(inner, running, jnp.arange(num_rows // forward_stride))
    final_top, final_denom, final_numer = running
    log_total = final_top + jnp.log(final_denom)
    attended = final_numer / final_denom[..., None]
    attended_rows = jnp.transpose(attended, (2, 0, 1, 3)).reshape(flat_rows, width)
    middle = inputs + jnp.dot(
        attended_rows.astype(jnp.bfloat16), w_out, preferred_element_type=jnp.float32
    )
    normed_two = layer_norm(middle, ln2_gain, ln2_bias).astype(jnp.bfloat16)
    hidden_pre = jnp.dot(normed_two, w_fc, preferred_element_type=jnp.float32)
    hidden_act = gelu_tanh(hidden_pre).astype(jnp.bfloat16)
    outputs = middle + jnp.dot(hidden_act, w_proj, preferred_element_type=jnp.float32)
    block_out = outputs.astype(jnp.bfloat16).reshape(pos_dev, row_count, width)
    grad_out = cotangent.reshape(flat_rows, width)
    grad_act = jnp.dot(grad_out, w_proj.T, preferred_element_type=jnp.float32)
    _, gelu_back = jax.vjp(gelu_tanh, hidden_pre)
    grad_pre = gelu_back(grad_act)[0].astype(jnp.bfloat16)
    grad_norm_two = jnp.dot(grad_pre, w_fc.T, preferred_element_type=jnp.float32)
    _, norm_two_back = jax.vjp(partial(layer_norm, gain=ln2_gain, bias=ln2_bias), middle)
    grad_middle = grad_out.astype(jnp.float32) + norm_two_back(grad_norm_two)[0]
    grad_attended = jnp.dot(
        grad_middle.astype(jnp.bfloat16), w_out.T, preferred_element_type=jnp.float32
    ).astype(jnp.bfloat16)
    grad_flat = grad_attended.reshape(pos_dev, row_count, width)
    grad_heads = split_heads(grad_flat)
    slope_base = jnp.sum(jnp.transpose(grad_heads.astype(jnp.float32), (1, 2, 0, 3)) * attended, -1)
    prefix_weights = jnp.exp(prefix_scores - log_total[..., None])
    prefix_dw = jnp.einsum(
        "prhd,jhd->rhpj", grad_heads, prefix_values, preferred_element_type=jnp.float32
    )
    prefix_slopes = (prefix_weights * (prefix_dw - slope_base[..., None])).astype(jnp.bfloat16)
    grad_query = score_scale * jnp.einsum(
        "rhpj,jhd->prhd", prefix_slopes, prefix_keys, preferred_element_type=jnp.float32
    )
    grad_pkeys = score_scale * jnp.einsum(
        "rhpj,prhd->jhd", prefix_slopes, query_heads, preferred_element_type=jnp.float32
    )
    grad_pvalues = jnp.einsum(
        "rhpj,prhd->jhd",
        prefix_weights.astype(jnp.bfloat16),
        grad_heads,
        preferred_element_type=jnp.float32,
    )
    grad_prefix_kv = jnp.concatenate(
        [grad_pkeys.reshape(-1, width), grad_pvalues.reshape(-1, width)], -1
    )
    keys_all, values_all, segs_all = (
        lax.all_gather(keys, "blk", axis=0, tiled=True),
        lax.all_gather(values, "blk", axis=0, tiled=True),
        lax.all_gather(segment_ids, "blk", axis=0, tiled=True),
    )
    length = keys_all.shape[0]
    stride = math.gcd(length, 512)

    def backward_step(grad_q, block_index):
        offset = block_index * stride
        key_block = lax.dynamic_slice_in_dim(keys_all, offset, stride, 0)
        value_block = lax.dynamic_slice_in_dim(values_all, offset, stride, 0)
        seg_block = lax.dynamic_slice_in_dim(segs_all, offset, stride, 0)
        key_pos = offset + jnp.arange(stride)
        weights_low, slopes = block_grads(
            query_heads,
            grad_heads,
            log_total,
            slope_base,
            own_pos,
            segment_ids,
            key_block,
            value_block,
            key_pos,
            seg_block,
            score_scale,
        )
        grad_q = grad_q + score_scale * jnp.einsum(
            "rhpk,krhd->prhd", slopes, split_heads(key_block), preferred_element_type=jnp.float32
        )
        key_term = score_scale * jnp.einsum(
            "rhpk,prhd->krhd", slopes, query_heads, preferred_element_type=jnp.float32
        )
        value_term = jnp.einsum(
            "rhpk,prhd->krhd", weights_low, grad_heads, preferred_element_type=jnp.float32
        )
        return (
            grad_q,
            (
                key_term.reshape(stride, row_count, width),
                value_term.reshape(stride, row_count, width),
            ),
        )

    grad_query, (key_terms, value_terms) = lax.scan(
        backward_step, grad_query, jnp.arange(length // stride)
    )
    key_terms = key_terms.reshape(length, row_count, width)
    value_terms = value_terms.reshape(length, row_count, width)
    grad_keys, grad_values = (
        lax.psum_scatter(key_terms, "blk", scatter_dimension=0, tiled=True),
        lax.psum_scatter(value_terms, "blk", scatter_dimension=0, tiled=True),
    )
    grad_proj = jnp.concatenate(
        [
            grad_query.reshape(flat_rows, width).astype(jnp.bfloat16),
            grad_keys.reshape(flat_rows, width).astype(jnp.bfloat16),
            grad_values.reshape(flat_rows, width).astype(jnp.bfloat16),
        ],
        -1,
    )
    grad_norm_one = jnp.dot(grad_proj, w_qkv.T, preferred_element_type=jnp.float32)
    _, norm_one_back = jax.vjp(partial(layer_norm, gain=ln1_gain, bias=ln1_bias), inputs)
    input_grad = (grad_middle + norm_one_back(grad_norm_one)[0]).reshape(pos_dev, row_count, width)
    _, adapter_back = jax.vjp(adapter, prefix_embed, w_mlp1, b_mlp1, w_mlp2, b_mlp2)
    local_grads = adapter_back(grad_prefix_kv)
    summed = lax.psum(
        (local_grads[0], local_grads[1], local_grads[2], local_grads[3], local_grads[4]),
        ("seq", "blk"),
    )
    return (block_out, input_grad, summed[0], summed[1], summed[2], summed[3], summed[4], log_total)


def solution(mesh):
    placed = (
        P("blk", "seq", None),
        P("blk", "seq"),
        P(),
        P(),
        P(),
        P(),
        P(),
        P(),
        P(),
        P(),
        P(),
        P(),
        P(),
        P(),
        P(),
        P("blk", "seq", None),
    )
    return jax.shard_map(
        body,
        mesh=mesh,
        in_specs=placed,
        out_specs=(
            P("blk", "seq", None),
            P("blk", "seq", None),
            P(),
            P(),
            P(),
            P(),
            P(),
            P("seq", None, "blk"),
        ),
        check_vma=False,
    )
```

profile of v0, /device:TPU:1, one launch (start us, length us, event | category | flops | bytes accessed | tf_op | source)
XLA Modules:
  0.0 634.5 jit_solution(9837110971770974125)
XLA Ops:
  7.2 1.4 convert_reduce_fusion
  8.8 1.4 multiply_reduce_fusion.3
  10.2 1.0 reshape.230
  11.4 0.5 copy-done.45
  11.9 0.5 copy-done.41
  12.5 3.9 convolution_convert_fusion
  16.5 0.8 reshape.233
  17.3 0.8 reshape.235
  18.2 18.0 %all-gather = s32[8,64,2]{1,2,0:T(2,128)S(1)} all-gather(s32[1,64,2]{1,2,0:T(2,128)S(1)} %bitcast.139), channel_id=1, replica_groups=mesh['seq'=4,'blk'=8] {'blk'}, dimensions={0}, use_global_device_ids=true | all-gather | bytes 4608 | tf_op jit(solution)/shard_map/all_gather | solution.py:121
  36.3 0.7 reshape.245
  36.9 2.7 fusion.39
  39.7 4.3 fusion.3
  44.3 0.8 reshape.238
  45.4 1.4 copy.138
  46.8 1.2 dynamic-slice
  48.7 0.6 fusion.108
  49.3 0.7 fusion.76
  50.1 0.8 compare_and_fusion
  50.9 1.3 fusion.80
  52.2 15.5 %all-gather.4.cloned.1.call-done = bf16[512,2,1024]{2,1,0:T(2,128)(2,1)} async-done(((bf16[64,2,1024]{2,1,0:T(2,128)(2,1)}), bf16[512,2,1024]{2,1,0:T(2,128)(2,1)}) %all-gather.4.cloned.1.call-update) | async-done | bytes 2097168 | tf_op jit(solution)/shard_map/all_gather | solution.py:119
  67.7 6.1 copy.117
  73.8 2.7 fusion.4
  76.6 2.6 fusion
  79.2 0.6 log_add_fusion
  79.9 37.8 %all-gather.6.cloned.1.call-done = bf16[512,2,1024]{2,1,0:T(2,128)(2,1)} async-done(((bf16[64,2,1024]{2,1,0:T(2,128)(2,1)}), bf16[512,2,1024]{2,1,0:T(2,128)(2,1)}) %all-gather.6.cloned.1.call-update) | async-done | bytes 2097168 | tf_op jit(solution)/shard_map/all_gather | solution.py:120
  117.7 6.3 copy.122
  124.0 4.5 fusion.45
  128.5 1.8 copy.125
  130.3 1.1 convert_element_type.86
  131.3 1.6 fusion.109
  133.2 0.5 copy-done.47
  133.7 0.5 copy-done.37
  134.3 4.9 fusion.66
  139.2 1.3 copy-done.15
  140.5 2.3 fusion.32
  142.8 13.9 %multiply_reduce_fusion.1 = (f32[128]{0:T(128)}, f32[128,1024]{1,0:T(8,128)}) fusion(f32[128,1024]{1,0:T(8,128)S(1)} %get-tuple-element.139, f32[128]{0:T(128)} %copy-done.34, f32[1024]{0:T(1024)} %param.22, bf16[1024,4096]{1,0:T(8,128)(2,1)} %param.24, f32[128,4096]{1,0:T(8,128)} %copy-done.15, bf16[128,1024]{1,0:T(8,128)(2,1)} %reshape.238, ...), kind=kOutput, calls=%fused_computation.89 | convolution fusion | flops 2158493696 | bytes 20190208 | tf_op jit(solution)/shard_map/dot_general | solution.py:166
  156.7 0.7 multiply_multiply_fusion.3
  157.4 1.3 fusion.104
  158.7 0.8 copy-done.10
  159.5 1.8 convolution_convert_fusion.1
  161.7 0.6 copy.129
  162.3 1.4 copy.140
  163.7 2.0 fusion.56
  166.2 4.5 fusion.12
  170.8 1.6 multiply_convert_fusion
  172.4 0.7 fusion.24
  173.1 0.3 copy-done.12
  173.4 2.7 convolution_multiply_fusion
  176.7 5.7 fusion.110
  182.4 5.1 fusion.114
  187.6 0.8 reshape.237
  188.4 7.4 %copy.141 = f32[512,2,1024]{2,1,0:T(2,128)} copy(f32[512,2,1024]{0,2,1:T(8,128)} %bitcast.127) | data formatting | bytes 8388608 | tf_op jit(solution)/shard_map/reshape | solution.py:243
  195.8 0.4 fusion.31
  196.2 0.8 copy.137
  197.3 7.3 %copy.139 = f32[512,2,1024]{2,1,0:T(2,128)} copy(f32[512,2,1024]{0,2,1:T(8,128)} %bitcast.128) | data formatting | bytes 8388608 | tf_op jit(solution)/shard_map/reshape | solution.py:242
  204.7 3.2 convolution_bitcast_fusion
  207.8 361.9 %all-reduce.9 = (bf16[512,2,1024]{2,1,0:T(2,128)(2,1)}, bf16[512,2,1024]{2,1,0:T(2,128)(2,1)}) all-reduce(f32[512,2,1024]{2,1,0:T(2,128)} %copy.141, f32[512,2,1024]{2,1,0:T(2,128)} %copy.139), channel_id=3, replica_groups=mesh['seq'=4,'blk'=8] {'blk'}, use_global_device_ids=true, to_apply=%region_12.13.clone | all-reduce | flops 2097152 | bytes 12582912
  569.8 1.4 dynamic-slice_convert_fusion
  571.5 5.1 multiply_reduce_fusion
  577.2 1.1 reshape.241
  578.3 1.8 fusion.113
  580.1 39.7 %all-reduce.2 = (f32[10,1024]{1,0:T(8,128)}, f32[512]{0:T(512)}, f32[2048]{0:T(1024)}) all-reduce(f32[10,1024]{1,0:T(8,128)S(1)} %fusion.113, f32[512]{0:T(512)S(1)} %get-tuple-element.144, f32[2048]{0:T(1024)S(1)} %reduce_sum.148), channel_id=1, replica_groups=mesh['seq'=4,'blk'=8] {'seq','blk'}, use_global_device_ids=true, to_apply=%region_15.16 | all-reduce | flops 12800 | bytes 102400 | tf_op jit(solution)/shard_map/psum | solution.py:261
  619.8 2.9 copy.146
  622.6 4.8 copy.210
  (141 shorter events, 4.0 us)
Async XLA Ops:
  7.2 124.2 %copy-start = (bf16[1024,1024]{1,0:T(8,128)(2,1)S(1)}, bf16[1024,1024]{1,0:T(8,128)(2,1)}, u32[]{:S(2)}) copy-start(bf16[1024,1024]{1,0:T(8,128)(2,1)} %param.21) | copy-start | bytes 6291460
  7.2 60.5 %all-gather.4.cloned.1.call-start = ((), (), s32[]{:S(2)}) async-start(), calls=%async_computation | async-start | bytes 2359296 | tf_op jit(solution)/shard_map/all_gather | solution.py:119
  8.7 2.6 copy-start.35
  11.4 0.6 copy-start.45
  11.9 0.5 copy-start.41
  16.4 1.9 copy-start.39
  16.4 20.6 %copy-start.23 = (f32[10,1024]{1,0:T(8,128)S(1)}, f32[10,1024]{1,0:T(8,128)}, u32[]{:S(2)}) copy-start(f32[10,1024]{1,0:T(8,128)} %param.26) | copy-start | bytes 122884
  16.4 20.6 %copy-start.40 = (f32[512]{0:T(512)S(1)}, f32[512]{0:T(512)}, u32[]{:S(2)}) copy-start(f32[512]{0:T(512)} %param.28) | copy-start | bytes 6148
  16.5 23.2 %copy-start.33 = (f32[2048]{0:T(1024)S(1)}, f32[2048]{0:T(1024)}, u32[]{:S(2)}) copy-start(f32[2048]{0:T(1024)} %param.30) | copy-start | bytes 24580
  17.3 100.4 %all-gather.6.cloned.1.call-start = ((), (), s32[]{:S(2)}) async-start(), calls=%async_computation.1 | async-start | bytes 2359296 | tf_op jit(solution)/shard_map/all_gather | solution.py:120
  18.2 601.6 %all-reduce.8.cloned.1.call-start = ((), (), s32[]{:S(2)}) async-start(), calls=%async_computation.2 | async-start | bytes 12582912 | tf_op jit(solution)/shard_map/psum | solution.py:261
  39.7 4.3 copy-start.18
  39.7 4.6 copy-start.25
  45.4 28.4 %copy-start.8 = (bf16[64,2,16,64]{3,2,1,0:T(8,128)(2,1)}, bf16[64,2,16,64]{3,2,1,0:T(8,128)(2,1)S(1)}, u32[]{:S(2)}) copy-start(bf16[64,2,16,64]{3,2,1,0:T(8,128)(2,1)S(1)} %reshape_reshape.6) | copy-start | bytes 786436
  49.2 1.6 copy-start.16
  73.8 2.7 copy-start.17
  76.5 2.7 copy-start.2
  76.6 2.6 copy-start.28
  131.3 3.0 copy-start.31
  131.3 3.0 copy-start.32
  131.3 9.1 %slice-start = ((s8[8388608]{0:T(1024)(128)(4,1)}), s8[4194304]{0:T(1024)(128)(4,1)S(1)}, s32[]{:S(2)}) async-start(s8[8388608]{0:T(1024)(128)(4,1)} %bitcast.140), calls=%async_computation.3 | async-start | bytes 8388608
  133.0 0.8 copy-start.34
  133.2 0.5 copy-start.47
  133.7 0.5 copy-start.37
  134.3 6.2 slice-start.1
  139.2 1.3 copy-start.15
  158.7 0.8 copy-start.10
  158.7 2.6 copy-start.43
  161.3 2.4 copy-start.22
  161.3 2.4 copy-start.13
  161.3 2.4 copy-start.29
  161.3 2.4 copy-start.30
  163.7 7.1 %copy-start.27 = (f32[2,16,64]{2,1,0:T(8,128)}, f32[2,16,64]{2,1,0:T(8,128)S(1)}, u32[]{:S(2)}) copy-start(f32[2,16,64]{2,1,0:T(8,128)S(1)} %copy.132) | copy-start | bytes 24580
  163.7 2.5 copy-start.3
  165.9 10.2 %copy-start.20 = (bf16[2,16,64,10]{2,3,0,1:T(8,128)(2,1)}, bf16[2,16,64,10]{2,3,0,1:T(8,128)(2,1)S(1)}, u32[]{:S(2)}) copy-start(bf16[2,16,64,10]{2,3,0,1:T(8,128)(2,1)S(1)} %fusion.36) | copy-start | bytes 122884
  166.2 4.5 copy-start.4
  166.2 4.5 copy-start.7
  170.7 1.6 copy-start.6
  172.4 1.0 copy-start.12
  173.4 2.7 copy-start.9
  173.4 3.3 copy-start.19
  182.4 5.1 copy-start.26
  188.4 7.4 %copy-start.21 = (bf16[2,16,64,10]{2,3,0,1:T(8,128)(2,1)S(1)}, bf16[2,16,64,10]{2,3,0,1:T(8,128)(2,1)}, u32[]{:S(2)}) copy-start(bf16[2,16,64,10]{2,3,0,1:T(8,128)(2,1)} %copy-done.20) | copy-start | bytes 122884
  197.3 7.3 %copy-start.24 = (f32[10,1024]{1,0:T(8,128)S(1)}, f32[10,1024]{1,0:T(8,128)}, u32[]{:S(2)}) copy-start(f32[10,1024]{1,0:T(8,128)} %param.26) | copy-start | bytes 122884
  569.8 1.6 copy-start.36
  569.8 1.6 copy-start.38
  571.4 5.2 copy-start.46
  571.4 5.2 copy-start.42
  571.5 5.5 copy-start.11
  571.5 5.5 copy-start.14
  571.5 5.5 copy-start.44
  576.7 1.6 copy-start.5
  622.6 4.9 copy-start.1
Sparse Core Ops, SparseCore 0:
  17.4 50.2 all-gather.3
  69.8 47.8 all-gather.5
  208.0 247.6 all-reduce.7
where the time goes:
time: 645 us; the launch traced here: 634 us
  blocking collectives  420 us (65%)
  matrix products  76 us (12%)
  local copies, waits for them, and re-layouts  57.4 us (9%)
  waiting for transfers between devices  53.4 us (8%)
  between operations  15.6 us (2%)
  other arithmetic  12.4 us (2%)
    unnamed x1, blocking collectives  362 us
    psum x1, blocking collectives, body(): lax.psum((local_grads[0], local_grads[1], local_grads[2], local_grads[3],...  39.7 us
    all_gather x1, waiting for transfers between devices, body(): value_shards = lax.all_gather(values, 'blk', axis=0, tiled=True)  37.8 us
    all_gather x1, blocking collectives, body(): seg_shards = lax.all_gather(segment_ids, 'blk', axis=0, tiled=True)  18 us
    all_gather x1, waiting for transfers between devices, body(): key_shards = lax.all_gather(keys, 'blk', axis=0, tiled=True)  15.5 us
    dot_general x3, matrix products, adapter(): return jnp.dot(inner_act, w_mlp2, precision=HIGH) + b_mlp2  15.1 us
    unnamed x105, local copies, waits for them, and re-layouts  14.5 us
    dot_general x1, matrix products, body(): jnp.dot(grad_pre, w_fc.T, preferred_element_type=jnp.float32)  13.9 us
  transfers between devices with their start and end apart: 3, of which 2 were waited for; matrix products, arithmetic and copies ran while one was open for 6% of the time, Pallas kernels for 0%

commit v1 on v0

--- a/solution.py
+++ b/solution.py
@@ -4,6 +4,8 @@
 import jax
 import jax.numpy as jnp
 from jax import lax
+from jax.experimental import pallas as pl
+from jax.experimental.pallas import tpu as pltpu
 from jax.sharding import PartitionSpec as P
 
 HEADS = 16
@@ -70,7 +72,7 @@
     return (weights.astype(jnp.bfloat16), slopes)
 
 
-def body(
+def body_plain(
     tokens,
     segment_ids,
     ln1_gain,
@@ -265,7 +267,608 @@
     return (block_out, input_grad, summed[0], summed[1], summed[2], summed[3], summed[4], log_total)
 
 
+F32 = jnp.float32
+BF16 = jnp.bfloat16
+LANES = 128
+PRE_ROWS = 16
+MIB = 1 << 20
+PRE = 10
+
+
+def nn(left, right):
+    return jnp.dot(left, right, preferred_element_type=F32)
+
+
+def nt(left, right):
+    return lax.dot_general(left, right, (((1,), (1,)), ((), ())), preferred_element_type=F32)
+
+
+def norm_parts(value_in):
+    average = jnp.mean(value_in, axis=-1, keepdims=True)
+    centered = value_in - average
+    variance = jnp.mean(centered * centered, axis=-1, keepdims=True)
+    inverse = lax.rsqrt(variance + EPS)
+    return centered * inverse, inverse
+
+
+def norm_back(unit, inverse, gain, grad):
+    scaled = grad * gain
+    first = jnp.mean(scaled, axis=-1, keepdims=True)
+    second = jnp.mean(scaled * unit, axis=-1, keepdims=True)
+    return inverse * (scaled - first - unit * second)
+
+
+def iota(shape, dim):
+    return lax.broadcasted_iota(jnp.int32, shape, dim)
+
+
+def place():
+    blk = lax.axis_index("blk")
+    return (blk // 2) % 2, lax.axis_index("seq") % 2, blk % 2
+
+
+def positions(index, half, row, core, y_at):
+    upper = (index >= half).astype(jnp.int32)
+    slot = upper + row - 2 * upper * row
+    block = (2 * core + slot) * 2 + y_at
+    return block * half + index - upper * half
+
+
+def members(core, y_at):
+    return ((core, y_at), (1 - core, y_at), (core, 1 - y_at), (1 - core, 1 - y_at))
+
+
+def all_positions(shape, dim, half, row, core, y_at):
+    part = tuple(2 * half if d == dim else n for d, n in enumerate(shape))
+    return jnp.concatenate(
+        [positions(iota(part, dim), half, row, c, y) for c, y in members(core, y_at)], dim
+    )
+
+
+def vmem():
+    return pl.BlockSpec(memory_space=pltpu.VMEM)
+
+
+def hbm():
+    return pl.BlockSpec(memory_space=pl.ANY)
+
+
+def project_kernel(count, *refs):
+    messages, (gain, bias, weight, out, marks, normed) = refs[:count], refs[count:]
+    half, width = messages[0].shape[0], normed.shape[1]
+
+    @pl.when(pl.program_id(0) == 0)
+    def _():
+        for i, message in enumerate(messages):
+            rows = pl.ds(i * half, half)
+            unit, _ = norm_parts(message[:, :width].astype(F32))
+            normed[rows] = (unit * gain[...] + bias[...]).astype(BF16)
+            marks[rows] = message[:, width:]
+
+    out[...] = nn(normed[...], weight[...]).astype(BF16)
+
+
+def project(messages, gain, bias, weight, step=1024):
+    count, (half, wide) = len(messages), messages[0].shape
+    width, columns = weight.shape
+    rows = count * half
+    return pl.pallas_call(
+        partial(project_kernel, count),
+        grid=(columns // step,),
+        in_specs=[pl.BlockSpec((half, wide), lambda i: (0, 0))] * count
+        + [pl.BlockSpec((1, width), lambda i: (0, 0))] * 2
+        + [pl.BlockSpec((width, step), lambda i: (0, i))],
+        out_specs=[
+            pl.BlockSpec((rows, step), lambda i: (0, i)),
+            pl.BlockSpec((rows, LANES), lambda i: (0, 0)),
+        ],
+        out_shape=[
+            jax.ShapeDtypeStruct((rows, columns), BF16),
+            jax.ShapeDtypeStruct((rows, LANES), BF16),
+        ],
+        scratch_shapes=[pltpu.VMEM((rows, width), BF16)],
+        compiler_params=pltpu.CompilerParams(vmem_limit_bytes=30 * MIB),
+        cost_estimate=pl.CostEstimate(
+            flops=2 * rows * width * columns, bytes_accessed=2 * width * columns, transcendentals=0
+        ),
+        name="project",
+    )(*messages, gain[None], bias[None], weight)
+
+
+def head_mask(rows):
+    return iota((rows, LANES), 1) < HEAD
+
+
+def two_heads(pair, low):
+    zero = jnp.zeros_like(pair)
+    return jnp.concatenate([jnp.where(low, pair, zero), jnp.where(low, zero, pair)], 0)
+
+
+def join_heads(stacked, low):
+    rows = stacked.shape[0] // 2
+    return jnp.where(low, stacked[:rows], stacked[rows:])
+
+
+def picks(rows, pair, first, value):
+    lane = iota((rows, LANES), 1)
+    inside = jnp.logical_and(lane >= first, lane < first + 3 * HEADS)
+    parts = [
+        jnp.where(jnp.logical_and(inside, lane % HEADS == 2 * pair + i), value, 0.0) for i in range(2)
+    ]
+    return jnp.concatenate(parts, 0)
+
+
+def three_parts(value_in, first):
+    lane = iota(value_in.shape, 1)
+    high = value_in.astype(BF16).astype(F32)
+    rest = value_in - high
+    middle = rest.astype(BF16).astype(F32)
+    low = rest - middle
+    part = (lane - first) // HEADS
+    chosen = jnp.where(part == 0, high, jnp.where(part == 1, middle, low))
+    inside = jnp.logical_and(lane >= first, lane < first + 3 * HEADS)
+    return jnp.where(inside, chosen, 0.0)
+
+
+def key_bias(marks_own, marks_a, marks_b, half):
+    row, core, y_at = place()
+    rows = 2 * half
+    own = positions(iota((rows, 1), 0), half, row, core, y_at)
+    other = all_positions((1, 8 * half), 1, half, row, core, y_at)
+    same = nt(marks_own, jnp.concatenate([marks_a, marks_b], 0))
+    visible = jnp.logical_and(same > 0.5, other <= own)
+    token_bias = jnp.where(visible, 0.0, NEG)
+    prefix_bias = jnp.where(iota((rows, LANES), 1) < PRE, 0.0, NEG)
+    return jnp.concatenate([token_bias, prefix_bias], 1)
+
+
+def with_prefix(part_a, part_b, prefix):
+    pad = jnp.zeros((LANES - prefix.shape[0], prefix.shape[1]), prefix.dtype)
+    return jnp.concatenate([part_a, part_b, prefix, pad], 0)
+
+
+def middle_kernel(
+    qkv_a,
+    qkv_b,
+    marks_a,
+    marks_b,
+    prefix_kv,
+    own_0,
+    own_1,
+    cot_0,
+    cot_1,
+    gain,
+    bias,
+    w_out,
+    w_fc,
+    w_proj,
+    back_0,
+    back_1,
+    grad_out_heads,
+    grad_middle,
+    v_out,
+    v_fc,
+    v_proj,
+    sems,
+    scores_bias,
+    attended,
+    stats,
+    middle,
+    normed,
+    total,
+    grad_norm,
+    cot,
+):
+    half, rows = own_0.shape[0], 2 * own_0.shape[0]
+    width = middle.shape[1]
+    steps, step = v_fc.shape[0], v_fc.shape[2]
+    copies = [pltpu.make_async_copy(w_out, v_out, sems.at[0])]
+    for i in range(steps):
+        span = pl.ds(i * step, step)
+        copies.append(pltpu.make_async_copy(w_fc.at[:, span], v_fc.at[i], sems.at[1 + 2 * i]))
+        copies.append(pltpu.make_async_copy(w_proj.at[span], v_proj.at[i], sems.at[2 + 2 * i]))
+    for copy in copies:
+        copy.start()
+
+    scores_bias[...] = key_bias(marks_a[:rows], marks_a[...], marks_b[...], half)
+    low = head_mask(rows)
+    lane = iota((rows, LANES), 1)
+    stats[...] = jnp.zeros_like(stats)
+
+    def attend(pair, carry):
+        at = pl.ds(pl.multiple_of(pair * LANES, LANES), LANES)
+        at_k = pl.ds(pl.multiple_of(width + pair * LANES, LANES), LANES)
+        at_v = pl.ds(pl.multiple_of(2 * width + pair * LANES, LANES), LANES)
+        query = two_heads(qkv_a[:rows, at] * jnp.asarray(HEAD**-0.5, BF16), low)
+        keys = with_prefix(qkv_a[:, at_k], qkv_b[:, at_k], prefix_kv[:, at])
+        values = with_prefix(qkv_a[:, at_v], qkv_b[:, at_v], prefix_kv[:, at_k])
+        scores = nt(query, keys)
+        mask = scores_bias[...]
+        scores = scores + jnp.concatenate([mask, mask], 0)
+        top = jnp.max(scores, -1, keepdims=True)
+        weights = jnp.exp(scores - top)
+        denominator = jnp.sum(weights, -1, keepdims=True)
+        mixed = nn(weights.astype(BF16), values) / denominator
+        attended[:, at] = join_heads(mixed, low)
+        log_total = top + jnp.log(denominator)
+        inside = lane < 3 * HEADS
+        for i in range(2):
+            here = jnp.logical_and(inside, lane % HEADS == 2 * pair + i)
+            stats[...] = jnp.where(here, log_total[i * rows : (i + 1) * rows], stats[...])
+        return carry
+
+    lax.fori_loop(0, HEADS // 2, attend, 0)
+
+    copies[0].wait()
+    inputs = jnp.concatenate([own_0[:, :width], own_1[:, :width]], 0).astype(F32)
+    middle[...] = inputs + nn(attended[...].astype(BF16), v_out[...])
+    unit, _ = norm_parts(middle[...])
+    normed[...] = (unit * gain[...] + bias[...]).astype(BF16)
+    cot[...] = jnp.concatenate([cot_0[...], cot_1[...]], 0)
+    total[...] = middle[...]
+    grad_norm[...] = jnp.zeros_like(grad_norm)
+
+    def feed(i, carry):
+        for which in (0, 1):
+            pltpu.make_async_copy(
+                (v_fc, v_proj)[which].at[i], (v_fc, v_proj)[which].at[i], sems.at[1 + 2 * i + which]
+            ).wait()
+        fc, proj = v_fc[i], v_proj[i]
+        pre = nn(normed[...], fc)
+        grad_act = nt(cot[...], proj)
+        cubic = 0.044715 * pre * pre
+        curve = jnp.tanh(math.sqrt(2 / math.pi) * pre * (1.0 + cubic))
+        act = 0.5 * pre * (1.0 + curve)
+        slope = 0.5 * (1.0 + curve) + 0.5 * math.sqrt(2 / math.pi) * pre * (1.0 - curve * curve) * (
+            1.0 + 3.0 * cubic
+        )
+        grad_pre = (grad_act * slope).astype(BF16)
+        total[...] += nn(act.astype(BF16), proj)
+        grad_norm[...] += nt(grad_pre, fc)
+        return carry
+
+    lax.fori_loop(0, steps, feed, 0)
+
+    out = total[...].astype(BF16)
+    back_0[:, :width] = out[:half]
+    back_1[:, :width] = out[half:]
+    unit, inverse = norm_parts(middle[...])
+    grads = cot[...].astype(F32) + norm_back(unit, inverse, gain[...], grad_norm[...])
+    grad_middle[...] = grads
+    grad_heads = nt(grads.astype(BF16), v_out[...]).astype(BF16)
+    grad_out_heads[:, :width] = grad_heads
+    product = grad_heads.astype(F32) * attended[...]
+    ones = jnp.where(
+        jnp.logical_and(
+            iota((width, LANES), 0) // HEAD == iota((width, LANES), 1) % HEADS,
+            jnp.logical_and(
+                iota((width, LANES), 1) >= 3 * HEADS, iota((width, LANES), 1) < 6 * HEADS
+            ),
+        ),
+        1.0,
+        0.0,
+    ).astype(BF16)
+    bases = jnp.zeros((rows, LANES), F32)
+    for _ in range(3):
+        part = product.astype(BF16)
+        bases = bases + nn(part, ones)
+        product = product - part.astype(F32)
+    marks = three_parts(stats[...], 0) + three_parts(bases, 3 * HEADS)
+    marks = marks.astype(BF16)
+    grad_out_heads[:, width:] = marks
+    back_0[:, width:] = marks[:half]
+    back_1[:, width:] = marks[half:]
+
+
+def middle_part(qkv_a, qkv_b, marks_a, marks_b, prefix_kv, own, cots, gain, bias, w_out, w_fc, w_proj):
+    half, width = cots[0].shape
+    rows = 2 * half
+    hidden = w_fc.shape[1]
+    steps = 8
+    step = hidden // steps
+    wide = width + LANES
+    return pl.pallas_call(
+        middle_kernel,
+        in_specs=[vmem()] * 11 + [hbm()] * 3,
+        out_specs=[vmem()] * 4,
+        out_shape=[
+            jax.ShapeDtypeStruct((half, wide), BF16),
+            jax.ShapeDtypeStruct((half, wide), BF16),
+            jax.ShapeDtypeStruct((rows, wide), BF16),
+            jax.ShapeDtypeStruct((rows, width), F32),
+        ],
+        scratch_shapes=[
+            pltpu.VMEM((width, width), BF16),
+            pltpu.VMEM((steps, width, step), BF16),
+            pltpu.VMEM((steps, step, width), BF16),
+            pltpu.SemaphoreType.DMA((1 + 2 * steps,)),
+            pltpu.VMEM((rows, 4 * rows + LANES), F32),
+            pltpu.VMEM((rows, width), F32),
+            pltpu.VMEM((rows, LANES), F32),
+            pltpu.VMEM((rows, width), F32),
+            pltpu.VMEM((rows, width), BF16),
+            pltpu.VMEM((rows, width), F32),
+            pltpu.VMEM((rows, width), F32),
+            pltpu.VMEM((rows, width), BF16),
+        ],
+        compiler_params=pltpu.CompilerParams(vmem_limit_bytes=48 * MIB),
+        cost_estimate=pl.CostEstimate(
+            flops=2 * rows * width * (4 * hidden + 2 * width),
+            bytes_accessed=2 * width * (2 * hidden + width),
+            transcendentals=rows * hidden,
+        ),
+        name="middle",
+    )(
+        qkv_a, qkv_b, marks_a, marks_b, prefix_kv, *own, *cots, gain[None], bias[None], w_out, w_fc, w_proj
+    )
+
+
+def key_grads(keys, values, queries, grads, marks, pair, low, mask):
+    rows = keys.shape[0]
+    scale = jnp.asarray(HEAD**-0.5, BF16)
+    left = jnp.concatenate(
+        [two_heads(keys * scale, low), picks(rows, pair, 0, -1.0).astype(BF16)], 1
+    )
+    scores = nt(left, jnp.concatenate([queries, marks], 1))
+    weights = jnp.exp(scores + jnp.concatenate([mask, mask], 0))
+    left = jnp.concatenate(
+        [two_heads(values, low), picks(rows, pair, 3 * HEADS, -1.0).astype(BF16)], 1
+    )
+    slopes = weights * nt(left, jnp.concatenate([grads, marks], 1))
+    key_grad = nn(slopes.astype(BF16), queries)
+    value_grad = nn(weights.astype(BF16), grads)
+    return join_heads(key_grad, low) * HEAD**-0.5, join_heads(value_grad, low)
+
+
+def prefix_kernel(qkv_a, grads, prefix_kv, out):
+    rows, width = grads.shape[0], grads.shape[1] - LANES
+    count = prefix_kv.shape[0]
+    low = head_mask(count)
+    mask = jnp.where(iota((count, rows), 0) < PRE, 0.0, NEG)
+    marks = grads[:, width:]
+
+    def step(pair, carry):
+        at = pl.ds(pl.multiple_of(pair * LANES, LANES), LANES)
+        at_v = pl.ds(pl.multiple_of(width + pair * LANES, LANES), LANES)
+        key_grad, value_grad = key_grads(
+            prefix_kv[:, at], prefix_kv[:, at_v], qkv_a[:rows, at], grads[:, at], marks, pair, low, mask
+        )
+        out[:, at] = key_grad[:PRE]
+        out[:, at_v] = value_grad[:PRE]
+        return carry
+
+    lax.fori_loop(0, HEADS // 2, step, 0)
+
+
+def prefix_part(qkv_a, grads, prefix_kv):
+    return pl.pallas_call(
+        prefix_kernel,
+        in_specs=[vmem()] * 3,
+        out_specs=vmem(),
+        out_shape=jax.ShapeDtypeStruct((PRE, prefix_kv.shape[1]), F32),
+        compiler_params=pltpu.CompilerParams(vmem_limit_bytes=16 * MIB),
+        cost_estimate=pl.CostEstimate(flops=1 << 29, bytes_accessed=1 << 20, transcendentals=1 << 16),
+        name="prefix",
+    )(qkv_a, grads, prefix_kv)
+
+
+def query_kernel(qkv_a, qkv_b, marks_a, marks_b, prefix_kv, grads, weight, out, scores_bias, grad_query):
+    rows, width = grad_query.shape
+    scores_bias[...] = key_bias(marks_a[:rows], marks_a[...], marks_b[...], rows // 2)
+    low = head_mask(rows)
+    marks = grads[:, width:]
+    marks_twice = jnp.concatenate([marks, marks], 0)
+    ones = jnp.ones((4 * rows + LANES, LANES), BF16)
+
+    def step(pair, carry):
+        at = pl.ds(pl.multiple_of(pair * LANES, LANES), LANES)
+        at_k = pl.ds(pl.multiple_of(width + pair * LANES, LANES), LANES)
+        at_v = pl.ds(pl.multiple_of(2 * width + pair * LANES, LANES), LANES)
+        keys = with_prefix(qkv_a[:, at_k], qkv_b[:, at_k], prefix_kv[:, at])
+        values = with_prefix(qkv_a[:, at_v], qkv_b[:, at_v], prefix_kv[:, at_k])
+        query = two_heads(qkv_a[:rows, at] * jnp.asarray(HEAD**-0.5, BF16), low)
+        tops = marks_twice * picks(rows, pair, 0, -1.0).astype(BF16)
+        scores = nt(jnp.concatenate([query, tops], 1), jnp.concatenate([keys, ones], 1))
+        mask = scores_bias[...]
+        weights = jnp.exp(scores + jnp.concatenate([mask, mask], 0))
+        bases = marks_twice * picks(rows, pair, 3 * HEADS, -1.0).astype(BF16)
+        left = jnp.concatenate([two_heads(grads[:, at], low), bases], 1)
+        slopes = weights * nt(left, jnp.concatenate([values, ones], 1))
+        grad = join_heads(nn(slopes.astype(BF16), keys), low)
+        grad_query[:, at] = (grad * HEAD**-0.5).astype(BF16)
+        return carry
+
+    lax.fori_loop(0, HEADS // 2, step, 0)
+    out[...] = nt(grad_query[...], weight[...])
+
+
+def query_part(qkv_a, qkv_b, marks_a, marks_b, prefix_kv, grads, weight):
+    rows, width = grads.shape[0], grads.shape[1] - LANES
+    return pl.pallas_call(
+        query_kernel,
+        grid=(1,),
+        in_specs=[pl.BlockSpec(memory_space=pltpu.VMEM)] * 6 + [pl.BlockSpec((width, width), lambda i: (0, 0))],
+        out_specs=pl.BlockSpec(memory_space=pltpu.VMEM),
+        out_shape=jax.ShapeDtypeStruct((rows, width), F32),
+        scratch_shapes=[pltpu.VMEM((rows, 4 * rows + LANES), F32), pltpu.VMEM((rows, width), BF16)],
+        compiler_params=pltpu.CompilerParams(vmem_limit_bytes=30 * MIB),
+        cost_estimate=pl.CostEstimate(flops=1 << 32, bytes_accessed=1 << 23, transcendentals=1 << 20),
+        name="query",
+    )(qkv_a, qkv_b, marks_a, marks_b, prefix_kv, grads, weight)
+
+
+def final_kernel(
+    qkv_a,
+    qkv_b,
+    marks_a,
+    marks_b,
+    grads_0,
+    grads_1,
+    grads_2,
+    grads_3,
+    own_0,
+    own_1,
+    gain,
+    grad_middle,
+    grad_partial,
+    weight,
+    back_0,
+    back_1,
+    v_weight,
+    sem,
+    scores_bias,
+    grad_keys,
+):
+    half, rows = own_0.shape[0], 2 * own_0.shape[0]
+    width = grad_middle.shape[1]
+    load = pltpu.make_async_copy(weight.at[:, pl.ds(width, 2 * width)], v_weight, sem)
+    load.start()
+    row, core, y_at = place()
+    own = positions(iota((rows, 1), 0), half, row, core, y_at)
+    other = all_positions((1, 8 * half), 1, half, row, core, y_at)
+    same = nt(marks_a[:rows], jnp.concatenate([marks_a[...], marks_b[...]], 0))
+    visible = jnp.logical_and(same > 0.5, own <= other)
+    scores_bias[...] = jnp.where(visible, 0.0, NEG)
+    low = head_mask(rows)
+    blocks = (grads_0, grads_1, grads_2, grads_3)
+    marks = jnp.concatenate([g[:, width:] for g in blocks], 0)
+
+    def step(pair, carry):
+        at = pl.ds(pl.multiple_of(pair * LANES, LANES), LANES)
+        at_k = pl.ds(pl.multiple_of(width + pair * LANES, LANES), LANES)
+        at_v = pl.ds(pl.multiple_of(2 * width + pair * LANES, LANES), LANES)
+        queries = jnp.concatenate([qkv_a[:, at], qkv_b[:, at]], 0)
+        grads = jnp.concatenate([g[:, at] for g in blocks], 0)
+        key_grad, value_grad = key_grads(
+            qkv_a[:rows, at_k], qkv_a[:rows, at_v], queries, grads, marks, pair, low, scores_bias[...]
+        )
+        grad_keys[:, at] = key_grad.astype(BF16)
+        grad_keys[:, at_k] = value_grad.astype(BF16)
+        return carry
+
+    lax.fori_loop(0, HEADS // 2, step, 0)
+    load.wait()
+    grad_norm = grad_partial[...] + nt(grad_keys[...], v_weight[...])
+    inputs = jnp.concatenate([own_0[:, :width], own_1[:, :width]], 0).astype(F32)
+    unit, inverse = norm_parts(inputs)
+    out = (grad_middle[...] + norm_back(unit, inverse, gain[...], grad_norm)).astype(BF16)
+    back_0[...] = out[:half]
+    back_1[...] = out[half:]
+
+
+def final_part(qkv_a, qkv_b, marks_a, marks_b, grads, own, gain, grad_middle, grad_partial, weight):
+    rows, width = grad_middle.shape
+    half = rows // 2
+    return pl.pallas_call(
+        final_kernel,
+        in_specs=[vmem()] * 13 + [hbm()],
+        out_specs=[vmem()] * 2,
+        out_shape=[jax.ShapeDtypeStruct((half, width), BF16)] * 2,
+        scratch_shapes=[
+            pltpu.VMEM((width, 2 * width), BF16),
+            pltpu.SemaphoreType.DMA,
+            pltpu.VMEM((rows, 4 * rows), F32),
+            pltpu.VMEM((rows, 2 * width), BF16),
+        ],
+        compiler_params=pltpu.CompilerParams(vmem_limit_bytes=30 * MIB),
+        cost_estimate=pl.CostEstimate(flops=1 << 32, bytes_accessed=1 << 23, transcendentals=1 << 20),
+        name="final",
+    )(qkv_a, qkv_b, marks_a, marks_b, *grads, *own, gain[None], grad_middle, grad_partial, weight)
+
+
+def routes(k):
+    pairs = []
+    for seq in range(4):
+        for blk in range(8):
+            group, z_at, y_at = seq % 2, blk // 2, blk % 2
+            row = (z_at + k) % 2
+            pairs.append((seq * 8 + blk, (seq - group + z_at // 2) * 8 + (2 * group + row) * 2 + y_at))
+    return pairs
+
+
+def body_rows(
+    tokens,
+    segment_ids,
+    ln1_gain,
+    ln1_bias,
+    w_qkv,
+    w_out,
+    ln2_gain,
+    ln2_bias,
+    w_fc,
+    w_proj,
+    prefix_embed,
+    w_mlp1,
+    b_mlp1,
+    w_mlp2,
+    b_mlp2,
+    cotangent,
+):
+    half, _, width = tokens.shape
+    everyone = ("seq", "blk")
+    there = [routes(k) for k in range(2)]
+    back = [[(b, a) for a, b in pairs] for pairs in there]
+    swap_core = [(i, i ^ 1) for i in range(4)]
+    swap_y = [(i, i ^ 1) for i in range(8)]
+    odd = (lax.axis_index("blk") // 2) % 2 == 1
+
+    def sorted_rows(first, second):
+        return jnp.where(odd, second, first), jnp.where(odd, first, second)
+
+    marks = (segment_ids[:, :, None] == jnp.arange(LANES)[None, None]).astype(BF16)
+    marked = jnp.concatenate([tokens, marks], -1)
+    out_msgs = sorted_rows(marked[:, 0], marked[:, 1])
+    own = [lax.ppermute(m, everyone, there[k]) for k, m in enumerate(out_msgs)]
+    across = [lax.ppermute(m, "blk", swap_y) for m in own]
+    beside = [lax.ppermute(m, "seq", swap_core) for m in own]
+    cot_msgs = sorted_rows(cotangent[:, 0], cotangent[:, 1])
+    cots = [lax.ppermute(m, everyone, there[k]) for k, m in enumerate(cot_msgs)]
+    beyond = [lax.ppermute(m, "seq", swap_core) for m in across]
+
+    prefix_kv, adapter_back = jax.vjp(adapter, prefix_embed, w_mlp1, b_mlp1, w_mlp2, b_mlp2)
+    prefix_kv = jnp.pad(prefix_kv.astype(BF16), ((0, PRE_ROWS - prefix_kv.shape[0]), (0, 0)))
+
+    qkv_a, marks_a = project(own + beside, ln1_gain, ln1_bias, w_qkv)
+    qkv_b, marks_b = project(across + beyond, ln1_gain, ln1_bias, w_qkv)
+    back_0, back_1, grads, grad_middle = middle_part(
+        qkv_a, qkv_b, marks_a, marks_b, prefix_kv, own, cots, ln2_gain, ln2_bias, w_out, w_fc, w_proj
+    )
+    grads_y = lax.ppermute(grads, "blk", swap_y)
+    grads_c = lax.ppermute(grads, "seq", swap_core)
+    grads_yc = lax.ppermute(grads_y, "seq", swap_core)
+    home = [lax.ppermute(m, everyone, back[k]) for k, m in enumerate((back_0, back_1))]
+
+    grad_prefix_kv = prefix_part(qkv_a, grads, prefix_kv)
+    for axis, size, far in (("seq", 4, 2), ("blk", 8, 2), ("blk", 8, 4), ("blk", 8, 1), ("seq", 4, 1)):
+        grad_prefix_kv = grad_prefix_kv + lax.ppermute(
+            grad_prefix_kv, axis, [(i, i ^ far) for i in range(size)]
+        )
+    grad_partial = query_part(qkv_a, qkv_b, marks_a, marks_b, prefix_kv, grads, w_qkv)
+    final_0, final_1 = final_part(
+        qkv_a,
+        qkv_b,
+        marks_a,
+        marks_b,
+        (grads, grads_c, grads_y, grads_yc),
+        own,
+        ln1_gain,
+        grad_middle,
+        grad_partial,
+        w_qkv,
+    )
+    finals = [lax.ppermute(m, everyone, back[k]) for k, m in enumerate((final_0, final_1))]
+    summed = adapter_back(grad_prefix_kv)
+
+    home = sorted_rows(*home)
+    block_out = jnp.stack([m[:, :width] for m in home], 1)
+    logs = [m[:, width : width + 3 * HEADS].astype(F32).reshape(half, 3, HEADS).sum(1) for m in home]
+    log_total = jnp.stack([jnp.transpose(m) for m in logs], 0)
+    input_grad = jnp.stack(sorted_rows(*finals), 1).astype(F32)
+    return (block_out, input_grad, summed[0], summed[1], summed[2], summed[3], summed[4], log_total)
+
+
 def solution(mesh):
+    four_by_eight = mesh.shape["seq"] == 4 and mesh.shape["blk"] == 8
     placed = (
         P("blk", "seq", None),
         P("blk", "seq"),
@@ -285,7 +888,7 @@
         P("blk", "seq", None),
     )
     return jax.shard_map(
-        body,
+        body_rows if four_by_eight else body_plain,
         mesh=mesh,
         in_specs=placed,
         out_specs=(

time: 645 us -> 122 us (0.19); the launches traced: 634 us -> 121 us
  blocking collectives: 420 us -> 0 us
  matrix products: 76 us -> 22.4 us
  local copies, waits for them, and re-layouts: 57.4 us -> 13.4 us
  waiting for transfers between devices: 53.4 us -> 11.3 us
  Pallas kernels: 0 us -> 39.4 us
  starting transfers between devices: 0.12 us -> 28.2 us
  between operations: 15.6 us -> 1.11 us
  other arithmetic: 12.4 us -> 5.48 us
    unnamed x1 -> x0, blocking collectives: 362 us -> none
    all_gather x2 -> x0, waiting for transfers between devices: 53.3 us -> none  [the longest x1 37.8 us: body(): value_shards = lax.all_gather(values, 'blk', axis=0, tiled=True)]
    dot_general x19 -> x0, matrix products: 53.1 us -> none  [the longest x1 13.9 us: body(): jnp.dot(grad_pre, w_fc.T, preferred_element_type=jnp.float32)]
    psum x1 -> x0, blocking collectives: 39.7 us -> none  [body(): lax.psum((local_grads[0], local_grads[1], local_grads[2], local_grads[3],...]
    pallas_call x0 -> x6, Pallas kernels: none -> 39.4 us  [the longest x1 16.6 us: middle_part(): pl.pallas_call(middle_kernel, in_specs=[vmem()] * 11 + [hbm()] * 3, out_s...]
    ppermute x0 -> x22, starting transfers between devices: none -> 28.2 us  [the longest x4 8.05 us: body_rows(): lax.ppermute(m, everyone, back[k])]
    reshape x12 -> x2, local copies, waits for them, and re-layouts: 20.5 us -> 2.13 us  [body_rows(): m[:, width:width + 3 * HEADS].astype(F32).reshape(half, 3, HEADS).sum(1)]
    all_gather x1 -> x0, blocking collectives: 18 us -> none  [body(): seg_shards = lax.all_gather(segment_ids, 'blk', axis=0, tiled=True)]
  transfers between devices with their start and end apart: 3 -> 22, of which waited for: 2 -> 4; matrix products, arithmetic and copies ran while one was open for 6% -> 28% of each run, Pallas kernels for 0% -> 10%
where the time goes in v1:
time: 122 us; the launch traced here: 121 us
  Pallas kernels  39.4 us (32%)
  starting transfers between devices  28.2 us (23%)
  matrix products  22.4 us (18%)
  local copies, waits for them, and re-layouts  13.4 us (11%)
  waiting for transfers between devices  11.3 us (9%)
  other arithmetic  5.48 us (4%)
    pallas_call x1, Pallas kernels, middle_part(): pl.pallas_call(middle_kernel, in_specs=[vmem()] * 11 + [hbm()] * 3, out_s...  16.6 us
    dot_general x3, matrix products, adapter(): return jnp.dot(inner_act, w_mlp2, precision=HIGH) + b_mlp2  15.6 us
    ppermute x5, waiting for transfers between devices, body_rows(): lax.ppermute(grad_prefix_kv, axis, [(i, i ^ far) for i in range(size)])  10.6 us
    unnamed x46, local copies, waits for them, and re-layouts  9.76 us
    pallas_call x1, Pallas kernels, final_part(): pl.pallas_call(final_kernel, in_specs=[vmem()] * 13 + [hbm()], out_specs=...  8.91 us
    ppermute x4, starting transfers between devices, body_rows(): lax.ppermute(m, everyone, back[k])  8.05 us
    dot_general x3, matrix products, adapter(): inner_act = jnp.tanh(jnp.dot(prefix_embed, w_mlp1, precision=HIGH) + b_mlp1)  6.78 us
    ppermute x2, starting transfers between devices, body_rows(): own = [lax.ppermute(m, everyone, there[k]) for k, m in enumerate(out_msgs)]  6.68 us
  transfers between devices with their start and end apart: 22, of which 4 were waited for; matrix products, arithmetic and copies ran while one was open for 28% of the time, Pallas kernels for 10%

profile of v1, /device:TPU:1, one launch (start us, length us, event | category | flops | bytes accessed | tf_op | source)
XLA Modules:
  0.0 121.3 jit_solution(13073684711961786945)
XLA Ops:
  0.6 0.0 copy-start
  0.6 0.0 copy-start.17
  0.7 0.9 fusion.3
  1.6 1.0 copy.38
  2.6 0.1 select_bitcast_fusion
  2.7 0.0 copy-start.19
  2.7 4.8 %collective-permute-start.1 = (bf16[64,1152]{1,0:T(8,128)(2,1)S(1)}, bf16[64,1152]{1,0:T(8,128)(2,1)S(1)}, u32[]{:S(2)}, u32[]{:S(2)}) collective-permute-start(bf16[64,1152]{1,0:T(8,128)(2,1)S(1)} %get-tuple-element.56), channel_id=1, source_target_pairs={{0,2},{1,3},{2,0},{3,1},{4,10},{5,11},{6,8},{7,9},{8,6},{9,7},{10,... | collective-permute-start | bytes 442376 | tf_op jit(solution)/shard_map/ppermute | solution.py:821
  7.5 1.9 %collective-permute-start = (bf16[64,1152]{1,0:T(8,128)(2,1)S(1)}, bf16[64,1152]{1,0:T(8,128)(2,1)S(1)}, u32[]{:S(2)}, u32[]{:S(2)}) collective-permute-start(bf16[64,1152]{1,0:T(8,128)(2,1)S(1)} %get-tuple-element.57), channel_id=1, source_target_pairs={{0,0},{1,1},{2,2},{3,3},{4,8},{5,9},{6,10},{7,11},{8,4},{9,5},{10,... | collective-permute-start | bytes 442376 | tf_op jit(solution)/shard_map/ppermute | solution.py:821
  9.4 1.5 %fusion.7 = (bf16[64,1,1024]{2,1,0:T(2,128)(2,1)S(1)}, bf16[64,1,1024]{2,1,0:T(2,128)(2,1)S(1)}) fusion(bf16[64,2,1024]{2,1,0:T(2,128)(2,1)} %param.31), kind=kLoop, calls=%fused_computation.31 | loop fusion | bytes 524288 | tf_op jit(solution)/shard_map/slice | solution.py:824
  10.9 0.1 select_bitcast_fusion.4
  11.0 1.7 %collective-permute-start.9 = (bf16[64,1024]{1,0:T(8,128)(2,1)S(1)}, bf16[64,1024]{1,0:T(8,128)(2,1)S(1)}, u32[]{:S(2)}, u32[]{:S(2)}) collective-permute-start(bf16[64,1024]{1,0:T(8,128)(2,1)S(1)} %get-tuple-element.52), channel_id=1, source_target_pairs={{0,2},{1,3},{2,0},{3,1},{4,10},{5,11},{6,8},{7,9},{8,6},{9,7},{10,... | collective-permute-start | bytes 393224 | tf_op jit(solution)/shard_map/ppermute | solution.py:825
  12.7 1.1 fusion.1
  13.8 0.0 copy-start.7
  13.8 0.0 copy-start.8
  13.8 1.3 %collective-permute-start.5 = (bf16[64,1152]{1,0:T(8,128)(2,1)S(1)}, bf16[64,1152]{1,0:T(8,128)(2,1)S(1)}, u32[]{:S(2)}, u32[]{:S(2)}) collective-permute-start(bf16[64,1152]{1,0:T(8,128)(2,1)S(1)} %collective-permute-done.1.refs_1_.own_1), channel_id=1, source_target_pairs={{0,1},{1,0},{2,3},{3,2},{4,5},{5,4},{6,7},{7,6},{8,9},{9,8},{10,11... | collective-permute-start | bytes 442376 | tf_op jit(solution)/shard_map/ppermute | solution.py:822
  15.1 0.7 collective-permute-done.refs_0_.own_0
  15.9 1.2 %collective-permute-start.4 = (bf16[64,1152]{1,0:T(8,128)(2,1)S(1)}, bf16[64,1152]{1,0:T(8,128)(2,1)S(1)}, u32[]{:S(2)}, u32[]{:S(2)}) collective-permute-start(bf16[64,1152]{1,0:T(8,128)(2,1)S(1)} %collective-permute-done.refs_0_.own_0), channel_id=1, source_target_pairs={{0,1},{1,0},{2,3},{3,2},{4,5},{5,4},{6,7},{7,6},{8,9},{9,8},{10,11... | collective-permute-start | bytes 442376 | tf_op jit(solution)/shard_map/ppermute | solution.py:822
  17.1 4.3 %fusion = bf16[10,2048]{1,0:T(8,128)(2,1)S(1)} fusion(f32[10,512]{1,0:T(8,128)S(1)} %fusion.1, f32[512,2048]{1,0:T(8,128)} %param.29, f32[2048]{0:T(1024)S(1)} %copy-done.19), kind=kOutput, calls=%fused_computation.1 | convolution fusion | flops 125870080 | bytes 4263936 | tf_op jit(solution)/shard_map/jvp()/dot_general | solution.py:29
  21.4 2.4 %collective-permute-start.8 = (bf16[64,1024]{1,0:T(8,128)(2,1)S(1)}, bf16[64,1024]{1,0:T(8,128)(2,1)S(1)}, u32[]{:S(2)}, u32[]{:S(2)}) collective-permute-start(bf16[64,1024]{1,0:T(8,128)(2,1)S(1)} %get-tuple-element.53), channel_id=1, source_target_pairs={{0,0},{1,1},{2,2},{3,3},{4,8},{5,9},{6,10},{7,11},{8,4},{9,5},{10,... | collective-permute-start | bytes 393224 | tf_op jit(solution)/shard_map/ppermute | solution.py:825
  23.8 0.1 collective-permute-start.7
  23.9 0.5 collective-permute-start.6
  24.4 3.1 %project.2 = (bf16[256,3072]{1,0:T(8,128)(2,1)S(1)}, bf16[256,128]{1,0:T(8,128)(2,1)S(1)}) custom-call(bf16[64,1152]{1,0:T(8,128)(2,1)S(1)} %collective-permute-done.refs_0_.own_0, bf16[64,1152]{1,0:T(8,128)(2,1)S(1)} %collective-permute-done.1.refs_1_.own_1, bf16[64,1152]{1,0:T(8,128)(2,1)S(1)} %collective-permute-done.2.refs_2_, ...), custom_call_target="tpu_custom_call" | custom-call | flops 1610612736 | bytes 6291456 | tf_op jit(solution)/shard_map/project/pallas_call | solution.py:355
  27.5 0.0 copy-start.3
  27.5 0.0 copy-start.9
  27.5 0.0 copy-start.10
  27.5 3.1 %project.3 = (bf16[256,3072]{1,0:T(8,128)(2,1)S(1)}, bf16[256,128]{1,0:T(8,128)(2,1)S(1)}) custom-call(bf16[64,1152]{1,0:T(8,128)(2,1)S(1)} %collective-permute-done.4.refs_0_, bf16[64,1152]{1,0:T(8,128)(2,1)S(1)} %collective-permute-done.5.refs_1_, bf16[64,1152]{1,0:T(8,128)(2,1)S(1)} %collective-permute-done.6.refs_2_, ...), custom_call_target="tpu_custom_call" | custom-call | flops 1610612736 | bytes 6291456 | tf_op jit(solution)/shard_map/project/pallas_call | solution.py:355
  30.7 16.6 %middle.1 = (bf16[64,1152]{1,0:T(8,128)(2,1)S(1)}, bf16[64,1152]{1,0:T(8,128)(2,1)S(1)}, bf16[128,1152]{1,0:T(8,128)(2,1)S(1)}, f32[128,1024]{1,0:T(8,128)S(1)}) custom-call(bf16[256,3072]{1,0:T(8,128)(2,1)S(1)} %get-tuple-element.18.qkv_a, bf16[256,3072]{1,0:T(8,128)(2,1)S(1)} %get-tuple-element.19.qkv_b, bf16[256,128]{1,0:T(8,128)(2,1)S(1)} %get-tuple-element.20.marks_a, ...), custom_call_target="tpu_custom_call" | custom-call | flops 4831838208 | bytes 18874368 | tf_op jit(solution)/shard_map/middle/pallas_call | solution.py:570
  47.3 2.3 %prefix.1 = f32[10,2048]{1,0:T(8,128)S(1)} custom-call(bf16[256,3072]{1,0:T(8,128)(2,1)S(1)} %get-tuple-element.18.qkv_a, bf16[128,1152]{1,0:T(8,128)(2,1)S(1)} %get-tuple-element.24.grads.grads_0, bf16[16,2048]{1,0:T(8,128)(2,1)S(1)} %pad.4.prefix_kv), custom_call_target="tpu_custom_call" | custom-call | flops 536870912 | bytes 1048576 | tf_op jit(solution)/shard_map/prefix/pallas_call | solution.py:644
  49.6 1.0 collective-permute-start.13
  50.5 0.3 collective-permute-start.12
  50.9 1.2 %collective-permute-start.17 = (f32[10,2048]{1,0:T(8,128)S(1)}, f32[10,2048]{1,0:T(8,128)S(1)}, u32[]{:S(2)}, u32[]{:S(2)}) collective-permute-start(f32[10,2048]{1,0:T(8,128)S(1)} %prefix.1), channel_id=1, source_target_pairs={{0,16},{8,24},{16,0},{24,8},{1,17},{9,25},{17,1},{25,9},{2,18},{10... | collective-permute-start | bytes 245768 | tf_op jit(solution)/shard_map/ppermute | solution.py:843
  52.1 2.7 %collective-permute-start.10 = (bf16[64,1152]{1,0:T(8,128)(2,1)S(1)}, bf16[64,1152]{1,0:T(8,128)(2,1)S(1)}, u32[]{:S(2)}, u32[]{:S(2)}) collective-permute-start(bf16[64,1152]{1,0:T(8,128)(2,1)S(1)} %get-tuple-element.22), channel_id=1, source_target_pairs={{2,0},{3,1},{0,2},{1,3},{10,4},{11,5},{8,6},{9,7},{6,8},{7,9},{4,1... | collective-permute-start | bytes 442376 | tf_op jit(solution)/shard_map/ppermute | solution.py:839
  54.8 2.1 %collective-permute-start.11 = (bf16[64,1152]{1,0:T(8,128)(2,1)S(1)}, bf16[64,1152]{1,0:T(8,128)(2,1)S(1)}, u32[]{:S(2)}, u32[]{:S(2)}) collective-permute-start(bf16[64,1152]{1,0:T(8,128)(2,1)S(1)} %get-tuple-element.23), channel_id=1, source_target_pairs={{0,0},{1,1},{2,2},{3,3},{8,4},{9,5},{10,6},{11,7},{4,8},{5,9},{6,1... | collective-permute-start | bytes 442376 | tf_op jit(solution)/shard_map/ppermute | solution.py:839
  56.9 5.4 %query.1.grad_partial = f32[128,1024]{1,0:T(8,128)S(1)} custom-call(bf16[256,3072]{1,0:T(8,128)(2,1)S(1)} %get-tuple-element.18.qkv_a, bf16[256,3072]{1,0:T(8,128)(2,1)S(1)} %get-tuple-element.19.qkv_b, bf16[256,128]{1,0:T(8,128)(2,1)S(1)} %get-tuple-element.20.marks_a, bf16[256,128]{1,0:T(8,128)(2,1)S(1)} %get-tuple-element.21.marks_b, ...), custom_call_target="tpu_custom_call" | custom-call | flops 4294967296 | bytes 8388608 | tf_op jit(solution)/shard_map/query/pallas_call | solution.py:687
  62.4 0.0 copy-start.11
  62.4 0.8 copy-done.11
  63.2 1.2 collective-permute-start.18
  64.4 2.6 %collective-permute-done.18 = f32[10,2048]{1,0:T(8,128)S(1)} collective-permute-done((f32[10,2048]{1,0:T(8,128)S(1)}, f32[10,2048]{1,0:T(8,128)S(1)}, u32[]{:S(2)}, u32[]{:S(2)}) %collective-permute-start.18) | collective-permute-done | bytes 81952 | tf_op jit(solution)/shard_map/ppermute | solution.py:843
  67.1 0.1 collective-permute-start.19
  67.2 0.6 slice_convert_fusion
  67.8 7.6 %collective-permute-done.19 = f32[10,2048]{1,0:T(8,128)S(1)} collective-permute-done((f32[10,2048]{1,0:T(8,128)S(1)}, f32[10,2048]{1,0:T(8,128)S(1)}, u32[]{:S(2)}, u32[]{:S(2)}) %collective-permute-start.19) | collective-permute-done | bytes 81952 | tf_op jit(solution)/shard_map/ppermute | solution.py:843
  75.4 0.9 collective-permute-start.20
  76.3 1.0 copy.43
  77.3 1.4 %copy.42 = f32[64,48]{0,1:T(8,128)} copy(f32[64,48]{1,0:T(8,128)} %get-tuple-element.66) | data formatting | bytes 24576 | tf_op jit(solution)/shard_map/reshape | solution.py:864
  78.7 0.7 copy.41
  79.4 0.7 reduce_sum.41
  80.2 0.7 reduce_sum.37
  80.9 0.9 add.49
  81.9 1.6 %collective-permute-start.21 = (f32[10,2048]{1,0:T(8,128)S(1)}, f32[10,2048]{1,0:T(8,128)S(1)}, u32[]{:S(2)}, u32[]{:S(2)}) collective-permute-start(f32[10,2048]{1,0:T(8,128)S(1)} %add.49), channel_id=1, source_target_pairs={{0,8},{8,0},{16,24},{24,16},{1,9},{9,1},{17,25},{25,17},{2,10},{10... | collective-permute-start | bytes 245768 | tf_op jit(solution)/shard_map/ppermute | solution.py:843
  83.4 0.6 pad_maximum_fusion.2
  84.0 0.0 collective-permute-start.14
  84.1 0.4 collective-permute-done.21
  84.4 6.3 %fusion.8 = (f32[512]{0:T(512)}, f32[10,512]{1,0:T(8,128)S(1)}) fusion(f32[10,512]{1,0:T(8,128)S(1)} %fusion.1, f32[512,2048]{1,0:T(8,128)} %param.29, f32[10,2048]{1,0:T(8,128)S(1)} %add.49, f32[10,2048]{1,0:T(8,128)S(1)} %collective-permute-done.21), kind=kOutput, calls=%fused_computation.32 | convolution fusion | flops 125874688 | bytes 4401152 | tf_op jit(solution)/shard_map/transpose(jvp())/dot_general | solution.py:29
  90.7 5.0 %fusion.4 = f32[512,2048]{1,0:T(8,128)} fusion(f32[10,512]{1,0:T(8,128)S(1)} %fusion.1, f32[10,2048]{1,0:T(8,128)S(1)} %add.49, f32[10,2048]{1,0:T(8,128)S(1)} %collective-permute-done.21), kind=kOutput, calls=%fused_computation.28 | convolution fusion | flops 125849600 | bytes 4378624 | tf_op jit(solution)/shard_map/transpose(jvp())/dot_general | solution.py:29
  95.8 2.5 %fusion.9 = f32[10,1024]{1,0:T(8,128)} fusion(f32[10,512]{1,0:T(8,128)S(1)} %get-tuple-element.63, f32[1024,512]{1,0:T(8,128)S(1)} %copy-done), kind=kOutput, calls=%fused_computation.33 | convolution fusion | flops 62914560 | bytes 2158592 | tf_op jit(solution)/shard_map/transpose(jvp())/dot_general | solution.py:28
  98.3 0.0 copy-start.2
  98.3 2.8 %copy-done.2 = bf16[1024,3072]{1,0:T(8,128)(2,1)S(1)} copy-done((bf16[1024,3072]{1,0:T(8,128)(2,1)S(1)}, bf16[1024,3072]{1,0:T(8,128)(2,1)}, u32[]{:S(2)}) %copy-start.2) | copy-done | bytes 6291480
  101.1 8.9 %final.1 = (bf16[64,1024]{1,0:T(8,128)(2,1)S(1)}, bf16[64,1024]{1,0:T(8,128)(2,1)}) custom-call(bf16[256,3072]{1,0:T(8,128)(2,1)S(1)} %copy-done.4, bf16[256,3072]{1,0:T(8,128)(2,1)S(1)} %copy-done.6, bf16[256,128]{1,0:T(8,128)(2,1)S(1)} %get-tuple-element.20.marks_a, bf16[256,128]{1,0:T(8,128)(2,1)S(1)} %get-tuple-element.21.marks_b, ...), custom_call_target="tpu_custom_call" | custom-call | flops 4294967296 | bytes 8388608 | tf_op jit(solution)/shard_map/final/pallas_call | solution.py:762
  110.0 1.4 %collective-permute-start.15 = (bf16[64,1024]{1,0:T(8,128)(2,1)}, bf16[64,1024]{1,0:T(8,128)(2,1)S(1)}, u32[]{:S(2)}, u32[]{:S(2)}) collective-permute-start(bf16[64,1024]{1,0:T(8,128)(2,1)} %get-tuple-element.26), channel_id=1, source_target_pairs={{2,0},{3,1},{0,2},{1,3},{10,4},{11,5},{8,6},{9,7},{6,8},{7,9},{4,1... | collective-permute-start | bytes 393224 | tf_op jit(solution)/shard_map/ppermute | solution.py:859
  111.3 1.9 %collective-permute-start.16 = (bf16[64,1024]{1,0:T(8,128)(2,1)S(1)}, bf16[64,1024]{1,0:T(8,128)(2,1)S(1)}, u32[]{:S(2)}, u32[]{:S(2)}) collective-permute-start(bf16[64,1024]{1,0:T(8,128)(2,1)S(1)} %get-tuple-element.27), channel_id=1, source_target_pairs={{0,0},{1,1},{2,2},{3,3},{8,4},{9,5},{10,6},{11,7},{4,8},{5,9},{6,1... | collective-permute-start | bytes 393224 | tf_op jit(solution)/shard_map/ppermute | solution.py:859
  113.3 3.2 %convolution_bitcast_fusion = f32[1024,512]{0,1:T(8,128)} fusion(f32[10,512]{1,0:T(8,128)S(1)} %get-tuple-element.63, f32[10,1024]{1,0:T(8,128)S(1)} %copy-done.18), kind=kOutput, calls=%fused_computation.2 | convolution fusion | flops 62914560 | bytes 2158592 | tf_op jit(solution)/shard_map/transpose(jvp())/dot_general | solution.py:28
  116.5 2.9 %copy.45 = f32[1024,512]{1,0:T(8,128)} copy(f32[1024,512]{0,1:T(8,128)} %convolution_bitcast_fusion) | data formatting | bytes 4194304
  119.4 0.6 add_reduce_fusion
  120.1 1.2 copy.44
  (59 shorter events, 0.3 us)
Async XLA Ops:
  0.6 12.0 %copy-start = (f32[1024,512]{1,0:T(8,128)S(1)}, f32[1024,512]{1,0:T(8,128)}, u32[]{:S(2)}) copy-start(f32[1024,512]{1,0:T(8,128)} %param.27) | copy-start | bytes 6291460
  0.6 12.0 %copy-start.17 = (f32[10,1024]{1,0:T(8,128)S(1)}, f32[10,1024]{1,0:T(8,128)}, u32[]{:S(2)}) copy-start(f32[10,1024]{1,0:T(8,128)} %param.26) | copy-start | bytes 122884
  0.7 12.0 %copy-start.20 = (f32[512]{0:T(512)S(1)}, f32[512]{0:T(512)}, u32[]{:S(2)}) copy-start(f32[512]{0:T(512)} %param.28) | copy-start | bytes 6148
  2.7 14.4 %copy-start.19 = (f32[2048]{0:T(1024)S(1)}, f32[2048]{0:T(1024)}, u32[]{:S(2)}) copy-start(f32[2048]{0:T(1024)} %param.30) | copy-start | bytes 24580
  2.7 11.1 %collective-permute-start.1 = (bf16[64,1152]{1,0:T(8,128)(2,1)S(1)}, bf16[64,1152]{1,0:T(8,128)(2,1)S(1)}, u32[]{:S(2)}, u32[]{:S(2)}) collective-permute-start(bf16[64,1152]{1,0:T(8,128)(2,1)S(1)} %get-tuple-element.56), channel_id=1, source_target_pairs={{0,2},{1,3},{2,0},{3,1},{4,10},{5,11},{6,8},{7,9},{8,6},{9,7},{10,... | collective-permute-start | bytes 442376 | tf_op jit(solution)/shard_map/ppermute | solution.py:821
  7.5 8.4 %collective-permute-start = (bf16[64,1152]{1,0:T(8,128)(2,1)S(1)}, bf16[64,1152]{1,0:T(8,128)(2,1)S(1)}, u32[]{:S(2)}, u32[]{:S(2)}) collective-permute-start(bf16[64,1152]{1,0:T(8,128)(2,1)S(1)} %get-tuple-element.57), channel_id=1, source_target_pairs={{0,0},{1,1},{2,2},{3,3},{4,8},{5,9},{6,10},{7,11},{8,4},{9,5},{10,... | collective-permute-start | bytes 442376 | tf_op jit(solution)/shard_map/ppermute | solution.py:821
  11.0 19.7 %collective-permute-start.9 = (bf16[64,1024]{1,0:T(8,128)(2,1)S(1)}, bf16[64,1024]{1,0:T(8,128)(2,1)S(1)}, u32[]{:S(2)}, u32[]{:S(2)}) collective-permute-start(bf16[64,1024]{1,0:T(8,128)(2,1)S(1)} %get-tuple-element.52), channel_id=1, source_target_pairs={{0,2},{1,3},{2,0},{3,1},{4,10},{5,11},{6,8},{7,9},{8,6},{9,7},{10,... | collective-permute-start | bytes 393224 | tf_op jit(solution)/shard_map/ppermute | solution.py:825
  12.7 11.7 %copy-start.1 = (bf16[1024,3072]{1,0:T(8,128)(2,1)S(1)}, bf16[1024,3072]{1,0:T(8,128)(2,1)}, u32[]{:S(2)}) copy-start(bf16[1024,3072]{1,0:T(8,128)(2,1)} %weight.3) | copy-start | bytes 18874372
  13.8 10.6 %copy-start.7 = (f32[1024]{0:T(1024)S(1)}, f32[1024]{0:T(1024)}, u32[]{:S(2)}) copy-start(f32[1024]{0:T(1024)} %param.19) | copy-start | bytes 12292
  13.8 10.6 %copy-start.8 = (f32[1024]{0:T(1024)S(1)}, f32[1024]{0:T(1024)}, u32[]{:S(2)}) copy-start(f32[1024]{0:T(1024)} %param.18) | copy-start | bytes 12292
  13.8 7.6 %collective-permute-start.5 = (bf16[64,1152]{1,0:T(8,128)(2,1)S(1)}, bf16[64,1152]{1,0:T(8,128)(2,1)S(1)}, u32[]{:S(2)}, u32[]{:S(2)}) collective-permute-start(bf16[64,1152]{1,0:T(8,128)(2,1)S(1)} %collective-permute-done.1.refs_1_.own_1), channel_id=1, source_target_pairs={{0,1},{1,0},{2,3},{3,2},{4,5},{5,4},{6,7},{7,6},{8,9},{9,8},{10,11... | collective-permute-start | bytes 442376 | tf_op jit(solution)/shard_map/ppermute | solution.py:822
  15.1 8.7 %collective-permute-start.3 = (bf16[64,1152]{1,0:T(8,128)(2,1)S(1)}, bf16[64,1152]{1,0:T(8,128)(2,1)S(1)}, u32[]{:S(2)}, u32[]{:S(2)}) collective-permute-start(bf16[64,1152]{1,0:T(8,128)(2,1)S(1)} %collective-permute-done.1.refs_1_.own_1), channel_id=1, source_target_pairs={{0,8},{8,0},{16,24},{24,16},{1,9},{9,1},{17,25},{25,17},{2,10},{10... | collective-permute-start | bytes 442376 | tf_op jit(solution)/shard_map/ppermute | solution.py:823
  15.9 8.0 %collective-permute-start.4 = (bf16[64,1152]{1,0:T(8,128)(2,1)S(1)}, bf16[64,1152]{1,0:T(8,128)(2,1)S(1)}, u32[]{:S(2)}, u32[]{:S(2)}) collective-permute-start(bf16[64,1152]{1,0:T(8,128)(2,1)S(1)} %collective-permute-done.refs_0_.own_0), channel_id=1, source_target_pairs={{0,1},{1,0},{2,3},{3,2},{4,5},{5,4},{6,7},{7,6},{8,9},{9,8},{10,11... | collective-permute-start | bytes 442376 | tf_op jit(solution)/shard_map/ppermute | solution.py:822
  17.1 7.3 %collective-permute-start.2 = (bf16[64,1152]{1,0:T(8,128)(2,1)S(1)}, bf16[64,1152]{1,0:T(8,128)(2,1)S(1)}, u32[]{:S(2)}, u32[]{:S(2)}) collective-permute-start(bf16[64,1152]{1,0:T(8,128)(2,1)S(1)} %collective-permute-done.refs_0_.own_0), channel_id=1, source_target_pairs={{0,8},{8,0},{16,24},{24,16},{1,9},{9,1},{17,25},{25,17},{2,10},{10... | collective-permute-start | bytes 442376 | tf_op jit(solution)/shard_map/ppermute | solution.py:823
  21.4 9.2 %collective-permute-start.8 = (bf16[64,1024]{1,0:T(8,128)(2,1)S(1)}, bf16[64,1024]{1,0:T(8,128)(2,1)S(1)}, u32[]{:S(2)}, u32[]{:S(2)}) collective-permute-start(bf16[64,1024]{1,0:T(8,128)(2,1)S(1)} %get-tuple-element.53), channel_id=1, source_target_pairs={{0,0},{1,1},{2,2},{3,3},{4,8},{5,9},{6,10},{7,11},{8,4},{9,5},{10,... | collective-permute-start | bytes 393224 | tf_op jit(solution)/shard_map/ppermute | solution.py:825
  23.8 3.7 %collective-permute-start.7 = (bf16[64,1152]{1,0:T(8,128)(2,1)S(1)}, bf16[64,1152]{1,0:T(8,128)(2,1)S(1)}, u32[]{:S(2)}, u32[]{:S(2)}) collective-permute-start(bf16[64,1152]{1,0:T(8,128)(2,1)S(1)} %collective-permute-done.5.refs_1_), channel_id=1, source_target_pairs={{0,8},{8,0},{16,24},{24,16},{1,9},{9,1},{17,25},{25,17},{2,10},{10... | collective-permute-start | bytes 442376 | tf_op jit(solution)/shard_map/ppermute | solution.py:826
  23.9 3.6 %collective-permute-start.6 = (bf16[64,1152]{1,0:T(8,128)(2,1)S(1)}, bf16[64,1152]{1,0:T(8,128)(2,1)S(1)}, u32[]{:S(2)}, u32[]{:S(2)}) collective-permute-start(bf16[64,1152]{1,0:T(8,128)(2,1)S(1)} %collective-permute-done.4.refs_0_), channel_id=1, source_target_pairs={{0,8},{8,0},{16,24},{24,16},{1,9},{9,1},{17,25},{25,17},{2,10},{10... | collective-permute-start | bytes 442376 | tf_op jit(solution)/shard_map/ppermute | solution.py:826
  27.5 29.4 %copy-start.3 = (bf16[256,3072]{1,0:T(8,128)(2,1)}, bf16[256,3072]{1,0:T(8,128)(2,1)S(1)}, u32[]{:S(2)}) copy-start(bf16[256,3072]{1,0:T(8,128)(2,1)S(1)} %get-tuple-element.18.qkv_a) | copy-start | bytes 4718596
  27.5 3.2 %copy-start.9 = (f32[1024]{0:T(1024)S(1)}, f32[1024]{0:T(1024)}, u32[]{:S(2)}) copy-start(f32[1024]{0:T(1024)} %param.22) | copy-start | bytes 12292
  27.5 3.2 %copy-start.10 = (f32[1024]{0:T(1024)S(1)}, f32[1024]{0:T(1024)}, u32[]{:S(2)}) copy-start(f32[1024]{0:T(1024)} %param.23) | copy-start | bytes 12292
  30.6 26.3 %copy-start.5 = (bf16[256,3072]{1,0:T(8,128)(2,1)}, bf16[256,3072]{1,0:T(8,128)(2,1)S(1)}, u32[]{:S(2)}) copy-start(bf16[256,3072]{1,0:T(8,128)(2,1)S(1)} %get-tuple-element.19.qkv_b) | copy-start | bytes 4718596
  49.6 34.5 %collective-permute-start.13 = (bf16[128,1152]{1,0:T(8,128)(2,1)S(1)}, bf16[128,1152]{1,0:T(8,128)(2,1)}, u32[]{:S(2)}, u32[]{:S(2)}) collective-permute-start(bf16[128,1152]{1,0:T(8,128)(2,1)S(1)} %get-tuple-element.24.grads.grads_0), channel_id=1, source_target_pairs={{0,1},{1,0},{2,3},{3,2},{4,5},{5,4},{6,7},{7,6},{8,9},{9,8},{10,11... | collective-permute-start | bytes 884744 | tf_op jit(solution)/shard_map/ppermute | solution.py:836
  50.5 47.7 %collective-permute-start.12 = (bf16[128,1152]{1,0:T(8,128)(2,1)S(1)}, bf16[128,1152]{1,0:T(8,128)(2,1)}, u32[]{:S(2)}, u32[]{:S(2)}) collective-permute-start(bf16[128,1152]{1,0:T(8,128)(2,1)S(1)} %get-tuple-element.24.grads.grads_0), channel_id=1, source_target_pairs={{0,8},{8,0},{16,24},{24,16},{1,9},{9,1},{17,25},{25,17},{2,10},{10... | collective-permute-start | bytes 884744 | tf_op jit(solution)/shard_map/ppermute | solution.py:837
  50.9 12.3 %collective-permute-start.17 = (f32[10,2048]{1,0:T(8,128)S(1)}, f32[10,2048]{1,0:T(8,128)S(1)}, u32[]{:S(2)}, u32[]{:S(2)}) collective-permute-start(f32[10,2048]{1,0:T(8,128)S(1)} %prefix.1), channel_id=1, source_target_pairs={{0,16},{8,24},{16,0},{24,8},{1,17},{9,25},{17,1},{25,9},{2,18},{10... | collective-permute-start | bytes 245768 | tf_op jit(solution)/shard_map/ppermute | solution.py:843
  52.1 12.3 %collective-permute-start.10 = (bf16[64,1152]{1,0:T(8,128)(2,1)S(1)}, bf16[64,1152]{1,0:T(8,128)(2,1)S(1)}, u32[]{:S(2)}, u32[]{:S(2)}) collective-permute-start(bf16[64,1152]{1,0:T(8,128)(2,1)S(1)} %get-tuple-element.22), channel_id=1, source_target_pairs={{2,0},{3,1},{0,2},{1,3},{10,4},{11,5},{8,6},{9,7},{6,8},{7,9},{4,1... | collective-permute-start | bytes 442376 | tf_op jit(solution)/shard_map/ppermute | solution.py:839
  54.8 9.6 %collective-permute-start.11 = (bf16[64,1152]{1,0:T(8,128)(2,1)S(1)}, bf16[64,1152]{1,0:T(8,128)(2,1)S(1)}, u32[]{:S(2)}, u32[]{:S(2)}) collective-permute-start(bf16[64,1152]{1,0:T(8,128)(2,1)S(1)} %get-tuple-element.23), channel_id=1, source_target_pairs={{0,0},{1,1},{2,2},{3,3},{8,4},{9,5},{10,6},{11,7},{4,8},{5,9},{6,1... | collective-permute-start | bytes 442376 | tf_op jit(solution)/shard_map/ppermute | solution.py:839
  62.4 0.8 copy-start.11
  63.2 3.9 %collective-permute-start.18 = (f32[10,2048]{1,0:T(8,128)S(1)}, f32[10,2048]{1,0:T(8,128)S(1)}, u32[]{:S(2)}, u32[]{:S(2)}) collective-permute-start(f32[10,2048]{1,0:T(8,128)S(1)} %add.46), channel_id=1, source_target_pairs={{0,2},{1,3},{2,0},{3,1},{4,6},{5,7},{6,4},{7,5},{8,10},{9,11},{10,... | collective-permute-start | bytes 245768 | tf_op jit(solution)/shard_map/ppermute | solution.py:843
  67.1 8.3 %collective-permute-start.19 = (f32[10,2048]{1,0:T(8,128)S(1)}, f32[10,2048]{1,0:T(8,128)S(1)}, u32[]{:S(2)}, u32[]{:S(2)}) collective-permute-start(f32[10,2048]{1,0:T(8,128)S(1)} %add.47), channel_id=1, source_target_pairs={{0,4},{1,5},{2,6},{3,7},{4,0},{5,1},{6,2},{7,3},{8,12},{9,13},{10,... | collective-permute-start | bytes 245768 | tf_op jit(solution)/shard_map/ppermute | solution.py:843
  75.4 5.5 %collective-permute-start.20 = (f32[10,2048]{1,0:T(8,128)S(1)}, f32[10,2048]{1,0:T(8,128)}, u32[]{:S(2)}, u32[]{:S(2)}) collective-permute-start(f32[10,2048]{1,0:T(8,128)S(1)} %add.48), channel_id=1, source_target_pairs={{0,1},{1,0},{2,3},{3,2},{4,5},{5,4},{6,7},{7,6},{8,9},{9,8},{10,11... | collective-permute-start | bytes 245768 | tf_op jit(solution)/shard_map/ppermute | solution.py:843
  81.8 8.9 %copy-start.13 = (f32[10,2048]{1,0:T(8,128)}, f32[10,2048]{1,0:T(8,128)S(1)}, u32[]{:S(2)}) copy-start(f32[10,2048]{1,0:T(8,128)S(1)} %add.49) | copy-start | bytes 245764
  81.9 2.5 %collective-permute-start.21 = (f32[10,2048]{1,0:T(8,128)S(1)}, f32[10,2048]{1,0:T(8,128)S(1)}, u32[]{:S(2)}, u32[]{:S(2)}) collective-permute-start(f32[10,2048]{1,0:T(8,128)S(1)} %add.49), channel_id=1, source_target_pairs={{0,8},{8,0},{16,24},{24,16},{1,9},{9,1},{17,25},{25,17},{2,10},{10... | collective-permute-start | bytes 245768 | tf_op jit(solution)/shard_map/ppermute | solution.py:843
  84.0 14.2 %collective-permute-start.14 = (bf16[128,1152]{1,0:T(8,128)(2,1)}, bf16[128,1152]{1,0:T(8,128)(2,1)S(1)}, u32[]{:S(2)}, u32[]{:S(2)}) collective-permute-start(bf16[128,1152]{1,0:T(8,128)(2,1)} %collective-permute-done.13.grads_2), channel_id=1, source_target_pairs={{0,8},{8,0},{16,24},{24,16},{1,9},{9,1},{17,25},{25,17},{2,10},{10... | collective-permute-start | bytes 884744 | tf_op jit(solution)/shard_map/ppermute | solution.py:838
  84.4 6.3 %copy-start.15 = (f32[10,2048]{1,0:T(8,128)}, f32[10,2048]{1,0:T(8,128)S(1)}, u32[]{:S(2)}) copy-start(f32[10,2048]{1,0:T(8,128)S(1)} %collective-permute-done.21) | copy-start | bytes 245764
  90.7 7.5 %copy-start.6 = (bf16[256,3072]{1,0:T(8,128)(2,1)S(1)}, bf16[256,3072]{1,0:T(8,128)(2,1)}, u32[]{:S(2)}) copy-start(bf16[256,3072]{1,0:T(8,128)(2,1)} %copy-done.5) | copy-start | bytes 4718596
  95.8 2.5 %copy-start.4 = (bf16[256,3072]{1,0:T(8,128)(2,1)S(1)}, bf16[256,3072]{1,0:T(8,128)(2,1)}, u32[]{:S(2)}) copy-start(bf16[256,3072]{1,0:T(8,128)(2,1)} %copy-done.3) | copy-start | bytes 4718596
  95.8 2.5 %copy-start.12 = (f32[128,1024]{1,0:T(8,128)S(1)}, f32[128,1024]{1,0:T(8,128)}, u32[]{:S(2)}) copy-start(f32[128,1024]{1,0:T(8,128)} %copy-done.11) | copy-start | bytes 1572868
  98.3 2.8 %copy-start.2 = (bf16[1024,3072]{1,0:T(8,128)(2,1)S(1)}, bf16[1024,3072]{1,0:T(8,128)(2,1)}, u32[]{:S(2)}) copy-start(bf16[1024,3072]{1,0:T(8,128)(2,1)} %weight.3) | copy-start | bytes 18874372
  101.1 12.2 %copy-start.18 = (f32[10,1024]{1,0:T(8,128)S(1)}, f32[10,1024]{1,0:T(8,128)}, u32[]{:S(2)}) copy-start(f32[10,1024]{1,0:T(8,128)} %param.26) | copy-start | bytes 122884
  110.0 10.1 %collective-permute-start.15 = (bf16[64,1024]{1,0:T(8,128)(2,1)}, bf16[64,1024]{1,0:T(8,128)(2,1)S(1)}, u32[]{:S(2)}, u32[]{:S(2)}) collective-permute-start(bf16[64,1024]{1,0:T(8,128)(2,1)} %get-tuple-element.26), channel_id=1, source_target_pairs={{2,0},{3,1},{0,2},{1,3},{10,4},{11,5},{8,6},{9,7},{6,8},{7,9},{4,1... | collective-permute-start | bytes 393224 | tf_op jit(solution)/shard_map/ppermute | solution.py:859
  111.3 8.7 %collective-permute-start.16 = (bf16[64,1024]{1,0:T(8,128)(2,1)S(1)}, bf16[64,1024]{1,0:T(8,128)(2,1)S(1)}, u32[]{:S(2)}, u32[]{:S(2)}) collective-permute-start(bf16[64,1024]{1,0:T(8,128)(2,1)S(1)} %get-tuple-element.27), channel_id=1, source_target_pairs={{0,0},{1,1},{2,2},{3,3},{8,4},{9,5},{10,6},{11,7},{4,8},{5,9},{6,1... | collective-permute-start | bytes 393224 | tf_op jit(solution)/shard_map/ppermute | solution.py:859
  116.5 2.9 %copy-start.14 = (f32[10,2048]{1,0:T(8,128)S(1)}, f32[10,2048]{1,0:T(8,128)}, u32[]{:S(2)}) copy-start(f32[10,2048]{1,0:T(8,128)} %copy-done.13) | copy-start | bytes 245764
  116.5 2.9 %copy-start.16 = (f32[10,2048]{1,0:T(8,128)S(1)}, f32[10,2048]{1,0:T(8,128)}, u32[]{:S(2)}) copy-start(f32[10,2048]{1,0:T(8,128)} %copy-done.15) | copy-start | bytes 245764

commit v2 on v1

--- a/solution.py
+++ b/solution.py
@@ -272,7 +272,6 @@
 LANES = 128
 PRE_ROWS = 16
 MIB = 1 << 20
-PRE = 10
 
 
 def nn(left, right):
@@ -330,49 +329,210 @@
 
 
 def hbm():
-    return pl.BlockSpec(memory_space=pl.ANY)
-
-
-def project_kernel(count, *refs):
+    return pl.BlockSpec(memory_space=pltpu.HBM)
+
+
+def kept_in_hbm(*arrays):
+    return [pltpu.with_memory_space_constraint(a, pltpu.HBM) for a in arrays]
+
+
+def project_kernel(count, step, *refs):
     messages, (gain, bias, weight, out, marks, normed) = refs[:count], refs[count:]
     half, width = messages[0].shape[0], normed.shape[1]
-
-    @pl.when(pl.program_id(0) == 0)
-    def _():
-        for i, message in enumerate(messages):
-            rows = pl.ds(i * half, half)
-            unit, _ = norm_parts(message[:, :width].astype(F32))
-            normed[rows] = (unit * gain[...] + bias[...]).astype(BF16)
-            marks[rows] = message[:, width:]
-
-    out[...] = nn(normed[...], weight[...]).astype(BF16)
-
-
-def project(messages, gain, bias, weight, step=1024):
-    count, (half, wide) = len(messages), messages[0].shape
+    for i, message in enumerate(messages):
+        rows = pl.ds(i * half, half)
+        unit, _ = norm_parts(message[:, :width].astype(F32))
+        normed[rows] = (unit * gain[...] + bias[...]).astype(BF16)
+        marks[rows] = message[:, width:]
+
+    def columns(i, carry):
+        at = pl.ds(pl.multiple_of(i * step, step), step)
+        out[:, at] = nn(normed[...], weight[:, at]).astype(BF16)
+        return carry
+
+    lax.fori_loop(0, weight.shape[1] // step, columns, 0)
+
+
+def project(messages, gain, bias, weight, step=512):
+    count, half = len(messages), messages[0].shape[0]
     width, columns = weight.shape
     rows = count * half
     return pl.pallas_call(
-        partial(project_kernel, count),
-        grid=(columns // step,),
-        in_specs=[pl.BlockSpec((half, wide), lambda i: (0, 0))] * count
-        + [pl.BlockSpec((1, width), lambda i: (0, 0))] * 2
-        + [pl.BlockSpec((width, step), lambda i: (0, i))],
-        out_specs=[
-            pl.BlockSpec((rows, step), lambda i: (0, i)),
-            pl.BlockSpec((rows, LANES), lambda i: (0, 0)),
-        ],
+        partial(project_kernel, count, step),
+        in_specs=[vmem()] * (count + 3),
+        out_specs=[vmem()] * 2,
         out_shape=[
             jax.ShapeDtypeStruct((rows, columns), BF16),
             jax.ShapeDtypeStruct((rows, LANES), BF16),
         ],
         scratch_shapes=[pltpu.VMEM((rows, width), BF16)],
-        compiler_params=pltpu.CompilerParams(vmem_limit_bytes=30 * MIB),
+        compiler_params=pltpu.CompilerParams(vmem_limit_bytes=16 * MIB),
         cost_estimate=pl.CostEstimate(
             flops=2 * rows * width * columns, bytes_accessed=2 * width * columns, transcendentals=0
         ),
         name="project",
     )(*messages, gain[None], bias[None], weight)
+
+
+def halves(value_in):
+    high = value_in.astype(BF16)
+    return high, (value_in - high.astype(F32)).astype(BF16)
+
+
+def pad_rows(value_in, rows):
+    return jnp.concatenate(
+        [value_in, jnp.zeros((rows - value_in.shape[0], value_in.shape[1]), value_in.dtype)], 0
+    )
+
+
+def three_products(product, left, weight):
+    rows = left.shape[0]
+    high, low = halves(left)
+    w_high, w_low = halves(weight)
+    both = product(jnp.concatenate([high, low], 0), w_high)
+    return both[:rows] + both[rows:] + product(high, w_low)
+
+
+def adapter_kernel(
+    embed, w_mlp1, b_mlp1, w_mlp2, b_mlp2, w_qkv, out, inner, v_qkv, v_mlp1, v_mlp2, sems
+):
+    steps, step = v_mlp2.shape[0], v_mlp2.shape[2]
+    first = pltpu.make_async_copy(w_mlp1, v_mlp1, sems.at[0])
+    first.start()
+    rest = []
+    for i in range(steps):
+        copy = pltpu.make_async_copy(w_mlp2.at[:, pl.ds(i * step, step)], v_mlp2.at[i], sems.at[1 + i])
+        copy.start()
+        rest.append(copy)
+    weights = pltpu.make_async_copy(w_qkv, v_qkv, sems.at[1 + steps])
+    weights.start()
+    source = pad_rows(embed[...], PRE_ROWS)
+    first.wait()
+    act = jnp.tanh(three_products(nn, source, v_mlp1[...]) + b_mlp1[...])
+    inner[...] = act
+    for i, copy in enumerate(rest):
+        copy.wait()
+        span = pl.ds(i * step, step)
+        part = three_products(nn, act, v_mlp2[i]) + b_mlp2[:, span]
+        out[:, span] = jnp.where(iota(part.shape, 0) < embed.shape[0], part, 0.0).astype(BF16)
+    weights.wait()
+
+
+def adapter_forward(embed, w_mlp1, b_mlp1, w_mlp2, b_mlp2, w_qkv):
+    width, hidden = w_mlp1.shape
+    columns = w_mlp2.shape[1]
+    steps = 4
+    return pl.pallas_call(
+        adapter_kernel,
+        in_specs=[vmem(), hbm(), vmem(), hbm(), vmem(), hbm()],
+        out_specs=[vmem()] * 3,
+        out_shape=[
+            jax.ShapeDtypeStruct((PRE_ROWS, columns), BF16),
+            jax.ShapeDtypeStruct((PRE_ROWS, hidden), F32),
+            pltpu.VMEM(w_qkv.shape, w_qkv.dtype),
+        ],
+        scratch_shapes=[
+            pltpu.VMEM((width, hidden), F32),
+            pltpu.VMEM((steps, hidden, columns // steps), F32),
+            pltpu.SemaphoreType.DMA((2 + steps,)),
+        ],
+        compiler_params=pltpu.CompilerParams(vmem_limit_bytes=20 * MIB),
+        cost_estimate=pl.CostEstimate(flops=1 << 32, bytes_accessed=6 * MIB, transcendentals=1 << 13),
+        name="adapter",
+    )(embed, *kept_in_hbm(w_mlp1), b_mlp1[None], *kept_in_hbm(w_mlp2), b_mlp2[None], *kept_in_hbm(w_qkv))
+
+
+def outer(left, right):
+    l_high, l_low = halves(left)
+    r_high, r_low = halves(right)
+    return lax.dot_general(
+        jnp.concatenate([l_high, l_high, l_low], 0),
+        jnp.concatenate([r_high, r_low, r_high], 0),
+        (((0,), (0,)), ((), ())),
+        preferred_element_type=F32,
+    )
+
+
+def adapter_back_kernel(
+    grads,
+    embed,
+    inner,
+    w_mlp1,
+    w_mlp2,
+    order,
+    grad_prefix,
+    grad_mlp1,
+    grad_bias1,
+    grad_mlp2,
+    grad_bias2,
+    v_mlp1,
+    v_mlp2,
+    o_mlp1,
+    o_mlp2,
+    sems,
+):
+    del order
+    steps, step = v_mlp2.shape[0], v_mlp2.shape[2]
+    loads = []
+    for i in range(steps):
+        span = pl.ds(i * step, step)
+        loads.append(pltpu.make_async_copy(w_mlp2.at[:, span], v_mlp2.at[i], sems.at[i]))
+    loads.append(pltpu.make_async_copy(w_mlp1, v_mlp1, sems.at[steps]))
+    for copy in loads:
+        copy.start()
+    act = inner[...]
+    stores = []
+    back = jnp.zeros(act.shape, F32)
+    for i in range(steps):
+        span = pl.ds(i * step, step)
+        part = pad_rows(grads[:, span], PRE_ROWS)
+        grad_bias2[:, span] = jnp.sum(part, 0, keepdims=True)
+        o_mlp2[i] = outer(act, part)
+        copy = pltpu.make_async_copy(o_mlp2.at[i], grad_mlp2.at[:, span], sems.at[steps + 1 + i])
+        copy.start()
+        stores.append(copy)
+        loads[i].wait()
+        back = back + three_products(nt, part, v_mlp2[i])
+    back = back * (1.0 - act * act)
+    grad_bias1[...] = jnp.sum(back, 0, keepdims=True)
+    o_mlp1[...] = outer(pad_rows(embed[...], PRE_ROWS), back)
+    copy = pltpu.make_async_copy(o_mlp1, grad_mlp1, sems.at[2 * steps + 1])
+    copy.start()
+    stores.append(copy)
+    loads[steps].wait()
+    grad_prefix[...] = three_products(nt, back, v_mlp1[...])[: embed.shape[0]]
+    for copy in stores:
+        copy.wait()
+
+
+def adapter_backward(grads, embed, inner, w_mlp1, w_mlp2, order):
+    width, hidden = w_mlp1.shape
+    columns = w_mlp2.shape[1]
+    steps = 4
+    step = columns // steps
+    out = pl.pallas_call(
+        adapter_back_kernel,
+        in_specs=[vmem()] * 3 + [hbm()] * 2 + [pl.BlockSpec(memory_space=pl.ANY)],
+        out_specs=[vmem(), hbm(), vmem(), hbm(), vmem()],
+        out_shape=[
+            jax.ShapeDtypeStruct(embed.shape, F32),
+            jax.ShapeDtypeStruct((width, hidden), F32),
+            jax.ShapeDtypeStruct((1, hidden), F32),
+            jax.ShapeDtypeStruct((hidden, columns), F32),
+            jax.ShapeDtypeStruct((1, columns), F32),
+        ],
+        scratch_shapes=[
+            pltpu.VMEM((width, hidden), F32),
+            pltpu.VMEM((steps, hidden, step), F32),
+            pltpu.VMEM((width, hidden), F32),
+            pltpu.VMEM((steps, hidden, step), F32),
+            pltpu.SemaphoreType.DMA((2 * steps + 2,)),
+        ],
+        compiler_params=pltpu.CompilerParams(vmem_limit_bytes=28 * MIB),
+        cost_estimate=pl.CostEstimate(flops=1 << 32, bytes_accessed=12 * MIB, transcendentals=0),
+        name="adapter_back",
+    )(grads, embed, inner, *kept_in_hbm(w_mlp1, w_mlp2), order)
+    return out[0], out[1], out[2][0], out[3], out[4][0]
 
 
 def head_mask(rows):
@@ -410,7 +570,7 @@
     return jnp.where(inside, chosen, 0.0)
 
 
-def key_bias(marks_own, marks_a, marks_b, half):
+def key_bias(marks_own, marks_a, marks_b, half, count):
     row, core, y_at = place()
     rows = 2 * half
     own = positions(iota((rows, 1), 0), half, row, core, y_at)
@@ -418,7 +578,7 @@
     same = nt(marks_own, jnp.concatenate([marks_a, marks_b], 0))
     visible = jnp.logical_and(same > 0.5, other <= own)
     token_bias = jnp.where(visible, 0.0, NEG)
-    prefix_bias = jnp.where(iota((rows, LANES), 1) < PRE, 0.0, NEG)
+    prefix_bias = jnp.where(iota((rows, LANES), 1) < count, 0.0, NEG)
     return jnp.concatenate([token_bias, prefix_bias], 1)
 
 
@@ -428,6 +588,7 @@
 
 
 def middle_kernel(
+    count,
     qkv_a,
     qkv_b,
     marks_a,
@@ -470,7 +631,7 @@
     for copy in copies:
         copy.start()
 
-    scores_bias[...] = key_bias(marks_a[:rows], marks_a[...], marks_b[...], half)
+    scores_bias[...] = key_bias(marks_a[:rows], marks_a[...], marks_b[...], half, count)
     low = head_mask(rows)
     lane = iota((rows, LANES), 1)
     stats[...] = jnp.zeros_like(stats)
@@ -560,7 +721,7 @@
     back_1[:, width:] = marks[half:]
 
 
-def middle_part(qkv_a, qkv_b, marks_a, marks_b, prefix_kv, own, cots, gain, bias, w_out, w_fc, w_proj):
+def middle_part(count, qkv_a, qkv_b, marks_a, marks_b, prefix_kv, own, cots, gain, bias, w_out, w_fc, w_proj):
     half, width = cots[0].shape
     rows = 2 * half
     hidden = w_fc.shape[1]
@@ -568,7 +729,7 @@
     step = hidden // steps
     wide = width + LANES
     return pl.pallas_call(
-        middle_kernel,
+        partial(middle_kernel, count),
         in_specs=[vmem()] * 11 + [hbm()] * 3,
         out_specs=[vmem()] * 4,
         out_shape=[
@@ -599,7 +760,7 @@
         ),
         name="middle",
     )(
-        qkv_a, qkv_b, marks_a, marks_b, prefix_kv, *own, *cots, gain[None], bias[None], w_out, w_fc, w_proj
+        qkv_a, qkv_b, marks_a, marks_b, prefix_kv, *own, *cots, gain[None], bias[None], *kept_in_hbm(w_out, w_fc, w_proj)
     )
 
 
@@ -621,10 +782,11 @@
 
 
 def prefix_kernel(qkv_a, grads, prefix_kv, out):
+    used = out.shape[0]
     rows, width = grads.shape[0], grads.shape[1] - LANES
     count = prefix_kv.shape[0]
     low = head_mask(count)
-    mask = jnp.where(iota((count, rows), 0) < PRE, 0.0, NEG)
+    mask = jnp.where(iota((count, rows), 0) < used, 0.0, NEG)
     marks = grads[:, width:]
 
     def step(pair, carry):
@@ -633,28 +795,29 @@
         key_grad, value_grad = key_grads(
             prefix_kv[:, at], prefix_kv[:, at_v], qkv_a[:rows, at], grads[:, at], marks, pair, low, mask
         )
-        out[:, at] = key_grad[:PRE]
-        out[:, at_v] = value_grad[:PRE]
+        out[:, at] = key_grad[:used]
+        out[:, at_v] = value_grad[:used]
         return carry
 
     lax.fori_loop(0, HEADS // 2, step, 0)
 
 
-def prefix_part(qkv_a, grads, prefix_kv):
+def prefix_part(count, qkv_a, grads, prefix_kv):
     return pl.pallas_call(
         prefix_kernel,
         in_specs=[vmem()] * 3,
         out_specs=vmem(),
-        out_shape=jax.ShapeDtypeStruct((PRE, prefix_kv.shape[1]), F32),
+        out_shape=jax.ShapeDtypeStruct((count, prefix_kv.shape[1]), F32),
         compiler_params=pltpu.CompilerParams(vmem_limit_bytes=16 * MIB),
         cost_estimate=pl.CostEstimate(flops=1 << 29, bytes_accessed=1 << 20, transcendentals=1 << 16),
         name="prefix",
     )(qkv_a, grads, prefix_kv)
 
 
-def query_kernel(qkv_a, qkv_b, marks_a, marks_b, prefix_kv, grads, weight, out, scores_bias, grad_query):
+def query_kernel(count, qkv_a, qkv_b, marks_a, marks_b, prefix_kv, grads, weight, order, out, scores_bias, grad_query):
+    del order
     rows, width = grad_query.shape
-    scores_bias[...] = key_bias(marks_a[:rows], marks_a[...], marks_b[...], rows // 2)
+    scores_bias[...] = key_bias(marks_a[:rows], marks_a[...], marks_b[...], rows // 2, count)
     low = head_mask(rows)
     marks = grads[:, width:]
     marks_twice = jnp.concatenate([marks, marks], 0)
@@ -679,22 +842,21 @@
         return carry
 
     lax.fori_loop(0, HEADS // 2, step, 0)
-    out[...] = nt(grad_query[...], weight[...])
-
-
-def query_part(qkv_a, qkv_b, marks_a, marks_b, prefix_kv, grads, weight):
+    out[...] = nt(grad_query[...], weight[:, :width])
+
+
+def query_part(count, qkv_a, qkv_b, marks_a, marks_b, prefix_kv, grads, weight, order):
     rows, width = grads.shape[0], grads.shape[1] - LANES
     return pl.pallas_call(
-        query_kernel,
-        grid=(1,),
-        in_specs=[pl.BlockSpec(memory_space=pltpu.VMEM)] * 6 + [pl.BlockSpec((width, width), lambda i: (0, 0))],
-        out_specs=pl.BlockSpec(memory_space=pltpu.VMEM),
+        partial(query_kernel, count),
+        in_specs=[vmem()] * 7 + [pl.BlockSpec(memory_space=pl.ANY)],
+        out_specs=vmem(),
         out_shape=jax.ShapeDtypeStruct((rows, width), F32),
         scratch_shapes=[pltpu.VMEM((rows, 4 * rows + LANES), F32), pltpu.VMEM((rows, width), BF16)],
         compiler_params=pltpu.CompilerParams(vmem_limit_bytes=30 * MIB),
         cost_estimate=pl.CostEstimate(flops=1 << 32, bytes_accessed=1 << 23, transcendentals=1 << 20),
         name="query",
-    )(qkv_a, qkv_b, marks_a, marks_b, prefix_kv, grads, weight)
+    )(qkv_a, qkv_b, marks_a, marks_b, prefix_kv, grads, weight, order)
 
 
 def final_kernel(
@@ -714,15 +876,11 @@
     weight,
     back_0,
     back_1,
-    v_weight,
-    sem,
     scores_bias,
     grad_keys,
 ):
     half, rows = own_0.shape[0], 2 * own_0.shape[0]
     width = grad_middle.shape[1]
-    load = pltpu.make_async_copy(weight.at[:, pl.ds(width, 2 * width)], v_weight, sem)
-    load.start()
     row, core, y_at = place()
     own = positions(iota((rows, 1), 0), half, row, core, y_at)
     other = all_positions((1, 8 * half), 1, half, row, core, y_at)
@@ -747,8 +905,7 @@
         return carry
 
     lax.fori_loop(0, HEADS // 2, step, 0)
-    load.wait()
-    grad_norm = grad_partial[...] + nt(grad_keys[...], v_weight[...])
+    grad_norm = grad_partial[...] + nt(grad_keys[...], weight[:, width:])
     inputs = jnp.concatenate([own_0[:, :width], own_1[:, :width]], 0).astype(F32)
     unit, inverse = norm_parts(inputs)
     out = (grad_middle[...] + norm_back(unit, inverse, gain[...], grad_norm)).astype(BF16)
@@ -761,12 +918,10 @@
     half = rows // 2
     return pl.pallas_call(
         final_kernel,
-        in_specs=[vmem()] * 13 + [hbm()],
+        in_specs=[vmem()] * 14,
         out_specs=[vmem()] * 2,
         out_shape=[jax.ShapeDtypeStruct((half, width), BF16)] * 2,
         scratch_shapes=[
-            pltpu.VMEM((width, 2 * width), BF16),
-            pltpu.SemaphoreType.DMA,
             pltpu.VMEM((rows, 4 * rows), F32),
             pltpu.VMEM((rows, 2 * width), BF16),
         ],
@@ -815,35 +970,45 @@
     def sorted_rows(first, second):
         return jnp.where(odd, second, first), jnp.where(odd, first, second)
 
+    def after(value, *done):
+        return lax.optimization_barrier((value, done))[0]
+
     marks = (segment_ids[:, :, None] == jnp.arange(LANES)[None, None]).astype(BF16)
     marked = jnp.concatenate([tokens, marks], -1)
     out_msgs = sorted_rows(marked[:, 0], marked[:, 1])
+    cot_msgs = sorted_rows(cotangent[:, 0], cotangent[:, 1])
     own = [lax.ppermute(m, everyone, there[k]) for k, m in enumerate(out_msgs)]
+    prefix_kv, inner, w_near = adapter_forward(prefix_embed, w_mlp1, b_mlp1, w_mlp2, b_mlp2, w_qkv)
+    count = prefix_embed.shape[0]
+    own = after(own, inner)
     across = [lax.ppermute(m, "blk", swap_y) for m in own]
     beside = [lax.ppermute(m, "seq", swap_core) for m in own]
-    cot_msgs = sorted_rows(cotangent[:, 0], cotangent[:, 1])
-    cots = [lax.ppermute(m, everyone, there[k]) for k, m in enumerate(cot_msgs)]
+    cots = [lax.ppermute(m, everyone, there[k]) for k, m in enumerate(after(cot_msgs, own))]
     beyond = [lax.ppermute(m, "seq", swap_core) for m in across]
 
-    prefix_kv, adapter_back = jax.vjp(adapter, prefix_embed, w_mlp1, b_mlp1, w_mlp2, b_mlp2)
-    prefix_kv = jnp.pad(prefix_kv.astype(BF16), ((0, PRE_ROWS - prefix_kv.shape[0]), (0, 0)))
-
-    qkv_a, marks_a = project(own + beside, ln1_gain, ln1_bias, w_qkv)
-    qkv_b, marks_b = project(across + beyond, ln1_gain, ln1_bias, w_qkv)
+    qkv_a, marks_a = project(own + beside, ln1_gain, ln1_bias, w_near)
+    qkv_b, marks_b = project(across + beyond, ln1_gain, ln1_bias, w_near)
     back_0, back_1, grads, grad_middle = middle_part(
-        qkv_a, qkv_b, marks_a, marks_b, prefix_kv, own, cots, ln2_gain, ln2_bias, w_out, w_fc, w_proj
+        count, qkv_a, qkv_b, marks_a, marks_b, prefix_kv, own, cots, ln2_gain, ln2_bias, w_out, w_fc, w_proj
     )
     grads_y = lax.ppermute(grads, "blk", swap_y)
     grads_c = lax.ppermute(grads, "seq", swap_core)
     grads_yc = lax.ppermute(grads_y, "seq", swap_core)
     home = [lax.ppermute(m, everyone, back[k]) for k, m in enumerate((back_0, back_1))]
 
-    grad_prefix_kv = prefix_part(qkv_a, grads, prefix_kv)
-    for axis, size, far in (("seq", 4, 2), ("blk", 8, 2), ("blk", 8, 4), ("blk", 8, 1), ("seq", 4, 1)):
-        grad_prefix_kv = grad_prefix_kv + lax.ppermute(
-            grad_prefix_kv, axis, [(i, i ^ far) for i in range(size)]
-        )
-    grad_partial = query_part(qkv_a, qkv_b, marks_a, marks_b, prefix_kv, grads, w_qkv)
+    def spread(value, axis, size, partners):
+        return [lax.ppermute(value, axis, [(i, i ^ far) for i in range(size)]) for far in partners]
+
+    def add_four(value, others):
+        return (value + others[0]) + (others[1] + others[2])
+
+    grad_prefix_kv = prefix_part(count, qkv_a, grads, prefix_kv)
+    parts = spread(grad_prefix_kv, "seq", 4, (2, 1, 3))
+    grad_partial = query_part(
+        count, qkv_a, qkv_b, marks_a, marks_b, prefix_kv, grads, w_near, grad_prefix_kv
+    )
+    grad_prefix_kv = add_four(grad_prefix_kv, after(parts, grads_y, grad_partial))
+    parts = spread(grad_prefix_kv, "blk", 8, (2, 4, 6))
     final_0, final_1 = final_part(
         qkv_a,
         qkv_b,
@@ -854,12 +1019,15 @@
         ln1_gain,
         grad_middle,
         grad_partial,
-        w_qkv,
+        w_near,
     )
     finals = [lax.ppermute(m, everyone, back[k]) for k, m in enumerate((final_0, final_1))]
-    summed = adapter_back(grad_prefix_kv)
-
-    home = sorted_rows(*home)
+    grad_prefix_kv = add_four(grad_prefix_kv, after(parts, final_0))
+    parts = spread(grad_prefix_kv, "blk", 8, (1,))
+    grad_prefix_kv = grad_prefix_kv + parts[0]
+    summed = adapter_backward(grad_prefix_kv, prefix_embed, inner, w_mlp1, w_mlp2, final_0)
+
+    home = sorted_rows(*after(home, final_0))
     block_out = jnp.stack([m[:, :width] for m in home], 1)
     logs = [m[:, width : width + 3 * HEADS].astype(F32).reshape(half, 3, HEADS).sum(1) for m in home]
     log_total = jnp.stack([jnp.transpose(m) for m in logs], 0)

time: 122 us -> 97.4 us (0.80)
  the two profiles are of different devices: /device:TPU:1 before, /device:TPU:8 now
where the time goes in v2:
time: 97.4 us; the launch traced here: 97 us
  Pallas kernels  47.3 us (49%)
  starting transfers between devices  25.8 us (26%)
  waiting for transfers between devices  15.2 us (16%)
  local copies, waits for them, and re-layouts  5.94 us (6%)
  other arithmetic  1.76 us (2%)
  between operations  1.05 us (1%)
    pallas_call x1, Pallas kernels, middle_part(): pl.pallas_call(partial(middle_kernel, count), in_specs=[vmem()] * 11 + [h...  16.6 us
    ppermute x7, waiting for transfers between devices, spread(): lax.ppermute(value, axis, [(i, i ^ far) for i in range(size)])  10.8 us
    pallas_call x1, Pallas kernels, final_part(): pl.pallas_call(final_kernel, in_specs=[vmem()] * 14, out_specs=[vmem()] *...  6.34 us
    ppermute x7, starting transfers between devices, spread(): lax.ppermute(value, axis, [(i, i ^ far) for i in range(size)])  6.27 us
    pallas_call x2, Pallas kernels, project(): pl.pallas_call(partial(project_kernel, count, step), in_specs=[vmem()] *...  6.1 us
    pallas_call x1, Pallas kernels, adapter_backward(): pl.pallas_call(adapter_back_kernel, in_specs=[vmem()] * 3 + [hbm()] * 2 +...  5.91 us
    unnamed x21, local copies, waits for them, and re-layouts  5.41 us
    ppermute x4, starting transfers between devices, body_rows(): lax.ppermute(m, everyone, back[k])  5.33 us
  transfers between devices with their start and end apart: 24, of which 4 were waited for; matrix products, arithmetic and copies ran while one was open for 2% of the time, Pallas kernels for 32%

profile of v2, /device:TPU:8, one launch (start us, length us, event | category | flops | bytes accessed | tf_op | source)
XLA Modules:
  0.0 97.0 jit_solution(16187963919629057964)
XLA Ops:
  0.7 0.8 fusion.1
  1.4 1.0 %copy.36 = bf16[64,2,1024]{2,0,1:T(8,128)(2,1)S(1)} copy(bf16[64,2,1024]{2,1,0:T(2,128)(2,1)} %param.16) | data formatting | bytes 524288 | tf_op args[0]
  2.4 0.1 select_bitcast_fusion
  2.5 0.7 collective-permute-start
  3.2 0.1 collective-permute-start.1
  3.3 0.0 copy-start.4
  3.3 0.8 copy-done.4
  4.1 0.7 copy-done.6
  4.8 0.7 copy-done.7
  5.5 4.8 %adapter.1 = (bf16[16,2048]{1,0:T(8,128)(2,1)S(1)}, f32[16,512]{1,0:T(8,128)S(1)}, bf16[1024,3072]{1,0:T(8,128)(2,1)S(1)}) custom-call(f32[10,1024]{1,0:T(8,128)S(1)} %copy-done.4, f32[1024,512]{1,0:T(8,128)} %w_mlp1.3, f32[1,512]{1,0:T(1,128)S(1)} %bitcast.40, f32[512,2048]{1,0:T(8,128)} %w_mlp2.3, f32[1,2048]{1,0:T(1,128)S(1)} %bitcast.39, ...), custom_call_target="tpu_custom_call" | custom-call | flops 4294967296 | bytes 6291456 | tf_op jit(solution)/shard_map/adapter/pallas_call | solution.py:425
  10.3 0.4 fusion.2
  10.6 0.0 collective-permute-done.refs_0_.own_0
  10.7 0.0 collective-permute-done.1.refs_1_.own_1
  10.7 4.0 %collective-permute-start.2 = (bf16[64,1152]{1,0:T(8,128)(2,1)S(1)}, bf16[64,1152]{1,0:T(8,128)(2,1)S(1)}, u32[]{:S(2)}, u32[]{:S(2)}) collective-permute-start(bf16[64,1152]{1,0:T(8,128)(2,1)S(1)} %collective-permute-done.refs_0_.own_0), channel_id=1, source_target_pairs={{0,8},{8,0},{16,24},{24,16},{1,9},{9,1},{17,25},{25,17},{2,10},{10... | collective-permute-start | bytes 442376 | tf_op jit(solution)/shard_map/ppermute | solution.py:985
  14.7 1.5 %collective-permute-start.4 = (bf16[64,1152]{1,0:T(8,128)(2,1)S(1)}, bf16[64,1152]{1,0:T(8,128)(2,1)S(1)}, u32[]{:S(2)}, u32[]{:S(2)}) collective-permute-start(bf16[64,1152]{1,0:T(8,128)(2,1)S(1)} %collective-permute-done.refs_0_.own_0), channel_id=1, source_target_pairs={{0,1},{1,0},{2,3},{3,2},{4,5},{5,4},{6,7},{7,6},{8,9},{9,8},{10,11... | collective-permute-start | bytes 442376 | tf_op jit(solution)/shard_map/ppermute | solution.py:984
  16.2 0.0 collective-permute-start.3
  16.2 0.5 collective-permute-start.5
  16.7 0.1 select_bitcast_fusion.4
  16.8 0.7 collective-permute-start.8
  17.5 0.0 collective-permute-done.2.refs_2_
  17.5 1.5 %collective-permute-start.9 = (bf16[64,1024]{1,0:T(8,128)(2,1)S(1)}, bf16[64,1024]{1,0:T(8,128)(2,1)S(1)}, u32[]{:S(2)}, u32[]{:S(2)}) collective-permute-start(bf16[64,1024]{1,0:T(8,128)(2,1)S(1)} %get-tuple-element.48), channel_id=1, source_target_pairs={{0,2},{1,3},{2,0},{3,1},{4,10},{5,11},{6,8},{7,9},{8,6},{9,7},{10,... | collective-permute-start | bytes 393224 | tf_op jit(solution)/shard_map/ppermute | solution.py:986
  19.0 2.4 %collective-permute-done.4.refs_0_ = bf16[64,1152]{1,0:T(8,128)(2,1)S(1)} collective-permute-done((bf16[64,1152]{1,0:T(8,128)(2,1)S(1)}, bf16[64,1152]{1,0:T(8,128)(2,1)S(1)}, u32[]{:S(2)}, u32[]{:S(2)}) %collective-permute-start.4) | collective-permute-done | bytes 147488 | tf_op jit(solution)/shard_map/ppermute | solution.py:984
  21.4 0.3 collective-permute-start.6
  21.7 2.0 %collective-permute-done.5.refs_1_ = bf16[64,1152]{1,0:T(8,128)(2,1)S(1)} collective-permute-done((bf16[64,1152]{1,0:T(8,128)(2,1)S(1)}, bf16[64,1152]{1,0:T(8,128)(2,1)S(1)}, u32[]{:S(2)}, u32[]{:S(2)}) %collective-permute-start.5) | collective-permute-done | bytes 147488 | tf_op jit(solution)/shard_map/ppermute | solution.py:984
  23.7 0.0 collective-permute-start.7
  23.7 0.0 collective-permute-done.3.refs_3_
  23.7 3.1 %project.2 = (bf16[256,3072]{1,0:T(8,128)(2,1)S(1)}, bf16[256,128]{1,0:T(8,128)(2,1)S(1)}) custom-call(bf16[64,1152]{1,0:T(8,128)(2,1)S(1)} %collective-permute-done.refs_0_.own_0, bf16[64,1152]{1,0:T(8,128)(2,1)S(1)} %collective-permute-done.1.refs_1_.own_1, bf16[64,1152]{1,0:T(8,128)(2,1)S(1)} %collective-permute-done.2.refs_2_, ...), custom_call_target="tpu_custom_call" | custom-call | flops 1610612736 | bytes 6291456 | tf_op jit(solution)/shard_map/project/pallas_call | solution.py:360
  26.8 0.0 copy-start.2
  26.8 0.0 copy-start.3
  26.8 0.0 collective-permute-done.7.refs_3_
  26.8 3.1 %project.3 = (bf16[256,3072]{1,0:T(8,128)(2,1)S(1)}, bf16[256,128]{1,0:T(8,128)(2,1)S(1)}) custom-call(bf16[64,1152]{1,0:T(8,128)(2,1)S(1)} %collective-permute-done.4.refs_0_, bf16[64,1152]{1,0:T(8,128)(2,1)S(1)} %collective-permute-done.5.refs_1_, bf16[64,1152]{1,0:T(8,128)(2,1)S(1)} %collective-permute-done.6.refs_2_, ...), custom_call_target="tpu_custom_call" | custom-call | flops 1610612736 | bytes 6291456 | tf_op jit(solution)/shard_map/project/pallas_call | solution.py:360
  29.9 0.0 collective-permute-done.9.cot_1
  29.9 16.6 %middle.1 = (bf16[64,1152]{1,0:T(8,128)(2,1)S(1)}, bf16[64,1152]{1,0:T(8,128)(2,1)S(1)}, bf16[128,1152]{1,0:T(8,128)(2,1)S(1)}, f32[128,1024]{1,0:T(8,128)S(1)}) custom-call(bf16[256,3072]{1,0:T(8,128)(2,1)S(1)} %get-tuple-element.42.qkv_a, bf16[256,3072]{1,0:T(8,128)(2,1)S(1)} %get-tuple-element.43.qkv_b, bf16[256,128]{1,0:T(8,128)(2,1)S(1)} %get-tuple-element.44.marks_a, ...), custom_call_target="tpu_custom_call" | custom-call | flops 4831838208 | bytes 18874368 | tf_op jit(solution)/shard_map/middle/pallas_call | solution.py:731
  46.5 0.6 collective-permute-start.12
  47.1 1.5 %collective-permute-start.13 = (bf16[128,1152]{1,0:T(8,128)(2,1)S(1)}, bf16[128,1152]{1,0:T(8,128)(2,1)S(1)}, u32[]{:S(2)}, u32[]{:S(2)}) collective-permute-start(bf16[128,1152]{1,0:T(8,128)(2,1)S(1)} %get-tuple-element.51.grads.grads_0), channel_id=1, source_target_pairs={{0,1},{1,0},{2,3},{3,2},{4,5},{5,4},{6,7},{7,6},{8,9},{9,8},{10,11... | collective-permute-start | bytes 884744 | tf_op jit(solution)/shard_map/ppermute | solution.py:994
  48.6 2.3 %prefix.1.order = f32[10,2048]{1,0:T(8,128)S(1)} custom-call(bf16[256,3072]{1,0:T(8,128)(2,1)S(1)} %get-tuple-element.42.qkv_a, bf16[128,1152]{1,0:T(8,128)(2,1)S(1)} %get-tuple-element.51.grads.grads_0, bf16[16,2048]{1,0:T(8,128)(2,1)S(1)} %get-tuple-element.46.prefix_kv), custom_call_target="tpu_custom_call" | custom-call | flops 536870912 | bytes 1048576 | tf_op jit(solution)/shard_map/prefix/pallas_call | solution.py:806
  50.9 1.5 %collective-permute-start.17 = (f32[10,2048]{1,0:T(8,128)S(1)}, f32[10,2048]{1,0:T(8,128)S(1)}, u32[]{:S(2)}, u32[]{:S(2)}) collective-permute-start(f32[10,2048]{1,0:T(8,128)S(1)} %prefix.1.order), channel_id=1, source_target_pairs={{0,16},{8,24},{16,0},{24,8},{1,17},{9,25},{17,1},{25,9},{2,18},{10... | collective-permute-start | bytes 245768 | tf_op jit(solution)/shard_map/ppermute | solution.py:1000
  52.4 0.0 collective-permute-start.18
  52.4 0.6 collective-permute-start.19
  53.0 5.3 %query.1.grad_partial = f32[128,1024]{1,0:T(8,128)S(1)} custom-call(bf16[256,3072]{1,0:T(8,128)(2,1)S(1)} %get-tuple-element.42.qkv_a, bf16[256,3072]{1,0:T(8,128)(2,1)S(1)} %get-tuple-element.43.qkv_b, bf16[256,128]{1,0:T(8,128)(2,1)S(1)} %get-tuple-element.44.marks_a, bf16[256,128]{1,0:T(8,128)(2,1)S(1)} %get-tuple-element.45.marks_b, ...), custom_call_target="tpu_custom_call" | custom-call | flops 4294967296 | bytes 8388608 | tf_op jit(solution)/shard_map/query/pallas_call | solution.py:850
  58.3 0.0 collective-permute-done.17
  58.3 0.7 collective-permute-start.10
  59.0 0.0 collective-permute-done.18
  59.0 1.5 %collective-permute-start.11 = (bf16[64,1152]{1,0:T(8,128)(2,1)S(1)}, bf16[64,1152]{1,0:T(8,128)(2,1)S(1)}, u32[]{:S(2)}, u32[]{:S(2)}) collective-permute-start(bf16[64,1152]{1,0:T(8,128)(2,1)S(1)} %get-tuple-element.50), channel_id=1, source_target_pairs={{2,0},{3,1},{0,2},{1,3},{10,4},{11,5},{8,6},{9,7},{6,8},{7,9},{4,1... | collective-permute-start | bytes 442376 | tf_op jit(solution)/shard_map/ppermute | solution.py:997
  60.6 0.0 collective-permute-done.19
  60.6 0.0 collective-permute-done.13.grads_2
  60.6 2.8 %collective-permute-start.14 = (bf16[128,1152]{1,0:T(8,128)(2,1)S(1)}, bf16[128,1152]{1,0:T(8,128)(2,1)S(1)}, u32[]{:S(2)}, u32[]{:S(2)}) collective-permute-start(bf16[128,1152]{1,0:T(8,128)(2,1)S(1)} %collective-permute-done.13.grads_2), channel_id=1, source_target_pairs={{0,8},{8,0},{16,24},{24,16},{1,9},{9,1},{17,25},{25,17},{2,10},{10... | collective-permute-start | bytes 884744 | tf_op jit(solution)/shard_map/ppermute | solution.py:996
  63.4 1.4 %collective-permute-start.20 = (f32[10,2048]{1,0:T(8,128)S(1)}, f32[10,2048]{1,0:T(8,128)S(1)}, u32[]{:S(2)}, u32[]{:S(2)}) collective-permute-start(f32[10,2048]{1,0:T(8,128)S(1)} %add_add_fusion.1), channel_id=1, source_target_pairs={{0,2},{1,3},{2,0},{3,1},{4,6},{5,7},{6,4},{7,5},{8,10},{9,11},{10,... | collective-permute-start | bytes 245768 | tf_op jit(solution)/shard_map/ppermute | solution.py:1000
  64.9 1.6 %collective-permute-start.21 = (f32[10,2048]{1,0:T(8,128)S(1)}, f32[10,2048]{1,0:T(8,128)S(1)}, u32[]{:S(2)}, u32[]{:S(2)}) collective-permute-start(f32[10,2048]{1,0:T(8,128)S(1)} %add_add_fusion.1), channel_id=1, source_target_pairs={{0,4},{1,5},{2,6},{3,7},{4,0},{5,1},{6,2},{7,3},{8,12},{9,13},{10,... | collective-permute-start | bytes 245768 | tf_op jit(solution)/shard_map/ppermute | solution.py:1000
  66.5 0.0 collective-permute-done.14.grads_3
  66.5 0.5 collective-permute-start.22
  67.0 6.3 %final.1 = (bf16[64,1024]{1,0:T(8,128)(2,1)S(1)}, bf16[64,1024]{1,0:T(8,128)(2,1)S(1)}) custom-call(bf16[256,3072]{1,0:T(8,128)(2,1)S(1)} %get-tuple-element.42.qkv_a, bf16[256,3072]{1,0:T(8,128)(2,1)S(1)} %get-tuple-element.43.qkv_b, bf16[256,128]{1,0:T(8,128)(2,1)S(1)} %get-tuple-element.44.marks_a, bf16[256,128]{1,0:T(8,128)(2,1)S(1)} %get-tuple-element.45.marks_b, ...), custom_call_target="tpu_custom_call" | custom-call | flops 4294967296 | bytes 8388608 | tf_op jit(solution)/shard_map/final/pallas_call | solution.py:919
  73.4 0.8 collective-permute-start.16
  74.4 1.0 %copy.41 = bf16[64,2,1024]{2,1,0:T(2,128)(2,1)} copy(bf16[64,2,1024]{2,0,1:T(8,128)(2,1)S(1)} %pad_maximum_fusion) | data formatting | bytes 524288
  75.3 2.3 %collective-permute-start.15 = (bf16[64,1024]{1,0:T(8,128)(2,1)S(1)}, bf16[64,1024]{1,0:T(8,128)(2,1)S(1)}, u32[]{:S(2)}, u32[]{:S(2)}) collective-permute-start(bf16[64,1024]{1,0:T(8,128)(2,1)S(1)} %get-tuple-element.56), channel_id=1, source_target_pairs={{2,0},{3,1},{0,2},{1,3},{10,4},{11,5},{8,6},{9,7},{6,8},{7,9},{4,1... | collective-permute-start | bytes 393224 | tf_op jit(solution)/shard_map/ppermute | solution.py:1024
  77.6 7.1 %collective-permute-done.22 = f32[10,2048]{1,0:T(8,128)S(1)} collective-permute-done((f32[10,2048]{1,0:T(8,128)S(1)}, f32[10,2048]{1,0:T(8,128)S(1)}, u32[]{:S(2)}, u32[]{:S(2)}) %collective-permute-start.22) | collective-permute-done | bytes 81952 | tf_op jit(solution)/shard_map/ppermute | solution.py:1000
  84.7 0.6 collective-permute-start.23
  85.3 0.1 copy.40
  85.4 0.1 copy.39
  85.5 0.6 pad_maximum_fusion.2
  86.1 3.7 %collective-permute-done.23 = f32[10,2048]{1,0:T(8,128)S(1)} collective-permute-done((f32[10,2048]{1,0:T(8,128)S(1)}, f32[10,2048]{1,0:T(8,128)S(1)}, u32[]{:S(2)}, u32[]{:S(2)}) %collective-permute-start.23) | collective-permute-done | bytes 81952 | tf_op jit(solution)/shard_map/ppermute | solution.py:1000
  89.8 5.9 %adapter_back.1 = (f32[10,1024]{1,0:T(8,128)}, f32[1024,512]{1,0:T(8,128)}, f32[1,512]{1,0:T(1,128)}, f32[512,2048]{1,0:T(8,128)}, f32[1,2048]{1,0:T(1,128)}) custom-call(f32[10,2048]{1,0:T(8,128)S(1)} %add.33.grads, f32[10,1024]{1,0:T(8,128)S(1)} %copy-done.5, f32[16,512]{1,0:T(8,128)S(1)} %get-tuple-element.38.inner, f32[1024,512]{1,0:T(8,128)} %w_mlp1.3, ...), custom_call_target="tpu_custom_call" | custom-call | flops 4294967296 | bytes 12582912 | tf_op jit(solution)/shard_map/adapter_back/pallas_call | solution.py:513
  95.7 0.0 collective-permute-done.16
  95.8 1.2 %copy.42 = f32[64,2,1024]{2,1,0:T(2,128)} copy(f32[64,2,1024]{2,0,1:T(8,128)S(1)} %maximum_convert_fusion) | data formatting | bytes 1048576
  (31 shorter events, 0.3 us)
Async XLA Ops:
  2.5 8.2 %collective-permute-start = (bf16[64,1152]{1,0:T(8,128)(2,1)S(1)}, bf16[64,1152]{1,0:T(8,128)(2,1)S(1)}, u32[]{:S(2)}, u32[]{:S(2)}) collective-permute-start(bf16[64,1152]{1,0:T(8,128)(2,1)S(1)} %get-tuple-element.97), channel_id=1, source_target_pairs={{0,0},{1,1},{2,2},{3,3},{4,8},{5,9},{6,10},{7,11},{8,4},{9,5},{10,... | collective-permute-start | bytes 442376 | tf_op jit(solution)/shard_map/ppermute | solution.py:980
  3.2 7.5 %collective-permute-start.1 = (bf16[64,1152]{1,0:T(8,128)(2,1)S(1)}, bf16[64,1152]{1,0:T(8,128)(2,1)S(1)}, u32[]{:S(2)}, u32[]{:S(2)}) collective-permute-start(bf16[64,1152]{1,0:T(8,128)(2,1)S(1)} %get-tuple-element.96), channel_id=1, source_target_pairs={{0,2},{1,3},{2,0},{3,1},{4,10},{5,11},{6,8},{7,9},{8,6},{9,7},{10,... | collective-permute-start | bytes 442376 | tf_op jit(solution)/shard_map/ppermute | solution.py:980
  3.3 0.8 copy-start.4
  4.1 0.7 copy-start.6
  4.8 0.7 copy-start.7
  5.5 4.8 %copy-start.8 = (bf16[64,2,1024]{2,1,0:T(2,128)(2,1)S(1)}, bf16[64,2,1024]{2,1,0:T(2,128)(2,1)}, u32[]{:S(2)}) copy-start(bf16[64,2,1024]{2,1,0:T(2,128)(2,1)} %param.31) | copy-start | bytes 786436
  5.5 18.2 %copy-start = (f32[1024]{0:T(1024)S(1)}, f32[1024]{0:T(1024)}, u32[]{:S(2)}) copy-start(f32[1024]{0:T(1024)} %param.19) | copy-start | bytes 12292
  5.5 18.2 %copy-start.1 = (f32[1024]{0:T(1024)S(1)}, f32[1024]{0:T(1024)}, u32[]{:S(2)}) copy-start(f32[1024]{0:T(1024)} %param.18) | copy-start | bytes 12292
  10.7 6.8 %collective-permute-start.2 = (bf16[64,1152]{1,0:T(8,128)(2,1)S(1)}, bf16[64,1152]{1,0:T(8,128)(2,1)S(1)}, u32[]{:S(2)}, u32[]{:S(2)}) collective-permute-start(bf16[64,1152]{1,0:T(8,128)(2,1)S(1)} %collective-permute-done.refs_0_.own_0), channel_id=1, source_target_pairs={{0,8},{8,0},{16,24},{24,16},{1,9},{9,1},{17,25},{25,17},{2,10},{10... | collective-permute-start | bytes 442376 | tf_op jit(solution)/shard_map/ppermute | solution.py:985
  14.7 6.7 %collective-permute-start.4 = (bf16[64,1152]{1,0:T(8,128)(2,1)S(1)}, bf16[64,1152]{1,0:T(8,128)(2,1)S(1)}, u32[]{:S(2)}, u32[]{:S(2)}) collective-permute-start(bf16[64,1152]{1,0:T(8,128)(2,1)S(1)} %collective-permute-done.refs_0_.own_0), channel_id=1, source_target_pairs={{0,1},{1,0},{2,3},{3,2},{4,5},{5,4},{6,7},{7,6},{8,9},{9,8},{10,11... | collective-permute-start | bytes 442376 | tf_op jit(solution)/shard_map/ppermute | solution.py:984
  16.2 7.5 %collective-permute-start.3 = (bf16[64,1152]{1,0:T(8,128)(2,1)S(1)}, bf16[64,1152]{1,0:T(8,128)(2,1)S(1)}, u32[]{:S(2)}, u32[]{:S(2)}) collective-permute-start(bf16[64,1152]{1,0:T(8,128)(2,1)S(1)} %collective-permute-done.1.refs_1_.own_1), channel_id=1, source_target_pairs={{0,8},{8,0},{16,24},{24,16},{1,9},{9,1},{17,25},{25,17},{2,10},{10... | collective-permute-start | bytes 442376 | tf_op jit(solution)/shard_map/ppermute | solution.py:985
  16.2 7.5 %collective-permute-start.5 = (bf16[64,1152]{1,0:T(8,128)(2,1)S(1)}, bf16[64,1152]{1,0:T(8,128)(2,1)S(1)}, u32[]{:S(2)}, u32[]{:S(2)}) collective-permute-start(bf16[64,1152]{1,0:T(8,128)(2,1)S(1)} %collective-permute-done.1.refs_1_.own_1), channel_id=1, source_target_pairs={{0,1},{1,0},{2,3},{3,2},{4,5},{5,4},{6,7},{7,6},{8,9},{9,8},{10,11... | collective-permute-start | bytes 442376 | tf_op jit(solution)/shard_map/ppermute | solution.py:984
  16.8 13.1 %collective-permute-start.8 = (bf16[64,1024]{1,0:T(8,128)(2,1)S(1)}, bf16[64,1024]{1,0:T(8,128)(2,1)S(1)}, u32[]{:S(2)}, u32[]{:S(2)}) collective-permute-start(bf16[64,1024]{1,0:T(8,128)(2,1)S(1)} %get-tuple-element.47), channel_id=1, source_target_pairs={{0,0},{1,1},{2,2},{3,3},{4,8},{5,9},{6,10},{7,11},{8,4},{9,5},{10,... | collective-permute-start | bytes 393224 | tf_op jit(solution)/shard_map/ppermute | solution.py:986
  17.5 12.4 %collective-permute-start.9 = (bf16[64,1024]{1,0:T(8,128)(2,1)S(1)}, bf16[64,1024]{1,0:T(8,128)(2,1)S(1)}, u32[]{:S(2)}, u32[]{:S(2)}) collective-permute-start(bf16[64,1024]{1,0:T(8,128)(2,1)S(1)} %get-tuple-element.48), channel_id=1, source_target_pairs={{0,2},{1,3},{2,0},{3,1},{4,10},{5,11},{6,8},{7,9},{8,6},{9,7},{10,... | collective-permute-start | bytes 393224 | tf_op jit(solution)/shard_map/ppermute | solution.py:986
  21.4 5.4 %collective-permute-start.6 = (bf16[64,1152]{1,0:T(8,128)(2,1)S(1)}, bf16[64,1152]{1,0:T(8,128)(2,1)S(1)}, u32[]{:S(2)}, u32[]{:S(2)}) collective-permute-start(bf16[64,1152]{1,0:T(8,128)(2,1)S(1)} %collective-permute-done.4.refs_0_), channel_id=1, source_target_pairs={{0,8},{8,0},{16,24},{24,16},{1,9},{9,1},{17,25},{25,17},{2,10},{10... | collective-permute-start | bytes 442376 | tf_op jit(solution)/shard_map/ppermute | solution.py:987
  23.7 3.1 %collective-permute-start.7 = (bf16[64,1152]{1,0:T(8,128)(2,1)S(1)}, bf16[64,1152]{1,0:T(8,128)(2,1)S(1)}, u32[]{:S(2)}, u32[]{:S(2)}) collective-permute-start(bf16[64,1152]{1,0:T(8,128)(2,1)S(1)} %collective-permute-done.5.refs_1_), channel_id=1, source_target_pairs={{0,8},{8,0},{16,24},{24,16},{1,9},{9,1},{17,25},{25,17},{2,10},{10... | collective-permute-start | bytes 442376 | tf_op jit(solution)/shard_map/ppermute | solution.py:987
  26.8 3.1 %copy-start.2 = (f32[1024]{0:T(1024)S(1)}, f32[1024]{0:T(1024)}, u32[]{:S(2)}) copy-start(f32[1024]{0:T(1024)} %param.22) | copy-start | bytes 12292
  26.8 3.1 %copy-start.3 = (f32[1024]{0:T(1024)S(1)}, f32[1024]{0:T(1024)}, u32[]{:S(2)}) copy-start(f32[1024]{0:T(1024)} %param.23) | copy-start | bytes 12292
  46.5 18.4 %collective-permute-start.12 = (bf16[128,1152]{1,0:T(8,128)(2,1)S(1)}, bf16[128,1152]{1,0:T(8,128)(2,1)S(1)}, u32[]{:S(2)}, u32[]{:S(2)}) collective-permute-start(bf16[128,1152]{1,0:T(8,128)(2,1)S(1)} %get-tuple-element.51.grads.grads_0), channel_id=1, source_target_pairs={{0,8},{8,0},{16,24},{24,16},{1,9},{9,1},{17,25},{25,17},{2,10},{10... | collective-permute-start | bytes 884744 | tf_op jit(solution)/shard_map/ppermute | solution.py:995
  47.1 13.5 %collective-permute-start.13 = (bf16[128,1152]{1,0:T(8,128)(2,1)S(1)}, bf16[128,1152]{1,0:T(8,128)(2,1)S(1)}, u32[]{:S(2)}, u32[]{:S(2)}) collective-permute-start(bf16[128,1152]{1,0:T(8,128)(2,1)S(1)} %get-tuple-element.51.grads.grads_0), channel_id=1, source_target_pairs={{0,1},{1,0},{2,3},{3,2},{4,5},{5,4},{6,7},{7,6},{8,9},{9,8},{10,11... | collective-permute-start | bytes 884744 | tf_op jit(solution)/shard_map/ppermute | solution.py:994
  50.9 7.5 %collective-permute-start.17 = (f32[10,2048]{1,0:T(8,128)S(1)}, f32[10,2048]{1,0:T(8,128)S(1)}, u32[]{:S(2)}, u32[]{:S(2)}) collective-permute-start(f32[10,2048]{1,0:T(8,128)S(1)} %prefix.1.order), channel_id=1, source_target_pairs={{0,16},{8,24},{16,0},{24,8},{1,17},{9,25},{17,1},{25,9},{2,18},{10... | collective-permute-start | bytes 245768 | tf_op jit(solution)/shard_map/ppermute | solution.py:1000
  52.4 6.6 %collective-permute-start.18 = (f32[10,2048]{1,0:T(8,128)S(1)}, f32[10,2048]{1,0:T(8,128)S(1)}, u32[]{:S(2)}, u32[]{:S(2)}) collective-permute-start(f32[10,2048]{1,0:T(8,128)S(1)} %prefix.1.order), channel_id=1, source_target_pairs={{0,8},{8,0},{16,24},{24,16},{1,9},{9,1},{17,25},{25,17},{2,10},{10... | collective-permute-start | bytes 245768 | tf_op jit(solution)/shard_map/ppermute | solution.py:1000
  52.4 8.2 %collective-permute-start.19 = (f32[10,2048]{1,0:T(8,128)S(1)}, f32[10,2048]{1,0:T(8,128)S(1)}, u32[]{:S(2)}, u32[]{:S(2)}) collective-permute-start(f32[10,2048]{1,0:T(8,128)S(1)} %prefix.1.order), channel_id=1, source_target_pairs={{0,24},{8,16},{16,8},{24,0},{1,25},{9,17},{17,9},{25,1},{2,26},{10... | collective-permute-start | bytes 245768 | tf_op jit(solution)/shard_map/ppermute | solution.py:1000
  58.3 15.0 %collective-permute-start.10 = (bf16[64,1152]{1,0:T(8,128)(2,1)S(1)}, bf16[64,1152]{1,0:T(8,128)(2,1)S(1)}, u32[]{:S(2)}, u32[]{:S(2)}) collective-permute-start(bf16[64,1152]{1,0:T(8,128)(2,1)S(1)} %get-tuple-element.49), channel_id=1, source_target_pairs={{0,0},{1,1},{2,2},{3,3},{8,4},{9,5},{10,6},{11,7},{4,8},{5,9},{6,1... | collective-permute-start | bytes 442376 | tf_op jit(solution)/shard_map/ppermute | solution.py:997
  59.0 15.2 %collective-permute-start.11 = (bf16[64,1152]{1,0:T(8,128)(2,1)S(1)}, bf16[64,1152]{1,0:T(8,128)(2,1)S(1)}, u32[]{:S(2)}, u32[]{:S(2)}) collective-permute-start(bf16[64,1152]{1,0:T(8,128)(2,1)S(1)} %get-tuple-element.50), channel_id=1, source_target_pairs={{2,0},{3,1},{0,2},{1,3},{10,4},{11,5},{8,6},{9,7},{6,8},{7,9},{4,1... | collective-permute-start | bytes 442376 | tf_op jit(solution)/shard_map/ppermute | solution.py:997
  60.6 6.0 %collective-permute-start.14 = (bf16[128,1152]{1,0:T(8,128)(2,1)S(1)}, bf16[128,1152]{1,0:T(8,128)(2,1)S(1)}, u32[]{:S(2)}, u32[]{:S(2)}) collective-permute-start(bf16[128,1152]{1,0:T(8,128)(2,1)S(1)} %collective-permute-done.13.grads_2), channel_id=1, source_target_pairs={{0,8},{8,0},{16,24},{24,16},{1,9},{9,1},{17,25},{25,17},{2,10},{10... | collective-permute-start | bytes 884744 | tf_op jit(solution)/shard_map/ppermute | solution.py:996
  63.4 14.2 %collective-permute-start.20 = (f32[10,2048]{1,0:T(8,128)S(1)}, f32[10,2048]{1,0:T(8,128)S(1)}, u32[]{:S(2)}, u32[]{:S(2)}) collective-permute-start(f32[10,2048]{1,0:T(8,128)S(1)} %add_add_fusion.1), channel_id=1, source_target_pairs={{0,2},{1,3},{2,0},{3,1},{4,6},{5,7},{6,4},{7,5},{8,10},{9,11},{10,... | collective-permute-start | bytes 245768 | tf_op jit(solution)/shard_map/ppermute | solution.py:1000
  64.9 12.7 %collective-permute-start.21 = (f32[10,2048]{1,0:T(8,128)S(1)}, f32[10,2048]{1,0:T(8,128)S(1)}, u32[]{:S(2)}, u32[]{:S(2)}) collective-permute-start(f32[10,2048]{1,0:T(8,128)S(1)} %add_add_fusion.1), channel_id=1, source_target_pairs={{0,4},{1,5},{2,6},{3,7},{4,0},{5,1},{6,2},{7,3},{8,12},{9,13},{10,... | collective-permute-start | bytes 245768 | tf_op jit(solution)/shard_map/ppermute | solution.py:1000
  66.5 18.2 %collective-permute-start.22 = (f32[10,2048]{1,0:T(8,128)S(1)}, f32[10,2048]{1,0:T(8,128)S(1)}, u32[]{:S(2)}, u32[]{:S(2)}) collective-permute-start(f32[10,2048]{1,0:T(8,128)S(1)} %add_add_fusion.1), channel_id=1, source_target_pairs={{0,6},{1,7},{2,4},{3,5},{4,2},{5,3},{6,0},{7,1},{8,14},{9,15},{10,... | collective-permute-start | bytes 245768 | tf_op jit(solution)/shard_map/ppermute | solution.py:1000
  67.0 22.8 %copy-start.5 = (f32[10,1024]{1,0:T(8,128)S(1)}, f32[10,1024]{1,0:T(8,128)}, u32[]{:S(2)}) copy-start(f32[10,1024]{1,0:T(8,128)} %embed.3) | copy-start | bytes 122884
  73.4 22.4 %collective-permute-start.16 = (bf16[64,1024]{1,0:T(8,128)(2,1)S(1)}, bf16[64,1024]{1,0:T(8,128)(2,1)S(1)}, u32[]{:S(2)}, u32[]{:S(2)}) collective-permute-start(bf16[64,1024]{1,0:T(8,128)(2,1)S(1)} %get-tuple-element.53.order), channel_id=1, source_target_pairs={{0,0},{1,1},{2,2},{3,3},{8,4},{9,5},{10,6},{11,7},{4,8},{5,9},{6,1... | collective-permute-start | bytes 393224 | tf_op jit(solution)/shard_map/ppermute | solution.py:1024
  75.3 20.4 %collective-permute-start.15 = (bf16[64,1024]{1,0:T(8,128)(2,1)S(1)}, bf16[64,1024]{1,0:T(8,128)(2,1)S(1)}, u32[]{:S(2)}, u32[]{:S(2)}) collective-permute-start(bf16[64,1024]{1,0:T(8,128)(2,1)S(1)} %get-tuple-element.56), channel_id=1, source_target_pairs={{2,0},{3,1},{0,2},{1,3},{10,4},{11,5},{8,6},{9,7},{6,8},{7,9},{4,1... | collective-permute-start | bytes 393224 | tf_op jit(solution)/shard_map/ppermute | solution.py:1024
  84.7 5.0 %collective-permute-start.23 = (f32[10,2048]{1,0:T(8,128)S(1)}, f32[10,2048]{1,0:T(8,128)S(1)}, u32[]{:S(2)}, u32[]{:S(2)}) collective-permute-start(f32[10,2048]{1,0:T(8,128)S(1)} %add_add_fusion), channel_id=1, source_target_pairs={{0,1},{1,0},{2,3},{3,2},{4,5},{5,4},{6,7},{7,6},{8,9},{9,8},{10,11... | collective-permute-start | bytes 245768 | tf_op jit(solution)/shard_map/ppermute | solution.py:1000

commit v3 on v2

--- a/solution.py
+++ b/solution.py
@@ -336,7 +336,7 @@
     return [pltpu.with_memory_space_constraint(a, pltpu.HBM) for a in arrays]
 
 
-def project_kernel(count, step, *refs):
+def project_kernel(count, *refs):
     messages, (gain, bias, weight, out, marks, normed) = refs[:count], refs[count:]
     half, width = messages[0].shape[0], normed.shape[1]
     for i, message in enumerate(messages):
@@ -344,21 +344,17 @@
         unit, _ = norm_parts(message[:, :width].astype(F32))
         normed[rows] = (unit * gain[...] + bias[...]).astype(BF16)
         marks[rows] = message[:, width:]
-
-    def columns(i, carry):
-        at = pl.ds(pl.multiple_of(i * step, step), step)
+    for i in range(3):
+        at = pl.ds(i * width, width)
         out[:, at] = nn(normed[...], weight[:, at]).astype(BF16)
-        return carry
-
-    lax.fori_loop(0, weight.shape[1] // step, columns, 0)
-
-
-def project(messages, gain, bias, weight, step=512):
+
+
+def project(messages, gain, bias, weight):
     count, half = len(messages), messages[0].shape[0]
     width, columns = weight.shape
     rows = count * half
     return pl.pallas_call(
-        partial(project_kernel, count, step),
+        partial(project_kernel, count),
         in_specs=[vmem()] * (count + 3),
         out_specs=[vmem()] * 2,
         out_shape=[
@@ -394,20 +390,39 @@
 
 
 def adapter_kernel(
-    embed, w_mlp1, b_mlp1, w_mlp2, b_mlp2, w_qkv, out, inner, v_qkv, v_mlp1, v_mlp2, sems
+    h_embed,
+    w_mlp1,
+    h_mlp1,
+    w_mlp2,
+    h_mlp2,
+    w_qkv,
+    out,
+    inner,
+    v_qkv,
+    embed,
+    v_mlp1,
+    v_mlp2,
+    b_mlp1,
+    b_mlp2,
+    sems,
 ):
     steps, step = v_mlp2.shape[0], v_mlp2.shape[2]
-    first = pltpu.make_async_copy(w_mlp1, v_mlp1, sems.at[0])
-    first.start()
+    small = []
+    for i, (source, target) in enumerate(
+        ((h_embed, embed), (h_mlp1, b_mlp1), (h_mlp2, b_mlp2), (w_mlp1, v_mlp1))
+    ):
+        small.append(pltpu.make_async_copy(source, target, sems.at[steps + i]))
+        small[-1].start()
     rest = []
     for i in range(steps):
-        copy = pltpu.make_async_copy(w_mlp2.at[:, pl.ds(i * step, step)], v_mlp2.at[i], sems.at[1 + i])
+        copy = pltpu.make_async_copy(w_mlp2.at[:, pl.ds(i * step, step)], v_mlp2.at[i], sems.at[i])
         copy.start()
         rest.append(copy)
-    weights = pltpu.make_async_copy(w_qkv, v_qkv, sems.at[1 + steps])
+    weights = pltpu.make_async_copy(w_qkv, v_qkv, sems.at[steps + len(small)])
     weights.start()
+    for copy in small:
+        copy.wait()
     source = pad_rows(embed[...], PRE_ROWS)
-    first.wait()
     act = jnp.tanh(three_products(nn, source, v_mlp1[...]) + b_mlp1[...])
     inner[...] = act
     for i, copy in enumerate(rest):
@@ -424,22 +439,25 @@
     steps = 4
     return pl.pallas_call(
         adapter_kernel,
-        in_specs=[vmem(), hbm(), vmem(), hbm(), vmem(), hbm()],
-        out_specs=[vmem()] * 3,
+        in_specs=[hbm()] * 6,
+        out_specs=[vmem()] * 6,
         out_shape=[
             jax.ShapeDtypeStruct((PRE_ROWS, columns), BF16),
             jax.ShapeDtypeStruct((PRE_ROWS, hidden), F32),
             pltpu.VMEM(w_qkv.shape, w_qkv.dtype),
+            pltpu.VMEM(embed.shape, F32),
+            pltpu.VMEM((width, hidden), F32),
+            pltpu.VMEM((steps, hidden, columns // steps), F32),
         ],
         scratch_shapes=[
-            pltpu.VMEM((width, hidden), F32),
-            pltpu.VMEM((steps, hidden, columns // steps), F32),
-            pltpu.SemaphoreType.DMA((2 + steps,)),
+            pltpu.VMEM((1, hidden), F32),
+            pltpu.VMEM((1, columns), F32),
+            pltpu.SemaphoreType.DMA((5 + steps,)),
         ],
         compiler_params=pltpu.CompilerParams(vmem_limit_bytes=20 * MIB),
         cost_estimate=pl.CostEstimate(flops=1 << 32, bytes_accessed=6 * MIB, transcendentals=1 << 13),
         name="adapter",
-    )(embed, *kept_in_hbm(w_mlp1), b_mlp1[None], *kept_in_hbm(w_mlp2), b_mlp2[None], *kept_in_hbm(w_qkv))
+    )(*kept_in_hbm(embed, w_mlp1, b_mlp1[None], w_mlp2, b_mlp2[None], w_qkv))
 
 
 def outer(left, right):
@@ -454,65 +472,60 @@
 
 
 def adapter_back_kernel(
-    grads,
+    mine,
+    mine_y,
+    other,
+    other_y,
     embed,
     inner,
-    w_mlp1,
-    w_mlp2,
+    v_mlp1,
+    v_mlp2,
     order,
     grad_prefix,
     grad_mlp1,
     grad_bias1,
     grad_mlp2,
     grad_bias2,
-    v_mlp1,
-    v_mlp2,
     o_mlp1,
     o_mlp2,
     sems,
 ):
     del order
     steps, step = v_mlp2.shape[0], v_mlp2.shape[2]
-    loads = []
-    for i in range(steps):
-        span = pl.ds(i * step, step)
-        loads.append(pltpu.make_async_copy(w_mlp2.at[:, span], v_mlp2.at[i], sems.at[i]))
-    loads.append(pltpu.make_async_copy(w_mlp1, v_mlp1, sems.at[steps]))
-    for copy in loads:
-        copy.start()
+    first = lax.axis_index("seq") % 2 == 0
+    own, beside = mine[...] + mine_y[...], other[...] + other_y[...]
+    grads = jnp.concatenate([jnp.where(first, own, beside), jnp.where(first, beside, own)], 1)
+    grads = pad_rows(grads, PRE_ROWS)
     act = inner[...]
     stores = []
     back = jnp.zeros(act.shape, F32)
+    grad_bias2[...] = jnp.sum(grads, 0, keepdims=True)
     for i in range(steps):
-        span = pl.ds(i * step, step)
-        part = pad_rows(grads[:, span], PRE_ROWS)
-        grad_bias2[:, span] = jnp.sum(part, 0, keepdims=True)
+        part = grads[:, i * step : (i + 1) * step]
         o_mlp2[i] = outer(act, part)
-        copy = pltpu.make_async_copy(o_mlp2.at[i], grad_mlp2.at[:, span], sems.at[steps + 1 + i])
-        copy.start()
-        stores.append(copy)
-        loads[i].wait()
-        back = back + three_products(nt, part, v_mlp2[i])
+        stores.append(
+            pltpu.make_async_copy(o_mlp2.at[i], grad_mlp2.at[:, pl.ds(i * step, step)], sems.at[i])
+        )
+        stores[-1].start()
+    for i in range(steps):
+        back = back + three_products(nt, grads[:, i * step : (i + 1) * step], v_mlp2[i])
     back = back * (1.0 - act * act)
     grad_bias1[...] = jnp.sum(back, 0, keepdims=True)
     o_mlp1[...] = outer(pad_rows(embed[...], PRE_ROWS), back)
-    copy = pltpu.make_async_copy(o_mlp1, grad_mlp1, sems.at[2 * steps + 1])
-    copy.start()
-    stores.append(copy)
-    loads[steps].wait()
+    stores.append(pltpu.make_async_copy(o_mlp1, grad_mlp1, sems.at[steps]))
+    stores[-1].start()
     grad_prefix[...] = three_products(nt, back, v_mlp1[...])[: embed.shape[0]]
     for copy in stores:
         copy.wait()
 
 
-def adapter_backward(grads, embed, inner, w_mlp1, w_mlp2, order):
-    width, hidden = w_mlp1.shape
-    columns = w_mlp2.shape[1]
-    steps = 4
-    step = columns // steps
+def adapter_backward(parts, embed, inner, v_mlp1, v_mlp2, order):
+    width, hidden = v_mlp1.shape
+    steps, _, step = v_mlp2.shape
+    columns = steps * step
     out = pl.pallas_call(
         adapter_back_kernel,
-        in_specs=[vmem()] * 3 + [hbm()] * 2 + [pl.BlockSpec(memory_space=pl.ANY)],
+        in_specs=[vmem()] * 8 + [pl.BlockSpec(memory_space=pl.ANY)],
         out_specs=[vmem(), hbm(), vmem(), hbm(), vmem()],
         out_shape=[
             jax.ShapeDtypeStruct(embed.shape, F32),
@@ -524,14 +537,12 @@
         scratch_shapes=[
             pltpu.VMEM((width, hidden), F32),
             pltpu.VMEM((steps, hidden, step), F32),
-            pltpu.VMEM((width, hidden), F32),
-            pltpu.VMEM((steps, hidden, step), F32),
-            pltpu.SemaphoreType.DMA((2 * steps + 2,)),
+            pltpu.SemaphoreType.DMA((steps + 1,)),
         ],
         compiler_params=pltpu.CompilerParams(vmem_limit_bytes=28 * MIB),
-        cost_estimate=pl.CostEstimate(flops=1 << 32, bytes_accessed=12 * MIB, transcendentals=0),
+        cost_estimate=pl.CostEstimate(flops=1 << 32, bytes_accessed=6 * MIB, transcendentals=0),
         name="adapter_back",
-    )(grads, embed, inner, *kept_in_hbm(w_mlp1, w_mlp2), order)
+    )(*parts, embed, inner, v_mlp1, v_mlp2, order)
     return out[0], out[1], out[2][0], out[3], out[4][0]
 
 
@@ -658,7 +669,7 @@
             stats[...] = jnp.where(here, log_total[i * rows : (i + 1) * rows], stats[...])
         return carry
 
-    lax.fori_loop(0, HEADS // 2, attend, 0)
+    lax.fori_loop(0, HEADS // 2, attend, 0, unroll=4)
 
     copies[0].wait()
     inputs = jnp.concatenate([own_0[:, :width], own_1[:, :width]], 0).astype(F32)
@@ -688,7 +699,7 @@
         grad_norm[...] += nt(grad_pre, fc)
         return carry
 
-    lax.fori_loop(0, steps, feed, 0)
+    lax.fori_loop(0, steps, feed, 0, unroll=True)
 
     out = total[...].astype(BF16)
     back_0[:, :width] = out[:half]
@@ -725,7 +736,7 @@
     half, width = cots[0].shape
     rows = 2 * half
     hidden = w_fc.shape[1]
-    steps = 8
+    steps = 2
     step = hidden // steps
     wide = width + LANES
     return pl.pallas_call(
@@ -781,8 +792,9 @@
     return join_heads(key_grad, low) * HEAD**-0.5, join_heads(value_grad, low)
 
 
-def prefix_kernel(qkv_a, grads, prefix_kv, out):
-    used = out.shape[0]
+def prefix_kernel(qkv_a, grads, prefix_kv, mine, theirs):
+    used = mine.shape[0]
+    first = lax.axis_index("seq") % 2 == 0
     rows, width = grads.shape[0], grads.shape[1] - LANES
     count = prefix_kv.shape[0]
     low = head_mask(count)
@@ -795,19 +807,20 @@
         key_grad, value_grad = key_grads(
             prefix_kv[:, at], prefix_kv[:, at_v], qkv_a[:rows, at], grads[:, at], marks, pair, low, mask
         )
-        out[:, at] = key_grad[:used]
-        out[:, at_v] = value_grad[:used]
+        mine[:, at] = jnp.where(first, key_grad, value_grad)[:used]
+        theirs[:, at] = jnp.where(first, value_grad, key_grad)[:used]
         return carry
 
-    lax.fori_loop(0, HEADS // 2, step, 0)
+    lax.fori_loop(0, HEADS // 2, step, 0, unroll=True)
 
 
 def prefix_part(count, qkv_a, grads, prefix_kv):
+    half = prefix_kv.shape[1] // 2
     return pl.pallas_call(
         prefix_kernel,
         in_specs=[vmem()] * 3,
-        out_specs=vmem(),
-        out_shape=jax.ShapeDtypeStruct((count, prefix_kv.shape[1]), F32),
+        out_specs=[vmem()] * 2,
+        out_shape=[jax.ShapeDtypeStruct((count, half), F32)] * 2,
         compiler_params=pltpu.CompilerParams(vmem_limit_bytes=16 * MIB),
         cost_estimate=pl.CostEstimate(flops=1 << 29, bytes_accessed=1 << 20, transcendentals=1 << 16),
         name="prefix",
@@ -841,7 +854,7 @@
         grad_query[:, at] = (grad * HEAD**-0.5).astype(BF16)
         return carry
 
-    lax.fori_loop(0, HEADS // 2, step, 0)
+    lax.fori_loop(0, HEADS // 2, step, 0, unroll=True)
     out[...] = nt(grad_query[...], weight[:, :width])
 
 
@@ -904,7 +917,7 @@
         grad_keys[:, at_k] = value_grad.astype(BF16)
         return carry
 
-    lax.fori_loop(0, HEADS // 2, step, 0)
+    lax.fori_loop(0, HEADS // 2, step, 0, unroll=True)
     grad_norm = grad_partial[...] + nt(grad_keys[...], weight[:, width:])
     inputs = jnp.concatenate([own_0[:, :width], own_1[:, :width]], 0).astype(F32)
     unit, inverse = norm_parts(inputs)
@@ -965,6 +978,7 @@
     back = [[(b, a) for a, b in pairs] for pairs in there]
     swap_core = [(i, i ^ 1) for i in range(4)]
     swap_y = [(i, i ^ 1) for i in range(8)]
+    swap_both = [(i, i ^ 9) for i in range(32)]
     odd = (lax.axis_index("blk") // 2) % 2 == 1
 
     def sorted_rows(first, second):
@@ -978,12 +992,14 @@
     out_msgs = sorted_rows(marked[:, 0], marked[:, 1])
     cot_msgs = sorted_rows(cotangent[:, 0], cotangent[:, 1])
     own = [lax.ppermute(m, everyone, there[k]) for k, m in enumerate(out_msgs)]
-    prefix_kv, inner, w_near = adapter_forward(prefix_embed, w_mlp1, b_mlp1, w_mlp2, b_mlp2, w_qkv)
+    prefix_kv, inner, w_near, near_embed, near_mlp1, near_mlp2 = adapter_forward(
+        prefix_embed, w_mlp1, b_mlp1, w_mlp2, b_mlp2, w_qkv
+    )
     count = prefix_embed.shape[0]
     own = after(own, inner)
     across = [lax.ppermute(m, "blk", swap_y) for m in own]
     beside = [lax.ppermute(m, "seq", swap_core) for m in own]
-    cots = [lax.ppermute(m, everyone, there[k]) for k, m in enumerate(after(cot_msgs, own))]
+    cots = [lax.ppermute(m, everyone, there[k]) for k, m in enumerate(after(cot_msgs, beside))]
     beyond = [lax.ppermute(m, "seq", swap_core) for m in across]
 
     qkv_a, marks_a = project(own + beside, ln1_gain, ln1_bias, w_near)
@@ -1002,13 +1018,9 @@
     def add_four(value, others):
         return (value + others[0]) + (others[1] + others[2])
 
-    grad_prefix_kv = prefix_part(count, qkv_a, grads, prefix_kv)
-    parts = spread(grad_prefix_kv, "seq", 4, (2, 1, 3))
-    grad_partial = query_part(
-        count, qkv_a, qkv_b, marks_a, marks_b, prefix_kv, grads, w_near, grad_prefix_kv
-    )
-    grad_prefix_kv = add_four(grad_prefix_kv, after(parts, grads_y, grad_partial))
-    parts = spread(grad_prefix_kv, "blk", 8, (2, 4, 6))
+    mine, theirs = prefix_part(count, qkv_a, grads, prefix_kv)
+    parts = spread(mine, "seq", 4, (2,)) + spread(theirs, "seq", 4, (1, 3))
+    grad_partial = query_part(count, qkv_a, qkv_b, marks_a, marks_b, prefix_kv, grads, w_near, mine)
     final_0, final_1 = final_part(
         qkv_a,
         qkv_b,
@@ -1022,10 +1034,12 @@
         w_near,
     )
     finals = [lax.ppermute(m, everyone, back[k]) for k, m in enumerate((final_0, final_1))]
-    grad_prefix_kv = add_four(grad_prefix_kv, after(parts, final_0))
-    parts = spread(grad_prefix_kv, "blk", 8, (1,))
-    grad_prefix_kv = grad_prefix_kv + parts[0]
-    summed = adapter_backward(grad_prefix_kv, prefix_embed, inner, w_mlp1, w_mlp2, final_0)
+    mine = add_four(mine, after(parts, grads_y, grad_partial))
+    mine = add_four(mine, spread(mine, "blk", 8, (2, 4, 6)))
+    halves_in = [mine]
+    halves_in += [lax.ppermute(mine, "blk", swap_y), lax.ppermute(mine, "seq", swap_core)]
+    halves_in += [lax.ppermute(mine, everyone, swap_both)]
+    summed = adapter_backward(halves_in, near_embed, inner, near_mlp1, near_mlp2, final_0)
 
     home = sorted_rows(*after(home, final_0))
     block_out = jnp.stack([m[:, :width] for m in home], 1)

time: 97.4 us -> 85.3 us (0.88)
  the two profiles are of different devices: /device:TPU:8 before, /device:TPU:1 now
where the time goes in v3:
time: 85.3 us; the launch traced here: 85.1 us
  Pallas kernels  37.4 us (44%)
  starting transfers between devices  35.3 us (41%)
  waiting for transfers between devices  5.97 us (7%)
  local copies, waits for them, and re-layouts  3.73 us (4%)
  other arithmetic  1.7 us (2%)
  between operations  1.02 us (1%)
    pallas_call x1, Pallas kernels, middle_part(): pl.pallas_call(partial(middle_kernel, count), in_specs=[vmem()] * 11 + [h...  14 us
    ppermute x4, starting transfers between devices, body_rows(): lax.ppermute(m, everyone, back[k])  10.7 us
    ppermute x2, starting transfers between devices, body_rows(): own = [lax.ppermute(m, everyone, there[k]) for k, m in enumerate(out_msgs)]  6.7 us
    ppermute x2, starting transfers between devices, body_rows(): lax.ppermute(m, everyone, there[k])  5.77 us
    ppermute x6, starting transfers between devices, spread(): lax.ppermute(value, axis, [(i, i ^ far) for i in range(size)])  5.24 us
    pallas_call x1, Pallas kernels, adapter_forward(): pl.pallas_call(adapter_kernel, in_specs=[hbm()] * 6, out_specs=[vmem()] *...  4.87 us
    pallas_call x1, Pallas kernels, final_part(): pl.pallas_call(final_kernel, in_specs=[vmem()] * 14, out_specs=[vmem()] *...  4.8 us
    pallas_call x1, Pallas kernels, adapter_backward(): pl.pallas_call(adapter_back_kernel, in_specs=[vmem()] * 8 + [pl.BlockSpec...  4.65 us
  transfers between devices with their start and end apart: 26, of which 5 were waited for; matrix products, arithmetic and copies ran while one was open for 3% of the time, Pallas kernels for 27%

profile of v3, /device:TPU:1, one launch (start us, length us, event | category | flops | bytes accessed | tf_op | source)
XLA Modules:
  0.0 85.1 jit_solution(3662976966273116937)
XLA Ops:
  0.7 0.8 fusion.1
  1.4 1.0 %copy.36 = bf16[64,2,1024]{2,0,1:T(8,128)(2,1)S(1)} copy(bf16[64,2,1024]{2,1,0:T(2,128)(2,1)} %param.16) | data formatting | bytes 524288 | tf_op args[0]
  2.4 0.1 select_bitcast_fusion
  2.5 5.6 %collective-permute-start = (bf16[64,1152]{1,0:T(8,128)(2,1)S(1)}, bf16[64,1152]{1,0:T(8,128)(2,1)S(1)}, u32[]{:S(2)}, u32[]{:S(2)}) collective-permute-start(bf16[64,1152]{1,0:T(8,128)(2,1)S(1)} %get-tuple-element.101), channel_id=1, source_target_pairs={{0,0},{1,1},{2,2},{3,3},{4,8},{5,9},{6,10},{7,11},{8,4},{9,5},{10,... | collective-permute-start | bytes 442376 | tf_op jit(solution)/shard_map/ppermute | solution.py:994
  8.1 1.1 %collective-permute-start.1 = (bf16[64,1152]{1,0:T(8,128)(2,1)S(1)}, bf16[64,1152]{1,0:T(8,128)(2,1)S(1)}, u32[]{:S(2)}, u32[]{:S(2)}) collective-permute-start(bf16[64,1152]{1,0:T(8,128)(2,1)S(1)} %get-tuple-element.100), channel_id=1, source_target_pairs={{0,2},{1,3},{2,0},{3,1},{4,10},{5,11},{6,8},{7,9},{8,6},{9,7},{10,... | collective-permute-start | bytes 442376 | tf_op jit(solution)/shard_map/ppermute | solution.py:994
  9.2 4.9 %adapter.1 = (bf16[16,2048]{1,0:T(8,128)(2,1)S(1)}, f32[16,512]{1,0:T(8,128)S(1)}, bf16[1024,3072]{1,0:T(8,128)(2,1)S(1)}, f32[10,1024]{1,0:T(8,128)S(1)}, f32[1...) custom-call(f32[10,1024]{1,0:T(8,128)} %h_embed.1, f32[1024,512]{1,0:T(8,128)} %w_mlp1.1, f32[1,512]{1,0:T(1,128)} %bitcast.44, ...), custom_call_target="tpu_custom_call" | custom-call | flops 4294967296 | bytes 6291456 | tf_op jit(solution)/shard_map/adapter/pallas_call | solution.py:440
  14.1 0.0 copy-start.4
  14.1 0.4 fusion.2
  14.5 0.0 collective-permute-done.refs_0_.own_0
  14.5 0.2 collective-permute-done.1.refs_1_.own_1
  14.7 0.0 collective-permute-start.2
  14.7 1.2 %collective-permute-start.4 = (bf16[64,1152]{1,0:T(8,128)(2,1)S(1)}, bf16[64,1152]{1,0:T(8,128)(2,1)S(1)}, u32[]{:S(2)}, u32[]{:S(2)}) collective-permute-start(bf16[64,1152]{1,0:T(8,128)(2,1)S(1)} %collective-permute-done.refs_0_.own_0), channel_id=1, source_target_pairs={{0,1},{1,0},{2,3},{3,2},{4,5},{5,4},{6,7},{7,6},{8,9},{9,8},{10,11... | collective-permute-start | bytes 442376 | tf_op jit(solution)/shard_map/ppermute | solution.py:1000
  15.9 0.8 collective-permute-start.3
  16.7 0.2 collective-permute-start.5
  16.9 0.1 select_bitcast_fusion.4
  17.0 0.0 collective-permute-done.2.refs_2_
  17.0 0.7 collective-permute-done.3.refs_3_
  17.7 5.4 %collective-permute-start.8 = (bf16[64,1024]{1,0:T(8,128)(2,1)S(1)}, bf16[64,1024]{1,0:T(8,128)(2,1)S(1)}, u32[]{:S(2)}, u32[]{:S(2)}) collective-permute-start(bf16[64,1024]{1,0:T(8,128)(2,1)S(1)} %get-tuple-element.49), channel_id=1, source_target_pairs={{0,0},{1,1},{2,2},{3,3},{4,8},{5,9},{6,10},{7,11},{8,4},{9,5},{10,... | collective-permute-start | bytes 393224 | tf_op jit(solution)/shard_map/ppermute | solution.py:1002
  23.1 0.4 collective-permute-start.9
  23.5 0.0 collective-permute-done.4.refs_0_
  23.5 0.0 collective-permute-start.6
  23.5 0.0 collective-permute-done.5.refs_1_
  23.5 0.6 collective-permute-start.7
  24.1 2.1 %project.2 = (bf16[256,3072]{1,0:T(8,128)(2,1)S(1)}, bf16[256,128]{1,0:T(8,128)(2,1)S(1)}) custom-call(bf16[64,1152]{1,0:T(8,128)(2,1)S(1)} %collective-permute-done.refs_0_.own_0, bf16[64,1152]{1,0:T(8,128)(2,1)S(1)} %collective-permute-done.1.refs_1_.own_1, bf16[64,1152]{1,0:T(8,128)(2,1)S(1)} %collective-permute-done.2.refs_2_, ...), custom_call_target="tpu_custom_call" | custom-call | flops 1610612736 | bytes 6291456 | tf_op jit(solution)/shard_map/project/pallas_call | solution.py:356
  26.2 0.0 copy-start.2
  26.2 0.0 copy-start.3
  26.2 0.0 collective-permute-done.6.refs_2_
  26.2 2.1 %project.3 = (bf16[256,3072]{1,0:T(8,128)(2,1)S(1)}, bf16[256,128]{1,0:T(8,128)(2,1)S(1)}) custom-call(bf16[64,1152]{1,0:T(8,128)(2,1)S(1)} %collective-permute-done.4.refs_0_, bf16[64,1152]{1,0:T(8,128)(2,1)S(1)} %collective-permute-done.5.refs_1_, bf16[64,1152]{1,0:T(8,128)(2,1)S(1)} %collective-permute-done.6.refs_2_, ...), custom_call_target="tpu_custom_call" | custom-call | flops 1610612736 | bytes 6291456 | tf_op jit(solution)/shard_map/project/pallas_call | solution.py:356
  28.4 1.1 %collective-permute-done.9.cot_1 = bf16[64,1024]{1,0:T(8,128)(2,1)S(1)} collective-permute-done((bf16[64,1024]{1,0:T(8,128)(2,1)S(1)}, bf16[64,1024]{1,0:T(8,128)(2,1)S(1)}, u32[]{:S(2)}, u32[]{:S(2)}) %collective-permute-start.9) | collective-permute-done | bytes 131104 | tf_op jit(solution)/shard_map/ppermute | solution.py:1002
  29.5 14.0 %middle.1 = (bf16[64,1152]{1,0:T(8,128)(2,1)S(1)}, bf16[64,1152]{1,0:T(8,128)(2,1)S(1)}, bf16[128,1152]{1,0:T(8,128)(2,1)S(1)}, f32[128,1024]{1,0:T(8,128)S(1)}) custom-call(bf16[256,3072]{1,0:T(8,128)(2,1)S(1)} %get-tuple-element.44.qkv_a, bf16[256,3072]{1,0:T(8,128)(2,1)S(1)} %get-tuple-element.45.qkv_b, bf16[256,128]{1,0:T(8,128)(2,1)S(1)} %get-tuple-element.46.marks_a, ...), custom_call_target="tpu_custom_call" | custom-call | flops 4831838208 | bytes 18874368 | tf_op jit(solution)/shard_map/middle/pallas_call | solution.py:742
  43.5 0.1 collective-permute-start.12
  43.6 0.8 collective-permute-start.13
  44.4 1.4 %prefix.1 = (f32[10,1024]{1,0:T(8,128)S(1)}, f32[10,1024]{1,0:T(8,128)S(1)}) custom-call(bf16[256,3072]{1,0:T(8,128)(2,1)S(1)} %get-tuple-element.44.qkv_a, bf16[128,1152]{1,0:T(8,128)(2,1)S(1)} %get-tuple-element.53.grads.grads_0, bf16[16,2048]{1,0:T(8,128)(2,1)S(1)} %get-tuple-element.48.prefix_kv), custom_call_target="tpu_custom_call" | custom-call | flops 536870912 | bytes 1048576 | tf_op jit(solution)/shard_map/prefix/pallas_call | solution.py:819
  45.8 0.7 collective-permute-start.18
  46.5 1.1 %collective-permute-start.19 = (f32[10,1024]{1,0:T(8,128)S(1)}, f32[10,1024]{1,0:T(8,128)S(1)}, u32[]{:S(2)}, u32[]{:S(2)}) collective-permute-start(f32[10,1024]{1,0:T(8,128)S(1)} %get-tuple-element.60), channel_id=1, source_target_pairs={{0,24},{8,16},{16,8},{24,0},{1,25},{9,17},{17,9},{25,1},{2,26},{10... | collective-permute-start | bytes 122888 | tf_op jit(solution)/shard_map/ppermute | solution.py:1016
  47.6 0.3 collective-permute-start.17
  47.9 3.4 %query.1.grad_partial = f32[128,1024]{1,0:T(8,128)S(1)} custom-call(bf16[256,3072]{1,0:T(8,128)(2,1)S(1)} %get-tuple-element.44.qkv_a, bf16[256,3072]{1,0:T(8,128)(2,1)S(1)} %get-tuple-element.45.qkv_b, bf16[256,128]{1,0:T(8,128)(2,1)S(1)} %get-tuple-element.46.marks_a, bf16[256,128]{1,0:T(8,128)(2,1)S(1)} %get-tuple-element.47.marks_b, ...), custom_call_target="tpu_custom_call" | custom-call | flops 4294967296 | bytes 8388608 | tf_op jit(solution)/shard_map/query/pallas_call | solution.py:863
  51.3 0.0 collective-permute-done.17
  51.4 0.0 collective-permute-done.18
  51.4 0.4 collective-permute-done.13.grads_2
  51.8 1.3 %collective-permute-start.14 = (bf16[128,1152]{1,0:T(8,128)(2,1)S(1)}, bf16[128,1152]{1,0:T(8,128)(2,1)S(1)}, u32[]{:S(2)}, u32[]{:S(2)}) collective-permute-start(bf16[128,1152]{1,0:T(8,128)(2,1)S(1)} %collective-permute-done.13.grads_2), channel_id=1, source_target_pairs={{0,8},{8,0},{16,24},{24,16},{1,9},{9,1},{17,25},{25,17},{2,10},{10... | collective-permute-start | bytes 884744 | tf_op jit(solution)/shard_map/ppermute | solution.py:1012
  53.1 2.8 %collective-permute-start.21 = (f32[10,1024]{1,0:T(8,128)S(1)}, f32[10,1024]{1,0:T(8,128)S(1)}, u32[]{:S(2)}, u32[]{:S(2)}) collective-permute-start(f32[10,1024]{1,0:T(8,128)S(1)} %add_add_fusion.1), channel_id=1, source_target_pairs={{0,4},{1,5},{2,6},{3,7},{4,0},{5,1},{6,2},{7,3},{8,12},{9,13},{10,... | collective-permute-start | bytes 122888 | tf_op jit(solution)/shard_map/ppermute | solution.py:1016
  55.8 0.2 collective-permute-start.22
  56.0 0.2 collective-permute-start.20
  56.2 3.6 %collective-permute-done.21 = f32[10,1024]{1,0:T(8,128)S(1)} collective-permute-done((f32[10,1024]{1,0:T(8,128)S(1)}, f32[10,1024]{1,0:T(8,128)S(1)}, u32[]{:S(2)}, u32[]{:S(2)}) %collective-permute-start.21) | collective-permute-done | bytes 40992 | tf_op jit(solution)/shard_map/ppermute | solution.py:1016
  59.8 4.0 %collective-permute-start.10 = (bf16[64,1152]{1,0:T(8,128)(2,1)S(1)}, bf16[64,1152]{1,0:T(8,128)(2,1)S(1)}, u32[]{:S(2)}, u32[]{:S(2)}) collective-permute-start(bf16[64,1152]{1,0:T(8,128)(2,1)S(1)} %get-tuple-element.51), channel_id=1, source_target_pairs={{0,0},{1,1},{2,2},{3,3},{8,4},{9,5},{10,6},{11,7},{4,8},{5,9},{6,1... | collective-permute-start | bytes 442376 | tf_op jit(solution)/shard_map/ppermute | solution.py:1013
  63.7 0.0 collective-permute-done.22
  63.8 2.1 %collective-permute-start.11 = (bf16[64,1152]{1,0:T(8,128)(2,1)S(1)}, bf16[64,1152]{1,0:T(8,128)(2,1)S(1)}, u32[]{:S(2)}, u32[]{:S(2)}) collective-permute-start(bf16[64,1152]{1,0:T(8,128)(2,1)S(1)} %get-tuple-element.52), channel_id=1, source_target_pairs={{2,0},{3,1},{0,2},{1,3},{10,4},{11,5},{8,6},{9,7},{6,8},{7,9},{4,1... | collective-permute-start | bytes 442376 | tf_op jit(solution)/shard_map/ppermute | solution.py:1013
  65.9 0.0 collective-permute-done.20
  65.9 1.1 %collective-permute-start.23 = (f32[10,1024]{1,0:T(8,128)S(1)}, f32[10,1024]{1,0:T(8,128)S(1)}, u32[]{:S(2)}, u32[]{:S(2)}) collective-permute-start(f32[10,1024]{1,0:T(8,128)S(1)} %add_add_fusion.mine), channel_id=1, source_target_pairs={{0,1},{1,0},{2,3},{3,2},{4,5},{5,4},{6,7},{7,6},{8,9},{9,8},{10,11... | collective-permute-start | bytes 122888 | tf_op jit(solution)/shard_map/ppermute | solution.py:1040
  67.0 0.0 collective-permute-done.12.grads_1
  67.0 0.8 collective-permute-start.25
  67.8 4.8 %final.1 = (bf16[64,1024]{1,0:T(8,128)(2,1)S(1)}, bf16[64,1024]{1,0:T(8,128)(2,1)S(1)}) custom-call(bf16[256,3072]{1,0:T(8,128)(2,1)S(1)} %get-tuple-element.44.qkv_a, bf16[256,3072]{1,0:T(8,128)(2,1)S(1)} %get-tuple-element.45.qkv_b, bf16[256,128]{1,0:T(8,128)(2,1)S(1)} %get-tuple-element.46.marks_a, bf16[256,128]{1,0:T(8,128)(2,1)S(1)} %get-tuple-element.47.marks_b, ...), custom_call_target="tpu_custom_call" | custom-call | flops 4294967296 | bytes 8388608 | tf_op jit(solution)/shard_map/final/pallas_call | solution.py:932
  72.6 0.0 collective-permute-done.10
  72.6 3.9 %collective-permute-start.16 = (bf16[64,1024]{1,0:T(8,128)(2,1)S(1)}, bf16[64,1024]{1,0:T(8,128)(2,1)S(1)}, u32[]{:S(2)}, u32[]{:S(2)}) collective-permute-start(bf16[64,1024]{1,0:T(8,128)(2,1)S(1)} %get-tuple-element.56.order), channel_id=1, source_target_pairs={{0,0},{1,1},{2,2},{3,3},{8,4},{9,5},{10,6},{11,7},{4,8},{5,9},{6,1... | collective-permute-start | bytes 393224 | tf_op jit(solution)/shard_map/ppermute | solution.py:1036
  76.7 0.7 collective-permute-start.15
  77.3 0.0 collective-permute-done.25.other_y
  77.4 4.6 %adapter_back.1 = (f32[10,1024]{1,0:T(8,128)}, f32[1024,512]{1,0:T(8,128)}, f32[1,512]{1,0:T(1,128)}, f32[512,2048]{1,0:T(8,128)}, f32[1,2048]{1,0:T(1,128)}) custom-call(f32[10,1024]{1,0:T(8,128)S(1)} %add_add_fusion.mine, f32[10,1024]{1,0:T(8,128)S(1)} %collective-permute-done.23.mine_y, f32[10,1024]{1,0:T(8,128)S(1)} %collective-permute-done.24.other, ...), custom_call_target="tpu_custom_call" | custom-call | flops 4294967296 | bytes 6291456 | tf_op jit(solution)/shard_map/adapter_back/pallas_call | solution.py:526
  82.1 1.0 %copy.41 = bf16[64,2,1024]{2,1,0:T(2,128)(2,1)} copy(bf16[64,2,1024]{2,0,1:T(8,128)(2,1)S(1)} %pad_maximum_fusion) | data formatting | bytes 524288
  83.0 0.1 copy.40
  83.1 0.1 copy.39
  83.2 0.6 pad_maximum_fusion.2
  83.8 0.0 collective-permute-done.16
  83.9 1.2 %copy.42 = f32[64,2,1024]{2,1,0:T(2,128)} copy(f32[64,2,1024]{2,0,1:T(8,128)S(1)} %maximum_convert_fusion) | data formatting | bytes 1048576
  (30 shorter events, 0.3 us)
Async XLA Ops:
  2.5 12.0 %collective-permute-start = (bf16[64,1152]{1,0:T(8,128)(2,1)S(1)}, bf16[64,1152]{1,0:T(8,128)(2,1)S(1)}, u32[]{:S(2)}, u32[]{:S(2)}) collective-permute-start(bf16[64,1152]{1,0:T(8,128)(2,1)S(1)} %get-tuple-element.101), channel_id=1, source_target_pairs={{0,0},{1,1},{2,2},{3,3},{4,8},{5,9},{6,10},{7,11},{8,4},{9,5},{10,... | collective-permute-start | bytes 442376 | tf_op jit(solution)/shard_map/ppermute | solution.py:994
  8.1 6.5 %collective-permute-start.1 = (bf16[64,1152]{1,0:T(8,128)(2,1)S(1)}, bf16[64,1152]{1,0:T(8,128)(2,1)S(1)}, u32[]{:S(2)}, u32[]{:S(2)}) collective-permute-start(bf16[64,1152]{1,0:T(8,128)(2,1)S(1)} %get-tuple-element.100), channel_id=1, source_target_pairs={{0,2},{1,3},{2,0},{3,1},{4,10},{5,11},{6,8},{7,9},{8,6},{9,7},{10,... | collective-permute-start | bytes 442376 | tf_op jit(solution)/shard_map/ppermute | solution.py:994
  9.2 4.9 %copy-start.6 = (bf16[64,2,1024]{2,1,0:T(2,128)(2,1)S(1)}, bf16[64,2,1024]{2,1,0:T(2,128)(2,1)}, u32[]{:S(2)}) copy-start(bf16[64,2,1024]{2,1,0:T(2,128)(2,1)} %param.31) | copy-start | bytes 786436
  9.2 14.9 %copy-start = (f32[1024]{0:T(1024)S(1)}, f32[1024]{0:T(1024)}, u32[]{:S(2)}) copy-start(f32[1024]{0:T(1024)} %param.19) | copy-start | bytes 12292
  9.2 14.9 %copy-start.1 = (f32[1024]{0:T(1024)S(1)}, f32[1024]{0:T(1024)}, u32[]{:S(2)}) copy-start(f32[1024]{0:T(1024)} %param.18) | copy-start | bytes 12292
  14.1 12.1 %copy-start.4 = (f32[4,512,512]{2,1,0:T(8,128)}, f32[4,512,512]{2,1,0:T(8,128)S(1)}, u32[]{:S(2)}) copy-start(f32[4,512,512]{2,1,0:T(8,128)S(1)} %get-tuple-element.66.v_mlp2) | copy-start | bytes 12582916
  14.7 2.3 %collective-permute-start.2 = (bf16[64,1152]{1,0:T(8,128)(2,1)S(1)}, bf16[64,1152]{1,0:T(8,128)(2,1)S(1)}, u32[]{:S(2)}, u32[]{:S(2)}) collective-permute-start(bf16[64,1152]{1,0:T(8,128)(2,1)S(1)} %collective-permute-done.refs_0_.own_0), channel_id=1, source_target_pairs={{0,8},{8,0},{16,24},{24,16},{1,9},{9,1},{17,25},{25,17},{2,10},{10... | collective-permute-start | bytes 442376 | tf_op jit(solution)/shard_map/ppermute | solution.py:1001
  14.7 8.8 %collective-permute-start.4 = (bf16[64,1152]{1,0:T(8,128)(2,1)S(1)}, bf16[64,1152]{1,0:T(8,128)(2,1)S(1)}, u32[]{:S(2)}, u32[]{:S(2)}) collective-permute-start(bf16[64,1152]{1,0:T(8,128)(2,1)S(1)} %collective-permute-done.refs_0_.own_0), channel_id=1, source_target_pairs={{0,1},{1,0},{2,3},{3,2},{4,5},{5,4},{6,7},{7,6},{8,9},{9,8},{10,11... | collective-permute-start | bytes 442376 | tf_op jit(solution)/shard_map/ppermute | solution.py:1000
  15.9 1.8 %collective-permute-start.3 = (bf16[64,1152]{1,0:T(8,128)(2,1)S(1)}, bf16[64,1152]{1,0:T(8,128)(2,1)S(1)}, u32[]{:S(2)}, u32[]{:S(2)}) collective-permute-start(bf16[64,1152]{1,0:T(8,128)(2,1)S(1)} %collective-permute-done.1.refs_1_.own_1), channel_id=1, source_target_pairs={{0,8},{8,0},{16,24},{24,16},{1,9},{9,1},{17,25},{25,17},{2,10},{10... | collective-permute-start | bytes 442376 | tf_op jit(solution)/shard_map/ppermute | solution.py:1001
  16.7 6.8 %collective-permute-start.5 = (bf16[64,1152]{1,0:T(8,128)(2,1)S(1)}, bf16[64,1152]{1,0:T(8,128)(2,1)S(1)}, u32[]{:S(2)}, u32[]{:S(2)}) collective-permute-start(bf16[64,1152]{1,0:T(8,128)(2,1)S(1)} %collective-permute-done.1.refs_1_.own_1), channel_id=1, source_target_pairs={{0,1},{1,0},{2,3},{3,2},{4,5},{5,4},{6,7},{7,6},{8,9},{9,8},{10,11... | collective-permute-start | bytes 442376 | tf_op jit(solution)/shard_map/ppermute | solution.py:1000
  17.7 10.7 %collective-permute-start.8 = (bf16[64,1024]{1,0:T(8,128)(2,1)S(1)}, bf16[64,1024]{1,0:T(8,128)(2,1)S(1)}, u32[]{:S(2)}, u32[]{:S(2)}) collective-permute-start(bf16[64,1024]{1,0:T(8,128)(2,1)S(1)} %get-tuple-element.49), channel_id=1, source_target_pairs={{0,0},{1,1},{2,2},{3,3},{4,8},{5,9},{6,10},{7,11},{8,4},{9,5},{10,... | collective-permute-start | bytes 393224 | tf_op jit(solution)/shard_map/ppermute | solution.py:1002
  23.1 6.4 %collective-permute-start.9 = (bf16[64,1024]{1,0:T(8,128)(2,1)S(1)}, bf16[64,1024]{1,0:T(8,128)(2,1)S(1)}, u32[]{:S(2)}, u32[]{:S(2)}) collective-permute-start(bf16[64,1024]{1,0:T(8,128)(2,1)S(1)} %get-tuple-element.50), channel_id=1, source_target_pairs={{0,2},{1,3},{2,0},{3,1},{4,10},{5,11},{6,8},{7,9},{8,6},{9,7},{10,... | collective-permute-start | bytes 393224 | tf_op jit(solution)/shard_map/ppermute | solution.py:1002
  23.5 2.8 %collective-permute-start.6 = (bf16[64,1152]{1,0:T(8,128)(2,1)S(1)}, bf16[64,1152]{1,0:T(8,128)(2,1)S(1)}, u32[]{:S(2)}, u32[]{:S(2)}) collective-permute-start(bf16[64,1152]{1,0:T(8,128)(2,1)S(1)} %collective-permute-done.4.refs_0_), channel_id=1, source_target_pairs={{0,8},{8,0},{16,24},{24,16},{1,9},{9,1},{17,25},{25,17},{2,10},{10... | collective-permute-start | bytes 442376 | tf_op jit(solution)/shard_map/ppermute | solution.py:1003
  23.5 2.8 %collective-permute-start.7 = (bf16[64,1152]{1,0:T(8,128)(2,1)S(1)}, bf16[64,1152]{1,0:T(8,128)(2,1)S(1)}, u32[]{:S(2)}, u32[]{:S(2)}) collective-permute-start(bf16[64,1152]{1,0:T(8,128)(2,1)S(1)} %collective-permute-done.5.refs_1_), channel_id=1, source_target_pairs={{0,8},{8,0},{16,24},{24,16},{1,9},{9,1},{17,25},{25,17},{2,10},{10... | collective-permute-start | bytes 442376 | tf_op jit(solution)/shard_map/ppermute | solution.py:1003
  26.2 3.3 %copy-start.2 = (f32[1024]{0:T(1024)S(1)}, f32[1024]{0:T(1024)}, u32[]{:S(2)}) copy-start(f32[1024]{0:T(1024)} %param.22) | copy-start | bytes 12292
  26.2 3.3 %copy-start.3 = (f32[1024]{0:T(1024)S(1)}, f32[1024]{0:T(1024)}, u32[]{:S(2)}) copy-start(f32[1024]{0:T(1024)} %param.23) | copy-start | bytes 12292
  43.5 23.5 %collective-permute-start.12 = (bf16[128,1152]{1,0:T(8,128)(2,1)S(1)}, bf16[128,1152]{1,0:T(8,128)(2,1)S(1)}, u32[]{:S(2)}, u32[]{:S(2)}) collective-permute-start(bf16[128,1152]{1,0:T(8,128)(2,1)S(1)} %get-tuple-element.53.grads.grads_0), channel_id=1, source_target_pairs={{0,8},{8,0},{16,24},{24,16},{1,9},{9,1},{17,25},{25,17},{2,10},{10... | collective-permute-start | bytes 884744 | tf_op jit(solution)/shard_map/ppermute | solution.py:1011
  43.6 8.2 %collective-permute-start.13 = (bf16[128,1152]{1,0:T(8,128)(2,1)S(1)}, bf16[128,1152]{1,0:T(8,128)(2,1)S(1)}, u32[]{:S(2)}, u32[]{:S(2)}) collective-permute-start(bf16[128,1152]{1,0:T(8,128)(2,1)S(1)} %get-tuple-element.53.grads.grads_0), channel_id=1, source_target_pairs={{0,1},{1,0},{2,3},{3,2},{4,5},{5,4},{6,7},{7,6},{8,9},{9,8},{10,11... | collective-permute-start | bytes 884744 | tf_op jit(solution)/shard_map/ppermute | solution.py:1010
  45.8 5.6 %collective-permute-start.18 = (f32[10,1024]{1,0:T(8,128)S(1)}, f32[10,1024]{1,0:T(8,128)S(1)}, u32[]{:S(2)}, u32[]{:S(2)}) collective-permute-start(f32[10,1024]{1,0:T(8,128)S(1)} %get-tuple-element.60), channel_id=1, source_target_pairs={{0,8},{8,0},{16,24},{24,16},{1,9},{9,1},{17,25},{25,17},{2,10},{10... | collective-permute-start | bytes 122888 | tf_op jit(solution)/shard_map/ppermute | solution.py:1016
  46.5 4.9 %collective-permute-start.19 = (f32[10,1024]{1,0:T(8,128)S(1)}, f32[10,1024]{1,0:T(8,128)S(1)}, u32[]{:S(2)}, u32[]{:S(2)}) collective-permute-start(f32[10,1024]{1,0:T(8,128)S(1)} %get-tuple-element.60), channel_id=1, source_target_pairs={{0,24},{8,16},{16,8},{24,0},{1,25},{9,17},{17,9},{25,1},{2,26},{10... | collective-permute-start | bytes 122888 | tf_op jit(solution)/shard_map/ppermute | solution.py:1016
  47.6 3.7 %collective-permute-start.17 = (f32[10,1024]{1,0:T(8,128)S(1)}, f32[10,1024]{1,0:T(8,128)S(1)}, u32[]{:S(2)}, u32[]{:S(2)}) collective-permute-start(f32[10,1024]{1,0:T(8,128)S(1)} %get-tuple-element.55.order), channel_id=1, source_target_pairs={{0,16},{8,24},{16,0},{24,8},{1,17},{9,25},{17,1},{25,9},{2,18},{10... | collective-permute-start | bytes 122888 | tf_op jit(solution)/shard_map/ppermute | solution.py:1016
  51.8 15.2 %collective-permute-start.14 = (bf16[128,1152]{1,0:T(8,128)(2,1)S(1)}, bf16[128,1152]{1,0:T(8,128)(2,1)S(1)}, u32[]{:S(2)}, u32[]{:S(2)}) collective-permute-start(bf16[128,1152]{1,0:T(8,128)(2,1)S(1)} %collective-permute-done.13.grads_2), channel_id=1, source_target_pairs={{0,8},{8,0},{16,24},{24,16},{1,9},{9,1},{17,25},{25,17},{2,10},{10... | collective-permute-start | bytes 884744 | tf_op jit(solution)/shard_map/ppermute | solution.py:1012
  53.1 6.7 %collective-permute-start.21 = (f32[10,1024]{1,0:T(8,128)S(1)}, f32[10,1024]{1,0:T(8,128)S(1)}, u32[]{:S(2)}, u32[]{:S(2)}) collective-permute-start(f32[10,1024]{1,0:T(8,128)S(1)} %add_add_fusion.1), channel_id=1, source_target_pairs={{0,4},{1,5},{2,6},{3,7},{4,0},{5,1},{6,2},{7,3},{8,12},{9,13},{10,... | collective-permute-start | bytes 122888 | tf_op jit(solution)/shard_map/ppermute | solution.py:1016
  55.8 7.9 %collective-permute-start.22 = (f32[10,1024]{1,0:T(8,128)S(1)}, f32[10,1024]{1,0:T(8,128)S(1)}, u32[]{:S(2)}, u32[]{:S(2)}) collective-permute-start(f32[10,1024]{1,0:T(8,128)S(1)} %add_add_fusion.1), channel_id=1, source_target_pairs={{0,6},{1,7},{2,4},{3,5},{4,2},{5,3},{6,0},{7,1},{8,14},{9,15},{10,... | collective-permute-start | bytes 122888 | tf_op jit(solution)/shard_map/ppermute | solution.py:1016
  56.0 9.9 %collective-permute-start.20 = (f32[10,1024]{1,0:T(8,128)S(1)}, f32[10,1024]{1,0:T(8,128)S(1)}, u32[]{:S(2)}, u32[]{:S(2)}) collective-permute-start(f32[10,1024]{1,0:T(8,128)S(1)} %add_add_fusion.1), channel_id=1, source_target_pairs={{0,2},{1,3},{2,0},{3,1},{4,6},{5,7},{6,4},{7,5},{8,10},{9,11},{10,... | collective-permute-start | bytes 122888 | tf_op jit(solution)/shard_map/ppermute | solution.py:1016
  59.8 12.9 %collective-permute-start.10 = (bf16[64,1152]{1,0:T(8,128)(2,1)S(1)}, bf16[64,1152]{1,0:T(8,128)(2,1)S(1)}, u32[]{:S(2)}, u32[]{:S(2)}) collective-permute-start(bf16[64,1152]{1,0:T(8,128)(2,1)S(1)} %get-tuple-element.51), channel_id=1, source_target_pairs={{0,0},{1,1},{2,2},{3,3},{8,4},{9,5},{10,6},{11,7},{4,8},{5,9},{6,1... | collective-permute-start | bytes 442376 | tf_op jit(solution)/shard_map/ppermute | solution.py:1013
  63.8 12.8 %collective-permute-start.11 = (bf16[64,1152]{1,0:T(8,128)(2,1)S(1)}, bf16[64,1152]{1,0:T(8,128)(2,1)S(1)}, u32[]{:S(2)}, u32[]{:S(2)}) collective-permute-start(bf16[64,1152]{1,0:T(8,128)(2,1)S(1)} %get-tuple-element.52), channel_id=1, source_target_pairs={{2,0},{3,1},{0,2},{1,3},{10,4},{11,5},{8,6},{9,7},{6,8},{7,9},{4,1... | collective-permute-start | bytes 442376 | tf_op jit(solution)/shard_map/ppermute | solution.py:1013
  65.9 11.5 %collective-permute-start.23 = (f32[10,1024]{1,0:T(8,128)S(1)}, f32[10,1024]{1,0:T(8,128)S(1)}, u32[]{:S(2)}, u32[]{:S(2)}) collective-permute-start(f32[10,1024]{1,0:T(8,128)S(1)} %add_add_fusion.mine), channel_id=1, source_target_pairs={{0,1},{1,0},{2,3},{3,2},{4,5},{5,4},{6,7},{7,6},{8,9},{9,8},{10,11... | collective-permute-start | bytes 122888 | tf_op jit(solution)/shard_map/ppermute | solution.py:1040
  67.0 10.3 %collective-permute-start.24 = (f32[10,1024]{1,0:T(8,128)S(1)}, f32[10,1024]{1,0:T(8,128)S(1)}, u32[]{:S(2)}, u32[]{:S(2)}) collective-permute-start(f32[10,1024]{1,0:T(8,128)S(1)} %add_add_fusion.mine), channel_id=1, source_target_pairs={{0,8},{8,0},{16,24},{24,16},{1,9},{9,1},{17,25},{25,17},{2,10},{10... | collective-permute-start | bytes 122888 | tf_op jit(solution)/shard_map/ppermute | solution.py:1040
  67.0 10.3 %collective-permute-start.25 = (f32[10,1024]{1,0:T(8,128)S(1)}, f32[10,1024]{1,0:T(8,128)S(1)}, u32[]{:S(2)}, u32[]{:S(2)}) collective-permute-start(f32[10,1024]{1,0:T(8,128)S(1)} %add_add_fusion.mine), channel_id=1, source_target_pairs={{0,9},{1,8},{2,11},{3,10},{4,13},{5,12},{6,15},{7,14},{8,1},{9,0},... | collective-permute-start | bytes 122888 | tf_op jit(solution)/shard_map/ppermute | solution.py:1041
  67.8 9.5 %copy-start.5 = (f32[4,512,512]{2,1,0:T(8,128)S(1)}, f32[4,512,512]{2,1,0:T(8,128)}, u32[]{:S(2)}) copy-start(f32[4,512,512]{2,1,0:T(8,128)} %copy-done.4) | copy-start | bytes 12582916
  72.6 11.2 %collective-permute-start.16 = (bf16[64,1024]{1,0:T(8,128)(2,1)S(1)}, bf16[64,1024]{1,0:T(8,128)(2,1)S(1)}, u32[]{:S(2)}, u32[]{:S(2)}) collective-permute-start(bf16[64,1024]{1,0:T(8,128)(2,1)S(1)} %get-tuple-element.56.order), channel_id=1, source_target_pairs={{0,0},{1,1},{2,2},{3,3},{8,4},{9,5},{10,6},{11,7},{4,8},{5,9},{6,1... | collective-permute-start | bytes 393224 | tf_op jit(solution)/shard_map/ppermute | solution.py:1036
  76.7 7.2 %collective-permute-start.15 = (bf16[64,1024]{1,0:T(8,128)(2,1)S(1)}, bf16[64,1024]{1,0:T(8,128)(2,1)S(1)}, u32[]{:S(2)}, u32[]{:S(2)}) collective-permute-start(bf16[64,1024]{1,0:T(8,128)(2,1)S(1)} %get-tuple-element.59), channel_id=1, source_target_pairs={{2,0},{3,1},{0,2},{1,3},{10,4},{11,5},{8,6},{9,7},{6,8},{7,9},{4,1... | collective-permute-start | bytes 393224 | tf_op jit(solution)/shard_map/ppermute | solution.py:1036

commit v4 on v3

--- a/solution.py
+++ b/solution.py
@@ -336,6 +336,95 @@
     return [pltpu.with_memory_space_constraint(a, pltpu.HBM) for a in arrays]
 
 
+def by_tiles(block):
+    half, pair, width = block.shape
+    tiles = jnp.transpose(block.reshape(half, pair, width // LANES, LANES), (0, 2, 1, 3))
+    return tiles.reshape(half, pair * width // LANES, LANES)
+
+
+def from_tiles(tiles, width):
+    half, count, _ = tiles.shape
+    pair = count * LANES // width
+    block = jnp.transpose(tiles.reshape(half, width // LANES, pair, LANES), (0, 2, 1, 3))
+    return block.reshape(half, pair, width)
+
+
+def odd_place():
+    return (lax.axis_index("blk") // 2) % 2 == 1
+
+
+def split_kernel(marked, *refs):
+    tokens, ids, (out_0, out_1, work) = refs[0], refs[1], refs[-3:]
+    half, count, _ = tokens.shape
+    odd = odd_place()
+    work[...] = tokens[...].astype(F32).reshape(half * count, LANES)
+    for i in range(count // 2):
+        at = pl.ds(i * LANES, LANES)
+        first, second = (work[pl.ds(2 * i + r, half, stride=count)] for r in range(2))
+        out_0[:, at] = jnp.where(odd, second, first).astype(BF16)
+        out_1[:, at] = jnp.where(odd, first, second).astype(BF16)
+    if marked:
+        width = count // 2 * LANES
+        first, second = (
+            jnp.where(iota((LANES, half), 0) == ids[r : r + 1], 1.0, 0.0).T for r in range(2)
+        )
+        out_0[:, width:] = jnp.where(odd, second, first).astype(BF16)
+        out_1[:, width:] = jnp.where(odd, first, second).astype(BF16)
+
+
+def split_rows(block, segment_ids=None):
+    tiles = by_tiles(block)
+    half, count, _ = tiles.shape
+    extra = () if segment_ids is None else kept_in_hbm(segment_ids.T)
+    width = count // 2 * LANES + LANES * len(extra)
+    return pl.pallas_call(
+        partial(split_kernel, bool(extra)),
+        in_specs=[vmem()] * (1 + len(extra)),
+        out_specs=[vmem()] * 2,
+        out_shape=[jax.ShapeDtypeStruct((half, width), BF16)] * 2,
+        scratch_shapes=[pltpu.VMEM((half * count, LANES), F32)],
+        compiler_params=pltpu.CompilerParams(vmem_limit_bytes=4 * MIB),
+        cost_estimate=pl.CostEstimate(flops=1 << 20, bytes_accessed=1 << 19, transcendentals=0),
+        name="split",
+    )(*kept_in_hbm(tiles), *extra)
+
+
+def land_kernel(logs, *refs):
+    msg_0, msg_1, out = refs[0], refs[1], refs[2]
+    work = refs[-1]
+    half, count, _ = out.shape
+    width = count // 2 * LANES
+    odd = odd_place()
+    for i in range(count // 2):
+        at = pl.ds(i * LANES, LANES)
+        one, two = msg_0[:half, at].astype(F32), msg_1[:half, at].astype(F32)
+        work[pl.ds(2 * i, half, stride=count)] = jnp.where(odd, two, one)
+        work[pl.ds(2 * i + 1, half, stride=count)] = jnp.where(odd, one, two)
+    out[...] = work[...].reshape(out.shape).astype(out.dtype)
+    if logs:
+        heads = refs[3].shape[1]
+        one, two = (m[:half, width:].astype(F32) for m in (msg_0, msg_1))
+        for r, chosen in enumerate((jnp.where(odd, two, one), jnp.where(odd, one, two))):
+            summed = chosen + jnp.roll(chosen, -heads, 1) + jnp.roll(chosen, -2 * heads, 1)
+            refs[3][r] = summed.T[:heads]
+
+
+def land(messages, half, width, dtype, logs):
+    count = 2 * width // LANES
+    out = pl.pallas_call(
+        partial(land_kernel, logs),
+        in_specs=[vmem()] * 2,
+        out_specs=[vmem()] * (1 + logs),
+        out_shape=[jax.ShapeDtypeStruct((half, count, LANES), dtype)]
+        + [jax.ShapeDtypeStruct((2, HEADS, half), F32)] * logs,
+        scratch_shapes=[pltpu.VMEM((half * count, LANES), F32)],
+        compiler_params=pltpu.CompilerParams(vmem_limit_bytes=4 * MIB),
+        cost_estimate=pl.CostEstimate(flops=1000, bytes_accessed=1000, transcendentals=0),
+        name="land",
+    )(*messages)
+    return (from_tiles(out[0], width), *out[1:])
+
+
 def project_kernel(count, *refs):
     messages, (gain, bias, weight, out, marks, normed) = refs[:count], refs[count:]
     half, width = messages[0].shape[0], normed.shape[1]
@@ -400,6 +489,7 @@
     inner,
     v_qkv,
     embed,
+    turned,
     v_mlp1,
     v_mlp2,
     b_mlp1,
@@ -425,8 +515,13 @@
     source = pad_rows(embed[...], PRE_ROWS)
     act = jnp.tanh(three_products(nn, source, v_mlp1[...]) + b_mlp1[...])
     inner[...] = act
+    columns, hidden = steps * step, v_mlp1.shape[1]
+    for i in range(v_mlp1.shape[0] // hidden):
+        part = v_mlp1[pl.ds(i * hidden, hidden)].astype(BF16)
+        turned[pl.ds(columns + i * hidden, hidden)] = part.T
     for i, copy in enumerate(rest):
         copy.wait()
+        turned[pl.ds(i * step, step)] = v_mlp2[i].astype(BF16).T
         span = pl.ds(i * step, step)
         part = three_products(nn, act, v_mlp2[i]) + b_mlp2[:, span]
         out[:, span] = jnp.where(iota(part.shape, 0) < embed.shape[0], part, 0.0).astype(BF16)
@@ -440,16 +535,17 @@
     return pl.pallas_call(
         adapter_kernel,
         in_specs=[hbm()] * 6,
-        out_specs=[vmem()] * 6,
+        out_specs=[vmem()] * 5,
         out_shape=[
             jax.ShapeDtypeStruct((PRE_ROWS, columns), BF16),
             jax.ShapeDtypeStruct((PRE_ROWS, hidden), F32),
             pltpu.VMEM(w_qkv.shape, w_qkv.dtype),
             pltpu.VMEM(embed.shape, F32),
+            pltpu.VMEM((columns + width, hidden), BF16),
+        ],
+        scratch_shapes=[
             pltpu.VMEM((width, hidden), F32),
             pltpu.VMEM((steps, hidden, columns // steps), F32),
-        ],
-        scratch_shapes=[
             pltpu.VMEM((1, hidden), F32),
             pltpu.VMEM((1, columns), F32),
             pltpu.SemaphoreType.DMA((5 + steps,)),
@@ -471,15 +567,20 @@
     )
 
 
+def two_products(left, weight):
+    high, low = halves(left)
+    both = nn(jnp.concatenate([high, low], 0), weight)
+    return both[: left.shape[0]] + both[left.shape[0] :]
+
+
 def adapter_back_kernel(
-    mine,
-    mine_y,
-    other,
-    other_y,
+    part_0,
+    part_1,
+    part_2,
+    part_3,
     embed,
     inner,
-    v_mlp1,
-    v_mlp2,
+    turned,
     order,
     grad_prefix,
     grad_mlp1,
@@ -491,41 +592,38 @@
     sems,
 ):
     del order
-    steps, step = v_mlp2.shape[0], v_mlp2.shape[2]
-    first = lax.axis_index("seq") % 2 == 0
-    own, beside = mine[...] + mine_y[...], other[...] + other_y[...]
-    grads = jnp.concatenate([jnp.where(first, own, beside), jnp.where(first, beside, own)], 1)
-    grads = pad_rows(grads, PRE_ROWS)
+    steps, step = o_mlp2.shape[0], o_mlp2.shape[2]
+    first, second, third, fourth = (p[...].astype(F32) for p in (part_0, part_1, part_2, part_3))
+    grads = (first + second) + (third + fourth)
     act = inner[...]
     stores = []
-    back = jnp.zeros(act.shape, F32)
     grad_bias2[...] = jnp.sum(grads, 0, keepdims=True)
     for i in range(steps):
-        part = grads[:, i * step : (i + 1) * step]
-        o_mlp2[i] = outer(act, part)
+        o_mlp2[i] = outer(act, grads[:, i * step : (i + 1) * step])
         stores.append(
             pltpu.make_async_copy(o_mlp2.at[i], grad_mlp2.at[:, pl.ds(i * step, step)], sems.at[i])
         )
         stores[-1].start()
-    for i in range(steps):
-        back = back + three_products(nt, grads[:, i * step : (i + 1) * step], v_mlp2[i])
-    back = back * (1.0 - act * act)
+    columns, (width, hidden) = steps * step, o_mlp1.shape
+    back = two_products(grads, turned[:columns]) * (1.0 - act * act)
     grad_bias1[...] = jnp.sum(back, 0, keepdims=True)
     o_mlp1[...] = outer(pad_rows(embed[...], PRE_ROWS), back)
     stores.append(pltpu.make_async_copy(o_mlp1, grad_mlp1, sems.at[steps]))
     stores[-1].start()
-    grad_prefix[...] = three_products(nt, back, v_mlp1[...])[: embed.shape[0]]
+    for i in range(width // hidden):
+        part = two_products(back, turned[pl.ds(columns + i * hidden, hidden)])
+        grad_prefix[:, pl.ds(i * hidden, hidden)] = part[: embed.shape[0]]
     for copy in stores:
         copy.wait()
 
 
-def adapter_backward(parts, embed, inner, v_mlp1, v_mlp2, order):
-    width, hidden = v_mlp1.shape
-    steps, _, step = v_mlp2.shape
-    columns = steps * step
+def adapter_backward(parts, embed, inner, turned, order):
+    hidden, width = turned.shape[1], embed.shape[1]
+    columns = turned.shape[0] - width
+    steps = 4
     out = pl.pallas_call(
         adapter_back_kernel,
-        in_specs=[vmem()] * 8 + [pl.BlockSpec(memory_space=pl.ANY)],
+        in_specs=[vmem()] * 7 + [pl.BlockSpec(memory_space=pl.ANY)],
         out_specs=[vmem(), hbm(), vmem(), hbm(), vmem()],
         out_shape=[
             jax.ShapeDtypeStruct(embed.shape, F32),
@@ -536,13 +634,13 @@
         ],
         scratch_shapes=[
             pltpu.VMEM((width, hidden), F32),
-            pltpu.VMEM((steps, hidden, step), F32),
+            pltpu.VMEM((steps, hidden, columns // steps), F32),
             pltpu.SemaphoreType.DMA((steps + 1,)),
         ],
-        compiler_params=pltpu.CompilerParams(vmem_limit_bytes=28 * MIB),
-        cost_estimate=pl.CostEstimate(flops=1 << 32, bytes_accessed=6 * MIB, transcendentals=0),
+        compiler_params=pltpu.CompilerParams(vmem_limit_bytes=16 * MIB),
+        cost_estimate=pl.CostEstimate(flops=1000, bytes_accessed=1000, transcendentals=0),
         name="adapter_back",
-    )(*parts, embed, inner, v_mlp1, v_mlp2, order)
+    )(*parts, embed, inner, turned, order)
     return out[0], out[1], out[2][0], out[3], out[4][0]
 
 
@@ -618,6 +716,7 @@
     back_1,
     grad_out_heads,
     grad_middle,
+    grad_prefix_kv,
     v_out,
     v_fc,
     v_proj,
@@ -702,8 +801,8 @@
     lax.fori_loop(0, steps, feed, 0, unroll=True)
 
     out = total[...].astype(BF16)
-    back_0[:, :width] = out[:half]
-    back_1[:, :width] = out[half:]
+    back_0[:half, :width] = out[:half]
+    back_1[:half, :width] = out[half:]
     unit, inverse = norm_parts(middle[...])
     grads = cot[...].astype(F32) + norm_back(unit, inverse, gain[...], grad_norm[...])
     grad_middle[...] = grads
@@ -728,8 +827,11 @@
     marks = three_parts(stats[...], 0) + three_parts(bases, 3 * HEADS)
     marks = marks.astype(BF16)
     grad_out_heads[:, width:] = marks
-    back_0[:, width:] = marks[:half]
-    back_1[:, width:] = marks[half:]
+    back_0[:half, width:] = marks[:half]
+    back_1[:half, width:] = marks[half:]
+    back_0[half:] = jnp.zeros_like(back_0[half:])
+    back_1[half:] = jnp.zeros_like(back_1[half:])
+    prefix_grads(qkv_a, grad_out_heads, marks, prefix_kv, count, grad_prefix_kv)
 
 
 def middle_part(count, qkv_a, qkv_b, marks_a, marks_b, prefix_kv, own, cots, gain, bias, w_out, w_fc, w_proj):
@@ -742,12 +844,13 @@
     return pl.pallas_call(
         partial(middle_kernel, count),
         in_specs=[vmem()] * 11 + [hbm()] * 3,
-        out_specs=[vmem()] * 4,
+        out_specs=[vmem()] * 5,
         out_shape=[
-            jax.ShapeDtypeStruct((half, wide), BF16),
-            jax.ShapeDtypeStruct((half, wide), BF16),
+            jax.ShapeDtypeStruct((half + tail_rows(count), wide), BF16),
+            jax.ShapeDtypeStruct((half + tail_rows(count), wide), BF16),
             jax.ShapeDtypeStruct((rows, wide), BF16),
             jax.ShapeDtypeStruct((rows, width), F32),
+            jax.ShapeDtypeStruct(prefix_kv.shape, BF16),
         ],
         scratch_shapes=[
             pltpu.VMEM((width, width), BF16),
@@ -763,12 +866,8 @@
             pltpu.VMEM((rows, width), F32),
             pltpu.VMEM((rows, width), BF16),
         ],
-        compiler_params=pltpu.CompilerParams(vmem_limit_bytes=48 * MIB),
-        cost_estimate=pl.CostEstimate(
-            flops=2 * rows * width * (4 * hidden + 2 * width),
-            bytes_accessed=2 * width * (2 * hidden + width),
-            transcendentals=rows * hidden,
-        ),
+        compiler_params=pltpu.CompilerParams(vmem_limit_bytes=36 * MIB),
+        cost_estimate=pl.CostEstimate(flops=1 << 31, bytes_accessed=1000, transcendentals=0),
         name="middle",
     )(
         qkv_a, qkv_b, marks_a, marks_b, prefix_kv, *own, *cots, gain[None], bias[None], *kept_in_hbm(w_out, w_fc, w_proj)
@@ -792,42 +891,88 @@
     return join_heads(key_grad, low) * HEAD**-0.5, join_heads(value_grad, low)
 
 
-def prefix_kernel(qkv_a, grads, prefix_kv, mine, theirs):
-    used = mine.shape[0]
-    first = lax.axis_index("seq") % 2 == 0
-    rows, width = grads.shape[0], grads.shape[1] - LANES
-    count = prefix_kv.shape[0]
+def tail_rows(count):
+    return -(-2 * count // PRE_ROWS) * PRE_ROWS
+
+
+def prefix_grads(queries, grads, marks, prefix_kv, used, out):
+    count, rows, width = prefix_kv.shape[0], grads.shape[0], grads.shape[1] - LANES
     low = head_mask(count)
     mask = jnp.where(iota((count, rows), 0) < used, 0.0, NEG)
-    marks = grads[:, width:]
 
     def step(pair, carry):
         at = pl.ds(pl.multiple_of(pair * LANES, LANES), LANES)
         at_v = pl.ds(pl.multiple_of(width + pair * LANES, LANES), LANES)
         key_grad, value_grad = key_grads(
-            prefix_kv[:, at], prefix_kv[:, at_v], qkv_a[:rows, at], grads[:, at], marks, pair, low, mask
+            prefix_kv[:, at], prefix_kv[:, at_v], queries[:rows, at], grads[:, at], marks, pair, low, mask
         )
-        mine[:, at] = jnp.where(first, key_grad, value_grad)[:used]
-        theirs[:, at] = jnp.where(first, value_grad, key_grad)[:used]
+        out[:, at] = key_grad.astype(BF16)
+        out[:, at_v] = value_grad.astype(BF16)
         return carry
 
     lax.fori_loop(0, HEADS // 2, step, 0, unroll=True)
 
 
-def prefix_part(count, qkv_a, grads, prefix_kv):
-    half = prefix_kv.shape[1] // 2
+def pack_kernel(count, own, part_0, part_1, part_2, _0, _1, back_0, back_1):
+    total = own[...].astype(F32) + part_0[...].astype(F32)
+    total = total + (part_1[...].astype(F32) + part_2[...].astype(F32))
+    width = total.shape[1] // 2
+    rows = tail_rows(count)
+    tail = pad_rows(jnp.concatenate([total[:count, :width], total[:count, width:]], 0), rows).astype(BF16)
+    at = pl.ds(back_0.shape[0] - rows, rows)
+    back_0[at, :width] = tail
+    back_1[at, :width] = tail
+
+
+def pack(count, terms, back_0, back_1):
     return pl.pallas_call(
-        prefix_kernel,
-        in_specs=[vmem()] * 3,
+        partial(pack_kernel, count),
+        in_specs=[vmem()] * 6,
         out_specs=[vmem()] * 2,
-        out_shape=[jax.ShapeDtypeStruct((count, half), F32)] * 2,
-        compiler_params=pltpu.CompilerParams(vmem_limit_bytes=16 * MIB),
-        cost_estimate=pl.CostEstimate(flops=1 << 29, bytes_accessed=1 << 20, transcendentals=1 << 16),
-        name="prefix",
-    )(qkv_a, grads, prefix_kv)
-
-
-def query_kernel(count, qkv_a, qkv_b, marks_a, marks_b, prefix_kv, grads, weight, order, out, scores_bias, grad_query):
+        out_shape=[jax.ShapeDtypeStruct(back_0.shape, BF16)] * 2,
+        input_output_aliases={4: 0, 5: 1},
+        compiler_params=pltpu.CompilerParams(vmem_limit_bytes=4 * MIB),
+        cost_estimate=pl.CostEstimate(flops=1 << 20, bytes_accessed=1 << 19, transcendentals=0),
+        name="pack",
+    )(*terms, back_0, back_1)
+
+
+def unpack_kernel(count, home_0, home_1, out):
+    width = out.shape[1] // 2
+    rows = tail_rows(count)
+    at = pl.ds(home_0.shape[0] - rows, rows)
+    first, second = home_0[at, :width].astype(F32), home_1[at, :width].astype(F32)
+    total = first + second
+    out[:, :width] = pad_rows(total[:count], PRE_ROWS).astype(BF16)
+    out[:, width:] = pad_rows(total[count : 2 * count], PRE_ROWS).astype(BF16)
+
+
+def unpack(count, width, home_0, home_1):
+    return pl.pallas_call(
+        partial(unpack_kernel, count),
+        in_specs=[vmem()] * 2,
+        out_specs=vmem(),
+        out_shape=jax.ShapeDtypeStruct((PRE_ROWS, 2 * width), BF16),
+        compiler_params=pltpu.CompilerParams(vmem_limit_bytes=4 * MIB),
+        cost_estimate=pl.CostEstimate(flops=1000, bytes_accessed=1000, transcendentals=0),
+        name="unpack",
+    )(home_0, home_1)
+
+
+def query_kernel(
+    count,
+    qkv_a,
+    qkv_b,
+    marks_a,
+    marks_b,
+    prefix_kv,
+    grads,
+    weight,
+    order,
+    out,
+    scores_bias,
+    grad_query,
+):
     del order
     rows, width = grad_query.shape
     scores_bias[...] = key_bias(marks_a[:rows], marks_a[...], marks_b[...], rows // 2, count)
@@ -866,8 +1011,8 @@
         out_specs=vmem(),
         out_shape=jax.ShapeDtypeStruct((rows, width), F32),
         scratch_shapes=[pltpu.VMEM((rows, 4 * rows + LANES), F32), pltpu.VMEM((rows, width), BF16)],
-        compiler_params=pltpu.CompilerParams(vmem_limit_bytes=30 * MIB),
-        cost_estimate=pl.CostEstimate(flops=1 << 32, bytes_accessed=1 << 23, transcendentals=1 << 20),
+        compiler_params=pltpu.CompilerParams(vmem_limit_bytes=16 * MIB),
+        cost_estimate=pl.CostEstimate(flops=1000, bytes_accessed=1000, transcendentals=0),
         name="query",
     )(qkv_a, qkv_b, marks_a, marks_b, prefix_kv, grads, weight, order)
 
@@ -939,7 +1084,7 @@
             pltpu.VMEM((rows, 2 * width), BF16),
         ],
         compiler_params=pltpu.CompilerParams(vmem_limit_bytes=30 * MIB),
-        cost_estimate=pl.CostEstimate(flops=1 << 32, bytes_accessed=1 << 23, transcendentals=1 << 20),
+        cost_estimate=pl.CostEstimate(flops=1000, bytes_accessed=1000, transcendentals=0),
         name="final",
     )(qkv_a, qkv_b, marks_a, marks_b, *grads, *own, gain[None], grad_middle, grad_partial, weight)
 
@@ -979,20 +1124,13 @@
     swap_core = [(i, i ^ 1) for i in range(4)]
     swap_y = [(i, i ^ 1) for i in range(8)]
     swap_both = [(i, i ^ 9) for i in range(32)]
-    odd = (lax.axis_index("blk") // 2) % 2 == 1
-
-    def sorted_rows(first, second):
-        return jnp.where(odd, second, first), jnp.where(odd, first, second)
-
     def after(value, *done):
         return lax.optimization_barrier((value, done))[0]
 
-    marks = (segment_ids[:, :, None] == jnp.arange(LANES)[None, None]).astype(BF16)
-    marked = jnp.concatenate([tokens, marks], -1)
-    out_msgs = sorted_rows(marked[:, 0], marked[:, 1])
-    cot_msgs = sorted_rows(cotangent[:, 0], cotangent[:, 1])
+    out_msgs = split_rows(tokens, segment_ids)
+    cot_msgs = split_rows(cotangent)
     own = [lax.ppermute(m, everyone, there[k]) for k, m in enumerate(out_msgs)]
-    prefix_kv, inner, w_near, near_embed, near_mlp1, near_mlp2 = adapter_forward(
+    prefix_kv, inner, w_near, near_embed, turned = adapter_forward(
         prefix_embed, w_mlp1, b_mlp1, w_mlp2, b_mlp2, w_qkv
     )
     count = prefix_embed.shape[0]
@@ -1004,23 +1142,18 @@
 
     qkv_a, marks_a = project(own + beside, ln1_gain, ln1_bias, w_near)
     qkv_b, marks_b = project(across + beyond, ln1_gain, ln1_bias, w_near)
-    back_0, back_1, grads, grad_middle = middle_part(
+    back_0, back_1, grads, grad_middle, grad_prefix_kv = middle_part(
         count, qkv_a, qkv_b, marks_a, marks_b, prefix_kv, own, cots, ln2_gain, ln2_bias, w_out, w_fc, w_proj
     )
     grads_y = lax.ppermute(grads, "blk", swap_y)
     grads_c = lax.ppermute(grads, "seq", swap_core)
-    grads_yc = lax.ppermute(grads_y, "seq", swap_core)
-    home = [lax.ppermute(m, everyone, back[k]) for k, m in enumerate((back_0, back_1))]
-
-    def spread(value, axis, size, partners):
-        return [lax.ppermute(value, axis, [(i, i ^ far) for i in range(size)]) for far in partners]
-
-    def add_four(value, others):
-        return (value + others[0]) + (others[1] + others[2])
-
-    mine, theirs = prefix_part(count, qkv_a, grads, prefix_kv)
-    parts = spread(mine, "seq", 4, (2,)) + spread(theirs, "seq", 4, (1, 3))
-    grad_partial = query_part(count, qkv_a, qkv_b, marks_a, marks_b, prefix_kv, grads, w_near, mine)
+    parts = [lax.ppermute(grad_prefix_kv, "seq", [(i, i ^ far) for i in range(4)]) for far in (2, 1, 3)]
+    packed = pack(count, (grad_prefix_kv, *parts), back_0, back_1)
+    home = [lax.ppermute(m, everyone, back[k]) for k, m in enumerate(packed)]
+    grad_partial = query_part(
+        count, qkv_a, qkv_b, marks_a, marks_b, prefix_kv, grads, w_near, packed[0]
+    )
+    grads_yc = lax.ppermute(after(grads_y, grad_partial), "seq", swap_core)
     final_0, final_1 = final_part(
         qkv_a,
         qkv_b,
@@ -1034,18 +1167,13 @@
         w_near,
     )
     finals = [lax.ppermute(m, everyone, back[k]) for k, m in enumerate((final_0, final_1))]
-    mine = add_four(mine, after(parts, grads_y, grad_partial))
-    mine = add_four(mine, spread(mine, "blk", 8, (2, 4, 6)))
-    halves_in = [mine]
-    halves_in += [lax.ppermute(mine, "blk", swap_y), lax.ppermute(mine, "seq", swap_core)]
-    halves_in += [lax.ppermute(mine, everyone, swap_both)]
-    summed = adapter_backward(halves_in, near_embed, inner, near_mlp1, near_mlp2, final_0)
-
-    home = sorted_rows(*after(home, final_0))
-    block_out = jnp.stack([m[:, :width] for m in home], 1)
-    logs = [m[:, width : width + 3 * HEADS].astype(F32).reshape(half, 3, HEADS).sum(1) for m in home]
-    log_total = jnp.stack([jnp.transpose(m) for m in logs], 0)
-    input_grad = jnp.stack(sorted_rows(*finals), 1).astype(F32)
+    gathered = [unpack(count, width, *home)]
+    gathered += [lax.ppermute(gathered[0], "seq", swap_core), lax.ppermute(gathered[0], "blk", swap_y)]
+    gathered += [lax.ppermute(gathered[0], everyone, swap_both)]
+    summed = adapter_backward(gathered, near_embed, inner, turned, finals[0])
+
+    block_out, log_total = land(after(home, final_0), half, width, BF16, True)
+    (input_grad,) = land(finals, half, width, F32, False)
     return (block_out, input_grad, summed[0], summed[1], summed[2], summed[3], summed[4], log_total)
 
 

time: 85.3 us -> 81 us (0.950)
  starting transfers between devices: 35.3 us -> 30.9 us
  local copies, waits for them, and re-layouts: 3.73 us -> 0.02 us
  Pallas kernels: 37.4 us -> 41.1 us
  waiting for transfers between devices: 5.97 us -> 7.67 us
  other arithmetic: 1.7 us -> 0 us
    ppermute x4 -> x2, starting transfers between devices: 10.7 us -> 4.85 us  [body_rows(): lax.ppermute(m, everyone, back[k])]
    unnamed x17 -> x8, local copies, waits for them, and re-layouts: 3.21 us -> 0.02 us
    pallas_call x2 -> x7, Pallas kernels: 6.06 us -> 8.31 us  [the longest x1 3.77 us: adapter_backward(): pl.pallas_call(adapter_back_kernel, in_specs=[vmem()] * 7 + [pl.BlockSpec...]
    ppermute x4 -> x2, waiting for transfers between devices: 0.01 us -> 1.84 us  [body_rows(): lax.ppermute(m, everyone, back[k])]
    pallas_call x1, Pallas kernels: 14 us -> 15.4 us  [middle_part(): pl.pallas_call(partial(middle_kernel, count), in_specs=[vmem()] * 11 + [h...]
    ppermute x10 -> x9, starting transfers between devices: 8.44 us -> 9.34 us  [the longest x2 5.01 us: body_rows(): home = [lax.ppermute(m, everyone, back[k]) for k, m in enumerate(packed)]]
    ppermute x10 -> x9, waiting for transfers between devices: 3.59 us -> 3.86 us  [the longest x3 3.84 us: body_rows(): lax.ppermute(grad_prefix_kv, 'seq', [(i, i ^ far) for i in range(4)])]
  transfers between devices with their start and end apart: 26 -> 23, of which waited for: 5 -> 5; matrix products, arithmetic and copies ran while one was open for 3% -> 0% of each run, Pallas kernels for 27% -> 26%
where the time goes in v4:
time: 81 us; the launch traced here: 80.8 us
  Pallas kernels  41.1 us (51%)
  starting transfers between devices  30.9 us (38%)
  waiting for transfers between devices  7.67 us (9%)
  between operations  1.04 us (1%)
    pallas_call x1, Pallas kernels, middle_part(): pl.pallas_call(partial(middle_kernel, count), in_specs=[vmem()] * 11 + [h...  15.4 us
    ppermute x2, starting transfers between devices, body_rows(): own = [lax.ppermute(m, everyone, there[k]) for k, m in enumerate(out_msgs)]  6.7 us
    ppermute x2, starting transfers between devices, body_rows(): lax.ppermute(m, everyone, there[k])  6.19 us
    ppermute x2, starting transfers between devices, body_rows(): home = [lax.ppermute(m, everyone, back[k]) for k, m in enumerate(packed)]  5.01 us
    pallas_call x1, Pallas kernels, adapter_forward(): pl.pallas_call(adapter_kernel, in_specs=[hbm()] * 6, out_specs=[vmem()] *...  4.85 us
    ppermute x2, starting transfers between devices, body_rows(): lax.ppermute(m, everyone, back[k])  4.85 us
    pallas_call x1, Pallas kernels, final_part(): pl.pallas_call(final_kernel, in_specs=[vmem()] * 14, out_specs=[vmem()] *...  4.81 us
    pallas_call x2, Pallas kernels, project(): pl.pallas_call(partial(project_kernel, count), in_specs=[vmem()] * (count...  4.24 us
  transfers between devices with their start and end apart: 23, of which 5 were waited for; matrix products, arithmetic and copies ran while one was open for 0% of the time, Pallas kernels for 26%

profile of v4, /device:TPU:1, one launch (start us, length us, event | category | flops | bytes accessed | tf_op | source)
XLA Modules:
  0.0 80.8 jit_solution(8143511582169516196)
XLA Ops:
  0.6 1.2 %split.2 = (bf16[64,1152]{1,0:T(8,128)(2,1)S(1)}, bf16[64,1152]{1,0:T(8,128)(2,1)S(1)}) custom-call(bf16[64,16,128]{2,1,0:T(8,128)(2,1)} %bitcast.37, s32[2,64]{1,0:T(2,128)} %bitcast.39), custom_call_target="tpu_custom_call" | custom-call | flops 1048576 | bytes 524288 | tf_op jit(solution)/shard_map/split/pallas_call | solution.py:380
  1.8 5.6 %collective-permute-start = (bf16[64,1152]{1,0:T(8,128)(2,1)S(1)}, bf16[64,1152]{1,0:T(8,128)(2,1)S(1)}, u32[]{:S(2)}, u32[]{:S(2)}) collective-permute-start(bf16[64,1152]{1,0:T(8,128)(2,1)S(1)} %get-tuple-element.44), channel_id=1, source_target_pairs={{0,0},{1,1},{2,2},{3,3},{4,8},{5,9},{6,10},{7,11},{8,4},{9,5},{10,... | collective-permute-start | bytes 442376 | tf_op jit(solution)/shard_map/ppermute | solution.py:1132
  7.4 1.1 %collective-permute-start.1 = (bf16[64,1152]{1,0:T(8,128)(2,1)S(1)}, bf16[64,1152]{1,0:T(8,128)(2,1)S(1)}, u32[]{:S(2)}, u32[]{:S(2)}) collective-permute-start(bf16[64,1152]{1,0:T(8,128)(2,1)S(1)} %get-tuple-element.45), channel_id=1, source_target_pairs={{0,2},{1,3},{2,0},{3,1},{4,10},{5,11},{6,8},{7,9},{8,6},{9,7},{10,... | collective-permute-start | bytes 442376 | tf_op jit(solution)/shard_map/ppermute | solution.py:1132
  8.5 0.0 copy-start
  8.5 4.9 %adapter.1 = (bf16[16,2048]{1,0:T(8,128)(2,1)S(1)}, f32[16,512]{1,0:T(8,128)S(1)}, bf16[1024,3072]{1,0:T(8,128)(2,1)S(1)}, f32[10,1024]{1,0:T(8,128)S(1)}, bf16[3072,512]{1,0:T(8,128)(2,1)S(1)}) custom-call(f32[10,1024]{1,0:T(8,128)} %h_embed.1, f32[1024,512]{1,0:T(8,128)} %w_mlp1.1, f32[1,512]{1,0:T(1,128)} %bitcast.43, f32[512,2048]{1,0:T(8,128)} %w_mlp2.1, ...), custom_call_target="tpu_custom_call" | custom-call | flops 4294967296 | bytes 6291456 | tf_op jit(solution)/shard_map/adapter/pallas_call | solution.py:535
  13.4 0.0 collective-permute-done.refs_0_.own_0
  13.4 0.6 collective-permute-done.1.refs_1_.own_1
  14.0 0.0 collective-permute-start.2
  14.0 0.5 collective-permute-start.3
  14.5 1.2 %collective-permute-start.4 = (bf16[64,1152]{1,0:T(8,128)(2,1)S(1)}, bf16[64,1152]{1,0:T(8,128)(2,1)S(1)}, u32[]{:S(2)}, u32[]{:S(2)}) collective-permute-start(bf16[64,1152]{1,0:T(8,128)(2,1)S(1)} %collective-permute-done.refs_0_.own_0), channel_id=1, source_target_pairs={{0,1},{1,0},{2,3},{3,2},{4,5},{5,4},{6,7},{7,6},{8,9},{9,8},{10,11... | collective-permute-start | bytes 442376 | tf_op jit(solution)/shard_map/ppermute | solution.py:1138
  15.7 0.2 collective-permute-start.5
  15.9 1.2 %split.3 = (bf16[64,1024]{1,0:T(8,128)(2,1)S(1)}, bf16[64,1024]{1,0:T(8,128)(2,1)S(1)}) custom-call(bf16[64,16,128]{2,1,0:T(8,128)(2,1)} %bitcast.38), custom_call_target="tpu_custom_call" | custom-call | flops 1048576 | bytes 524288 | tf_op jit(solution)/shard_map/split/pallas_call | solution.py:380
  17.1 0.0 collective-permute-done.2.refs_2_
  17.1 0.0 collective-permute-done.3.refs_3_
  17.1 6.1 %collective-permute-start.8 = (bf16[64,1024]{1,0:T(8,128)(2,1)S(1)}, bf16[64,1024]{1,0:T(8,128)(2,1)S(1)}, u32[]{:S(2)}, u32[]{:S(2)}) collective-permute-start(bf16[64,1024]{1,0:T(8,128)(2,1)S(1)} %get-tuple-element.57), channel_id=1, source_target_pairs={{0,0},{1,1},{2,2},{3,3},{4,8},{5,9},{6,10},{7,11},{8,4},{9,5},{10,... | collective-permute-start | bytes 393224 | tf_op jit(solution)/shard_map/ppermute | solution.py:1140
  23.2 0.1 collective-permute-start.9
  23.3 0.0 collective-permute-done.4.refs_0_
  23.3 0.1 collective-permute-start.6
  23.4 0.0 collective-permute-done.5.refs_1_
  23.4 0.5 collective-permute-start.7
  23.9 0.0 copy-done
  23.9 0.0 copy-done.1
  23.9 2.1 %project.2 = (bf16[256,3072]{1,0:T(8,128)(2,1)S(1)}, bf16[256,128]{1,0:T(8,128)(2,1)S(1)}) custom-call(bf16[64,1152]{1,0:T(8,128)(2,1)S(1)} %collective-permute-done.refs_0_.own_0, bf16[64,1152]{1,0:T(8,128)(2,1)S(1)} %collective-permute-done.1.refs_1_.own_1, bf16[64,1152]{1,0:T(8,128)(2,1)S(1)} %collective-permute-done.2.refs_2_, ...), custom_call_target="tpu_custom_call" | custom-call | flops 1610612736 | bytes 6291456 | tf_op jit(solution)/shard_map/project/pallas_call | solution.py:445
  26.1 0.0 copy-start.2
  26.1 0.0 copy-start.3
  26.1 0.0 collective-permute-done.6.refs_2_
  26.1 0.0 collective-permute-done.7.refs_3_
  26.1 2.1 %project.3 = (bf16[256,3072]{1,0:T(8,128)(2,1)S(1)}, bf16[256,128]{1,0:T(8,128)(2,1)S(1)}) custom-call(bf16[64,1152]{1,0:T(8,128)(2,1)S(1)} %collective-permute-done.4.refs_0_, bf16[64,1152]{1,0:T(8,128)(2,1)S(1)} %collective-permute-done.5.refs_1_, bf16[64,1152]{1,0:T(8,128)(2,1)S(1)} %collective-permute-done.6.refs_2_, ...), custom_call_target="tpu_custom_call" | custom-call | flops 1610612736 | bytes 6291456 | tf_op jit(solution)/shard_map/project/pallas_call | solution.py:445
  28.2 0.0 collective-permute-done.8.cot_0
  28.2 1.4 %collective-permute-done.9.cot_1 = bf16[64,1024]{1,0:T(8,128)(2,1)S(1)} collective-permute-done((bf16[64,1024]{1,0:T(8,128)(2,1)S(1)}, bf16[64,1024]{1,0:T(8,128)(2,1)S(1)}, u32[]{:S(2)}, u32[]{:S(2)}) %collective-permute-start.9) | collective-permute-done | bytes 131104 | tf_op jit(solution)/shard_map/ppermute | solution.py:1140
  29.6 0.0 copy-done.2
  29.6 0.0 copy-done.3
  29.6 15.4 %middle.1 = (bf16[96,1152]{1,0:T(8,128)(2,1)S(1)}, bf16[96,1152]{1,0:T(8,128)(2,1)S(1)}, bf16[128,1152]{1,0:T(8,128)(2,1)S(1)}, f32[128,1024]{1,0:T(8,128)S(1)}, bf16[16,2048]{1,0:T(8,128)(2,1)S(1)}) custom-call(bf16[256,3072]{1,0:T(8,128)(2,1)S(1)} %get-tuple-element.50.qkv_a, bf16[256,3072]{1,0:T(8,128)(2,1)S(1)} %get-tuple-element.51.qkv_b, ...), custom_call_target="tpu_custom_call" | custom-call | flops 2147483648 | bytes 1000 | tf_op jit(solution)/shard_map/middle/pallas_call | solution.py:844
  45.0 1.3 %collective-permute-start.16 = (bf16[128,1152]{1,0:T(8,128)(2,1)S(1)}, bf16[128,1152]{1,0:T(8,128)(2,1)S(1)}, u32[]{:S(2)}, u32[]{:S(2)}) collective-permute-start(bf16[128,1152]{1,0:T(8,128)(2,1)S(1)} %get-tuple-element.64.grads.grads_0), channel_id=1, source_target_pairs={{0,1},{1,0},{2,3},{3,2},{4,5},{5,4},{6,7},{7,6},{8,9},{9,8},{10,11... | collective-permute-start | bytes 884744 | tf_op jit(solution)/shard_map/ppermute | solution.py:1148
  46.4 1.2 %collective-permute-start.10 = (bf16[16,2048]{1,0:T(8,128)(2,1)S(1)}, bf16[16,2048]{1,0:T(8,128)(2,1)S(1)}, u32[]{:S(2)}, u32[]{:S(2)}) collective-permute-start(bf16[16,2048]{1,0:T(8,128)(2,1)S(1)} %get-tuple-element.59.own), channel_id=1, source_target_pairs={{0,16},{8,24},{16,0},{24,8},{1,17},{9,25},{17,1},{25,9},{2,18},{10... | collective-permute-start | bytes 196616 | tf_op jit(solution)/shard_map/ppermute | solution.py:1150
  47.6 0.0 collective-permute-start.11
  47.6 0.7 collective-permute-start.12
  48.2 0.0 collective-permute-start.15
  48.2 1.7 %collective-permute-done.10.part_0 = bf16[16,2048]{1,0:T(8,128)(2,1)S(1)} collective-permute-done((bf16[16,2048]{1,0:T(8,128)(2,1)S(1)}, bf16[16,2048]{1,0:T(8,128)(2,1)S(1)}, u32[]{:S(2)}, u32[]{:S(2)}) %collective-permute-start.10) | collective-permute-done | bytes 65568 | tf_op jit(solution)/shard_map/ppermute | solution.py:1150
  49.9 0.0 collective-permute-done.11.part_1
  49.9 2.1 %collective-permute-done.12.part_2 = bf16[16,2048]{1,0:T(8,128)(2,1)S(1)} collective-permute-done((bf16[16,2048]{1,0:T(8,128)(2,1)S(1)}, bf16[16,2048]{1,0:T(8,128)(2,1)S(1)}, u32[]{:S(2)}, u32[]{:S(2)}) %collective-permute-start.12) | collective-permute-done | bytes 65568 | tf_op jit(solution)/shard_map/ppermute | solution.py:1150
  52.1 3.5 %query.1.grad_partial = f32[128,1024]{1,0:T(8,128)S(1)} custom-call(bf16[256,3072]{1,0:T(8,128)(2,1)S(1)} %get-tuple-element.50.qkv_a, bf16[256,3072]{1,0:T(8,128)(2,1)S(1)} %get-tuple-element.51.qkv_b, bf16[256,128]{1,0:T(8,128)(2,1)S(1)} %get-tuple-element.52.marks_a, bf16[256,128]{1,0:T(8,128)(2,1)S(1)} %get-tuple-element.53.marks_b, ...), custom_call_target="tpu_custom_call" | custom-call | flops 1000 | bytes 1000 | tf_op jit(solution)/shard_map/query/pallas_call | solution.py:1008
  55.6 0.0 collective-permute-done.16.grads_2
  55.6 0.3 collective-permute-start.17
  55.9 4.3 %collective-permute-start.13 = (bf16[96,1152]{1,0:T(8,128)(2,1)S(1)}, bf16[96,1152]{1,0:T(8,128)(2,1)S(1)}, u32[]{:S(2)}, u32[]{:S(2)}) collective-permute-start(bf16[96,1152]{1,0:T(8,128)(2,1)S(1)} %get-tuple-element.62.order), channel_id=1, source_target_pairs={{0,0},{1,1},{2,2},{3,3},{8,4},{9,5},{10,6},{11,7},{4,8},{5,9},{6,1... | collective-permute-start | bytes 663560 | tf_op jit(solution)/shard_map/ppermute | solution.py:1152
  60.2 0.7 collective-permute-start.14
  60.9 0.0 collective-permute-done.15.grads_1
  60.9 0.0 collective-permute-done.17.grads_3
  60.9 4.8 %final.1 = (bf16[64,1024]{1,0:T(8,128)(2,1)S(1)}, bf16[64,1024]{1,0:T(8,128)(2,1)S(1)}) custom-call(bf16[256,3072]{1,0:T(8,128)(2,1)S(1)} %get-tuple-element.50.qkv_a, bf16[256,3072]{1,0:T(8,128)(2,1)S(1)} %get-tuple-element.51.qkv_b, bf16[256,128]{1,0:T(8,128)(2,1)S(1)} %get-tuple-element.52.marks_a, bf16[256,128]{1,0:T(8,128)(2,1)S(1)} %get-tuple-element.53.marks_b, ...), custom_call_target="tpu_custom_call" | custom-call | flops 1000 | bytes 1000 | tf_op jit(solution)/shard_map/final/pallas_call | solution.py:1077
  65.7 3.3 %collective-permute-start.18 = (bf16[64,1024]{1,0:T(8,128)(2,1)S(1)}, bf16[64,1024]{1,0:T(8,128)(2,1)S(1)}, u32[]{:S(2)}, u32[]{:S(2)}) collective-permute-start(bf16[64,1024]{1,0:T(8,128)(2,1)S(1)} %get-tuple-element.67), channel_id=1, source_target_pairs={{0,0},{1,1},{2,2},{3,3},{8,4},{9,5},{10,6},{11,7},{4,8},{5,9},{6,1... | collective-permute-start | bytes 393224 | tf_op jit(solution)/shard_map/ppermute | solution.py:1169
  69.0 1.6 %collective-permute-start.19 = (bf16[64,1024]{1,0:T(8,128)(2,1)S(1)}, bf16[64,1024]{1,0:T(8,128)(2,1)S(1)}, u32[]{:S(2)}, u32[]{:S(2)}) collective-permute-start(bf16[64,1024]{1,0:T(8,128)(2,1)S(1)} %get-tuple-element.71), channel_id=1, source_target_pairs={{2,0},{3,1},{0,2},{1,3},{10,4},{11,5},{8,6},{9,7},{6,8},{7,9},{4,1... | collective-permute-start | bytes 393224 | tf_op jit(solution)/shard_map/ppermute | solution.py:1169
  70.6 0.0 collective-permute-done.13.refs_0_.home_0
  70.6 0.0 collective-permute-done.14.refs_1_.home_1
  70.6 0.1 collective-permute-start.20
  70.7 0.3 collective-permute-start.21
  71.0 1.8 %collective-permute-start.22 = (bf16[16,2048]{1,0:T(8,128)(2,1)S(1)}, bf16[16,2048]{1,0:T(8,128)(2,1)S(1)}, u32[]{:S(2)}, u32[]{:S(2)}) collective-permute-start(bf16[16,2048]{1,0:T(8,128)(2,1)S(1)} %unpack.1.part_0), channel_id=1, source_target_pairs={{0,9},{1,8},{2,11},{3,10},{4,13},{5,12},{6,15},{7,14},{8,1},{9,0},... | collective-permute-start | bytes 196616 | tf_op jit(solution)/shard_map/ppermute | solution.py:1172
  72.8 1.1 %land.2 = (bf16[64,16,128]{2,1,0:T(8,128)(2,1)}, f32[2,16,64]{2,1,0:T(8,128)}) custom-call(bf16[96,1152]{1,0:T(8,128)(2,1)S(1)} %collective-permute-done.13.refs_0_.home_0, bf16[96,1152]{1,0:T(8,128)(2,1)S(1)} %collective-permute-done.14.refs_1_.home_1), custom_call_target="tpu_custom_call" | custom-call | flops 1000 | bytes 1000 | tf_op jit(solution)/shard_map/land/pallas_call | solution.py:414
  73.9 1.8 %collective-permute-done.18.refs_0_.order = bf16[64,1024]{1,0:T(8,128)(2,1)S(1)} collective-permute-done((bf16[64,1024]{1,0:T(8,128)(2,1)S(1)}, bf16[64,1024]{1,0:T(8,128)(2,1)S(1)}, u32[]{:S(2)}, u32[]{:S(2)}) %collective-permute-start.18) | collective-permute-done | bytes 131104 | tf_op jit(solution)/shard_map/ppermute | solution.py:1169
  75.7 0.0 collective-permute-done.19.refs_1_
  75.7 1.1 %land.3 = f32[64,16,128]{2,1,0:T(8,128)} custom-call(bf16[64,1024]{1,0:T(8,128)(2,1)S(1)} %collective-permute-done.18.refs_0_.order, bf16[64,1024]{1,0:T(8,128)(2,1)S(1)} %collective-permute-done.19.refs_1_), custom_call_target="tpu_custom_call" | custom-call | flops 1000 | bytes 1000 | tf_op jit(solution)/shard_map/land/pallas_call | solution.py:414
  76.8 0.0 collective-permute-done.20.part_1
  76.8 0.0 collective-permute-done.21.part_2
  76.8 0.0 collective-permute-done.22.part_3
  76.8 3.8 %adapter_back.1 = (f32[10,1024]{1,0:T(8,128)}, f32[1024,512]{1,0:T(8,128)}, f32[1,512]{1,0:T(1,128)}, f32[512,2048]{1,0:T(8,128)}, f32[1,2048]{1,0:T(1,128)}) custom-call(bf16[16,2048]{1,0:T(8,128)(2,1)S(1)} %unpack.1.part_0, bf16[16,2048]{1,0:T(8,128)(2,1)S(1)} %collective-permute-done.20.part_1, bf16[16,2048]{1,0:T(8,128)(2,1)S(1)} %collective-permute-done.21.part_2, ...), custom_call_target="tpu_custom_call" | custom-call | flops 1000 | bytes 1000 | tf_op jit(solution)/shard_map/adapter_back/pallas_call | solution.py:624
  (3 shorter events, 0.1 us)
Async XLA Ops:
  1.8 11.6 %collective-permute-start = (bf16[64,1152]{1,0:T(8,128)(2,1)S(1)}, bf16[64,1152]{1,0:T(8,128)(2,1)S(1)}, u32[]{:S(2)}, u32[]{:S(2)}) collective-permute-start(bf16[64,1152]{1,0:T(8,128)(2,1)S(1)} %get-tuple-element.44), channel_id=1, source_target_pairs={{0,0},{1,1},{2,2},{3,3},{4,8},{5,9},{6,10},{7,11},{8,4},{9,5},{10,... | collective-permute-start | bytes 442376 | tf_op jit(solution)/shard_map/ppermute | solution.py:1132
  7.4 6.5 %collective-permute-start.1 = (bf16[64,1152]{1,0:T(8,128)(2,1)S(1)}, bf16[64,1152]{1,0:T(8,128)(2,1)S(1)}, u32[]{:S(2)}, u32[]{:S(2)}) collective-permute-start(bf16[64,1152]{1,0:T(8,128)(2,1)S(1)} %get-tuple-element.45), channel_id=1, source_target_pairs={{0,2},{1,3},{2,0},{3,1},{4,10},{5,11},{6,8},{7,9},{8,6},{9,7},{10,... | collective-permute-start | bytes 442376 | tf_op jit(solution)/shard_map/ppermute | solution.py:1132
  8.5 15.4 %copy-start = (f32[1024]{0:T(1024)S(1)}, f32[1024]{0:T(1024)}, u32[]{:S(2)}) copy-start(f32[1024]{0:T(1024)} %param.18) | copy-start | bytes 12292
  8.5 15.4 %copy-start.1 = (f32[1024]{0:T(1024)S(1)}, f32[1024]{0:T(1024)}, u32[]{:S(2)}) copy-start(f32[1024]{0:T(1024)} %param.19) | copy-start | bytes 12292
  14.0 3.1 %collective-permute-start.2 = (bf16[64,1152]{1,0:T(8,128)(2,1)S(1)}, bf16[64,1152]{1,0:T(8,128)(2,1)S(1)}, u32[]{:S(2)}, u32[]{:S(2)}) collective-permute-start(bf16[64,1152]{1,0:T(8,128)(2,1)S(1)} %collective-permute-done.refs_0_.own_0), channel_id=1, source_target_pairs={{0,8},{8,0},{16,24},{24,16},{1,9},{9,1},{17,25},{25,17},{2,10},{10... | collective-permute-start | bytes 442376 | tf_op jit(solution)/shard_map/ppermute | solution.py:1139
  14.0 3.2 %collective-permute-start.3 = (bf16[64,1152]{1,0:T(8,128)(2,1)S(1)}, bf16[64,1152]{1,0:T(8,128)(2,1)S(1)}, u32[]{:S(2)}, u32[]{:S(2)}) collective-permute-start(bf16[64,1152]{1,0:T(8,128)(2,1)S(1)} %collective-permute-done.1.refs_1_.own_1), channel_id=1, source_target_pairs={{0,8},{8,0},{16,24},{24,16},{1,9},{9,1},{17,25},{25,17},{2,10},{10... | collective-permute-start | bytes 442376 | tf_op jit(solution)/shard_map/ppermute | solution.py:1139
  14.5 8.9 %collective-permute-start.4 = (bf16[64,1152]{1,0:T(8,128)(2,1)S(1)}, bf16[64,1152]{1,0:T(8,128)(2,1)S(1)}, u32[]{:S(2)}, u32[]{:S(2)}) collective-permute-start(bf16[64,1152]{1,0:T(8,128)(2,1)S(1)} %collective-permute-done.refs_0_.own_0), channel_id=1, source_target_pairs={{0,1},{1,0},{2,3},{3,2},{4,5},{5,4},{6,7},{7,6},{8,9},{9,8},{10,11... | collective-permute-start | bytes 442376 | tf_op jit(solution)/shard_map/ppermute | solution.py:1138
  15.7 7.7 %collective-permute-start.5 = (bf16[64,1152]{1,0:T(8,128)(2,1)S(1)}, bf16[64,1152]{1,0:T(8,128)(2,1)S(1)}, u32[]{:S(2)}, u32[]{:S(2)}) collective-permute-start(bf16[64,1152]{1,0:T(8,128)(2,1)S(1)} %collective-permute-done.1.refs_1_.own_1), channel_id=1, source_target_pairs={{0,1},{1,0},{2,3},{3,2},{4,5},{5,4},{6,7},{7,6},{8,9},{9,8},{10,11... | collective-permute-start | bytes 442376 | tf_op jit(solution)/shard_map/ppermute | solution.py:1138
  17.1 11.1 %collective-permute-start.8 = (bf16[64,1024]{1,0:T(8,128)(2,1)S(1)}, bf16[64,1024]{1,0:T(8,128)(2,1)S(1)}, u32[]{:S(2)}, u32[]{:S(2)}) collective-permute-start(bf16[64,1024]{1,0:T(8,128)(2,1)S(1)} %get-tuple-element.57), channel_id=1, source_target_pairs={{0,0},{1,1},{2,2},{3,3},{4,8},{5,9},{6,10},{7,11},{8,4},{9,5},{10,... | collective-permute-start | bytes 393224 | tf_op jit(solution)/shard_map/ppermute | solution.py:1140
  23.2 6.4 %collective-permute-start.9 = (bf16[64,1024]{1,0:T(8,128)(2,1)S(1)}, bf16[64,1024]{1,0:T(8,128)(2,1)S(1)}, u32[]{:S(2)}, u32[]{:S(2)}) collective-permute-start(bf16[64,1024]{1,0:T(8,128)(2,1)S(1)} %get-tuple-element.58), channel_id=1, source_target_pairs={{0,2},{1,3},{2,0},{3,1},{4,10},{5,11},{6,8},{7,9},{8,6},{9,7},{10,... | collective-permute-start | bytes 393224 | tf_op jit(solution)/shard_map/ppermute | solution.py:1140
  23.3 2.7 %collective-permute-start.6 = (bf16[64,1152]{1,0:T(8,128)(2,1)S(1)}, bf16[64,1152]{1,0:T(8,128)(2,1)S(1)}, u32[]{:S(2)}, u32[]{:S(2)}) collective-permute-start(bf16[64,1152]{1,0:T(8,128)(2,1)S(1)} %collective-permute-done.4.refs_0_), channel_id=1, source_target_pairs={{0,8},{8,0},{16,24},{24,16},{1,9},{9,1},{17,25},{25,17},{2,10},{10... | collective-permute-start | bytes 442376 | tf_op jit(solution)/shard_map/ppermute | solution.py:1141
  23.4 2.7 %collective-permute-start.7 = (bf16[64,1152]{1,0:T(8,128)(2,1)S(1)}, bf16[64,1152]{1,0:T(8,128)(2,1)S(1)}, u32[]{:S(2)}, u32[]{:S(2)}) collective-permute-start(bf16[64,1152]{1,0:T(8,128)(2,1)S(1)} %collective-permute-done.5.refs_1_), channel_id=1, source_target_pairs={{0,8},{8,0},{16,24},{24,16},{1,9},{9,1},{17,25},{25,17},{2,10},{10... | collective-permute-start | bytes 442376 | tf_op jit(solution)/shard_map/ppermute | solution.py:1141
  26.1 3.6 %copy-start.2 = (f32[1024]{0:T(1024)S(1)}, f32[1024]{0:T(1024)}, u32[]{:S(2)}) copy-start(f32[1024]{0:T(1024)} %param.22) | copy-start | bytes 12292
  26.1 3.6 %copy-start.3 = (f32[1024]{0:T(1024)S(1)}, f32[1024]{0:T(1024)}, u32[]{:S(2)}) copy-start(f32[1024]{0:T(1024)} %param.23) | copy-start | bytes 12292
  45.0 10.6 %collective-permute-start.16 = (bf16[128,1152]{1,0:T(8,128)(2,1)S(1)}, bf16[128,1152]{1,0:T(8,128)(2,1)S(1)}, u32[]{:S(2)}, u32[]{:S(2)}) collective-permute-start(bf16[128,1152]{1,0:T(8,128)(2,1)S(1)} %get-tuple-element.64.grads.grads_0), channel_id=1, source_target_pairs={{0,1},{1,0},{2,3},{3,2},{4,5},{5,4},{6,7},{7,6},{8,9},{9,8},{10,11... | collective-permute-start | bytes 884744 | tf_op jit(solution)/shard_map/ppermute | solution.py:1148
  46.4 3.6 %collective-permute-start.10 = (bf16[16,2048]{1,0:T(8,128)(2,1)S(1)}, bf16[16,2048]{1,0:T(8,128)(2,1)S(1)}, u32[]{:S(2)}, u32[]{:S(2)}) collective-permute-start(bf16[16,2048]{1,0:T(8,128)(2,1)S(1)} %get-tuple-element.59.own), channel_id=1, source_target_pairs={{0,16},{8,24},{16,0},{24,8},{1,17},{9,25},{17,1},{25,9},{2,18},{10... | collective-permute-start | bytes 196616 | tf_op jit(solution)/shard_map/ppermute | solution.py:1150
  47.6 2.4 %collective-permute-start.11 = (bf16[16,2048]{1,0:T(8,128)(2,1)S(1)}, bf16[16,2048]{1,0:T(8,128)(2,1)S(1)}, u32[]{:S(2)}, u32[]{:S(2)}) collective-permute-start(bf16[16,2048]{1,0:T(8,128)(2,1)S(1)} %get-tuple-element.59.own), channel_id=1, source_target_pairs={{0,8},{8,0},{16,24},{24,16},{1,9},{9,1},{17,25},{25,17},{2,10},{10... | collective-permute-start | bytes 196616 | tf_op jit(solution)/shard_map/ppermute | solution.py:1150
  47.6 4.5 %collective-permute-start.12 = (bf16[16,2048]{1,0:T(8,128)(2,1)S(1)}, bf16[16,2048]{1,0:T(8,128)(2,1)S(1)}, u32[]{:S(2)}, u32[]{:S(2)}) collective-permute-start(bf16[16,2048]{1,0:T(8,128)(2,1)S(1)} %get-tuple-element.59.own), channel_id=1, source_target_pairs={{0,24},{8,16},{16,8},{24,0},{1,25},{9,17},{17,9},{25,1},{2,26},{10... | collective-permute-start | bytes 196616 | tf_op jit(solution)/shard_map/ppermute | solution.py:1150
  48.2 12.7 %collective-permute-start.15 = (bf16[128,1152]{1,0:T(8,128)(2,1)S(1)}, bf16[128,1152]{1,0:T(8,128)(2,1)S(1)}, u32[]{:S(2)}, u32[]{:S(2)}) collective-permute-start(bf16[128,1152]{1,0:T(8,128)(2,1)S(1)} %get-tuple-element.64.grads.grads_0), channel_id=1, source_target_pairs={{0,8},{8,0},{16,24},{24,16},{1,9},{9,1},{17,25},{25,17},{2,10},{10... | collective-permute-start | bytes 884744 | tf_op jit(solution)/shard_map/ppermute | solution.py:1149
  55.6 5.3 %collective-permute-start.17 = (bf16[128,1152]{1,0:T(8,128)(2,1)S(1)}, bf16[128,1152]{1,0:T(8,128)(2,1)S(1)}, u32[]{:S(2)}, u32[]{:S(2)}) collective-permute-start(bf16[128,1152]{1,0:T(8,128)(2,1)S(1)} %collective-permute-done.16.grads_2), channel_id=1, source_target_pairs={{0,8},{8,0},{16,24},{24,16},{1,9},{9,1},{17,25},{25,17},{2,10},{10... | collective-permute-start | bytes 884744 | tf_op jit(solution)/shard_map/ppermute | solution.py:1156
  55.9 14.7 %collective-permute-start.13 = (bf16[96,1152]{1,0:T(8,128)(2,1)S(1)}, bf16[96,1152]{1,0:T(8,128)(2,1)S(1)}, u32[]{:S(2)}, u32[]{:S(2)}) collective-permute-start(bf16[96,1152]{1,0:T(8,128)(2,1)S(1)} %get-tuple-element.62.order), channel_id=1, source_target_pairs={{0,0},{1,1},{2,2},{3,3},{8,4},{9,5},{10,6},{11,7},{4,8},{5,9},{6,1... | collective-permute-start | bytes 663560 | tf_op jit(solution)/shard_map/ppermute | solution.py:1152
  60.2 10.4 %collective-permute-start.14 = (bf16[96,1152]{1,0:T(8,128)(2,1)S(1)}, bf16[96,1152]{1,0:T(8,128)(2,1)S(1)}, u32[]{:S(2)}, u32[]{:S(2)}) collective-permute-start(bf16[96,1152]{1,0:T(8,128)(2,1)S(1)} %get-tuple-element.63), channel_id=1, source_target_pairs={{2,0},{3,1},{0,2},{1,3},{10,4},{11,5},{8,6},{9,7},{6,8},{7,9},{4,1... | collective-permute-start | bytes 663560 | tf_op jit(solution)/shard_map/ppermute | solution.py:1152
  65.7 10.0 %collective-permute-start.18 = (bf16[64,1024]{1,0:T(8,128)(2,1)S(1)}, bf16[64,1024]{1,0:T(8,128)(2,1)S(1)}, u32[]{:S(2)}, u32[]{:S(2)}) collective-permute-start(bf16[64,1024]{1,0:T(8,128)(2,1)S(1)} %get-tuple-element.67), channel_id=1, source_target_pairs={{0,0},{1,1},{2,2},{3,3},{8,4},{9,5},{10,6},{11,7},{4,8},{5,9},{6,1... | collective-permute-start | bytes 393224 | tf_op jit(solution)/shard_map/ppermute | solution.py:1169
  69.0 6.7 %collective-permute-start.19 = (bf16[64,1024]{1,0:T(8,128)(2,1)S(1)}, bf16[64,1024]{1,0:T(8,128)(2,1)S(1)}, u32[]{:S(2)}, u32[]{:S(2)}) collective-permute-start(bf16[64,1024]{1,0:T(8,128)(2,1)S(1)} %get-tuple-element.71), channel_id=1, source_target_pairs={{2,0},{3,1},{0,2},{1,3},{10,4},{11,5},{8,6},{9,7},{6,8},{7,9},{4,1... | collective-permute-start | bytes 393224 | tf_op jit(solution)/shard_map/ppermute | solution.py:1169
  70.6 6.2 %collective-permute-start.20 = (bf16[16,2048]{1,0:T(8,128)(2,1)S(1)}, bf16[16,2048]{1,0:T(8,128)(2,1)S(1)}, u32[]{:S(2)}, u32[]{:S(2)}) collective-permute-start(bf16[16,2048]{1,0:T(8,128)(2,1)S(1)} %unpack.1.part_0), channel_id=1, source_target_pairs={{0,8},{8,0},{16,24},{24,16},{1,9},{9,1},{17,25},{25,17},{2,10},{10... | collective-permute-start | bytes 196616 | tf_op jit(solution)/shard_map/ppermute | solution.py:1171
  70.7 6.1 %collective-permute-start.21 = (bf16[16,2048]{1,0:T(8,128)(2,1)S(1)}, bf16[16,2048]{1,0:T(8,128)(2,1)S(1)}, u32[]{:S(2)}, u32[]{:S(2)}) collective-permute-start(bf16[16,2048]{1,0:T(8,128)(2,1)S(1)} %unpack.1.part_0), channel_id=1, source_target_pairs={{0,1},{1,0},{2,3},{3,2},{4,5},{5,4},{6,7},{7,6},{8,9},{9,8},{10,11... | collective-permute-start | bytes 196616 | tf_op jit(solution)/shard_map/ppermute | solution.py:1171
  71.0 5.8 %collective-permute-start.22 = (bf16[16,2048]{1,0:T(8,128)(2,1)S(1)}, bf16[16,2048]{1,0:T(8,128)(2,1)S(1)}, u32[]{:S(2)}, u32[]{:S(2)}) collective-permute-start(bf16[16,2048]{1,0:T(8,128)(2,1)S(1)} %unpack.1.part_0), channel_id=1, source_target_pairs={{0,9},{1,8},{2,11},{3,10},{4,13},{5,12},{6,15},{7,14},{8,1},{9,0},... | collective-permute-start | bytes 196616 | tf_op jit(solution)/shard_map/ppermute | solution.py:1172

commit v5 on v4

--- a/solution.py
+++ b/solution.py
@@ -389,40 +389,46 @@
     )(*kept_in_hbm(tiles), *extra)
 
 
-def land_kernel(logs, *refs):
-    msg_0, msg_1, out = refs[0], refs[1], refs[2]
-    work = refs[-1]
-    half, count, _ = out.shape
-    width = count // 2 * LANES
+def place_rows(msg_0, msg_1, work):
+    width = msg_0.shape[1] // LANES * LANES
+    count = 2 * (width // LANES)
+    half = work.shape[0] // count
     odd = odd_place()
     for i in range(count // 2):
         at = pl.ds(i * LANES, LANES)
         one, two = msg_0[:half, at].astype(F32), msg_1[:half, at].astype(F32)
         work[pl.ds(2 * i, half, stride=count)] = jnp.where(odd, two, one)
         work[pl.ds(2 * i + 1, half, stride=count)] = jnp.where(odd, one, two)
+
+
+def land_kernel(msg_0, msg_1, out, logs, work):
+    half, count, _ = out.shape
+    heads, width = logs.shape[1], count // 2 * LANES
+    place_rows(msg_0.at[:, pl.ds(0, width)], msg_1.at[:, pl.ds(0, width)], work)
     out[...] = work[...].reshape(out.shape).astype(out.dtype)
-    if logs:
-        heads = refs[3].shape[1]
-        one, two = (m[:half, width:].astype(F32) for m in (msg_0, msg_1))
-        for r, chosen in enumerate((jnp.where(odd, two, one), jnp.where(odd, one, two))):
-            summed = chosen + jnp.roll(chosen, -heads, 1) + jnp.roll(chosen, -2 * heads, 1)
-            refs[3][r] = summed.T[:heads]
-
-
-def land(messages, half, width, dtype, logs):
+    odd = odd_place()
+    one, two = (m[:half, width:].astype(F32) for m in (msg_0, msg_1))
+    for r, chosen in enumerate((jnp.where(odd, two, one), jnp.where(odd, one, two))):
+        summed = chosen + jnp.roll(chosen, -heads, 1) + jnp.roll(chosen, -2 * heads, 1)
+        logs[r] = summed.T[:heads]
+
+
+def land(messages, half, width):
     count = 2 * width // LANES
     out = pl.pallas_call(
-        partial(land_kernel, logs),
+        land_kernel,
         in_specs=[vmem()] * 2,
-        out_specs=[vmem()] * (1 + logs),
-        out_shape=[jax.ShapeDtypeStruct((half, count, LANES), dtype)]
-        + [jax.ShapeDtypeStruct((2, HEADS, half), F32)] * logs,
+        out_specs=[vmem()] * 2,
+        out_shape=[
+            jax.ShapeDtypeStruct((half, count, LANES), BF16),
+            jax.ShapeDtypeStruct((2, HEADS, half), F32),
+        ],
         scratch_shapes=[pltpu.VMEM((half * count, LANES), F32)],
         compiler_params=pltpu.CompilerParams(vmem_limit_bytes=4 * MIB),
         cost_estimate=pl.CostEstimate(flops=1000, bytes_accessed=1000, transcendentals=0),
         name="land",
     )(*messages)
-    return (from_tiles(out[0], width), *out[1:])
+    return from_tiles(out[0], width), out[1]
 
 
 def project_kernel(count, *refs):
@@ -574,6 +580,8 @@
 
 
 def adapter_back_kernel(
+    home_0,
+    home_1,
     part_0,
     part_1,
     part_2,
@@ -581,17 +589,17 @@
     embed,
     inner,
     turned,
-    order,
+    block,
     grad_prefix,
     grad_mlp1,
     grad_bias1,
     grad_mlp2,
     grad_bias2,
+    o_block,
     o_mlp1,
     o_mlp2,
     sems,
 ):
-    del order
     steps, step = o_mlp2.shape[0], o_mlp2.shape[2]
     first, second, third, fourth = (p[...].astype(F32) for p in (part_0, part_1, part_2, part_3))
     grads = (first + second) + (third + fourth)
@@ -605,6 +613,9 @@
         )
         stores[-1].start()
     columns, (width, hidden) = steps * step, o_mlp1.shape
+    place_rows(home_0, home_1, o_block)
+    stores.append(pltpu.make_async_copy(o_block, block, sems.at[steps + 1]))
+    stores[-1].start()
     back = two_products(grads, turned[:columns]) * (1.0 - act * act)
     grad_bias1[...] = jnp.sum(back, 0, keepdims=True)
     o_mlp1[...] = outer(pad_rows(embed[...], PRE_ROWS), back)
@@ -617,15 +628,18 @@
         copy.wait()
 
 
-def adapter_backward(parts, embed, inner, turned, order):
+def finish(finals, parts, embed, inner, turned):
     hidden, width = turned.shape[1], embed.shape[1]
     columns = turned.shape[0] - width
+    half = finals[0].shape[0]
     steps = 4
+    tiles = 2 * width // LANES
     out = pl.pallas_call(
         adapter_back_kernel,
-        in_specs=[vmem()] * 7 + [pl.BlockSpec(memory_space=pl.ANY)],
-        out_specs=[vmem(), hbm(), vmem(), hbm(), vmem()],
+        in_specs=[vmem()] * 9,
+        out_specs=[hbm(), vmem(), hbm(), vmem(), hbm(), vmem()],
         out_shape=[
+            jax.ShapeDtypeStruct((half * tiles, LANES), F32),
             jax.ShapeDtypeStruct(embed.shape, F32),
             jax.ShapeDtypeStruct((width, hidden), F32),
             jax.ShapeDtypeStruct((1, hidden), F32),
@@ -633,15 +647,17 @@
             jax.ShapeDtypeStruct((1, columns), F32),
         ],
         scratch_shapes=[
+            pltpu.VMEM((half * tiles, LANES), F32),
             pltpu.VMEM((width, hidden), F32),
             pltpu.VMEM((steps, hidden, columns // steps), F32),
-            pltpu.SemaphoreType.DMA((steps + 1,)),
+            pltpu.SemaphoreType.DMA((steps + 2,)),
         ],
         compiler_params=pltpu.CompilerParams(vmem_limit_bytes=16 * MIB),
         cost_estimate=pl.CostEstimate(flops=1000, bytes_accessed=1000, transcendentals=0),
-        name="adapter_back",
-    )(*parts, embed, inner, turned, order)
-    return out[0], out[1], out[2][0], out[3], out[4][0]
+        name="finish",
+    )(*finals, *parts, embed, inner, turned)
+    block = from_tiles(out[0].reshape(half, tiles, LANES), width)
+    return block, (out[1], out[2], out[3][0], out[4], out[5][0])
 
 
 def head_mask(rows):
@@ -716,7 +732,6 @@
     back_1,
     grad_out_heads,
     grad_middle,
-    grad_prefix_kv,
     v_out,
     v_fc,
     v_proj,
@@ -831,7 +846,6 @@
     back_1[:half, width:] = marks[half:]
     back_0[half:] = jnp.zeros_like(back_0[half:])
     back_1[half:] = jnp.zeros_like(back_1[half:])
-    prefix_grads(qkv_a, grad_out_heads, marks, prefix_kv, count, grad_prefix_kv)
 
 
 def middle_part(count, qkv_a, qkv_b, marks_a, marks_b, prefix_kv, own, cots, gain, bias, w_out, w_fc, w_proj):
@@ -844,13 +858,12 @@
     return pl.pallas_call(
         partial(middle_kernel, count),
         in_specs=[vmem()] * 11 + [hbm()] * 3,
-        out_specs=[vmem()] * 5,
+        out_specs=[vmem()] * 4,
         out_shape=[
             jax.ShapeDtypeStruct((half + tail_rows(count), wide), BF16),
             jax.ShapeDtypeStruct((half + tail_rows(count), wide), BF16),
             jax.ShapeDtypeStruct((rows, wide), BF16),
             jax.ShapeDtypeStruct((rows, width), F32),
-            jax.ShapeDtypeStruct(prefix_kv.shape, BF16),
         ],
         scratch_shapes=[
             pltpu.VMEM((width, width), BF16),
@@ -895,8 +908,9 @@
     return -(-2 * count // PRE_ROWS) * PRE_ROWS
 
 
-def prefix_grads(queries, grads, marks, prefix_kv, used, out):
+def prefix_kernel(used, queries, grads, prefix_kv, out):
     count, rows, width = prefix_kv.shape[0], grads.shape[0], grads.shape[1] - LANES
+    marks = grads[:, width:]
     low = head_mask(count)
     mask = jnp.where(iota((count, rows), 0) < used, 0.0, NEG)
 
@@ -911,6 +925,18 @@
         return carry
 
     lax.fori_loop(0, HEADS // 2, step, 0, unroll=True)
+
+
+def prefix_part(count, qkv_a, grads, prefix_kv):
+    return pl.pallas_call(
+        partial(prefix_kernel, count),
+        in_specs=[vmem()] * 3,
+        out_specs=vmem(),
+        out_shape=jax.ShapeDtypeStruct(prefix_kv.shape, BF16),
+        compiler_params=pltpu.CompilerParams(vmem_limit_bytes=8 * MIB),
+        cost_estimate=pl.CostEstimate(flops=1000, bytes_accessed=1000, transcendentals=0),
+        name="prefix",
+    )(qkv_a, grads, prefix_kv)
 
 
 def pack_kernel(count, own, part_0, part_1, part_2, _0, _1, back_0, back_1):
@@ -1012,7 +1038,7 @@
         out_shape=jax.ShapeDtypeStruct((rows, width), F32),
         scratch_shapes=[pltpu.VMEM((rows, 4 * rows + LANES), F32), pltpu.VMEM((rows, width), BF16)],
         compiler_params=pltpu.CompilerParams(vmem_limit_bytes=16 * MIB),
-        cost_estimate=pl.CostEstimate(flops=1000, bytes_accessed=1000, transcendentals=0),
+        cost_estimate=pl.CostEstimate(flops=1 << 31, bytes_accessed=1000, transcendentals=0),
         name="query",
     )(qkv_a, qkv_b, marks_a, marks_b, prefix_kv, grads, weight, order)
 
@@ -1142,18 +1168,19 @@
 
     qkv_a, marks_a = project(own + beside, ln1_gain, ln1_bias, w_near)
     qkv_b, marks_b = project(across + beyond, ln1_gain, ln1_bias, w_near)
-    back_0, back_1, grads, grad_middle, grad_prefix_kv = middle_part(
+    back_0, back_1, grads, grad_middle = middle_part(
         count, qkv_a, qkv_b, marks_a, marks_b, prefix_kv, own, cots, ln2_gain, ln2_bias, w_out, w_fc, w_proj
     )
     grads_y = lax.ppermute(grads, "blk", swap_y)
     grads_c = lax.ppermute(grads, "seq", swap_core)
+    grad_prefix_kv = prefix_part(count, qkv_a, grads, prefix_kv)
     parts = [lax.ppermute(grad_prefix_kv, "seq", [(i, i ^ far) for i in range(4)]) for far in (2, 1, 3)]
-    packed = pack(count, (grad_prefix_kv, *parts), back_0, back_1)
+    grad_partial = query_part(
+        count, qkv_a, qkv_b, marks_a, marks_b, prefix_kv, grads, w_near, grad_prefix_kv
+    )
+    packed = pack(count, (grad_prefix_kv, *after(parts, grad_partial)), back_0, back_1)
     home = [lax.ppermute(m, everyone, back[k]) for k, m in enumerate(packed)]
-    grad_partial = query_part(
-        count, qkv_a, qkv_b, marks_a, marks_b, prefix_kv, grads, w_near, packed[0]
-    )
-    grads_yc = lax.ppermute(after(grads_y, grad_partial), "seq", swap_core)
+    grads_yc = lax.ppermute(after(grads_y, packed), "seq", swap_core)
     final_0, final_1 = final_part(
         qkv_a,
         qkv_b,
@@ -1170,10 +1197,8 @@
     gathered = [unpack(count, width, *home)]
     gathered += [lax.ppermute(gathered[0], "seq", swap_core), lax.ppermute(gathered[0], "blk", swap_y)]
     gathered += [lax.ppermute(gathered[0], everyone, swap_both)]
-    summed = adapter_backward(gathered, near_embed, inner, turned, finals[0])
-
-    block_out, log_total = land(after(home, final_0), half, width, BF16, True)
-    (input_grad,) = land(finals, half, width, F32, False)
+    input_grad, summed = finish(finals, gathered, near_embed, inner, turned)
+    block_out, log_total = land(after(home, final_0), half, width)
     return (block_out, input_grad, summed[0], summed[1], summed[2], summed[3], summed[4], log_total)
 
 

time: 81 us -> 78.3 us (0.967)
  waiting for transfers between devices: 7.67 us -> 4.84 us
  Pallas kernels: 41.1 us -> 40.2 us
    ppermute x3, waiting for transfers between devices: 3.84 us -> 0.09 us  [body_rows(): lax.ppermute(grad_prefix_kv, 'seq', [(i, i ^ far) for i in range(4)])]
    ppermute x1, waiting for transfers between devices: 0.01 us -> 2.77 us  [body_rows(): gathered += [lax.ppermute(gathered[0], everyone, swap_both)]]
    ppermute x2, waiting for transfers between devices: 1.84 us -> 0.01 us  [body_rows(): lax.ppermute(m, everyone, back[k])]
    pallas_call x1, Pallas kernels: 15.4 us -> 14 us  [middle_part(): pl.pallas_call(partial(middle_kernel, count), in_specs=[vmem()] * 11 + [h...]
    ppermute x1, starting transfers between devices: 0.3 us -> 1.3 us  [body_rows(): lax.ppermute(gathered[0], 'blk', swap_y)]
    ppermute x1, starting transfers between devices: 1.83 us -> 0.82 us  [body_rows(): gathered += [lax.ppermute(gathered[0], everyone, swap_both)]]
  transfers between devices with their start and end apart: 23 -> 23, of which waited for: 5 -> 4; matrix products, arithmetic and copies ran while one was open for 0% -> 0% of each run, Pallas kernels for 26% -> 27%
where the time goes in v5:
time: 78.3 us; the launch traced here: 77.7 us
  Pallas kernels  40.2 us (51%)
  starting transfers between devices  31.5 us (40%)
  waiting for transfers between devices  4.84 us (6%)
  between operations  1.06 us (1%)
    pallas_call x1, Pallas kernels, middle_part(): pl.pallas_call(partial(middle_kernel, count), in_specs=[vmem()] * 11 + [h...  14 us
    ppermute x2, starting transfers between devices, body_rows(): own = [lax.ppermute(m, everyone, there[k]) for k, m in enumerate(out_msgs)]  6.7 us
    ppermute x2, starting transfers between devices, body_rows(): lax.ppermute(m, everyone, there[k])  6.19 us
    ppermute x2, starting transfers between devices, body_rows(): home = [lax.ppermute(m, everyone, back[k]) for k, m in enumerate(packed)]  5.79 us
    pallas_call x1, Pallas kernels, adapter_forward(): pl.pallas_call(adapter_kernel, in_specs=[hbm()] * 6, out_specs=[vmem()] *...  4.85 us
    pallas_call x1, Pallas kernels, final_part(): pl.pallas_call(final_kernel, in_specs=[vmem()] * 14, out_specs=[vmem()] *...  4.8 us
    ppermute x2, starting transfers between devices, body_rows(): lax.ppermute(m, everyone, back[k])  4.4 us
    pallas_call x2, Pallas kernels, project(): pl.pallas_call(partial(project_kernel, count), in_specs=[vmem()] * (count...  4.24 us
  transfers between devices with their start and end apart: 23, of which 4 were waited for; matrix products, arithmetic and copies ran while one was open for 0% of the time, Pallas kernels for 27%

profile of v5, /device:TPU:1, one launch (start us, length us, event | category | flops | bytes accessed | tf_op | source)
XLA Modules:
  0.0 77.7 jit_solution(6413594255897591226)
XLA Ops:
  0.6 1.2 %split.2 = (bf16[64,1152]{1,0:T(8,128)(2,1)S(1)}, bf16[64,1152]{1,0:T(8,128)(2,1)S(1)}) custom-call(bf16[64,16,128]{2,1,0:T(8,128)(2,1)} %bitcast.36, s32[2,64]{1,0:T(2,128)} %bitcast.38), custom_call_target="tpu_custom_call" | custom-call | flops 1048576 | bytes 524288 | tf_op jit(solution)/shard_map/split/pallas_call | solution.py:380
  1.8 5.6 %collective-permute-start = (bf16[64,1152]{1,0:T(8,128)(2,1)S(1)}, bf16[64,1152]{1,0:T(8,128)(2,1)S(1)}, u32[]{:S(2)}, u32[]{:S(2)}) collective-permute-start(bf16[64,1152]{1,0:T(8,128)(2,1)S(1)} %get-tuple-element.47), channel_id=1, source_target_pairs={{0,0},{1,1},{2,2},{3,3},{4,8},{5,9},{6,10},{7,11},{8,4},{9,5},{10,... | collective-permute-start | bytes 442376 | tf_op jit(solution)/shard_map/ppermute | solution.py:1158
  7.4 1.1 %collective-permute-start.1 = (bf16[64,1152]{1,0:T(8,128)(2,1)S(1)}, bf16[64,1152]{1,0:T(8,128)(2,1)S(1)}, u32[]{:S(2)}, u32[]{:S(2)}) collective-permute-start(bf16[64,1152]{1,0:T(8,128)(2,1)S(1)} %get-tuple-element.48), channel_id=1, source_target_pairs={{0,2},{1,3},{2,0},{3,1},{4,10},{5,11},{6,8},{7,9},{8,6},{9,7},{10,... | collective-permute-start | bytes 442376 | tf_op jit(solution)/shard_map/ppermute | solution.py:1158
  8.5 0.0 copy-start.1
  8.5 4.9 %adapter.1 = (bf16[16,2048]{1,0:T(8,128)(2,1)S(1)}, f32[16,512]{1,0:T(8,128)S(1)}, bf16[1024,3072]{1,0:T(8,128)(2,1)S(1)}, f32[10,1024]{1,0:T(8,128)S(1)}, bf16[3072,512]{1,0:T(8,128)(2,1)S(1)}) custom-call(f32[10,1024]{1,0:T(8,128)} %h_embed.1, f32[1024,512]{1,0:T(8,128)} %w_mlp1.1, f32[1,512]{1,0:T(1,128)} %bitcast.43, f32[512,2048]{1,0:T(8,128)} %w_mlp2.1, ...), custom_call_target="tpu_custom_call" | custom-call | flops 4294967296 | bytes 6291456 | tf_op jit(solution)/shard_map/adapter/pallas_call | solution.py:541
  13.4 0.0 collective-permute-done.refs_0_.own_0
  13.4 0.6 collective-permute-done.1.refs_1_.own_1
  14.0 0.0 collective-permute-start.2
  14.0 0.5 collective-permute-start.3
  14.5 1.2 %collective-permute-start.4 = (bf16[64,1152]{1,0:T(8,128)(2,1)S(1)}, bf16[64,1152]{1,0:T(8,128)(2,1)S(1)}, u32[]{:S(2)}, u32[]{:S(2)}) collective-permute-start(bf16[64,1152]{1,0:T(8,128)(2,1)S(1)} %collective-permute-done.refs_0_.own_0), channel_id=1, source_target_pairs={{0,1},{1,0},{2,3},{3,2},{4,5},{5,4},{6,7},{7,6},{8,9},{9,8},{10,11... | collective-permute-start | bytes 442376 | tf_op jit(solution)/shard_map/ppermute | solution.py:1164
  15.7 0.2 collective-permute-start.5
  15.9 1.2 %split.3 = (bf16[64,1024]{1,0:T(8,128)(2,1)S(1)}, bf16[64,1024]{1,0:T(8,128)(2,1)S(1)}) custom-call(bf16[64,16,128]{2,1,0:T(8,128)(2,1)} %bitcast.37), custom_call_target="tpu_custom_call" | custom-call | flops 1048576 | bytes 524288 | tf_op jit(solution)/shard_map/split/pallas_call | solution.py:380
  17.1 0.0 collective-permute-done.2.refs_2_
  17.1 0.0 collective-permute-done.3.refs_3_
  17.1 6.1 %collective-permute-start.8 = (bf16[64,1024]{1,0:T(8,128)(2,1)S(1)}, bf16[64,1024]{1,0:T(8,128)(2,1)S(1)}, u32[]{:S(2)}, u32[]{:S(2)}) collective-permute-start(bf16[64,1024]{1,0:T(8,128)(2,1)S(1)} %get-tuple-element.60), channel_id=1, source_target_pairs={{0,0},{1,1},{2,2},{3,3},{4,8},{5,9},{6,10},{7,11},{8,4},{9,5},{10,... | collective-permute-start | bytes 393224 | tf_op jit(solution)/shard_map/ppermute | solution.py:1166
  23.2 0.1 collective-permute-start.9
  23.3 0.0 collective-permute-done.4.refs_0_
  23.3 0.1 collective-permute-start.6
  23.4 0.0 collective-permute-done.5.refs_1_
  23.4 0.5 collective-permute-start.7
  23.9 0.0 copy-done
  23.9 0.0 copy-done.1
  23.9 2.1 %project.2 = (bf16[256,3072]{1,0:T(8,128)(2,1)S(1)}, bf16[256,128]{1,0:T(8,128)(2,1)S(1)}) custom-call(bf16[64,1152]{1,0:T(8,128)(2,1)S(1)} %collective-permute-done.refs_0_.own_0, bf16[64,1152]{1,0:T(8,128)(2,1)S(1)} %collective-permute-done.1.refs_1_.own_1, bf16[64,1152]{1,0:T(8,128)(2,1)S(1)} %collective-permute-done.2.refs_2_, ...), custom_call_target="tpu_custom_call" | custom-call | flops 1610612736 | bytes 6291456 | tf_op jit(solution)/shard_map/project/pallas_call | solution.py:451
  26.1 0.0 copy-start.2
  26.1 0.0 copy-start.3
  26.1 0.0 collective-permute-done.6.refs_2_
  26.1 0.0 collective-permute-done.7.refs_3_
  26.1 2.1 %project.3 = (bf16[256,3072]{1,0:T(8,128)(2,1)S(1)}, bf16[256,128]{1,0:T(8,128)(2,1)S(1)}) custom-call(bf16[64,1152]{1,0:T(8,128)(2,1)S(1)} %collective-permute-done.4.refs_0_, bf16[64,1152]{1,0:T(8,128)(2,1)S(1)} %collective-permute-done.5.refs_1_, bf16[64,1152]{1,0:T(8,128)(2,1)S(1)} %collective-permute-done.6.refs_2_, ...), custom_call_target="tpu_custom_call" | custom-call | flops 1610612736 | bytes 6291456 | tf_op jit(solution)/shard_map/project/pallas_call | solution.py:451
  28.2 0.0 collective-permute-done.8.cot_0
  28.2 1.4 %collective-permute-done.9.cot_1 = bf16[64,1024]{1,0:T(8,128)(2,1)S(1)} collective-permute-done((bf16[64,1024]{1,0:T(8,128)(2,1)S(1)}, bf16[64,1024]{1,0:T(8,128)(2,1)S(1)}, u32[]{:S(2)}, u32[]{:S(2)}) %collective-permute-start.9) | collective-permute-done | bytes 131104 | tf_op jit(solution)/shard_map/ppermute | solution.py:1166
  29.6 0.0 copy-done.2
  29.6 0.0 copy-done.3
  29.6 14.0 %middle.1 = (bf16[96,1152]{1,0:T(8,128)(2,1)S(1)}, bf16[96,1152]{1,0:T(8,128)(2,1)S(1)}, bf16[128,1152]{1,0:T(8,128)(2,1)S(1)}, f32[128,1024]{1,0:T(8,128)S(1)}) custom-call(bf16[256,3072]{1,0:T(8,128)(2,1)S(1)} %get-tuple-element.53.qkv_a.queries, bf16[256,3072]{1,0:T(8,128)(2,1)S(1)} %get-tuple-element.54.qkv_b, ...), custom_call_target="tpu_custom_call" | custom-call | flops 2147483648 | bytes 1000 | tf_op jit(solution)/shard_map/middle/pallas_call | solution.py:858
  43.6 1.3 %collective-permute-start.16 = (bf16[128,1152]{1,0:T(8,128)(2,1)S(1)}, bf16[128,1152]{1,0:T(8,128)(2,1)S(1)}, u32[]{:S(2)}, u32[]{:S(2)}) collective-permute-start(bf16[128,1152]{1,0:T(8,128)(2,1)S(1)} %get-tuple-element.62.grads.grads_0), channel_id=1, source_target_pairs={{0,1},{1,0},{2,3},{3,2},{4,5},{5,4},{6,7},{7,6},{8,9},{9,8},{10,11... | collective-permute-start | bytes 884744 | tf_op jit(solution)/shard_map/ppermute | solution.py:1174
  44.9 1.4 %prefix.1.order.own = bf16[16,2048]{1,0:T(8,128)(2,1)S(1)} custom-call(bf16[256,3072]{1,0:T(8,128)(2,1)S(1)} %get-tuple-element.53.qkv_a.queries, bf16[128,1152]{1,0:T(8,128)(2,1)S(1)} %get-tuple-element.62.grads.grads_0, bf16[16,2048]{1,0:T(8,128)(2,1)S(1)} %get-tuple-element.57.prefix_kv), custom_call_target="tpu_custom_call" | custom-call | flops 1000 | bytes 1000 | tf_op jit(solution)/shard_map/prefix/pallas_call | solution.py:931
  46.4 1.2 %collective-permute-start.10 = (bf16[16,2048]{1,0:T(8,128)(2,1)S(1)}, bf16[16,2048]{1,0:T(8,128)(2,1)S(1)}, u32[]{:S(2)}, u32[]{:S(2)}) collective-permute-start(bf16[16,2048]{1,0:T(8,128)(2,1)S(1)} %prefix.1.order.own), channel_id=1, source_target_pairs={{0,16},{8,24},{16,0},{24,8},{1,17},{9,25},{17,1},{25,9},{2,18},{10... | collective-permute-start | bytes 196616 | tf_op jit(solution)/shard_map/ppermute | solution.py:1177
  47.6 0.0 collective-permute-start.11
  47.6 0.6 collective-permute-start.12
  48.2 3.5 %query.1.grad_partial = f32[128,1024]{1,0:T(8,128)S(1)} custom-call(bf16[256,3072]{1,0:T(8,128)(2,1)S(1)} %get-tuple-element.53.qkv_a.queries, bf16[256,3072]{1,0:T(8,128)(2,1)S(1)} %get-tuple-element.54.qkv_b, bf16[256,128]{1,0:T(8,128)(2,1)S(1)} %get-tuple-element.55.marks_a, bf16[256,128]{1,0:T(8,128)(2,1)S(1)} %get-tuple-element.56.marks_b, ...), custom_call_target="tpu_custom_call" | custom-call | flops 2147483648 | bytes 1000 | tf_op jit(solution)/shard_map/query/pallas_call | solution.py:1034
  51.7 0.1 collective-permute-start.15
  51.8 0.0 collective-permute-done.10.part_0
  51.8 0.0 collective-permute-done.11.part_1
  51.8 0.1 collective-permute-done.12.part_2
  51.9 0.0 collective-permute-done.16.grads_2
  52.0 0.5 collective-permute-start.17
  52.4 4.6 %collective-permute-start.13 = (bf16[96,1152]{1,0:T(8,128)(2,1)S(1)}, bf16[96,1152]{1,0:T(8,128)(2,1)S(1)}, u32[]{:S(2)}, u32[]{:S(2)}) collective-permute-start(bf16[96,1152]{1,0:T(8,128)(2,1)S(1)} %get-tuple-element.68), channel_id=1, source_target_pairs={{0,0},{1,1},{2,2},{3,3},{8,4},{9,5},{10,6},{11,7},{4,8},{5,9},{6,1... | collective-permute-start | bytes 663560 | tf_op jit(solution)/shard_map/ppermute | solution.py:1182
  57.0 1.2 %collective-permute-start.14 = (bf16[96,1152]{1,0:T(8,128)(2,1)S(1)}, bf16[96,1152]{1,0:T(8,128)(2,1)S(1)}, u32[]{:S(2)}, u32[]{:S(2)}) collective-permute-start(bf16[96,1152]{1,0:T(8,128)(2,1)S(1)} %get-tuple-element.69), channel_id=1, source_target_pairs={{2,0},{3,1},{0,2},{1,3},{10,4},{11,5},{8,6},{9,7},{6,8},{7,9},{4,1... | collective-permute-start | bytes 663560 | tf_op jit(solution)/shard_map/ppermute | solution.py:1182
  58.2 0.0 collective-permute-done.15.grads_1
  58.2 0.0 collective-permute-done.17.grads_3
  58.2 4.8 %final.1 = (bf16[64,1024]{1,0:T(8,128)(2,1)S(1)}, bf16[64,1024]{1,0:T(8,128)(2,1)S(1)}) custom-call(bf16[256,3072]{1,0:T(8,128)(2,1)S(1)} %get-tuple-element.53.qkv_a.queries, bf16[256,3072]{1,0:T(8,128)(2,1)S(1)} %get-tuple-element.54.qkv_b, bf16[256,128]{1,0:T(8,128)(2,1)S(1)} %get-tuple-element.55.marks_a, ...), custom_call_target="tpu_custom_call" | custom-call | flops 1000 | bytes 1000 | tf_op jit(solution)/shard_map/final/pallas_call | solution.py:1103
  63.0 2.7 %collective-permute-start.18 = (bf16[64,1024]{1,0:T(8,128)(2,1)S(1)}, bf16[64,1024]{1,0:T(8,128)(2,1)S(1)}, u32[]{:S(2)}, u32[]{:S(2)}) collective-permute-start(bf16[64,1024]{1,0:T(8,128)(2,1)S(1)} %get-tuple-element.72), channel_id=1, source_target_pairs={{0,0},{1,1},{2,2},{3,3},{8,4},{9,5},{10,6},{11,7},{4,8},{5,9},{6,1... | collective-permute-start | bytes 393224 | tf_op jit(solution)/shard_map/ppermute | solution.py:1196
  65.8 1.7 %collective-permute-start.19 = (bf16[64,1024]{1,0:T(8,128)(2,1)S(1)}, bf16[64,1024]{1,0:T(8,128)(2,1)S(1)}, u32[]{:S(2)}, u32[]{:S(2)}) collective-permute-start(bf16[64,1024]{1,0:T(8,128)(2,1)S(1)} %get-tuple-element.76), channel_id=1, source_target_pairs={{2,0},{3,1},{0,2},{1,3},{10,4},{11,5},{8,6},{9,7},{6,8},{7,9},{4,1... | collective-permute-start | bytes 393224 | tf_op jit(solution)/shard_map/ppermute | solution.py:1196
  67.5 0.0 collective-permute-done.13.msg_0.home_0
  67.5 0.0 collective-permute-done.14.msg_1.home_1
  67.5 0.1 collective-permute-start.20
  67.6 1.3 %collective-permute-start.21 = (bf16[16,2048]{1,0:T(8,128)(2,1)S(1)}, bf16[16,2048]{1,0:T(8,128)(2,1)S(1)}, u32[]{:S(2)}, u32[]{:S(2)}) collective-permute-start(bf16[16,2048]{1,0:T(8,128)(2,1)S(1)} %unpack.1.part_0), channel_id=1, source_target_pairs={{0,1},{1,0},{2,3},{3,2},{4,5},{5,4},{6,7},{7,6},{8,9},{9,8},{10,11... | collective-permute-start | bytes 196616 | tf_op jit(solution)/shard_map/ppermute | solution.py:1198
  68.9 0.8 %collective-permute-start.22 = (bf16[16,2048]{1,0:T(8,128)(2,1)S(1)}, bf16[16,2048]{1,0:T(8,128)(2,1)S(1)}, u32[]{:S(2)}, u32[]{:S(2)}) collective-permute-start(bf16[16,2048]{1,0:T(8,128)(2,1)S(1)} %unpack.1.part_0), channel_id=1, source_target_pairs={{0,9},{1,8},{2,11},{3,10},{4,13},{5,12},{6,15},{7,14},{8,1},{9,0},... | collective-permute-start | bytes 196616 | tf_op jit(solution)/shard_map/ppermute | solution.py:1199
  69.7 1.1 %land.1 = (bf16[64,16,128]{2,1,0:T(8,128)(2,1)}, f32[2,16,64]{2,1,0:T(8,128)}) custom-call(bf16[96,1152]{1,0:T(8,128)(2,1)S(1)} %collective-permute-done.13.msg_0.home_0, bf16[96,1152]{1,0:T(8,128)(2,1)S(1)} %collective-permute-done.14.msg_1.home_1), custom_call_target="tpu_custom_call" | custom-call | flops 1000 | bytes 1000 | tf_op jit(solution)/shard_map/land/pallas_call | solution.py:418
  70.8 0.0 collective-permute-done.20.part_1
  70.8 0.0 collective-permute-done.21.part_2
  70.8 2.8 %collective-permute-done.22.part_3 = bf16[16,2048]{1,0:T(8,128)(2,1)S(1)} collective-permute-done((bf16[16,2048]{1,0:T(8,128)(2,1)S(1)}, bf16[16,2048]{1,0:T(8,128)(2,1)S(1)}, u32[]{:S(2)}, u32[]{:S(2)}) %collective-permute-start.22) | collective-permute-done | bytes 65568 | tf_op jit(solution)/shard_map/ppermute | solution.py:1199
  73.5 0.0 collective-permute-done.18.home_0
  73.5 0.0 collective-permute-done.19.home_1
  73.5 4.0 %finish.1 = (f32[1024,128]{1,0:T(8,128)}, f32[10,1024]{1,0:T(8,128)}, f32[1024,512]{1,0:T(8,128)}, f32[1,512]{1,0:T(1,128)}, f32[512,2048]{1,0:T(8,128)}, /*index=5*/f32[1,2048]{1,0:T(1,128)}) custom-call(bf16[64,1024]{1,0:T(8,128)(2,1)S(1)} %collective-permute-done.18.home_0, bf16[64,1024]{1,0:T(8,128)(2,1)S(1)} %collective-permute-done.19.home_1, ...), custom_call_target="tpu_custom_call" | custom-call | flops 1000 | bytes 1000 | tf_op jit(solution)/shard_map/finish/pallas_call | solution.py:637
  (3 shorter events, 0.1 us)
Async XLA Ops:
  1.8 11.6 %collective-permute-start = (bf16[64,1152]{1,0:T(8,128)(2,1)S(1)}, bf16[64,1152]{1,0:T(8,128)(2,1)S(1)}, u32[]{:S(2)}, u32[]{:S(2)}) collective-permute-start(bf16[64,1152]{1,0:T(8,128)(2,1)S(1)} %get-tuple-element.47), channel_id=1, source_target_pairs={{0,0},{1,1},{2,2},{3,3},{4,8},{5,9},{6,10},{7,11},{8,4},{9,5},{10,... | collective-permute-start | bytes 442376 | tf_op jit(solution)/shard_map/ppermute | solution.py:1158
  7.4 6.5 %collective-permute-start.1 = (bf16[64,1152]{1,0:T(8,128)(2,1)S(1)}, bf16[64,1152]{1,0:T(8,128)(2,1)S(1)}, u32[]{:S(2)}, u32[]{:S(2)}) collective-permute-start(bf16[64,1152]{1,0:T(8,128)(2,1)S(1)} %get-tuple-element.48), channel_id=1, source_target_pairs={{0,2},{1,3},{2,0},{3,1},{4,10},{5,11},{6,8},{7,9},{8,6},{9,7},{10,... | collective-permute-start | bytes 442376 | tf_op jit(solution)/shard_map/ppermute | solution.py:1158
  8.5 15.4 %copy-start = (f32[1024]{0:T(1024)S(1)}, f32[1024]{0:T(1024)}, u32[]{:S(2)}) copy-start(f32[1024]{0:T(1024)} %param.18) | copy-start | bytes 12292
  8.5 15.4 %copy-start.1 = (f32[1024]{0:T(1024)S(1)}, f32[1024]{0:T(1024)}, u32[]{:S(2)}) copy-start(f32[1024]{0:T(1024)} %param.19) | copy-start | bytes 12292
  14.0 3.1 %collective-permute-start.2 = (bf16[64,1152]{1,0:T(8,128)(2,1)S(1)}, bf16[64,1152]{1,0:T(8,128)(2,1)S(1)}, u32[]{:S(2)}, u32[]{:S(2)}) collective-permute-start(bf16[64,1152]{1,0:T(8,128)(2,1)S(1)} %collective-permute-done.refs_0_.own_0), channel_id=1, source_target_pairs={{0,8},{8,0},{16,24},{24,16},{1,9},{9,1},{17,25},{25,17},{2,10},{10... | collective-permute-start | bytes 442376 | tf_op jit(solution)/shard_map/ppermute | solution.py:1165
  14.0 3.2 %collective-permute-start.3 = (bf16[64,1152]{1,0:T(8,128)(2,1)S(1)}, bf16[64,1152]{1,0:T(8,128)(2,1)S(1)}, u32[]{:S(2)}, u32[]{:S(2)}) collective-permute-start(bf16[64,1152]{1,0:T(8,128)(2,1)S(1)} %collective-permute-done.1.refs_1_.own_1), channel_id=1, source_target_pairs={{0,8},{8,0},{16,24},{24,16},{1,9},{9,1},{17,25},{25,17},{2,10},{10... | collective-permute-start | bytes 442376 | tf_op jit(solution)/shard_map/ppermute | solution.py:1165
  14.5 8.9 %collective-permute-start.4 = (bf16[64,1152]{1,0:T(8,128)(2,1)S(1)}, bf16[64,1152]{1,0:T(8,128)(2,1)S(1)}, u32[]{:S(2)}, u32[]{:S(2)}) collective-permute-start(bf16[64,1152]{1,0:T(8,128)(2,1)S(1)} %collective-permute-done.refs_0_.own_0), channel_id=1, source_target_pairs={{0,1},{1,0},{2,3},{3,2},{4,5},{5,4},{6,7},{7,6},{8,9},{9,8},{10,11... | collective-permute-start | bytes 442376 | tf_op jit(solution)/shard_map/ppermute | solution.py:1164
  15.7 7.7 %collective-permute-start.5 = (bf16[64,1152]{1,0:T(8,128)(2,1)S(1)}, bf16[64,1152]{1,0:T(8,128)(2,1)S(1)}, u32[]{:S(2)}, u32[]{:S(2)}) collective-permute-start(bf16[64,1152]{1,0:T(8,128)(2,1)S(1)} %collective-permute-done.1.refs_1_.own_1), channel_id=1, source_target_pairs={{0,1},{1,0},{2,3},{3,2},{4,5},{5,4},{6,7},{7,6},{8,9},{9,8},{10,11... | collective-permute-start | bytes 442376 | tf_op jit(solution)/shard_map/ppermute | solution.py:1164
  17.1 11.1 %collective-permute-start.8 = (bf16[64,1024]{1,0:T(8,128)(2,1)S(1)}, bf16[64,1024]{1,0:T(8,128)(2,1)S(1)}, u32[]{:S(2)}, u32[]{:S(2)}) collective-permute-start(bf16[64,1024]{1,0:T(8,128)(2,1)S(1)} %get-tuple-element.60), channel_id=1, source_target_pairs={{0,0},{1,1},{2,2},{3,3},{4,8},{5,9},{6,10},{7,11},{8,4},{9,5},{10,... | collective-permute-start | bytes 393224 | tf_op jit(solution)/shard_map/ppermute | solution.py:1166
  23.2 6.4 %collective-permute-start.9 = (bf16[64,1024]{1,0:T(8,128)(2,1)S(1)}, bf16[64,1024]{1,0:T(8,128)(2,1)S(1)}, u32[]{:S(2)}, u32[]{:S(2)}) collective-permute-start(bf16[64,1024]{1,0:T(8,128)(2,1)S(1)} %get-tuple-element.61), channel_id=1, source_target_pairs={{0,2},{1,3},{2,0},{3,1},{4,10},{5,11},{6,8},{7,9},{8,6},{9,7},{10,... | collective-permute-start | bytes 393224 | tf_op jit(solution)/shard_map/ppermute | solution.py:1166
  23.3 2.7 %collective-permute-start.6 = (bf16[64,1152]{1,0:T(8,128)(2,1)S(1)}, bf16[64,1152]{1,0:T(8,128)(2,1)S(1)}, u32[]{:S(2)}, u32[]{:S(2)}) collective-permute-start(bf16[64,1152]{1,0:T(8,128)(2,1)S(1)} %collective-permute-done.4.refs_0_), channel_id=1, source_target_pairs={{0,8},{8,0},{16,24},{24,16},{1,9},{9,1},{17,25},{25,17},{2,10},{10... | collective-permute-start | bytes 442376 | tf_op jit(solution)/shard_map/ppermute | solution.py:1167
  23.4 2.7 %collective-permute-start.7 = (bf16[64,1152]{1,0:T(8,128)(2,1)S(1)}, bf16[64,1152]{1,0:T(8,128)(2,1)S(1)}, u32[]{:S(2)}, u32[]{:S(2)}) collective-permute-start(bf16[64,1152]{1,0:T(8,128)(2,1)S(1)} %collective-permute-done.5.refs_1_), channel_id=1, source_target_pairs={{0,8},{8,0},{16,24},{24,16},{1,9},{9,1},{17,25},{25,17},{2,10},{10... | collective-permute-start | bytes 442376 | tf_op jit(solution)/shard_map/ppermute | solution.py:1167
  26.1 3.6 %copy-start.2 = (f32[1024]{0:T(1024)S(1)}, f32[1024]{0:T(1024)}, u32[]{:S(2)}) copy-start(f32[1024]{0:T(1024)} %param.22) | copy-start | bytes 12292
  26.1 3.6 %copy-start.3 = (f32[1024]{0:T(1024)S(1)}, f32[1024]{0:T(1024)}, u32[]{:S(2)}) copy-start(f32[1024]{0:T(1024)} %param.23) | copy-start | bytes 12292
  43.6 8.3 %collective-permute-start.16 = (bf16[128,1152]{1,0:T(8,128)(2,1)S(1)}, bf16[128,1152]{1,0:T(8,128)(2,1)S(1)}, u32[]{:S(2)}, u32[]{:S(2)}) collective-permute-start(bf16[128,1152]{1,0:T(8,128)(2,1)S(1)} %get-tuple-element.62.grads.grads_0), channel_id=1, source_target_pairs={{0,1},{1,0},{2,3},{3,2},{4,5},{5,4},{6,7},{7,6},{8,9},{9,8},{10,11... | collective-permute-start | bytes 884744 | tf_op jit(solution)/shard_map/ppermute | solution.py:1174
  46.4 5.4 %collective-permute-start.10 = (bf16[16,2048]{1,0:T(8,128)(2,1)S(1)}, bf16[16,2048]{1,0:T(8,128)(2,1)S(1)}, u32[]{:S(2)}, u32[]{:S(2)}) collective-permute-start(bf16[16,2048]{1,0:T(8,128)(2,1)S(1)} %prefix.1.order.own), channel_id=1, source_target_pairs={{0,16},{8,24},{16,0},{24,8},{1,17},{9,25},{17,1},{25,9},{2,18},{10... | collective-permute-start | bytes 196616 | tf_op jit(solution)/shard_map/ppermute | solution.py:1177
  47.6 4.2 %collective-permute-start.11 = (bf16[16,2048]{1,0:T(8,128)(2,1)S(1)}, bf16[16,2048]{1,0:T(8,128)(2,1)S(1)}, u32[]{:S(2)}, u32[]{:S(2)}) collective-permute-start(bf16[16,2048]{1,0:T(8,128)(2,1)S(1)} %prefix.1.order.own), channel_id=1, source_target_pairs={{0,8},{8,0},{16,24},{24,16},{1,9},{9,1},{17,25},{25,17},{2,10},{10... | collective-permute-start | bytes 196616 | tf_op jit(solution)/shard_map/ppermute | solution.py:1177
  47.6 4.3 %collective-permute-start.12 = (bf16[16,2048]{1,0:T(8,128)(2,1)S(1)}, bf16[16,2048]{1,0:T(8,128)(2,1)S(1)}, u32[]{:S(2)}, u32[]{:S(2)}) collective-permute-start(bf16[16,2048]{1,0:T(8,128)(2,1)S(1)} %prefix.1.order.own), channel_id=1, source_target_pairs={{0,24},{8,16},{16,8},{24,0},{1,25},{9,17},{17,9},{25,1},{2,26},{10... | collective-permute-start | bytes 196616 | tf_op jit(solution)/shard_map/ppermute | solution.py:1177
  51.7 6.5 %collective-permute-start.15 = (bf16[128,1152]{1,0:T(8,128)(2,1)S(1)}, bf16[128,1152]{1,0:T(8,128)(2,1)S(1)}, u32[]{:S(2)}, u32[]{:S(2)}) collective-permute-start(bf16[128,1152]{1,0:T(8,128)(2,1)S(1)} %get-tuple-element.62.grads.grads_0), channel_id=1, source_target_pairs={{0,8},{8,0},{16,24},{24,16},{1,9},{9,1},{17,25},{25,17},{2,10},{10... | collective-permute-start | bytes 884744 | tf_op jit(solution)/shard_map/ppermute | solution.py:1175
  52.0 6.3 %collective-permute-start.17 = (bf16[128,1152]{1,0:T(8,128)(2,1)S(1)}, bf16[128,1152]{1,0:T(8,128)(2,1)S(1)}, u32[]{:S(2)}, u32[]{:S(2)}) collective-permute-start(bf16[128,1152]{1,0:T(8,128)(2,1)S(1)} %collective-permute-done.16.grads_2), channel_id=1, source_target_pairs={{0,8},{8,0},{16,24},{24,16},{1,9},{9,1},{17,25},{25,17},{2,10},{10... | collective-permute-start | bytes 884744 | tf_op jit(solution)/shard_map/ppermute | solution.py:1183
  52.4 15.0 %collective-permute-start.13 = (bf16[96,1152]{1,0:T(8,128)(2,1)S(1)}, bf16[96,1152]{1,0:T(8,128)(2,1)S(1)}, u32[]{:S(2)}, u32[]{:S(2)}) collective-permute-start(bf16[96,1152]{1,0:T(8,128)(2,1)S(1)} %get-tuple-element.68), channel_id=1, source_target_pairs={{0,0},{1,1},{2,2},{3,3},{8,4},{9,5},{10,6},{11,7},{4,8},{5,9},{6,1... | collective-permute-start | bytes 663560 | tf_op jit(solution)/shard_map/ppermute | solution.py:1182
  57.0 10.4 %collective-permute-start.14 = (bf16[96,1152]{1,0:T(8,128)(2,1)S(1)}, bf16[96,1152]{1,0:T(8,128)(2,1)S(1)}, u32[]{:S(2)}, u32[]{:S(2)}) collective-permute-start(bf16[96,1152]{1,0:T(8,128)(2,1)S(1)} %get-tuple-element.69), channel_id=1, source_target_pairs={{2,0},{3,1},{0,2},{1,3},{10,4},{11,5},{8,6},{9,7},{6,8},{7,9},{4,1... | collective-permute-start | bytes 663560 | tf_op jit(solution)/shard_map/ppermute | solution.py:1182
  63.0 10.5 %collective-permute-start.18 = (bf16[64,1024]{1,0:T(8,128)(2,1)S(1)}, bf16[64,1024]{1,0:T(8,128)(2,1)S(1)}, u32[]{:S(2)}, u32[]{:S(2)}) collective-permute-start(bf16[64,1024]{1,0:T(8,128)(2,1)S(1)} %get-tuple-element.72), channel_id=1, source_target_pairs={{0,0},{1,1},{2,2},{3,3},{8,4},{9,5},{10,6},{11,7},{4,8},{5,9},{6,1... | collective-permute-start | bytes 393224 | tf_op jit(solution)/shard_map/ppermute | solution.py:1196
  65.8 7.8 %collective-permute-start.19 = (bf16[64,1024]{1,0:T(8,128)(2,1)S(1)}, bf16[64,1024]{1,0:T(8,128)(2,1)S(1)}, u32[]{:S(2)}, u32[]{:S(2)}) collective-permute-start(bf16[64,1024]{1,0:T(8,128)(2,1)S(1)} %get-tuple-element.76), channel_id=1, source_target_pairs={{2,0},{3,1},{0,2},{1,3},{10,4},{11,5},{8,6},{9,7},{6,8},{7,9},{4,1... | collective-permute-start | bytes 393224 | tf_op jit(solution)/shard_map/ppermute | solution.py:1196
  67.5 3.3 %collective-permute-start.20 = (bf16[16,2048]{1,0:T(8,128)(2,1)S(1)}, bf16[16,2048]{1,0:T(8,128)(2,1)S(1)}, u32[]{:S(2)}, u32[]{:S(2)}) collective-permute-start(bf16[16,2048]{1,0:T(8,128)(2,1)S(1)} %unpack.1.part_0), channel_id=1, source_target_pairs={{0,8},{8,0},{16,24},{24,16},{1,9},{9,1},{17,25},{25,17},{2,10},{10... | collective-permute-start | bytes 196616 | tf_op jit(solution)/shard_map/ppermute | solution.py:1198
  67.6 3.2 %collective-permute-start.21 = (bf16[16,2048]{1,0:T(8,128)(2,1)S(1)}, bf16[16,2048]{1,0:T(8,128)(2,1)S(1)}, u32[]{:S(2)}, u32[]{:S(2)}) collective-permute-start(bf16[16,2048]{1,0:T(8,128)(2,1)S(1)} %unpack.1.part_0), channel_id=1, source_target_pairs={{0,1},{1,0},{2,3},{3,2},{4,5},{5,4},{6,7},{7,6},{8,9},{9,8},{10,11... | collective-permute-start | bytes 196616 | tf_op jit(solution)/shard_map/ppermute | solution.py:1198
  68.9 4.7 %collective-permute-start.22 = (bf16[16,2048]{1,0:T(8,128)(2,1)S(1)}, bf16[16,2048]{1,0:T(8,128)(2,1)S(1)}, u32[]{:S(2)}, u32[]{:S(2)}) collective-permute-start(bf16[16,2048]{1,0:T(8,128)(2,1)S(1)} %unpack.1.part_0), channel_id=1, source_target_pairs={{0,9},{1,8},{2,11},{3,10},{4,13},{5,12},{6,15},{7,14},{8,1},{9,0},... | collective-permute-start | bytes 196616 | tf_op jit(solution)/shard_map/ppermute | solution.py:1199

commit v6 on v5

--- a/solution.py
+++ b/solution.py
@@ -390,8 +390,7 @@
 
 
 def place_rows(msg_0, msg_1, work):
-    width = msg_0.shape[1] // LANES * LANES
-    count = 2 * (width // LANES)
+    count = 2 * msg_0.shape[1] // LANES
     half = work.shape[0] // count
     odd = odd_place()
     for i in range(count // 2):
@@ -401,22 +400,26 @@
         work[pl.ds(2 * i + 1, half, stride=count)] = jnp.where(odd, one, two)
 
 
-def land_kernel(msg_0, msg_1, out, logs, work):
-    half, count, _ = out.shape
-    heads, width = logs.shape[1], count // 2 * LANES
-    place_rows(msg_0.at[:, pl.ds(0, width)], msg_1.at[:, pl.ds(0, width)], work)
+def land_kernel(first_row, msg_0, msg_1, out, logs, work):
+    half = out.shape[0]
+    heads = logs.shape[1]
+    place_rows(msg_0, msg_1, work)
     out[...] = work[...].reshape(out.shape).astype(out.dtype)
     odd = odd_place()
-    one, two = (m[:half, width:].astype(F32) for m in (msg_0, msg_1))
-    for r, chosen in enumerate((jnp.where(odd, two, one), jnp.where(odd, one, two))):
-        summed = chosen + jnp.roll(chosen, -heads, 1) + jnp.roll(chosen, -2 * heads, 1)
-        logs[r] = summed.T[:heads]
-
-
-def land(messages, half, width):
+    found = []
+    for k, message in enumerate((msg_0, msg_1)):
+        rows = message[half:].astype(F32)[first_row : first_row + GROUP]
+        slots = [rows[:, i * LANES + k * half : i * LANES + (k + 1) * half] for i in range(3 * heads // GROUP)]
+        groups = [slots[i] + slots[i + 1] + slots[i + 2] for i in range(0, len(slots), 3)]
+        found.append(jnp.concatenate(groups, 0))
+    logs[0] = jnp.where(odd, found[1], found[0])
+    logs[1] = jnp.where(odd, found[0], found[1])
+
+
+def land(count_prefix, messages, half, width):
     count = 2 * width // LANES
     out = pl.pallas_call(
-        land_kernel,
+        partial(land_kernel, prefix_rows(count_prefix)),
         in_specs=[vmem()] * 2,
         out_specs=[vmem()] * 2,
         out_shape=[
@@ -471,6 +474,8 @@
 
 
 def pad_rows(value_in, rows):
+    if rows == value_in.shape[0]:
+        return value_in
     return jnp.concatenate(
         [value_in, jnp.zeros((rows - value_in.shape[0], value_in.shape[1]), value_in.dtype)], 0
     )
@@ -494,6 +499,7 @@
     out,
     inner,
     v_qkv,
+    w_back,
     embed,
     turned,
     v_mlp1,
@@ -509,13 +515,19 @@
     ):
         small.append(pltpu.make_async_copy(source, target, sems.at[steps + i]))
         small[-1].start()
+    width = w_qkv.shape[0]
+    weights = []
+    for i in range(3):
+        at = pl.ds(i * width, width)
+        weights.append(
+            pltpu.make_async_copy(w_qkv.at[:, at], v_qkv.at[:, at], sems.at[steps + len(small) + i])
+        )
+        weights[-1].start()
     rest = []
     for i in range(steps):
         copy = pltpu.make_async_copy(w_mlp2.at[:, pl.ds(i * step, step)], v_mlp2.at[i], sems.at[i])
         copy.start()
         rest.append(copy)
-    weights = pltpu.make_async_copy(w_qkv, v_qkv, sems.at[steps + len(small)])
-    weights.start()
     for copy in small:
         copy.wait()
     source = pad_rows(embed[...], PRE_ROWS)
@@ -525,13 +537,16 @@
     for i in range(v_mlp1.shape[0] // hidden):
         part = v_mlp1[pl.ds(i * hidden, hidden)].astype(BF16)
         turned[pl.ds(columns + i * hidden, hidden)] = part.T
+    for i, copy in enumerate(weights):
+        at = pl.ds(i * width, width)
+        copy.wait()
+        w_back[at] = v_qkv[:, at].T
     for i, copy in enumerate(rest):
         copy.wait()
         turned[pl.ds(i * step, step)] = v_mlp2[i].astype(BF16).T
         span = pl.ds(i * step, step)
         part = three_products(nn, act, v_mlp2[i]) + b_mlp2[:, span]
         out[:, span] = jnp.where(iota(part.shape, 0) < embed.shape[0], part, 0.0).astype(BF16)
-    weights.wait()
 
 
 def adapter_forward(embed, w_mlp1, b_mlp1, w_mlp2, b_mlp2, w_qkv):
@@ -541,11 +556,12 @@
     return pl.pallas_call(
         adapter_kernel,
         in_specs=[hbm()] * 6,
-        out_specs=[vmem()] * 5,
+        out_specs=[vmem()] * 6,
         out_shape=[
             jax.ShapeDtypeStruct((PRE_ROWS, columns), BF16),
             jax.ShapeDtypeStruct((PRE_ROWS, hidden), F32),
             pltpu.VMEM(w_qkv.shape, w_qkv.dtype),
+            pltpu.VMEM(w_qkv.shape[::-1], w_qkv.dtype),
             pltpu.VMEM(embed.shape, F32),
             pltpu.VMEM((columns + width, hidden), BF16),
         ],
@@ -554,7 +570,7 @@
             pltpu.VMEM((steps, hidden, columns // steps), F32),
             pltpu.VMEM((1, hidden), F32),
             pltpu.VMEM((1, columns), F32),
-            pltpu.SemaphoreType.DMA((5 + steps,)),
+            pltpu.SemaphoreType.DMA((7 + steps,)),
         ],
         compiler_params=pltpu.CompilerParams(vmem_limit_bytes=20 * MIB),
         cost_estimate=pl.CostEstimate(flops=1 << 32, bytes_accessed=6 * MIB, transcendentals=1 << 13),
@@ -816,8 +832,8 @@
     lax.fori_loop(0, steps, feed, 0, unroll=True)
 
     out = total[...].astype(BF16)
-    back_0[:half, :width] = out[:half]
-    back_1[:half, :width] = out[half:]
+    back_0[:half] = out[:half]
+    back_1[:half] = out[half:]
     unit, inverse = norm_parts(middle[...])
     grads = cot[...].astype(F32) + norm_back(unit, inverse, gain[...], grad_norm[...])
     grad_middle[...] = grads
@@ -835,17 +851,13 @@
         0.0,
     ).astype(BF16)
     bases = jnp.zeros((rows, LANES), F32)
-    for _ in range(3):
+    for _ in range(2):
         part = product.astype(BF16)
         bases = bases + nn(part, ones)
         product = product - part.astype(F32)
     marks = three_parts(stats[...], 0) + three_parts(bases, 3 * HEADS)
     marks = marks.astype(BF16)
     grad_out_heads[:, width:] = marks
-    back_0[:half, width:] = marks[:half]
-    back_1[:half, width:] = marks[half:]
-    back_0[half:] = jnp.zeros_like(back_0[half:])
-    back_1[half:] = jnp.zeros_like(back_1[half:])
 
 
 def middle_part(count, qkv_a, qkv_b, marks_a, marks_b, prefix_kv, own, cots, gain, bias, w_out, w_fc, w_proj):
@@ -860,8 +872,8 @@
         in_specs=[vmem()] * 11 + [hbm()] * 3,
         out_specs=[vmem()] * 4,
         out_shape=[
-            jax.ShapeDtypeStruct((half + tail_rows(count), wide), BF16),
-            jax.ShapeDtypeStruct((half + tail_rows(count), wide), BF16),
+            jax.ShapeDtypeStruct((half + tail_rows(count), width), BF16),
+            jax.ShapeDtypeStruct((half + tail_rows(count), width), BF16),
             jax.ShapeDtypeStruct((rows, wide), BF16),
             jax.ShapeDtypeStruct((rows, width), F32),
         ],
@@ -887,30 +899,37 @@
     )
 
 
-def key_grads(keys, values, queries, grads, marks, pair, low, mask):
+def key_grads(keys, values, queries, grads, turned_marks, pair, low, mask):
     rows = keys.shape[0]
     scale = jnp.asarray(HEAD**-0.5, BF16)
     left = jnp.concatenate(
         [two_heads(keys * scale, low), picks(rows, pair, 0, -1.0).astype(BF16)], 1
     )
-    scores = nt(left, jnp.concatenate([queries, marks], 1))
+    scores = nn(left, jnp.concatenate([queries.T, turned_marks], 0))
     weights = jnp.exp(scores + jnp.concatenate([mask, mask], 0))
     left = jnp.concatenate(
         [two_heads(values, low), picks(rows, pair, 3 * HEADS, -1.0).astype(BF16)], 1
     )
-    slopes = weights * nt(left, jnp.concatenate([grads, marks], 1))
+    slopes = weights * nn(left, jnp.concatenate([grads.T, turned_marks], 0))
     key_grad = nn(slopes.astype(BF16), queries)
     value_grad = nn(weights.astype(BF16), grads)
     return join_heads(key_grad, low) * HEAD**-0.5, join_heads(value_grad, low)
 
 
+GROUP = 8
+
+
+def prefix_rows(count):
+    return -(-2 * count // GROUP) * GROUP
+
+
 def tail_rows(count):
-    return -(-2 * count // PRE_ROWS) * PRE_ROWS
+    return -(-(prefix_rows(count) + GROUP) // PRE_ROWS) * PRE_ROWS
 
 
 def prefix_kernel(used, queries, grads, prefix_kv, out):
     count, rows, width = prefix_kv.shape[0], grads.shape[0], grads.shape[1] - LANES
-    marks = grads[:, width:]
+    marks = grads[:, width:].T
     low = head_mask(count)
     mask = jnp.where(iota((count, rows), 0) < used, 0.0, NEG)
 
@@ -939,35 +958,40 @@
     )(qkv_a, grads, prefix_kv)
 
 
-def pack_kernel(count, own, part_0, part_1, part_2, _0, _1, back_0, back_1):
+def pack_kernel(count, grads, own, part_0, part_1, part_2, _0, _1, back_0, back_1):
     total = own[...].astype(F32) + part_0[...].astype(F32)
     total = total + (part_1[...].astype(F32) + part_2[...].astype(F32))
     width = total.shape[1] // 2
     rows = tail_rows(count)
-    tail = pad_rows(jnp.concatenate([total[:count, :width], total[:count, width:]], 0), rows).astype(BF16)
+    both = jnp.concatenate([total[:count, :width], total[:count, width:]], 0)
+    marks = grads[:, width:].astype(F32).T
+    starts = [part * HEADS + first for first in range(0, HEADS, GROUP) for part in range(3)]
+    logs = jnp.concatenate([marks[i : i + GROUP] for i in starts], 1)
+    logs = jnp.concatenate([logs, jnp.zeros((GROUP, width - logs.shape[1]), F32)], 1)
+    tail = pad_rows(jnp.concatenate([pad_rows(both, prefix_rows(count)), logs], 0), rows).astype(BF16)
     at = pl.ds(back_0.shape[0] - rows, rows)
-    back_0[at, :width] = tail
-    back_1[at, :width] = tail
-
-
-def pack(count, terms, back_0, back_1):
+    back_0[at] = tail
+    back_1[at] = tail
+
+
+def pack(count, grads, terms, back_0, back_1):
     return pl.pallas_call(
         partial(pack_kernel, count),
-        in_specs=[vmem()] * 6,
+        in_specs=[vmem()] * 7,
         out_specs=[vmem()] * 2,
         out_shape=[jax.ShapeDtypeStruct(back_0.shape, BF16)] * 2,
-        input_output_aliases={4: 0, 5: 1},
+        input_output_aliases={5: 0, 6: 1},
         compiler_params=pltpu.CompilerParams(vmem_limit_bytes=4 * MIB),
         cost_estimate=pl.CostEstimate(flops=1 << 20, bytes_accessed=1 << 19, transcendentals=0),
         name="pack",
-    )(*terms, back_0, back_1)
+    )(grads, *terms, back_0, back_1)
 
 
 def unpack_kernel(count, home_0, home_1, out):
     width = out.shape[1] // 2
     rows = tail_rows(count)
     at = pl.ds(home_0.shape[0] - rows, rows)
-    first, second = home_0[at, :width].astype(F32), home_1[at, :width].astype(F32)
+    first, second = home_0[at].astype(F32), home_1[at].astype(F32)
     total = first + second
     out[:, :width] = pad_rows(total[:count], PRE_ROWS).astype(BF16)
     out[:, width:] = pad_rows(total[count : 2 * count], PRE_ROWS).astype(BF16)
@@ -1005,7 +1029,7 @@
     low = head_mask(rows)
     marks = grads[:, width:]
     marks_twice = jnp.concatenate([marks, marks], 0)
-    ones = jnp.ones((4 * rows + LANES, LANES), BF16)
+    ones = jnp.ones((LANES, 4 * rows + LANES), BF16)
 
     def step(pair, carry):
         at = pl.ds(pl.multiple_of(pair * LANES, LANES), LANES)
@@ -1015,18 +1039,18 @@
         values = with_prefix(qkv_a[:, at_v], qkv_b[:, at_v], prefix_kv[:, at_k])
         query = two_heads(qkv_a[:rows, at] * jnp.asarray(HEAD**-0.5, BF16), low)
         tops = marks_twice * picks(rows, pair, 0, -1.0).astype(BF16)
-        scores = nt(jnp.concatenate([query, tops], 1), jnp.concatenate([keys, ones], 1))
+        scores = nn(jnp.concatenate([query, tops], 1), jnp.concatenate([keys.T, ones], 0))
         mask = scores_bias[...]
         weights = jnp.exp(scores + jnp.concatenate([mask, mask], 0))
         bases = marks_twice * picks(rows, pair, 3 * HEADS, -1.0).astype(BF16)
         left = jnp.concatenate([two_heads(grads[:, at], low), bases], 1)
-        slopes = weights * nt(left, jnp.concatenate([values, ones], 1))
+        slopes = weights * nn(left, jnp.concatenate([values.T, ones], 0))
         grad = join_heads(nn(slopes.astype(BF16), keys), low)
         grad_query[:, at] = (grad * HEAD**-0.5).astype(BF16)
         return carry
 
     lax.fori_loop(0, HEADS // 2, step, 0, unroll=True)
-    out[...] = nt(grad_query[...], weight[:, :width])
+    out[...] = nn(grad_query[...], weight[:width])
 
 
 def query_part(count, qkv_a, qkv_b, marks_a, marks_b, prefix_kv, grads, weight, order):
@@ -1073,7 +1097,7 @@
     scores_bias[...] = jnp.where(visible, 0.0, NEG)
     low = head_mask(rows)
     blocks = (grads_0, grads_1, grads_2, grads_3)
-    marks = jnp.concatenate([g[:, width:] for g in blocks], 0)
+    marks = jnp.concatenate([g[:, width:] for g in blocks], 0).T
 
     def step(pair, carry):
         at = pl.ds(pl.multiple_of(pair * LANES, LANES), LANES)
@@ -1089,7 +1113,7 @@
         return carry
 
     lax.fori_loop(0, HEADS // 2, step, 0, unroll=True)
-    grad_norm = grad_partial[...] + nt(grad_keys[...], weight[:, width:])
+    grad_norm = grad_partial[...] + nn(grad_keys[...], weight[width:])
     inputs = jnp.concatenate([own_0[:, :width], own_1[:, :width]], 0).astype(F32)
     unit, inverse = norm_parts(inputs)
     out = (grad_middle[...] + norm_back(unit, inverse, gain[...], grad_norm)).astype(BF16)
@@ -1109,7 +1133,7 @@
             pltpu.VMEM((rows, 4 * rows), F32),
             pltpu.VMEM((rows, 2 * width), BF16),
         ],
-        compiler_params=pltpu.CompilerParams(vmem_limit_bytes=30 * MIB),
+        compiler_params=pltpu.CompilerParams(vmem_limit_bytes=16 * MIB),
         cost_estimate=pl.CostEstimate(flops=1000, bytes_accessed=1000, transcendentals=0),
         name="final",
     )(qkv_a, qkv_b, marks_a, marks_b, *grads, *own, gain[None], grad_middle, grad_partial, weight)
@@ -1156,7 +1180,7 @@
     out_msgs = split_rows(tokens, segment_ids)
     cot_msgs = split_rows(cotangent)
     own = [lax.ppermute(m, everyone, there[k]) for k, m in enumerate(out_msgs)]
-    prefix_kv, inner, w_near, near_embed, turned = adapter_forward(
+    prefix_kv, inner, w_near, w_back, near_embed, turned = adapter_forward(
         prefix_embed, w_mlp1, b_mlp1, w_mlp2, b_mlp2, w_qkv
     )
     count = prefix_embed.shape[0]
@@ -1176,9 +1200,9 @@
     grad_prefix_kv = prefix_part(count, qkv_a, grads, prefix_kv)
     parts = [lax.ppermute(grad_prefix_kv, "seq", [(i, i ^ far) for i in range(4)]) for far in (2, 1, 3)]
     grad_partial = query_part(
-        count, qkv_a, qkv_b, marks_a, marks_b, prefix_kv, grads, w_near, grad_prefix_kv
-    )
-    packed = pack(count, (grad_prefix_kv, *after(parts, grad_partial)), back_0, back_1)
+        count, qkv_a, qkv_b, marks_a, marks_b, prefix_kv, grads, w_back, grad_prefix_kv
+    )
+    packed = pack(count, grads, (grad_prefix_kv, *after(parts, grad_partial)), back_0, back_1)
     home = [lax.ppermute(m, everyone, back[k]) for k, m in enumerate(packed)]
     grads_yc = lax.ppermute(after(grads_y, packed), "seq", swap_core)
     final_0, final_1 = final_part(
@@ -1191,14 +1215,14 @@
         ln1_gain,
         grad_middle,
         grad_partial,
-        w_near,
+        w_back,
     )
     finals = [lax.ppermute(m, everyone, back[k]) for k, m in enumerate((final_0, final_1))]
     gathered = [unpack(count, width, *home)]
     gathered += [lax.ppermute(gathered[0], "seq", swap_core), lax.ppermute(gathered[0], "blk", swap_y)]
     gathered += [lax.ppermute(gathered[0], everyone, swap_both)]
     input_grad, summed = finish(finals, gathered, near_embed, inner, turned)
-    block_out, log_total = land(after(home, final_0), half, width)
+    block_out, log_total = land(count, after(home, final_0), half, width)
     return (block_out, input_grad, summed[0], summed[1], summed[2], summed[3], summed[4], log_total)
 
 

time: 78.3 us -> 77.2 us (0.986)
    pallas_call x1, Pallas kernels: 4.8 us -> 3.82 us  [final_part(): pl.pallas_call(final_kernel, in_specs=[vmem()] * 14, out_specs=[vmem()] *...]
where the time goes in v6:
time: 77.2 us; the launch traced here: 76.6 us
  Pallas kernels  39.5 us (51%)
  starting transfers between devices  31.5 us (41%)
  waiting for transfers between devices  4.49 us (6%)
  between operations  1.06 us (1%)
    pallas_call x1, Pallas kernels, middle_part(): pl.pallas_call(partial(middle_kernel, count), in_specs=[vmem()] * 11 + [h...  13.9 us
    ppermute x2, starting transfers between devices, body_rows(): own = [lax.ppermute(m, everyone, there[k]) for k, m in enumerate(out_msgs)]  6.7 us
    ppermute x2, starting transfers between devices, body_rows(): lax.ppermute(m, everyone, there[k])  5.91 us
    ppermute x2, starting transfers between devices, body_rows(): home = [lax.ppermute(m, everyone, back[k]) for k, m in enumerate(packed)]  5.78 us
    pallas_call x1, Pallas kernels, adapter_forward(): pl.pallas_call(adapter_kernel, in_specs=[hbm()] * 6, out_specs=[vmem()] *...  5.61 us
    ppermute x2, starting transfers between devices, body_rows(): lax.ppermute(m, everyone, back[k])  4.44 us
    pallas_call x2, Pallas kernels, project(): pl.pallas_call(partial(project_kernel, count), in_specs=[vmem()] * (count...  4.23 us
    pallas_call x1, Pallas kernels, finish(): pl.pallas_call(adapter_back_kernel, in_specs=[vmem()] * 9, out_specs=[hbm...  3.95 us
  transfers between devices with their start and end apart: 23, of which 4 were waited for; matrix products, arithmetic and copies ran while one was open for 0% of the time, Pallas kernels for 27%

profile of v6, /device:TPU:1, one launch (start us, length us, event | category | flops | bytes accessed | tf_op | source)
XLA Modules:
  0.0 76.6 jit_solution(7324615334244583190)
XLA Ops:
  0.6 1.2 %split.2 = (bf16[64,1152]{1,0:T(8,128)(2,1)S(1)}, bf16[64,1152]{1,0:T(8,128)(2,1)S(1)}) custom-call(bf16[64,16,128]{2,1,0:T(8,128)(2,1)} %bitcast.36, s32[2,64]{1,0:T(2,128)} %bitcast.38), custom_call_target="tpu_custom_call" | custom-call | flops 1048576 | bytes 524288 | tf_op jit(solution)/shard_map/split/pallas_call | solution.py:380
  1.8 5.6 %collective-permute-start = (bf16[64,1152]{1,0:T(8,128)(2,1)S(1)}, bf16[64,1152]{1,0:T(8,128)(2,1)S(1)}, u32[]{:S(2)}, u32[]{:S(2)}) collective-permute-start(bf16[64,1152]{1,0:T(8,128)(2,1)S(1)} %get-tuple-element.48), channel_id=1, source_target_pairs={{0,0},{1,1},{2,2},{3,3},{4,8},{5,9},{6,10},{7,11},{8,4},{9,5},{10,... | collective-permute-start | bytes 442376 | tf_op jit(solution)/shard_map/ppermute | solution.py:1182
  7.4 1.1 %collective-permute-start.1 = (bf16[64,1152]{1,0:T(8,128)(2,1)S(1)}, bf16[64,1152]{1,0:T(8,128)(2,1)S(1)}, u32[]{:S(2)}, u32[]{:S(2)}) collective-permute-start(bf16[64,1152]{1,0:T(8,128)(2,1)S(1)} %get-tuple-element.49), channel_id=1, source_target_pairs={{0,2},{1,3},{2,0},{3,1},{4,10},{5,11},{6,8},{7,9},{8,6},{9,7},{10,... | collective-permute-start | bytes 442376 | tf_op jit(solution)/shard_map/ppermute | solution.py:1182
  8.5 5.6 %adapter.1 = (bf16[16,2048]{1,0:T(8,128)(2,1)S(1)}, f32[16,512]{1,0:T(8,128)S(1)}, bf16[1024,3072]{1,0:T(8,128)(2,1)S(1)}, bf16[3072,1024]{1,0:T(8,128)(2,1)S(1)...) custom-call(f32[10,1024]{1,0:T(8,128)} %h_embed.1, f32[1024,512]{1,0:T(8,128)} %w_mlp1.1, f32[1,512]{1,0:T(1,128)} %bitcast.43, ...), custom_call_target="tpu_custom_call" | custom-call | flops 4294967296 | bytes 6291456 | tf_op jit(solution)/shard_map/adapter/pallas_call | solution.py:556
  14.1 0.0 collective-permute-done.refs_0_.own_0
  14.1 0.0 collective-permute-done.1.refs_1_.own_1
  14.2 0.1 collective-permute-start.2
  14.2 0.5 collective-permute-start.3
  14.7 1.3 %collective-permute-start.4 = (bf16[64,1152]{1,0:T(8,128)(2,1)S(1)}, bf16[64,1152]{1,0:T(8,128)(2,1)S(1)}, u32[]{:S(2)}, u32[]{:S(2)}) collective-permute-start(bf16[64,1152]{1,0:T(8,128)(2,1)S(1)} %collective-permute-done.refs_0_.own_0), channel_id=1, source_target_pairs={{0,1},{1,0},{2,3},{3,2},{4,5},{5,4},{6,7},{7,6},{8,9},{9,8},{10,11... | collective-permute-start | bytes 442376 | tf_op jit(solution)/shard_map/ppermute | solution.py:1188
  16.0 0.2 collective-permute-start.5
  16.2 1.2 %split.3 = (bf16[64,1024]{1,0:T(8,128)(2,1)S(1)}, bf16[64,1024]{1,0:T(8,128)(2,1)S(1)}) custom-call(bf16[64,16,128]{2,1,0:T(8,128)(2,1)} %bitcast.37), custom_call_target="tpu_custom_call" | custom-call | flops 1048576 | bytes 524288 | tf_op jit(solution)/shard_map/split/pallas_call | solution.py:380
  17.4 0.0 collective-permute-done.2.refs_2_
  17.4 0.0 collective-permute-done.3.refs_3_
  17.4 5.8 %collective-permute-start.8 = (bf16[64,1024]{1,0:T(8,128)(2,1)S(1)}, bf16[64,1024]{1,0:T(8,128)(2,1)S(1)}, u32[]{:S(2)}, u32[]{:S(2)}) collective-permute-start(bf16[64,1024]{1,0:T(8,128)(2,1)S(1)} %get-tuple-element.61), channel_id=1, source_target_pairs={{0,0},{1,1},{2,2},{3,3},{4,8},{5,9},{6,10},{7,11},{8,4},{9,5},{10,... | collective-permute-start | bytes 393224 | tf_op jit(solution)/shard_map/ppermute | solution.py:1190
  23.2 0.1 collective-permute-start.9
  23.3 0.0 collective-permute-done.4.refs_0_
  23.3 0.1 collective-permute-start.6
  23.4 0.0 collective-permute-done.5.refs_1_
  23.4 0.7 collective-permute-start.7
  24.2 0.0 copy-done
  24.2 0.0 copy-done.1
  24.2 2.1 %project.2 = (bf16[256,3072]{1,0:T(8,128)(2,1)S(1)}, bf16[256,128]{1,0:T(8,128)(2,1)S(1)}) custom-call(bf16[64,1152]{1,0:T(8,128)(2,1)S(1)} %collective-permute-done.refs_0_.own_0, bf16[64,1152]{1,0:T(8,128)(2,1)S(1)} %collective-permute-done.1.refs_1_.own_1, bf16[64,1152]{1,0:T(8,128)(2,1)S(1)} %collective-permute-done.2.refs_2_, ...), custom_call_target="tpu_custom_call" | custom-call | flops 1610612736 | bytes 6291456 | tf_op jit(solution)/shard_map/project/pallas_call | solution.py:454
  26.3 0.0 copy-start.2
  26.3 0.0 copy-start.3
  26.3 0.0 collective-permute-done.6.refs_2_
  26.3 0.0 collective-permute-done.7.refs_3_
  26.3 2.1 %project.3 = (bf16[256,3072]{1,0:T(8,128)(2,1)S(1)}, bf16[256,128]{1,0:T(8,128)(2,1)S(1)}) custom-call(bf16[64,1152]{1,0:T(8,128)(2,1)S(1)} %collective-permute-done.4.refs_0_, bf16[64,1152]{1,0:T(8,128)(2,1)S(1)} %collective-permute-done.5.refs_1_, bf16[64,1152]{1,0:T(8,128)(2,1)S(1)} %collective-permute-done.6.refs_2_, ...), custom_call_target="tpu_custom_call" | custom-call | flops 1610612736 | bytes 6291456 | tf_op jit(solution)/shard_map/project/pallas_call | solution.py:454
  28.5 0.0 collective-permute-done.8.cot_0
  28.5 1.1 %collective-permute-done.9.cot_1 = bf16[64,1024]{1,0:T(8,128)(2,1)S(1)} collective-permute-done((bf16[64,1024]{1,0:T(8,128)(2,1)S(1)}, bf16[64,1024]{1,0:T(8,128)(2,1)S(1)}, u32[]{:S(2)}, u32[]{:S(2)}) %collective-permute-start.9) | collective-permute-done | bytes 131104 | tf_op jit(solution)/shard_map/ppermute | solution.py:1190
  29.6 0.0 copy-done.2
  29.6 0.0 copy-done.3
  29.6 13.9 %middle.1 = (bf16[96,1024]{1,0:T(8,128)(2,1)S(1)}, bf16[96,1024]{1,0:T(8,128)(2,1)S(1)}, bf16[128,1152]{1,0:T(8,128)(2,1)S(1)}, f32[128,1024]{1,0:T(8,128)S(1)}) custom-call(bf16[256,3072]{1,0:T(8,128)(2,1)S(1)} %get-tuple-element.54.qkv_a.queries, bf16[256,3072]{1,0:T(8,128)(2,1)S(1)} %get-tuple-element.55.qkv_b, ...), custom_call_target="tpu_custom_call" | custom-call | flops 2147483648 | bytes 1000 | tf_op jit(solution)/shard_map/middle/pallas_call | solution.py:870
  43.5 1.3 %collective-permute-start.16 = (bf16[128,1152]{1,0:T(8,128)(2,1)S(1)}, bf16[128,1152]{1,0:T(8,128)(2,1)S(1)}, u32[]{:S(2)}, u32[]{:S(2)}) collective-permute-start(bf16[128,1152]{1,0:T(8,128)(2,1)S(1)} %get-tuple-element.63.grads.grads_0), channel_id=1, source_target_pairs={{0,1},{1,0},{2,3},{3,2},{4,5},{5,4},{6,7},{7,6},{8,9},{9,8},{10,11... | collective-permute-start | bytes 884744 | tf_op jit(solution)/shard_map/ppermute | solution.py:1198
  44.9 1.4 %prefix.1.order.own = bf16[16,2048]{1,0:T(8,128)(2,1)S(1)} custom-call(bf16[256,3072]{1,0:T(8,128)(2,1)S(1)} %get-tuple-element.54.qkv_a.queries, bf16[128,1152]{1,0:T(8,128)(2,1)S(1)} %get-tuple-element.63.grads.grads_0, bf16[16,2048]{1,0:T(8,128)(2,1)S(1)} %get-tuple-element.58.prefix_kv), custom_call_target="tpu_custom_call" | custom-call | flops 1000 | bytes 1000 | tf_op jit(solution)/shard_map/prefix/pallas_call | solution.py:950
  46.2 1.2 %collective-permute-start.10 = (bf16[16,2048]{1,0:T(8,128)(2,1)S(1)}, bf16[16,2048]{1,0:T(8,128)(2,1)S(1)}, u32[]{:S(2)}, u32[]{:S(2)}) collective-permute-start(bf16[16,2048]{1,0:T(8,128)(2,1)S(1)} %prefix.1.order.own), channel_id=1, source_target_pairs={{0,16},{8,24},{16,0},{24,8},{1,17},{9,25},{17,1},{25,9},{2,18},{10... | collective-permute-start | bytes 196616 | tf_op jit(solution)/shard_map/ppermute | solution.py:1201
  47.4 0.0 collective-permute-start.11
  47.4 0.6 collective-permute-start.12
  48.1 0.0 collective-permute-start.15
  48.1 3.2 %query.1.grad_partial = f32[128,1024]{1,0:T(8,128)S(1)} custom-call(bf16[256,3072]{1,0:T(8,128)(2,1)S(1)} %get-tuple-element.54.qkv_a.queries, bf16[256,3072]{1,0:T(8,128)(2,1)S(1)} %get-tuple-element.55.qkv_b, bf16[256,128]{1,0:T(8,128)(2,1)S(1)} %get-tuple-element.56.marks_a, bf16[256,128]{1,0:T(8,128)(2,1)S(1)} %get-tuple-element.57.marks_b, ...), custom_call_target="tpu_custom_call" | custom-call | flops 2147483648 | bytes 1000 | tf_op jit(solution)/shard_map/query/pallas_call | solution.py:1058
  51.3 0.0 collective-permute-done.10.part_0
  51.3 0.0 collective-permute-done.11.part_1
  51.3 0.5 collective-permute-done.12.part_2
  51.7 0.1 pack.1
  51.8 0.0 collective-permute-done.16.grads_2
  51.8 0.5 collective-permute-start.17
  52.3 4.6 %collective-permute-start.13 = (bf16[96,1024]{1,0:T(8,128)(2,1)S(1)}, bf16[96,1024]{1,0:T(8,128)(2,1)S(1)}, u32[]{:S(2)}, u32[]{:S(2)}) collective-permute-start(bf16[96,1024]{1,0:T(8,128)(2,1)S(1)} %get-tuple-element.70), channel_id=1, source_target_pairs={{0,0},{1,1},{2,2},{3,3},{8,4},{9,5},{10,6},{11,7},{4,8},{5,9},{6,1... | collective-permute-start | bytes 589832 | tf_op jit(solution)/shard_map/ppermute | solution.py:1206
  56.9 1.2 %collective-permute-start.14 = (bf16[96,1024]{1,0:T(8,128)(2,1)S(1)}, bf16[96,1024]{1,0:T(8,128)(2,1)S(1)}, u32[]{:S(2)}, u32[]{:S(2)}) collective-permute-start(bf16[96,1024]{1,0:T(8,128)(2,1)S(1)} %get-tuple-element.71), channel_id=1, source_target_pairs={{2,0},{3,1},{0,2},{1,3},{10,4},{11,5},{8,6},{9,7},{6,8},{7,9},{4,1... | collective-permute-start | bytes 589832 | tf_op jit(solution)/shard_map/ppermute | solution.py:1206
  58.1 0.0 collective-permute-done.15.grads_1
  58.1 0.0 collective-permute-done.17.grads_3
  58.1 3.8 %final.1 = (bf16[64,1024]{1,0:T(8,128)(2,1)S(1)}, bf16[64,1024]{1,0:T(8,128)(2,1)S(1)}) custom-call(bf16[256,3072]{1,0:T(8,128)(2,1)S(1)} %get-tuple-element.54.qkv_a.queries, bf16[256,3072]{1,0:T(8,128)(2,1)S(1)} %get-tuple-element.55.qkv_b, bf16[256,128]{1,0:T(8,128)(2,1)S(1)} %get-tuple-element.56.marks_a, ...), custom_call_target="tpu_custom_call" | custom-call | flops 1000 | bytes 1000 | tf_op jit(solution)/shard_map/final/pallas_call | solution.py:1127
  61.9 2.5 %collective-permute-start.18 = (bf16[64,1024]{1,0:T(8,128)(2,1)S(1)}, bf16[64,1024]{1,0:T(8,128)(2,1)S(1)}, u32[]{:S(2)}, u32[]{:S(2)}) collective-permute-start(bf16[64,1024]{1,0:T(8,128)(2,1)S(1)} %get-tuple-element.74), channel_id=1, source_target_pairs={{0,0},{1,1},{2,2},{3,3},{8,4},{9,5},{10,6},{11,7},{4,8},{5,9},{6,1... | collective-permute-start | bytes 393224 | tf_op jit(solution)/shard_map/ppermute | solution.py:1220
  64.4 1.9 %collective-permute-start.19 = (bf16[64,1024]{1,0:T(8,128)(2,1)S(1)}, bf16[64,1024]{1,0:T(8,128)(2,1)S(1)}, u32[]{:S(2)}, u32[]{:S(2)}) collective-permute-start(bf16[64,1024]{1,0:T(8,128)(2,1)S(1)} %get-tuple-element.78), channel_id=1, source_target_pairs={{2,0},{3,1},{0,2},{1,3},{10,4},{11,5},{8,6},{9,7},{6,8},{7,9},{4,1... | collective-permute-start | bytes 393224 | tf_op jit(solution)/shard_map/ppermute | solution.py:1220
  66.3 0.0 collective-permute-done.13.msg_0.home_0
  66.3 0.0 collective-permute-done.14.msg_1.home_1
  66.4 0.1 collective-permute-start.20
  66.5 1.3 %collective-permute-start.21 = (bf16[16,2048]{1,0:T(8,128)(2,1)S(1)}, bf16[16,2048]{1,0:T(8,128)(2,1)S(1)}, u32[]{:S(2)}, u32[]{:S(2)}) collective-permute-start(bf16[16,2048]{1,0:T(8,128)(2,1)S(1)} %unpack.1.part_0), channel_id=1, source_target_pairs={{0,1},{1,0},{2,3},{3,2},{4,5},{5,4},{6,7},{7,6},{8,9},{9,8},{10,11... | collective-permute-start | bytes 196616 | tf_op jit(solution)/shard_map/ppermute | solution.py:1222
  67.8 0.8 %collective-permute-start.22 = (bf16[16,2048]{1,0:T(8,128)(2,1)S(1)}, bf16[16,2048]{1,0:T(8,128)(2,1)S(1)}, u32[]{:S(2)}, u32[]{:S(2)}) collective-permute-start(bf16[16,2048]{1,0:T(8,128)(2,1)S(1)} %unpack.1.part_0), channel_id=1, source_target_pairs={{0,9},{1,8},{2,11},{3,10},{4,13},{5,12},{6,15},{7,14},{8,1},{9,0},... | collective-permute-start | bytes 196616 | tf_op jit(solution)/shard_map/ppermute | solution.py:1223
  68.6 1.0 %land.1 = (bf16[64,16,128]{2,1,0:T(8,128)(2,1)}, f32[2,16,64]{2,1,0:T(8,128)}) custom-call(bf16[96,1024]{1,0:T(8,128)(2,1)S(1)} %collective-permute-done.13.msg_0.home_0, bf16[96,1024]{1,0:T(8,128)(2,1)S(1)} %collective-permute-done.14.msg_1.home_1), custom_call_target="tpu_custom_call" | custom-call | flops 1000 | bytes 1000 | tf_op jit(solution)/shard_map/land/pallas_call | solution.py:421
  69.6 0.0 collective-permute-done.20.part_1
  69.6 0.1 collective-permute-done.21.part_2
  69.6 2.8 %collective-permute-done.22.part_3 = bf16[16,2048]{1,0:T(8,128)(2,1)S(1)} collective-permute-done((bf16[16,2048]{1,0:T(8,128)(2,1)S(1)}, bf16[16,2048]{1,0:T(8,128)(2,1)S(1)}, u32[]{:S(2)}, u32[]{:S(2)}) %collective-permute-start.22) | collective-permute-done | bytes 65568 | tf_op jit(solution)/shard_map/ppermute | solution.py:1223
  72.4 0.0 collective-permute-done.18.home_0
  72.4 0.0 collective-permute-done.19.home_1
  72.4 4.0 %finish.1 = (f32[1024,128]{1,0:T(8,128)}, f32[10,1024]{1,0:T(8,128)}, f32[1024,512]{1,0:T(8,128)}, f32[1,512]{1,0:T(1,128)}, f32[512,2048]{1,0:T(8,128)}, /*index=5*/f32[1,2048]{1,0:T(1,128)}) custom-call(bf16[64,1024]{1,0:T(8,128)(2,1)S(1)} %collective-permute-done.18.home_0, bf16[64,1024]{1,0:T(8,128)(2,1)S(1)} %collective-permute-done.19.home_1, ...), custom_call_target="tpu_custom_call" | custom-call | flops 1000 | bytes 1000 | tf_op jit(solution)/shard_map/finish/pallas_call | solution.py:653
  (3 shorter events, 0.0 us)
Async XLA Ops:
  1.8 12.3 %collective-permute-start = (bf16[64,1152]{1,0:T(8,128)(2,1)S(1)}, bf16[64,1152]{1,0:T(8,128)(2,1)S(1)}, u32[]{:S(2)}, u32[]{:S(2)}) collective-permute-start(bf16[64,1152]{1,0:T(8,128)(2,1)S(1)} %get-tuple-element.48), channel_id=1, source_target_pairs={{0,0},{1,1},{2,2},{3,3},{4,8},{5,9},{6,10},{7,11},{8,4},{9,5},{10,... | collective-permute-start | bytes 442376 | tf_op jit(solution)/shard_map/ppermute | solution.py:1182
  7.4 6.7 %collective-permute-start.1 = (bf16[64,1152]{1,0:T(8,128)(2,1)S(1)}, bf16[64,1152]{1,0:T(8,128)(2,1)S(1)}, u32[]{:S(2)}, u32[]{:S(2)}) collective-permute-start(bf16[64,1152]{1,0:T(8,128)(2,1)S(1)} %get-tuple-element.49), channel_id=1, source_target_pairs={{0,2},{1,3},{2,0},{3,1},{4,10},{5,11},{6,8},{7,9},{8,6},{9,7},{10,... | collective-permute-start | bytes 442376 | tf_op jit(solution)/shard_map/ppermute | solution.py:1182
  8.5 15.7 %copy-start = (f32[1024]{0:T(1024)S(1)}, f32[1024]{0:T(1024)}, u32[]{:S(2)}) copy-start(f32[1024]{0:T(1024)} %param.18) | copy-start | bytes 12292
  8.5 15.7 %copy-start.1 = (f32[1024]{0:T(1024)S(1)}, f32[1024]{0:T(1024)}, u32[]{:S(2)}) copy-start(f32[1024]{0:T(1024)} %param.19) | copy-start | bytes 12292
  14.2 3.2 %collective-permute-start.2 = (bf16[64,1152]{1,0:T(8,128)(2,1)S(1)}, bf16[64,1152]{1,0:T(8,128)(2,1)S(1)}, u32[]{:S(2)}, u32[]{:S(2)}) collective-permute-start(bf16[64,1152]{1,0:T(8,128)(2,1)S(1)} %collective-permute-done.refs_0_.own_0), channel_id=1, source_target_pairs={{0,8},{8,0},{16,24},{24,16},{1,9},{9,1},{17,25},{25,17},{2,10},{10... | collective-permute-start | bytes 442376 | tf_op jit(solution)/shard_map/ppermute | solution.py:1189
  14.2 3.2 %collective-permute-start.3 = (bf16[64,1152]{1,0:T(8,128)(2,1)S(1)}, bf16[64,1152]{1,0:T(8,128)(2,1)S(1)}, u32[]{:S(2)}, u32[]{:S(2)}) collective-permute-start(bf16[64,1152]{1,0:T(8,128)(2,1)S(1)} %collective-permute-done.1.refs_1_.own_1), channel_id=1, source_target_pairs={{0,8},{8,0},{16,24},{24,16},{1,9},{9,1},{17,25},{25,17},{2,10},{10... | collective-permute-start | bytes 442376 | tf_op jit(solution)/shard_map/ppermute | solution.py:1189
  14.7 8.6 %collective-permute-start.4 = (bf16[64,1152]{1,0:T(8,128)(2,1)S(1)}, bf16[64,1152]{1,0:T(8,128)(2,1)S(1)}, u32[]{:S(2)}, u32[]{:S(2)}) collective-permute-start(bf16[64,1152]{1,0:T(8,128)(2,1)S(1)} %collective-permute-done.refs_0_.own_0), channel_id=1, source_target_pairs={{0,1},{1,0},{2,3},{3,2},{4,5},{5,4},{6,7},{7,6},{8,9},{9,8},{10,11... | collective-permute-start | bytes 442376 | tf_op jit(solution)/shard_map/ppermute | solution.py:1188
  16.0 7.4 %collective-permute-start.5 = (bf16[64,1152]{1,0:T(8,128)(2,1)S(1)}, bf16[64,1152]{1,0:T(8,128)(2,1)S(1)}, u32[]{:S(2)}, u32[]{:S(2)}) collective-permute-start(bf16[64,1152]{1,0:T(8,128)(2,1)S(1)} %collective-permute-done.1.refs_1_.own_1), channel_id=1, source_target_pairs={{0,1},{1,0},{2,3},{3,2},{4,5},{5,4},{6,7},{7,6},{8,9},{9,8},{10,11... | collective-permute-start | bytes 442376 | tf_op jit(solution)/shard_map/ppermute | solution.py:1188
  17.4 11.1 %collective-permute-start.8 = (bf16[64,1024]{1,0:T(8,128)(2,1)S(1)}, bf16[64,1024]{1,0:T(8,128)(2,1)S(1)}, u32[]{:S(2)}, u32[]{:S(2)}) collective-permute-start(bf16[64,1024]{1,0:T(8,128)(2,1)S(1)} %get-tuple-element.61), channel_id=1, source_target_pairs={{0,0},{1,1},{2,2},{3,3},{4,8},{5,9},{6,10},{7,11},{8,4},{9,5},{10,... | collective-permute-start | bytes 393224 | tf_op jit(solution)/shard_map/ppermute | solution.py:1190
  23.2 6.4 %collective-permute-start.9 = (bf16[64,1024]{1,0:T(8,128)(2,1)S(1)}, bf16[64,1024]{1,0:T(8,128)(2,1)S(1)}, u32[]{:S(2)}, u32[]{:S(2)}) collective-permute-start(bf16[64,1024]{1,0:T(8,128)(2,1)S(1)} %get-tuple-element.62), channel_id=1, source_target_pairs={{0,2},{1,3},{2,0},{3,1},{4,10},{5,11},{6,8},{7,9},{8,6},{9,7},{10,... | collective-permute-start | bytes 393224 | tf_op jit(solution)/shard_map/ppermute | solution.py:1190
  23.3 3.0 %collective-permute-start.6 = (bf16[64,1152]{1,0:T(8,128)(2,1)S(1)}, bf16[64,1152]{1,0:T(8,128)(2,1)S(1)}, u32[]{:S(2)}, u32[]{:S(2)}) collective-permute-start(bf16[64,1152]{1,0:T(8,128)(2,1)S(1)} %collective-permute-done.4.refs_0_), channel_id=1, source_target_pairs={{0,8},{8,0},{16,24},{24,16},{1,9},{9,1},{17,25},{25,17},{2,10},{10... | collective-permute-start | bytes 442376 | tf_op jit(solution)/shard_map/ppermute | solution.py:1191
  23.4 2.9 %collective-permute-start.7 = (bf16[64,1152]{1,0:T(8,128)(2,1)S(1)}, bf16[64,1152]{1,0:T(8,128)(2,1)S(1)}, u32[]{:S(2)}, u32[]{:S(2)}) collective-permute-start(bf16[64,1152]{1,0:T(8,128)(2,1)S(1)} %collective-permute-done.5.refs_1_), channel_id=1, source_target_pairs={{0,8},{8,0},{16,24},{24,16},{1,9},{9,1},{17,25},{25,17},{2,10},{10... | collective-permute-start | bytes 442376 | tf_op jit(solution)/shard_map/ppermute | solution.py:1191
  26.3 3.3 %copy-start.2 = (f32[1024]{0:T(1024)S(1)}, f32[1024]{0:T(1024)}, u32[]{:S(2)}) copy-start(f32[1024]{0:T(1024)} %param.22) | copy-start | bytes 12292
  26.3 3.3 %copy-start.3 = (f32[1024]{0:T(1024)S(1)}, f32[1024]{0:T(1024)}, u32[]{:S(2)}) copy-start(f32[1024]{0:T(1024)} %param.23) | copy-start | bytes 12292
  43.5 8.3 %collective-permute-start.16 = (bf16[128,1152]{1,0:T(8,128)(2,1)S(1)}, bf16[128,1152]{1,0:T(8,128)(2,1)S(1)}, u32[]{:S(2)}, u32[]{:S(2)}) collective-permute-start(bf16[128,1152]{1,0:T(8,128)(2,1)S(1)} %get-tuple-element.63.grads.grads_0), channel_id=1, source_target_pairs={{0,1},{1,0},{2,3},{3,2},{4,5},{5,4},{6,7},{7,6},{8,9},{9,8},{10,11... | collective-permute-start | bytes 884744 | tf_op jit(solution)/shard_map/ppermute | solution.py:1198
  46.2 5.1 %collective-permute-start.10 = (bf16[16,2048]{1,0:T(8,128)(2,1)S(1)}, bf16[16,2048]{1,0:T(8,128)(2,1)S(1)}, u32[]{:S(2)}, u32[]{:S(2)}) collective-permute-start(bf16[16,2048]{1,0:T(8,128)(2,1)S(1)} %prefix.1.order.own), channel_id=1, source_target_pairs={{0,16},{8,24},{16,0},{24,8},{1,17},{9,25},{17,1},{25,9},{2,18},{10... | collective-permute-start | bytes 196616 | tf_op jit(solution)/shard_map/ppermute | solution.py:1201
  47.4 3.8 %collective-permute-start.11 = (bf16[16,2048]{1,0:T(8,128)(2,1)S(1)}, bf16[16,2048]{1,0:T(8,128)(2,1)S(1)}, u32[]{:S(2)}, u32[]{:S(2)}) collective-permute-start(bf16[16,2048]{1,0:T(8,128)(2,1)S(1)} %prefix.1.order.own), channel_id=1, source_target_pairs={{0,8},{8,0},{16,24},{24,16},{1,9},{9,1},{17,25},{25,17},{2,10},{10... | collective-permute-start | bytes 196616 | tf_op jit(solution)/shard_map/ppermute | solution.py:1201
  47.4 4.3 %collective-permute-start.12 = (bf16[16,2048]{1,0:T(8,128)(2,1)S(1)}, bf16[16,2048]{1,0:T(8,128)(2,1)S(1)}, u32[]{:S(2)}, u32[]{:S(2)}) collective-permute-start(bf16[16,2048]{1,0:T(8,128)(2,1)S(1)} %prefix.1.order.own), channel_id=1, source_target_pairs={{0,24},{8,16},{16,8},{24,0},{1,25},{9,17},{17,9},{25,1},{2,26},{10... | collective-permute-start | bytes 196616 | tf_op jit(solution)/shard_map/ppermute | solution.py:1201
  48.1 10.0 %collective-permute-start.15 = (bf16[128,1152]{1,0:T(8,128)(2,1)S(1)}, bf16[128,1152]{1,0:T(8,128)(2,1)S(1)}, u32[]{:S(2)}, u32[]{:S(2)}) collective-permute-start(bf16[128,1152]{1,0:T(8,128)(2,1)S(1)} %get-tuple-element.63.grads.grads_0), channel_id=1, source_target_pairs={{0,8},{8,0},{16,24},{24,16},{1,9},{9,1},{17,25},{25,17},{2,10},{10... | collective-permute-start | bytes 884744 | tf_op jit(solution)/shard_map/ppermute | solution.py:1199
  51.8 6.2 %collective-permute-start.17 = (bf16[128,1152]{1,0:T(8,128)(2,1)S(1)}, bf16[128,1152]{1,0:T(8,128)(2,1)S(1)}, u32[]{:S(2)}, u32[]{:S(2)}) collective-permute-start(bf16[128,1152]{1,0:T(8,128)(2,1)S(1)} %collective-permute-done.16.grads_2), channel_id=1, source_target_pairs={{0,8},{8,0},{16,24},{24,16},{1,9},{9,1},{17,25},{25,17},{2,10},{10... | collective-permute-start | bytes 884744 | tf_op jit(solution)/shard_map/ppermute | solution.py:1207
  52.3 14.1 %collective-permute-start.13 = (bf16[96,1024]{1,0:T(8,128)(2,1)S(1)}, bf16[96,1024]{1,0:T(8,128)(2,1)S(1)}, u32[]{:S(2)}, u32[]{:S(2)}) collective-permute-start(bf16[96,1024]{1,0:T(8,128)(2,1)S(1)} %get-tuple-element.70), channel_id=1, source_target_pairs={{0,0},{1,1},{2,2},{3,3},{8,4},{9,5},{10,6},{11,7},{4,8},{5,9},{6,1... | collective-permute-start | bytes 589832 | tf_op jit(solution)/shard_map/ppermute | solution.py:1206
  56.9 9.4 %collective-permute-start.14 = (bf16[96,1024]{1,0:T(8,128)(2,1)S(1)}, bf16[96,1024]{1,0:T(8,128)(2,1)S(1)}, u32[]{:S(2)}, u32[]{:S(2)}) collective-permute-start(bf16[96,1024]{1,0:T(8,128)(2,1)S(1)} %get-tuple-element.71), channel_id=1, source_target_pairs={{2,0},{3,1},{0,2},{1,3},{10,4},{11,5},{8,6},{9,7},{6,8},{7,9},{4,1... | collective-permute-start | bytes 589832 | tf_op jit(solution)/shard_map/ppermute | solution.py:1206
  61.9 10.5 %collective-permute-start.18 = (bf16[64,1024]{1,0:T(8,128)(2,1)S(1)}, bf16[64,1024]{1,0:T(8,128)(2,1)S(1)}, u32[]{:S(2)}, u32[]{:S(2)}) collective-permute-start(bf16[64,1024]{1,0:T(8,128)(2,1)S(1)} %get-tuple-element.74), channel_id=1, source_target_pairs={{0,0},{1,1},{2,2},{3,3},{8,4},{9,5},{10,6},{11,7},{4,8},{5,9},{6,1... | collective-permute-start | bytes 393224 | tf_op jit(solution)/shard_map/ppermute | solution.py:1220
  64.4 8.0 %collective-permute-start.19 = (bf16[64,1024]{1,0:T(8,128)(2,1)S(1)}, bf16[64,1024]{1,0:T(8,128)(2,1)S(1)}, u32[]{:S(2)}, u32[]{:S(2)}) collective-permute-start(bf16[64,1024]{1,0:T(8,128)(2,1)S(1)} %get-tuple-element.78), channel_id=1, source_target_pairs={{2,0},{3,1},{0,2},{1,3},{10,4},{11,5},{8,6},{9,7},{6,8},{7,9},{4,1... | collective-permute-start | bytes 393224 | tf_op jit(solution)/shard_map/ppermute | solution.py:1220
  66.4 3.2 %collective-permute-start.20 = (bf16[16,2048]{1,0:T(8,128)(2,1)S(1)}, bf16[16,2048]{1,0:T(8,128)(2,1)S(1)}, u32[]{:S(2)}, u32[]{:S(2)}) collective-permute-start(bf16[16,2048]{1,0:T(8,128)(2,1)S(1)} %unpack.1.part_0), channel_id=1, source_target_pairs={{0,8},{8,0},{16,24},{24,16},{1,9},{9,1},{17,25},{25,17},{2,10},{10... | collective-permute-start | bytes 196616 | tf_op jit(solution)/shard_map/ppermute | solution.py:1222
  66.5 3.2 %collective-permute-start.21 = (bf16[16,2048]{1,0:T(8,128)(2,1)S(1)}, bf16[16,2048]{1,0:T(8,128)(2,1)S(1)}, u32[]{:S(2)}, u32[]{:S(2)}) collective-permute-start(bf16[16,2048]{1,0:T(8,128)(2,1)S(1)} %unpack.1.part_0), channel_id=1, source_target_pairs={{0,1},{1,0},{2,3},{3,2},{4,5},{5,4},{6,7},{7,6},{8,9},{9,8},{10,11... | collective-permute-start | bytes 196616 | tf_op jit(solution)/shard_map/ppermute | solution.py:1222
  67.8 4.7 %collective-permute-start.22 = (bf16[16,2048]{1,0:T(8,128)(2,1)S(1)}, bf16[16,2048]{1,0:T(8,128)(2,1)S(1)}, u32[]{:S(2)}, u32[]{:S(2)}) collective-permute-start(bf16[16,2048]{1,0:T(8,128)(2,1)S(1)} %unpack.1.part_0), channel_id=1, source_target_pairs={{0,9},{1,8},{2,11},{3,10},{4,13},{5,12},{6,15},{7,14},{8,1},{9,0},... | collective-permute-start | bytes 196616 | tf_op jit(solution)/shard_map/ppermute | solution.py:1223

commit v7 on v6

--- a/solution.py
+++ b/solution.py
@@ -308,7 +308,7 @@
 
 def positions(index, half, row, core, y_at):
     upper = (index >= half).astype(jnp.int32)
-    slot = upper + row - 2 * upper * row
+    slot = 1 - (upper + row - 2 * upper * row)
     block = (2 * core + slot) * 2 + y_at
     return block * half + index - upper * half
 
@@ -350,7 +350,7 @@
 
 
 def odd_place():
-    return (lax.axis_index("blk") // 2) % 2 == 1
+    return (lax.axis_index("blk") // 2) % 2 == 0
 
 
 def split_kernel(marked, *refs):
@@ -384,7 +384,7 @@
         out_shape=[jax.ShapeDtypeStruct((half, width), BF16)] * 2,
         scratch_shapes=[pltpu.VMEM((half * count, LANES), F32)],
         compiler_params=pltpu.CompilerParams(vmem_limit_bytes=4 * MIB),
-        cost_estimate=pl.CostEstimate(flops=1 << 20, bytes_accessed=1 << 19, transcendentals=0),
+        cost_estimate=pl.CostEstimate(flops=1 << 31, bytes_accessed=1000, transcendentals=0),
         name="split",
     )(*kept_in_hbm(tiles), *extra)
 
@@ -434,7 +434,7 @@
     return from_tiles(out[0], width), out[1]
 
 
-def project_kernel(count, *refs):
+def project_kernel(count, first, *refs):
     messages, (gain, bias, weight, out, marks, normed) = refs[:count], refs[count:]
     half, width = messages[0].shape[0], normed.shape[1]
     for i, message in enumerate(messages):
@@ -442,24 +442,25 @@
         unit, _ = norm_parts(message[:, :width].astype(F32))
         normed[rows] = (unit * gain[...] + bias[...]).astype(BF16)
         marks[rows] = message[:, width:]
-    for i in range(3):
+    for i in range(first, 3):
         at = pl.ds(i * width, width)
         out[:, at] = nn(normed[...], weight[:, at]).astype(BF16)
 
 
-def project(messages, gain, bias, weight):
+def project(messages, gain, bias, weight, first=0):
     count, half = len(messages), messages[0].shape[0]
     width, columns = weight.shape
     rows = count * half
     return pl.pallas_call(
-        partial(project_kernel, count),
+        partial(project_kernel, count, first),
         in_specs=[vmem()] * (count + 3),
-        out_specs=[vmem()] * 2,
+        out_specs=[vmem()] * (2 + first),
         out_shape=[
             jax.ShapeDtypeStruct((rows, columns), BF16),
             jax.ShapeDtypeStruct((rows, LANES), BF16),
-        ],
-        scratch_shapes=[pltpu.VMEM((rows, width), BF16)],
+        ]
+        + [jax.ShapeDtypeStruct((rows, width), BF16)] * first,
+        scratch_shapes=[pltpu.VMEM((rows, width), BF16)] * (1 - first),
         compiler_params=pltpu.CompilerParams(vmem_limit_bytes=16 * MIB),
         cost_estimate=pl.CostEstimate(
             flops=2 * rows * width * columns, bytes_accessed=2 * width * columns, transcendentals=0
@@ -1018,8 +1019,11 @@
     prefix_kv,
     grads,
     weight,
+    normed_b,
+    w_queries,
     order,
     out,
+    qkv_out,
     scores_bias,
     grad_query,
 ):
@@ -1051,20 +1055,24 @@
 
     lax.fori_loop(0, HEADS // 2, step, 0, unroll=True)
     out[...] = nn(grad_query[...], weight[:width])
-
-
-def query_part(count, qkv_a, qkv_b, marks_a, marks_b, prefix_kv, grads, weight, order):
+    qkv_out[:, :width] = nn(normed_b[...], w_queries[:, :width]).astype(BF16)
+
+
+def query_part(
+    count, qkv_a, qkv_b, marks_a, marks_b, prefix_kv, grads, weight, normed_b, w_queries, order
+):
     rows, width = grads.shape[0], grads.shape[1] - LANES
     return pl.pallas_call(
         partial(query_kernel, count),
-        in_specs=[vmem()] * 7 + [pl.BlockSpec(memory_space=pl.ANY)],
-        out_specs=vmem(),
-        out_shape=jax.ShapeDtypeStruct((rows, width), F32),
+        in_specs=[vmem()] * 9 + [pl.BlockSpec(memory_space=pl.ANY)],
+        out_specs=[vmem()] * 2,
+        out_shape=[jax.ShapeDtypeStruct((rows, width), F32), jax.ShapeDtypeStruct(qkv_b.shape, BF16)],
+        input_output_aliases={1: 1},
         scratch_shapes=[pltpu.VMEM((rows, 4 * rows + LANES), F32), pltpu.VMEM((rows, width), BF16)],
         compiler_params=pltpu.CompilerParams(vmem_limit_bytes=16 * MIB),
         cost_estimate=pl.CostEstimate(flops=1 << 31, bytes_accessed=1000, transcendentals=0),
         name="query",
-    )(qkv_a, qkv_b, marks_a, marks_b, prefix_kv, grads, weight, order)
+    )(qkv_a, qkv_b, marks_a, marks_b, prefix_kv, grads, weight, normed_b, w_queries, order)
 
 
 def final_kernel(
@@ -1144,7 +1152,7 @@
     for seq in range(4):
         for blk in range(8):
             group, z_at, y_at = seq % 2, blk // 2, blk % 2
-            row = (z_at + k) % 2
+            row = (z_at + k + 1) % 2
             pairs.append((seq * 8 + blk, (seq - group + z_at // 2) * 8 + (2 * group + row) * 2 + y_at))
     return pairs
 
@@ -1191,16 +1199,16 @@
     beyond = [lax.ppermute(m, "seq", swap_core) for m in across]
 
     qkv_a, marks_a = project(own + beside, ln1_gain, ln1_bias, w_near)
-    qkv_b, marks_b = project(across + beyond, ln1_gain, ln1_bias, w_near)
+    kv_b, marks_b, normed_b = project(across + beyond, ln1_gain, ln1_bias, w_near, 1)
     back_0, back_1, grads, grad_middle = middle_part(
-        count, qkv_a, qkv_b, marks_a, marks_b, prefix_kv, own, cots, ln2_gain, ln2_bias, w_out, w_fc, w_proj
+        count, qkv_a, kv_b, marks_a, marks_b, prefix_kv, own, cots, ln2_gain, ln2_bias, w_out, w_fc, w_proj
     )
     grads_y = lax.ppermute(grads, "blk", swap_y)
     grads_c = lax.ppermute(grads, "seq", swap_core)
     grad_prefix_kv = prefix_part(count, qkv_a, grads, prefix_kv)
     parts = [lax.ppermute(grad_prefix_kv, "seq", [(i, i ^ far) for i in range(4)]) for far in (2, 1, 3)]
-    grad_partial = query_part(
-        count, qkv_a, qkv_b, marks_a, marks_b, prefix_kv, grads, w_back, grad_prefix_kv
+    grad_partial, qkv_b = query_part(
+        count, qkv_a, kv_b, marks_a, marks_b, prefix_kv, grads, w_back, normed_b, w_near, grad_prefix_kv
     )
     packed = pack(count, grads, (grad_prefix_kv, *after(parts, grad_partial)), back_0, back_1)
     home = [lax.ppermute(m, everyone, back[k]) for k, m in enumerate(packed)]

time: 77.2 us -> 75.1 us (0.973)
  starting transfers between devices: 31.5 us -> 30.1 us
    ppermute x1, waiting for transfers between devices: 2.78 us -> 0.76 us  [body_rows(): gathered += [lax.ppermute(gathered[0], everyone, swap_both)]]
    ppermute x1, starting transfers between devices: 0.07 us -> 1.83 us  [body_rows(): lax.ppermute(gathered[0], 'seq', swap_core)]
    ppermute x2, starting transfers between devices: 4.44 us -> 6.07 us  [body_rows(): lax.ppermute(m, everyone, back[k])]
    ppermute x2, starting transfers between devices: 5.91 us -> 4.32 us  [body_rows(): lax.ppermute(m, everyone, there[k])]
    ppermute x2, starting transfers between devices: 5.78 us -> 4.22 us  [body_rows(): home = [lax.ppermute(m, everyone, back[k]) for k, m in enumerate(packed)]]
    ppermute x1, starting transfers between devices: 1.3 us -> 0.29 us  [body_rows(): lax.ppermute(gathered[0], 'blk', swap_y)]
    ppermute x2, waiting for transfers between devices: 0.01 us -> 0.83 us  [body_rows(): lax.ppermute(m, everyone, back[k])]
where the time goes in v7:
time: 75.1 us; the launch traced here: 74.3 us
  Pallas kernels  39.4 us (52%)
  starting transfers between devices  30.1 us (40%)
  waiting for transfers between devices  3.75 us (5%)
  between operations  1.08 us (1%)
    pallas_call x1, Pallas kernels, middle_part(): pl.pallas_call(partial(middle_kernel, count), in_specs=[vmem()] * 11 + [h...  13.9 us
    ppermute x2, starting transfers between devices, body_rows(): own = [lax.ppermute(m, everyone, there[k]) for k, m in enumerate(out_msgs)]  6.68 us
    ppermute x2, starting transfers between devices, body_rows(): lax.ppermute(m, everyone, back[k])  6.07 us
    pallas_call x1, Pallas kernels, adapter_forward(): pl.pallas_call(adapter_kernel, in_specs=[hbm()] * 6, out_specs=[vmem()] *...  5.59 us
    ppermute x2, starting transfers between devices, body_rows(): lax.ppermute(m, everyone, there[k])  4.32 us
    ppermute x2, starting transfers between devices, body_rows(): home = [lax.ppermute(m, everyone, back[k]) for k, m in enumerate(packed)]  4.22 us
    pallas_call x1, Pallas kernels, finish(): pl.pallas_call(adapter_back_kernel, in_specs=[vmem()] * 9, out_specs=[hbm...  3.95 us
    pallas_call x1, Pallas kernels, final_part(): pl.pallas_call(final_kernel, in_specs=[vmem()] * 14, out_specs=[vmem()] *...  3.81 us
  transfers between devices with their start and end apart: 23, of which 4 were waited for; matrix products, arithmetic and copies ran while one was open for 0% of the time, Pallas kernels for 27%

profile of v7, /device:TPU:1, one launch (start us, length us, event | category | flops | bytes accessed | tf_op | source)
XLA Modules:
  0.0 74.3 jit_solution(15243361382201690501)
XLA Ops:
  0.6 1.2 %split.2 = (bf16[64,1152]{1,0:T(8,128)(2,1)S(1)}, bf16[64,1152]{1,0:T(8,128)(2,1)S(1)}) custom-call(bf16[64,16,128]{2,1,0:T(8,128)(2,1)} %bitcast.37, s32[2,64]{1,0:T(2,128)} %bitcast.44), custom_call_target="tpu_custom_call" | custom-call | flops 2147483648 | bytes 1000 | tf_op jit(solution)/shard_map/split/pallas_call | solution.py:380
  1.8 4.8 %collective-permute-start = (bf16[64,1152]{1,0:T(8,128)(2,1)S(1)}, bf16[64,1152]{1,0:T(8,128)(2,1)S(1)}, u32[]{:S(2)}, u32[]{:S(2)}) collective-permute-start(bf16[64,1152]{1,0:T(8,128)(2,1)S(1)} %get-tuple-element.51), channel_id=1, source_target_pairs={{0,2},{1,3},{2,0},{3,1},{4,10},{5,11},{6,8},{7,9},{8,6},{9,7},{10,... | collective-permute-start | bytes 442376 | tf_op jit(solution)/shard_map/ppermute | solution.py:1190
  6.6 1.9 %collective-permute-start.1 = (bf16[64,1152]{1,0:T(8,128)(2,1)S(1)}, bf16[64,1152]{1,0:T(8,128)(2,1)S(1)}, u32[]{:S(2)}, u32[]{:S(2)}) collective-permute-start(bf16[64,1152]{1,0:T(8,128)(2,1)S(1)} %get-tuple-element.52), channel_id=1, source_target_pairs={{0,0},{1,1},{2,2},{3,3},{4,8},{5,9},{6,10},{7,11},{8,4},{9,5},{10,... | collective-permute-start | bytes 442376 | tf_op jit(solution)/shard_map/ppermute | solution.py:1190
  8.5 5.6 %adapter.1 = (bf16[16,2048]{1,0:T(8,128)(2,1)S(1)}, f32[16,512]{1,0:T(8,128)S(1)}, bf16[1024,3072]{1,0:T(8,128)(2,1)S(1)}, bf16[3072,1024]{1,0:T(8,128)(2,1)S(1)...) custom-call(f32[10,1024]{1,0:T(8,128)} %h_embed.1, f32[1024,512]{1,0:T(8,128)} %w_mlp1.1, f32[1,512]{1,0:T(1,128)} %bitcast.42, ...), custom_call_target="tpu_custom_call" | custom-call | flops 4294967296 | bytes 6291456 | tf_op jit(solution)/shard_map/adapter/pallas_call | solution.py:557
  14.1 0.0 copy-start
  14.1 0.0 copy-start.1
  14.1 0.0 collective-permute-done.refs_0_.own_0
  14.1 0.4 collective-permute-done.1.refs_1_.own_1
  14.5 1.2 %collective-permute-start.4 = (bf16[64,1152]{1,0:T(8,128)(2,1)S(1)}, bf16[64,1152]{1,0:T(8,128)(2,1)S(1)}, u32[]{:S(2)}, u32[]{:S(2)}) collective-permute-start(bf16[64,1152]{1,0:T(8,128)(2,1)S(1)} %collective-permute-done.refs_0_.own_0), channel_id=1, source_target_pairs={{0,1},{1,0},{2,3},{3,2},{4,5},{5,4},{6,7},{7,6},{8,9},{9,8},{10,11... | collective-permute-start | bytes 442376 | tf_op jit(solution)/shard_map/ppermute | solution.py:1196
  15.7 0.0 collective-permute-start.2
  15.7 0.2 collective-permute-start.5
  16.0 0.8 %collective-permute-start.3 = (bf16[64,1152]{1,0:T(8,128)(2,1)S(1)}, bf16[64,1152]{1,0:T(8,128)(2,1)S(1)}, u32[]{:S(2)}, u32[]{:S(2)}) collective-permute-start(bf16[64,1152]{1,0:T(8,128)(2,1)S(1)} %collective-permute-done.1.refs_1_.own_1), channel_id=1, source_target_pairs={{0,8},{8,0},{16,24},{24,16},{1,9},{9,1},{17,25},{25,17},{2,10},{10... | collective-permute-start | bytes 442376 | tf_op jit(solution)/shard_map/ppermute | solution.py:1197
  16.8 1.2 %split.3 = (bf16[64,1024]{1,0:T(8,128)(2,1)S(1)}, bf16[64,1024]{1,0:T(8,128)(2,1)S(1)}) custom-call(bf16[64,16,128]{2,1,0:T(8,128)(2,1)} %bitcast.38), custom_call_target="tpu_custom_call" | custom-call | flops 2147483648 | bytes 1000 | tf_op jit(solution)/shard_map/split/pallas_call | solution.py:380
  17.9 0.0 collective-permute-done.2.refs_2_
  17.9 0.0 collective-permute-done.3.refs_3_
  17.9 1.8 %collective-permute-start.8 = (bf16[64,1024]{1,0:T(8,128)(2,1)S(1)}, bf16[64,1024]{1,0:T(8,128)(2,1)S(1)}, u32[]{:S(2)}, u32[]{:S(2)}) collective-permute-start(bf16[64,1024]{1,0:T(8,128)(2,1)S(1)} %get-tuple-element.64), channel_id=1, source_target_pairs={{0,2},{1,3},{2,0},{3,1},{4,10},{5,11},{6,8},{7,9},{8,6},{9,7},{10,... | collective-permute-start | bytes 393224 | tf_op jit(solution)/shard_map/ppermute | solution.py:1198
  19.7 2.5 %collective-permute-start.9 = (bf16[64,1024]{1,0:T(8,128)(2,1)S(1)}, bf16[64,1024]{1,0:T(8,128)(2,1)S(1)}, u32[]{:S(2)}, u32[]{:S(2)}) collective-permute-start(bf16[64,1024]{1,0:T(8,128)(2,1)S(1)} %get-tuple-element.65), channel_id=1, source_target_pairs={{0,0},{1,1},{2,2},{3,3},{4,8},{5,9},{6,10},{7,11},{8,4},{9,5},{10,... | collective-permute-start | bytes 393224 | tf_op jit(solution)/shard_map/ppermute | solution.py:1198
  22.3 0.0 collective-permute-done.4.refs_0_
  22.3 0.1 collective-permute-start.6
  22.4 0.0 collective-permute-done.5.refs_1_
  22.4 0.5 collective-permute-start.7
  22.9 0.0 copy-done
  22.9 0.0 copy-done.1
  22.9 2.1 %project.2 = (bf16[256,3072]{1,0:T(8,128)(2,1)S(1)}, bf16[256,128]{1,0:T(8,128)(2,1)S(1)}) custom-call(bf16[64,1152]{1,0:T(8,128)(2,1)S(1)} %collective-permute-done.refs_0_.own_0, bf16[64,1152]{1,0:T(8,128)(2,1)S(1)} %collective-permute-done.1.refs_1_.own_1, bf16[64,1152]{1,0:T(8,128)(2,1)S(1)} %collective-permute-done.2.refs_2_, ...), custom_call_target="tpu_custom_call" | custom-call | flops 1610612736 | bytes 6291456 | tf_op jit(solution)/shard_map/project/pallas_call | solution.py:454
  25.0 0.0 copy-start.2
  25.0 0.0 copy-start.3
  25.0 0.0 collective-permute-done.6.refs_2_
  25.0 0.0 collective-permute-done.7.refs_3_
  25.0 1.6 %project.3 = (bf16[256,3072]{1,0:T(8,128)(2,1)S(1)}, bf16[256,128]{1,0:T(8,128)(2,1)S(1)}, bf16[256,1024]{1,0:T(8,128)(2,1)S(1)}) custom-call(bf16[64,1152]{1,0:T(8,128)(2,1)S(1)} %collective-permute-done.4.refs_0_, bf16[64,1152]{1,0:T(8,128)(2,1)S(1)} %collective-permute-done.5.refs_1_, bf16[64,1152]{1,0:T(8,128)(2,1)S(1)} %collective-permute-done.6.refs_2_, ...), custom_call_target="tpu_custom_call" | custom-call | flops 1610612736 | bytes 6291456 | tf_op jit(solution)/shard_map/project/pallas_call | solution.py:454
  26.6 0.0 collective-permute-done.8.cot_0
  26.6 1.7 %collective-permute-done.9.cot_1 = bf16[64,1024]{1,0:T(8,128)(2,1)S(1)} collective-permute-done((bf16[64,1024]{1,0:T(8,128)(2,1)S(1)}, bf16[64,1024]{1,0:T(8,128)(2,1)S(1)}, u32[]{:S(2)}, u32[]{:S(2)}) %collective-permute-start.9) | collective-permute-done | bytes 131104 | tf_op jit(solution)/shard_map/ppermute | solution.py:1198
  28.3 13.9 %middle.1 = (bf16[96,1024]{1,0:T(8,128)(2,1)S(1)}, bf16[96,1024]{1,0:T(8,128)(2,1)S(1)}, bf16[128,1152]{1,0:T(8,128)(2,1)S(1)}, f32[128,1024]{1,0:T(8,128)S(1)}) custom-call(bf16[256,3072]{1,0:T(8,128)(2,1)S(1)} %get-tuple-element.57.qkv_a.queries, bf16[256,3072]{1,0:T(8,128)(2,1)S(1)} %get-tuple-element.58.qkv_b, ...), custom_call_target="tpu_custom_call" | custom-call | flops 2147483648 | bytes 1000 | tf_op jit(solution)/shard_map/middle/pallas_call | solution.py:871
  42.3 1.3 %collective-permute-start.16 = (bf16[128,1152]{1,0:T(8,128)(2,1)S(1)}, bf16[128,1152]{1,0:T(8,128)(2,1)S(1)}, u32[]{:S(2)}, u32[]{:S(2)}) collective-permute-start(bf16[128,1152]{1,0:T(8,128)(2,1)S(1)} %get-tuple-element.66.grads.grads_0), channel_id=1, source_target_pairs={{0,1},{1,0},{2,3},{3,2},{4,5},{5,4},{6,7},{7,6},{8,9},{9,8},{10,11... | collective-permute-start | bytes 884744 | tf_op jit(solution)/shard_map/ppermute | solution.py:1206
  43.6 1.4 %prefix.1.order.own = bf16[16,2048]{1,0:T(8,128)(2,1)S(1)} custom-call(bf16[256,3072]{1,0:T(8,128)(2,1)S(1)} %get-tuple-element.57.qkv_a.queries, bf16[128,1152]{1,0:T(8,128)(2,1)S(1)} %get-tuple-element.66.grads.grads_0, bf16[16,2048]{1,0:T(8,128)(2,1)S(1)} %get-tuple-element.61.prefix_kv), custom_call_target="tpu_custom_call" | custom-call | flops 1000 | bytes 1000 | tf_op jit(solution)/shard_map/prefix/pallas_call | solution.py:951
  44.9 0.0 collective-permute-start.12
  44.9 1.6 %collective-permute-start.11 = (bf16[16,2048]{1,0:T(8,128)(2,1)S(1)}, bf16[16,2048]{1,0:T(8,128)(2,1)S(1)}, u32[]{:S(2)}, u32[]{:S(2)}) collective-permute-start(bf16[16,2048]{1,0:T(8,128)(2,1)S(1)} %prefix.1.order.own), channel_id=1, source_target_pairs={{0,8},{8,0},{16,24},{24,16},{1,9},{9,1},{17,25},{25,17},{2,10},{10... | collective-permute-start | bytes 196616 | tf_op jit(solution)/shard_map/ppermute | solution.py:1209
  46.5 0.3 collective-permute-start.10
  46.8 0.3 collective-permute-start.15
  47.1 3.7 %query.1 = (f32[128,1024]{1,0:T(8,128)S(1)}, bf16[256,3072]{1,0:T(8,128)(2,1)S(1)}) custom-call(bf16[256,3072]{1,0:T(8,128)(2,1)S(1)} %get-tuple-element.57.qkv_a.queries, bf16[256,3072]{1,0:T(8,128)(2,1)S(1)} %get-tuple-element.58.qkv_b, bf16[256,128]{1,0:T(8,128)(2,1)S(1)} %get-tuple-element.59.marks_a, ...), custom_call_target="tpu_custom_call", output_to_operand_aliasing={{1}: (1, {})} | custom-call | flops 2147483648 | bytes 1000 | tf_op jit(solution)/shard_map/query/pallas_call | solution.py:1065
  50.8 0.0 collective-permute-done.12.part_2
  50.8 0.0 collective-permute-done.11.part_1
  50.8 0.0 collective-permute-done.10.part_0
  50.8 0.1 pack.1
  50.9 0.0 collective-permute-done.16.grads_2
  50.9 0.3 collective-permute-start.17
  51.2 2.1 %collective-permute-start.13 = (bf16[96,1024]{1,0:T(8,128)(2,1)S(1)}, bf16[96,1024]{1,0:T(8,128)(2,1)S(1)}, u32[]{:S(2)}, u32[]{:S(2)}) collective-permute-start(bf16[96,1024]{1,0:T(8,128)(2,1)S(1)} %get-tuple-element.75), channel_id=1, source_target_pairs={{2,0},{3,1},{0,2},{1,3},{10,4},{11,5},{8,6},{9,7},{6,8},{7,9},{4,1... | collective-permute-start | bytes 589832 | tf_op jit(solution)/shard_map/ppermute | solution.py:1214
  53.3 2.1 %collective-permute-start.14 = (bf16[96,1024]{1,0:T(8,128)(2,1)S(1)}, bf16[96,1024]{1,0:T(8,128)(2,1)S(1)}, u32[]{:S(2)}, u32[]{:S(2)}) collective-permute-start(bf16[96,1024]{1,0:T(8,128)(2,1)S(1)} %get-tuple-element.76), channel_id=1, source_target_pairs={{0,0},{1,1},{2,2},{3,3},{8,4},{9,5},{10,6},{11,7},{4,8},{5,9},{6,1... | collective-permute-start | bytes 589832 | tf_op jit(solution)/shard_map/ppermute | solution.py:1214
  55.4 0.0 collective-permute-done.15.grads_1
  55.5 0.0 collective-permute-done.17.grads_3
  55.5 3.8 %final.1 = (bf16[64,1024]{1,0:T(8,128)(2,1)S(1)}, bf16[64,1024]{1,0:T(8,128)(2,1)S(1)}) custom-call(bf16[256,3072]{1,0:T(8,128)(2,1)S(1)} %get-tuple-element.57.qkv_a.queries, bf16[256,3072]{1,0:T(8,128)(2,1)S(1)} %get-tuple-element.77.qkv_b, bf16[256,128]{1,0:T(8,128)(2,1)S(1)} %get-tuple-element.59.marks_a, ...), custom_call_target="tpu_custom_call" | custom-call | flops 1000 | bytes 1000 | tf_op jit(solution)/shard_map/final/pallas_call | solution.py:1135
  59.3 4.5 %collective-permute-start.19 = (bf16[64,1024]{1,0:T(8,128)(2,1)S(1)}, bf16[64,1024]{1,0:T(8,128)(2,1)S(1)}, u32[]{:S(2)}, u32[]{:S(2)}) collective-permute-start(bf16[64,1024]{1,0:T(8,128)(2,1)S(1)} %get-tuple-element.84), channel_id=1, source_target_pairs={{0,0},{1,1},{2,2},{3,3},{8,4},{9,5},{10,6},{11,7},{4,8},{5,9},{6,1... | collective-permute-start | bytes 393224 | tf_op jit(solution)/shard_map/ppermute | solution.py:1228
  63.8 1.5 %collective-permute-start.18 = (bf16[64,1024]{1,0:T(8,128)(2,1)S(1)}, bf16[64,1024]{1,0:T(8,128)(2,1)S(1)}, u32[]{:S(2)}, u32[]{:S(2)}) collective-permute-start(bf16[64,1024]{1,0:T(8,128)(2,1)S(1)} %get-tuple-element.80), channel_id=1, source_target_pairs={{2,0},{3,1},{0,2},{1,3},{10,4},{11,5},{8,6},{9,7},{6,8},{7,9},{4,1... | collective-permute-start | bytes 393224 | tf_op jit(solution)/shard_map/ppermute | solution.py:1228
  65.3 0.0 collective-permute-done.13.msg_0.home_0
  65.4 0.0 collective-permute-done.14.msg_1.home_1
  65.4 0.1 collective-permute-start.22
  65.5 0.3 collective-permute-start.21
  65.8 1.8 %collective-permute-start.20 = (bf16[16,2048]{1,0:T(8,128)(2,1)S(1)}, bf16[16,2048]{1,0:T(8,128)(2,1)S(1)}, u32[]{:S(2)}, u32[]{:S(2)}) collective-permute-start(bf16[16,2048]{1,0:T(8,128)(2,1)S(1)} %unpack.1.part_0), channel_id=1, source_target_pairs={{0,8},{8,0},{16,24},{24,16},{1,9},{9,1},{17,25},{25,17},{2,10},{10... | collective-permute-start | bytes 196616 | tf_op jit(solution)/shard_map/ppermute | solution.py:1230
  67.6 1.0 %land.1 = (bf16[64,16,128]{2,1,0:T(8,128)(2,1)}, f32[2,16,64]{2,1,0:T(8,128)}) custom-call(bf16[96,1024]{1,0:T(8,128)(2,1)S(1)} %collective-permute-done.13.msg_0.home_0, bf16[96,1024]{1,0:T(8,128)(2,1)S(1)} %collective-permute-done.14.msg_1.home_1), custom_call_target="tpu_custom_call" | custom-call | flops 1000 | bytes 1000 | tf_op jit(solution)/shard_map/land/pallas_call | solution.py:421
  68.6 0.8 %collective-permute-done.22.part_3 = bf16[16,2048]{1,0:T(8,128)(2,1)S(1)} collective-permute-done((bf16[16,2048]{1,0:T(8,128)(2,1)S(1)}, bf16[16,2048]{1,0:T(8,128)(2,1)S(1)}, u32[]{:S(2)}, u32[]{:S(2)}) %collective-permute-start.22) | collective-permute-done | bytes 65568 | tf_op jit(solution)/shard_map/ppermute | solution.py:1231
  69.3 0.0 collective-permute-done.21.part_2
  69.3 0.0 collective-permute-done.20.part_1
  69.3 0.0 collective-permute-done.19.home_1
  69.4 0.8 %collective-permute-done.18.home_0 = bf16[64,1024]{1,0:T(8,128)(2,1)S(1)} collective-permute-done((bf16[64,1024]{1,0:T(8,128)(2,1)S(1)}, bf16[64,1024]{1,0:T(8,128)(2,1)S(1)}, u32[]{:S(2)}, u32[]{:S(2)}) %collective-permute-start.18) | collective-permute-done | bytes 131104 | tf_op jit(solution)/shard_map/ppermute | solution.py:1228
  70.2 3.9 %finish.1 = (f32[1024,128]{1,0:T(8,128)}, f32[10,1024]{1,0:T(8,128)}, f32[1024,512]{1,0:T(8,128)}, f32[1,512]{1,0:T(1,128)}, f32[512,2048]{1,0:T(8,128)}, /*index=5*/f32[1,2048]{1,0:T(1,128)}) custom-call(bf16[64,1024]{1,0:T(8,128)(2,1)S(1)} %collective-permute-done.18.home_0, bf16[64,1024]{1,0:T(8,128)(2,1)S(1)} %collective-permute-done.19.home_1, ...), custom_call_target="tpu_custom_call" | custom-call | flops 1000 | bytes 1000 | tf_op jit(solution)/shard_map/finish/pallas_call | solution.py:654
  (3 shorter events, 0.0 us)
Async XLA Ops:
  1.8 12.3 %collective-permute-start = (bf16[64,1152]{1,0:T(8,128)(2,1)S(1)}, bf16[64,1152]{1,0:T(8,128)(2,1)S(1)}, u32[]{:S(2)}, u32[]{:S(2)}) collective-permute-start(bf16[64,1152]{1,0:T(8,128)(2,1)S(1)} %get-tuple-element.51), channel_id=1, source_target_pairs={{0,2},{1,3},{2,0},{3,1},{4,10},{5,11},{6,8},{7,9},{8,6},{9,7},{10,... | collective-permute-start | bytes 442376 | tf_op jit(solution)/shard_map/ppermute | solution.py:1190
  6.6 7.9 %collective-permute-start.1 = (bf16[64,1152]{1,0:T(8,128)(2,1)S(1)}, bf16[64,1152]{1,0:T(8,128)(2,1)S(1)}, u32[]{:S(2)}, u32[]{:S(2)}) collective-permute-start(bf16[64,1152]{1,0:T(8,128)(2,1)S(1)} %get-tuple-element.52), channel_id=1, source_target_pairs={{0,0},{1,1},{2,2},{3,3},{4,8},{5,9},{6,10},{7,11},{8,4},{9,5},{10,... | collective-permute-start | bytes 442376 | tf_op jit(solution)/shard_map/ppermute | solution.py:1190
  14.1 8.8 %copy-start = (f32[1024]{0:T(1024)S(1)}, f32[1024]{0:T(1024)}, u32[]{:S(2)}) copy-start(f32[1024]{0:T(1024)} %param.18) | copy-start | bytes 12292
  14.1 8.8 %copy-start.1 = (f32[1024]{0:T(1024)S(1)}, f32[1024]{0:T(1024)}, u32[]{:S(2)}) copy-start(f32[1024]{0:T(1024)} %param.19) | copy-start | bytes 12292
  14.5 7.8 %collective-permute-start.4 = (bf16[64,1152]{1,0:T(8,128)(2,1)S(1)}, bf16[64,1152]{1,0:T(8,128)(2,1)S(1)}, u32[]{:S(2)}, u32[]{:S(2)}) collective-permute-start(bf16[64,1152]{1,0:T(8,128)(2,1)S(1)} %collective-permute-done.refs_0_.own_0), channel_id=1, source_target_pairs={{0,1},{1,0},{2,3},{3,2},{4,5},{5,4},{6,7},{7,6},{8,9},{9,8},{10,11... | collective-permute-start | bytes 442376 | tf_op jit(solution)/shard_map/ppermute | solution.py:1196
  15.7 2.2 %collective-permute-start.2 = (bf16[64,1152]{1,0:T(8,128)(2,1)S(1)}, bf16[64,1152]{1,0:T(8,128)(2,1)S(1)}, u32[]{:S(2)}, u32[]{:S(2)}) collective-permute-start(bf16[64,1152]{1,0:T(8,128)(2,1)S(1)} %collective-permute-done.refs_0_.own_0), channel_id=1, source_target_pairs={{0,8},{8,0},{16,24},{24,16},{1,9},{9,1},{17,25},{25,17},{2,10},{10... | collective-permute-start | bytes 442376 | tf_op jit(solution)/shard_map/ppermute | solution.py:1197
  15.7 6.6 %collective-permute-start.5 = (bf16[64,1152]{1,0:T(8,128)(2,1)S(1)}, bf16[64,1152]{1,0:T(8,128)(2,1)S(1)}, u32[]{:S(2)}, u32[]{:S(2)}) collective-permute-start(bf16[64,1152]{1,0:T(8,128)(2,1)S(1)} %collective-permute-done.1.refs_1_.own_1), channel_id=1, source_target_pairs={{0,1},{1,0},{2,3},{3,2},{4,5},{5,4},{6,7},{7,6},{8,9},{9,8},{10,11... | collective-permute-start | bytes 442376 | tf_op jit(solution)/shard_map/ppermute | solution.py:1196
  16.0 2.0 %collective-permute-start.3 = (bf16[64,1152]{1,0:T(8,128)(2,1)S(1)}, bf16[64,1152]{1,0:T(8,128)(2,1)S(1)}, u32[]{:S(2)}, u32[]{:S(2)}) collective-permute-start(bf16[64,1152]{1,0:T(8,128)(2,1)S(1)} %collective-permute-done.1.refs_1_.own_1), channel_id=1, source_target_pairs={{0,8},{8,0},{16,24},{24,16},{1,9},{9,1},{17,25},{25,17},{2,10},{10... | collective-permute-start | bytes 442376 | tf_op jit(solution)/shard_map/ppermute | solution.py:1197
  17.9 8.6 %collective-permute-start.8 = (bf16[64,1024]{1,0:T(8,128)(2,1)S(1)}, bf16[64,1024]{1,0:T(8,128)(2,1)S(1)}, u32[]{:S(2)}, u32[]{:S(2)}) collective-permute-start(bf16[64,1024]{1,0:T(8,128)(2,1)S(1)} %get-tuple-element.64), channel_id=1, source_target_pairs={{0,2},{1,3},{2,0},{3,1},{4,10},{5,11},{6,8},{7,9},{8,6},{9,7},{10,... | collective-permute-start | bytes 393224 | tf_op jit(solution)/shard_map/ppermute | solution.py:1198
  19.7 8.6 %collective-permute-start.9 = (bf16[64,1024]{1,0:T(8,128)(2,1)S(1)}, bf16[64,1024]{1,0:T(8,128)(2,1)S(1)}, u32[]{:S(2)}, u32[]{:S(2)}) collective-permute-start(bf16[64,1024]{1,0:T(8,128)(2,1)S(1)} %get-tuple-element.65), channel_id=1, source_target_pairs={{0,0},{1,1},{2,2},{3,3},{4,8},{5,9},{6,10},{7,11},{8,4},{9,5},{10,... | collective-permute-start | bytes 393224 | tf_op jit(solution)/shard_map/ppermute | solution.py:1198
  22.3 2.7 %collective-permute-start.6 = (bf16[64,1152]{1,0:T(8,128)(2,1)S(1)}, bf16[64,1152]{1,0:T(8,128)(2,1)S(1)}, u32[]{:S(2)}, u32[]{:S(2)}) collective-permute-start(bf16[64,1152]{1,0:T(8,128)(2,1)S(1)} %collective-permute-done.4.refs_0_), channel_id=1, source_target_pairs={{0,8},{8,0},{16,24},{24,16},{1,9},{9,1},{17,25},{25,17},{2,10},{10... | collective-permute-start | bytes 442376 | tf_op jit(solution)/shard_map/ppermute | solution.py:1199
  22.4 2.6 %collective-permute-start.7 = (bf16[64,1152]{1,0:T(8,128)(2,1)S(1)}, bf16[64,1152]{1,0:T(8,128)(2,1)S(1)}, u32[]{:S(2)}, u32[]{:S(2)}) collective-permute-start(bf16[64,1152]{1,0:T(8,128)(2,1)S(1)} %collective-permute-done.5.refs_1_), channel_id=1, source_target_pairs={{0,8},{8,0},{16,24},{24,16},{1,9},{9,1},{17,25},{25,17},{2,10},{10... | collective-permute-start | bytes 442376 | tf_op jit(solution)/shard_map/ppermute | solution.py:1199
  25.0 3.3 %copy-start.2 = (f32[1024]{0:T(1024)S(1)}, f32[1024]{0:T(1024)}, u32[]{:S(2)}) copy-start(f32[1024]{0:T(1024)} %param.22) | copy-start | bytes 12292
  25.0 3.3 %copy-start.3 = (f32[1024]{0:T(1024)S(1)}, f32[1024]{0:T(1024)}, u32[]{:S(2)}) copy-start(f32[1024]{0:T(1024)} %param.23) | copy-start | bytes 12292
  42.3 8.7 %collective-permute-start.16 = (bf16[128,1152]{1,0:T(8,128)(2,1)S(1)}, bf16[128,1152]{1,0:T(8,128)(2,1)S(1)}, u32[]{:S(2)}, u32[]{:S(2)}) collective-permute-start(bf16[128,1152]{1,0:T(8,128)(2,1)S(1)} %get-tuple-element.66.grads.grads_0), channel_id=1, source_target_pairs={{0,1},{1,0},{2,3},{3,2},{4,5},{5,4},{6,7},{7,6},{8,9},{9,8},{10,11... | collective-permute-start | bytes 884744 | tf_op jit(solution)/shard_map/ppermute | solution.py:1206
  44.9 5.9 %collective-permute-start.12 = (bf16[16,2048]{1,0:T(8,128)(2,1)S(1)}, bf16[16,2048]{1,0:T(8,128)(2,1)S(1)}, u32[]{:S(2)}, u32[]{:S(2)}) collective-permute-start(bf16[16,2048]{1,0:T(8,128)(2,1)S(1)} %prefix.1.order.own), channel_id=1, source_target_pairs={{0,24},{8,16},{16,8},{24,0},{1,25},{9,17},{17,9},{25,1},{2,26},{10... | collective-permute-start | bytes 196616 | tf_op jit(solution)/shard_map/ppermute | solution.py:1209
  44.9 5.9 %collective-permute-start.11 = (bf16[16,2048]{1,0:T(8,128)(2,1)S(1)}, bf16[16,2048]{1,0:T(8,128)(2,1)S(1)}, u32[]{:S(2)}, u32[]{:S(2)}) collective-permute-start(bf16[16,2048]{1,0:T(8,128)(2,1)S(1)} %prefix.1.order.own), channel_id=1, source_target_pairs={{0,8},{8,0},{16,24},{24,16},{1,9},{9,1},{17,25},{25,17},{2,10},{10... | collective-permute-start | bytes 196616 | tf_op jit(solution)/shard_map/ppermute | solution.py:1209
  46.5 4.3 %collective-permute-start.10 = (bf16[16,2048]{1,0:T(8,128)(2,1)S(1)}, bf16[16,2048]{1,0:T(8,128)(2,1)S(1)}, u32[]{:S(2)}, u32[]{:S(2)}) collective-permute-start(bf16[16,2048]{1,0:T(8,128)(2,1)S(1)} %prefix.1.order.own), channel_id=1, source_target_pairs={{0,16},{8,24},{16,0},{24,8},{1,17},{9,25},{17,1},{25,9},{2,18},{10... | collective-permute-start | bytes 196616 | tf_op jit(solution)/shard_map/ppermute | solution.py:1209
  46.8 8.6 %collective-permute-start.15 = (bf16[128,1152]{1,0:T(8,128)(2,1)S(1)}, bf16[128,1152]{1,0:T(8,128)(2,1)S(1)}, u32[]{:S(2)}, u32[]{:S(2)}) collective-permute-start(bf16[128,1152]{1,0:T(8,128)(2,1)S(1)} %get-tuple-element.66.grads.grads_0), channel_id=1, source_target_pairs={{0,8},{8,0},{16,24},{24,16},{1,9},{9,1},{17,25},{25,17},{2,10},{10... | collective-permute-start | bytes 884744 | tf_op jit(solution)/shard_map/ppermute | solution.py:1207
  50.9 4.5 %collective-permute-start.17 = (bf16[128,1152]{1,0:T(8,128)(2,1)S(1)}, bf16[128,1152]{1,0:T(8,128)(2,1)S(1)}, u32[]{:S(2)}, u32[]{:S(2)}) collective-permute-start(bf16[128,1152]{1,0:T(8,128)(2,1)S(1)} %collective-permute-done.16.grads_2), channel_id=1, source_target_pairs={{0,8},{8,0},{16,24},{24,16},{1,9},{9,1},{17,25},{25,17},{2,10},{10... | collective-permute-start | bytes 884744 | tf_op jit(solution)/shard_map/ppermute | solution.py:1215
  51.2 14.1 %collective-permute-start.13 = (bf16[96,1024]{1,0:T(8,128)(2,1)S(1)}, bf16[96,1024]{1,0:T(8,128)(2,1)S(1)}, u32[]{:S(2)}, u32[]{:S(2)}) collective-permute-start(bf16[96,1024]{1,0:T(8,128)(2,1)S(1)} %get-tuple-element.75), channel_id=1, source_target_pairs={{2,0},{3,1},{0,2},{1,3},{10,4},{11,5},{8,6},{9,7},{6,8},{7,9},{4,1... | collective-permute-start | bytes 589832 | tf_op jit(solution)/shard_map/ppermute | solution.py:1214
  53.3 12.1 %collective-permute-start.14 = (bf16[96,1024]{1,0:T(8,128)(2,1)S(1)}, bf16[96,1024]{1,0:T(8,128)(2,1)S(1)}, u32[]{:S(2)}, u32[]{:S(2)}) collective-permute-start(bf16[96,1024]{1,0:T(8,128)(2,1)S(1)} %get-tuple-element.76), channel_id=1, source_target_pairs={{0,0},{1,1},{2,2},{3,3},{8,4},{9,5},{10,6},{11,7},{4,8},{5,9},{6,1... | collective-permute-start | bytes 589832 | tf_op jit(solution)/shard_map/ppermute | solution.py:1214
  59.3 10.1 %collective-permute-start.19 = (bf16[64,1024]{1,0:T(8,128)(2,1)S(1)}, bf16[64,1024]{1,0:T(8,128)(2,1)S(1)}, u32[]{:S(2)}, u32[]{:S(2)}) collective-permute-start(bf16[64,1024]{1,0:T(8,128)(2,1)S(1)} %get-tuple-element.84), channel_id=1, source_target_pairs={{0,0},{1,1},{2,2},{3,3},{8,4},{9,5},{10,6},{11,7},{4,8},{5,9},{6,1... | collective-permute-start | bytes 393224 | tf_op jit(solution)/shard_map/ppermute | solution.py:1228
  63.8 6.4 %collective-permute-start.18 = (bf16[64,1024]{1,0:T(8,128)(2,1)S(1)}, bf16[64,1024]{1,0:T(8,128)(2,1)S(1)}, u32[]{:S(2)}, u32[]{:S(2)}) collective-permute-start(bf16[64,1024]{1,0:T(8,128)(2,1)S(1)} %get-tuple-element.80), channel_id=1, source_target_pairs={{2,0},{3,1},{0,2},{1,3},{10,4},{11,5},{8,6},{9,7},{6,8},{7,9},{4,1... | collective-permute-start | bytes 393224 | tf_op jit(solution)/shard_map/ppermute | solution.py:1228
  65.4 4.0 %collective-permute-start.22 = (bf16[16,2048]{1,0:T(8,128)(2,1)S(1)}, bf16[16,2048]{1,0:T(8,128)(2,1)S(1)}, u32[]{:S(2)}, u32[]{:S(2)}) collective-permute-start(bf16[16,2048]{1,0:T(8,128)(2,1)S(1)} %unpack.1.part_0), channel_id=1, source_target_pairs={{0,9},{1,8},{2,11},{3,10},{4,13},{5,12},{6,15},{7,14},{8,1},{9,0},... | collective-permute-start | bytes 196616 | tf_op jit(solution)/shard_map/ppermute | solution.py:1231
  65.5 3.9 %collective-permute-start.21 = (bf16[16,2048]{1,0:T(8,128)(2,1)S(1)}, bf16[16,2048]{1,0:T(8,128)(2,1)S(1)}, u32[]{:S(2)}, u32[]{:S(2)}) collective-permute-start(bf16[16,2048]{1,0:T(8,128)(2,1)S(1)} %unpack.1.part_0), channel_id=1, source_target_pairs={{0,1},{1,0},{2,3},{3,2},{4,5},{5,4},{6,7},{7,6},{8,9},{9,8},{10,11... | collective-permute-start | bytes 196616 | tf_op jit(solution)/shard_map/ppermute | solution.py:1230
  65.8 3.6 %collective-permute-start.20 = (bf16[16,2048]{1,0:T(8,128)(2,1)S(1)}, bf16[16,2048]{1,0:T(8,128)(2,1)S(1)}, u32[]{:S(2)}, u32[]{:S(2)}) collective-permute-start(bf16[16,2048]{1,0:T(8,128)(2,1)S(1)} %unpack.1.part_0), channel_id=1, source_target_pairs={{0,8},{8,0},{16,24},{24,16},{1,9},{9,1},{17,25},{25,17},{2,10},{10... | collective-permute-start | bytes 196616 | tf_op jit(solution)/shard_map/ppermute | solution.py:1230

commit v8 on v7

--- a/solution.py
+++ b/solution.py
@@ -1230,7 +1230,7 @@
     gathered += [lax.ppermute(gathered[0], "seq", swap_core), lax.ppermute(gathered[0], "blk", swap_y)]
     gathered += [lax.ppermute(gathered[0], everyone, swap_both)]
     input_grad, summed = finish(finals, gathered, near_embed, inner, turned)
-    block_out, log_total = land(count, after(home, final_0), half, width)
+    block_out, log_total = land(count, after(home, gathered[0]), half, width)
     return (block_out, input_grad, summed[0], summed[1], summed[2], summed[3], summed[4], log_total)
 
 

time: 75.1 us -> 74.2 us (0.988)
  starting transfers between devices: 30.1 us -> 29.1 us
    ppermute x2, starting transfers between devices: 6.07 us -> 5.15 us  [body_rows(): lax.ppermute(m, everyone, back[k])]
  transfers between devices with their start and end apart: 23 -> 23, of which waited for: 4 -> 4; matrix products, arithmetic and copies ran while one was open for 0% -> 0% of each run, Pallas kernels for 27% -> 28%
where the time goes in v8:
time: 74.2 us; the launch traced here: 73.7 us
  Pallas kernels  39.4 us (53%)
  starting transfers between devices  29.1 us (39%)
  waiting for transfers between devices  4.05 us (5%)
  between operations  1.09 us (1%)
    pallas_call x1, Pallas kernels, middle_part(): pl.pallas_call(partial(middle_kernel, count), in_specs=[vmem()] * 11 + [h...  13.9 us
    ppermute x2, starting transfers between devices, body_rows(): own = [lax.ppermute(m, everyone, there[k]) for k, m in enumerate(out_msgs)]  6.68 us
    pallas_call x1, Pallas kernels, adapter_forward(): pl.pallas_call(adapter_kernel, in_specs=[hbm()] * 6, out_specs=[vmem()] *...  5.59 us
    ppermute x2, starting transfers between devices, body_rows(): lax.ppermute(m, everyone, back[k])  5.15 us
    ppermute x2, starting transfers between devices, body_rows(): lax.ppermute(m, everyone, there[k])  4.32 us
    ppermute x2, starting transfers between devices, body_rows(): home = [lax.ppermute(m, everyone, back[k]) for k, m in enumerate(packed)]  4.22 us
    pallas_call x1, Pallas kernels, finish(): pl.pallas_call(adapter_back_kernel, in_specs=[vmem()] * 9, out_specs=[hbm...  3.95 us
    pallas_call x1, Pallas kernels, final_part(): pl.pallas_call(final_kernel, in_specs=[vmem()] * 14, out_specs=[vmem()] *...  3.81 us
  transfers between devices with their start and end apart: 23, of which 4 were waited for; matrix products, arithmetic and copies ran while one was open for 0% of the time, Pallas kernels for 28%

profile of v8, /device:TPU:1, one launch (start us, length us, event | category | flops | bytes accessed | tf_op | source)
XLA Modules:
  0.0 73.7 jit_solution(1211197416899261162)
XLA Ops:
  0.6 1.2 %split.2 = (bf16[64,1152]{1,0:T(8,128)(2,1)S(1)}, bf16[64,1152]{1,0:T(8,128)(2,1)S(1)}) custom-call(bf16[64,16,128]{2,1,0:T(8,128)(2,1)} %bitcast.37, s32[2,64]{1,0:T(2,128)} %bitcast.44), custom_call_target="tpu_custom_call" | custom-call | flops 2147483648 | bytes 1000 | tf_op jit(solution)/shard_map/split/pallas_call | solution.py:380
  1.8 4.8 %collective-permute-start = (bf16[64,1152]{1,0:T(8,128)(2,1)S(1)}, bf16[64,1152]{1,0:T(8,128)(2,1)S(1)}, u32[]{:S(2)}, u32[]{:S(2)}) collective-permute-start(bf16[64,1152]{1,0:T(8,128)(2,1)S(1)} %get-tuple-element.51), channel_id=1, source_target_pairs={{0,2},{1,3},{2,0},{3,1},{4,10},{5,11},{6,8},{7,9},{8,6},{9,7},{10,... | collective-permute-start | bytes 442376 | tf_op jit(solution)/shard_map/ppermute | solution.py:1190
  6.6 1.9 %collective-permute-start.1 = (bf16[64,1152]{1,0:T(8,128)(2,1)S(1)}, bf16[64,1152]{1,0:T(8,128)(2,1)S(1)}, u32[]{:S(2)}, u32[]{:S(2)}) collective-permute-start(bf16[64,1152]{1,0:T(8,128)(2,1)S(1)} %get-tuple-element.52), channel_id=1, source_target_pairs={{0,0},{1,1},{2,2},{3,3},{4,8},{5,9},{6,10},{7,11},{8,4},{9,5},{10,... | collective-permute-start | bytes 442376 | tf_op jit(solution)/shard_map/ppermute | solution.py:1190
  8.5 5.6 %adapter.1 = (bf16[16,2048]{1,0:T(8,128)(2,1)S(1)}, f32[16,512]{1,0:T(8,128)S(1)}, bf16[1024,3072]{1,0:T(8,128)(2,1)S(1)}, bf16[3072,1024]{1,0:T(8,128)(2,1)S(1)...) custom-call(f32[10,1024]{1,0:T(8,128)} %h_embed.1, f32[1024,512]{1,0:T(8,128)} %w_mlp1.1, f32[1,512]{1,0:T(1,128)} %bitcast.42, ...), custom_call_target="tpu_custom_call" | custom-call | flops 4294967296 | bytes 6291456 | tf_op jit(solution)/shard_map/adapter/pallas_call | solution.py:557
  14.1 0.0 copy-start
  14.1 0.0 copy-start.1
  14.1 0.0 collective-permute-done.refs_0_.own_0
  14.1 0.4 collective-permute-done.1.refs_1_.own_1
  14.5 1.2 %collective-permute-start.4 = (bf16[64,1152]{1,0:T(8,128)(2,1)S(1)}, bf16[64,1152]{1,0:T(8,128)(2,1)S(1)}, u32[]{:S(2)}, u32[]{:S(2)}) collective-permute-start(bf16[64,1152]{1,0:T(8,128)(2,1)S(1)} %collective-permute-done.refs_0_.own_0), channel_id=1, source_target_pairs={{0,1},{1,0},{2,3},{3,2},{4,5},{5,4},{6,7},{7,6},{8,9},{9,8},{10,11... | collective-permute-start | bytes 442376 | tf_op jit(solution)/shard_map/ppermute | solution.py:1196
  15.7 0.0 collective-permute-start.2
  15.7 0.2 collective-permute-start.5
  16.0 0.8 %collective-permute-start.3 = (bf16[64,1152]{1,0:T(8,128)(2,1)S(1)}, bf16[64,1152]{1,0:T(8,128)(2,1)S(1)}, u32[]{:S(2)}, u32[]{:S(2)}) collective-permute-start(bf16[64,1152]{1,0:T(8,128)(2,1)S(1)} %collective-permute-done.1.refs_1_.own_1), channel_id=1, source_target_pairs={{0,8},{8,0},{16,24},{24,16},{1,9},{9,1},{17,25},{25,17},{2,10},{10... | collective-permute-start | bytes 442376 | tf_op jit(solution)/shard_map/ppermute | solution.py:1197
  16.8 1.2 %split.3 = (bf16[64,1024]{1,0:T(8,128)(2,1)S(1)}, bf16[64,1024]{1,0:T(8,128)(2,1)S(1)}) custom-call(bf16[64,16,128]{2,1,0:T(8,128)(2,1)} %bitcast.38), custom_call_target="tpu_custom_call" | custom-call | flops 2147483648 | bytes 1000 | tf_op jit(solution)/shard_map/split/pallas_call | solution.py:380
  17.9 0.0 collective-permute-done.2.refs_2_
  17.9 0.0 collective-permute-done.3.refs_3_
  17.9 1.8 %collective-permute-start.8 = (bf16[64,1024]{1,0:T(8,128)(2,1)S(1)}, bf16[64,1024]{1,0:T(8,128)(2,1)S(1)}, u32[]{:S(2)}, u32[]{:S(2)}) collective-permute-start(bf16[64,1024]{1,0:T(8,128)(2,1)S(1)} %get-tuple-element.64), channel_id=1, source_target_pairs={{0,2},{1,3},{2,0},{3,1},{4,10},{5,11},{6,8},{7,9},{8,6},{9,7},{10,... | collective-permute-start | bytes 393224 | tf_op jit(solution)/shard_map/ppermute | solution.py:1198
  19.7 2.5 %collective-permute-start.9 = (bf16[64,1024]{1,0:T(8,128)(2,1)S(1)}, bf16[64,1024]{1,0:T(8,128)(2,1)S(1)}, u32[]{:S(2)}, u32[]{:S(2)}) collective-permute-start(bf16[64,1024]{1,0:T(8,128)(2,1)S(1)} %get-tuple-element.65), channel_id=1, source_target_pairs={{0,0},{1,1},{2,2},{3,3},{4,8},{5,9},{6,10},{7,11},{8,4},{9,5},{10,... | collective-permute-start | bytes 393224 | tf_op jit(solution)/shard_map/ppermute | solution.py:1198
  22.3 0.0 collective-permute-done.4.refs_0_
  22.3 0.1 collective-permute-start.6
  22.4 0.0 collective-permute-done.5.refs_1_
  22.4 0.5 collective-permute-start.7
  22.9 0.0 copy-done
  22.9 0.0 copy-done.1
  22.9 2.1 %project.2 = (bf16[256,3072]{1,0:T(8,128)(2,1)S(1)}, bf16[256,128]{1,0:T(8,128)(2,1)S(1)}) custom-call(bf16[64,1152]{1,0:T(8,128)(2,1)S(1)} %collective-permute-done.refs_0_.own_0, bf16[64,1152]{1,0:T(8,128)(2,1)S(1)} %collective-permute-done.1.refs_1_.own_1, bf16[64,1152]{1,0:T(8,128)(2,1)S(1)} %collective-permute-done.2.refs_2_, ...), custom_call_target="tpu_custom_call" | custom-call | flops 1610612736 | bytes 6291456 | tf_op jit(solution)/shard_map/project/pallas_call | solution.py:454
  25.0 0.0 copy-start.2
  25.0 0.0 copy-start.3
  25.0 0.0 collective-permute-done.6.refs_2_
  25.0 0.0 collective-permute-done.7.refs_3_
  25.0 1.6 %project.3 = (bf16[256,3072]{1,0:T(8,128)(2,1)S(1)}, bf16[256,128]{1,0:T(8,128)(2,1)S(1)}, bf16[256,1024]{1,0:T(8,128)(2,1)S(1)}) custom-call(bf16[64,1152]{1,0:T(8,128)(2,1)S(1)} %collective-permute-done.4.refs_0_, bf16[64,1152]{1,0:T(8,128)(2,1)S(1)} %collective-permute-done.5.refs_1_, bf16[64,1152]{1,0:T(8,128)(2,1)S(1)} %collective-permute-done.6.refs_2_, ...), custom_call_target="tpu_custom_call" | custom-call | flops 1610612736 | bytes 6291456 | tf_op jit(solution)/shard_map/project/pallas_call | solution.py:454
  26.6 0.0 collective-permute-done.8.cot_0
  26.6 1.7 %collective-permute-done.9.cot_1 = bf16[64,1024]{1,0:T(8,128)(2,1)S(1)} collective-permute-done((bf16[64,1024]{1,0:T(8,128)(2,1)S(1)}, bf16[64,1024]{1,0:T(8,128)(2,1)S(1)}, u32[]{:S(2)}, u32[]{:S(2)}) %collective-permute-start.9) | collective-permute-done | bytes 131104 | tf_op jit(solution)/shard_map/ppermute | solution.py:1198
  28.3 13.9 %middle.1 = (bf16[96,1024]{1,0:T(8,128)(2,1)S(1)}, bf16[96,1024]{1,0:T(8,128)(2,1)S(1)}, bf16[128,1152]{1,0:T(8,128)(2,1)S(1)}, f32[128,1024]{1,0:T(8,128)S(1)}) custom-call(bf16[256,3072]{1,0:T(8,128)(2,1)S(1)} %get-tuple-element.57.qkv_a.queries, bf16[256,3072]{1,0:T(8,128)(2,1)S(1)} %get-tuple-element.58.qkv_b, ...), custom_call_target="tpu_custom_call" | custom-call | flops 2147483648 | bytes 1000 | tf_op jit(solution)/shard_map/middle/pallas_call | solution.py:871
  42.3 1.3 %collective-permute-start.16 = (bf16[128,1152]{1,0:T(8,128)(2,1)S(1)}, bf16[128,1152]{1,0:T(8,128)(2,1)S(1)}, u32[]{:S(2)}, u32[]{:S(2)}) collective-permute-start(bf16[128,1152]{1,0:T(8,128)(2,1)S(1)} %get-tuple-element.66.grads.grads_0), channel_id=1, source_target_pairs={{0,1},{1,0},{2,3},{3,2},{4,5},{5,4},{6,7},{7,6},{8,9},{9,8},{10,11... | collective-permute-start | bytes 884744 | tf_op jit(solution)/shard_map/ppermute | solution.py:1206
  43.6 1.4 %prefix.1.order.own = bf16[16,2048]{1,0:T(8,128)(2,1)S(1)} custom-call(bf16[256,3072]{1,0:T(8,128)(2,1)S(1)} %get-tuple-element.57.qkv_a.queries, bf16[128,1152]{1,0:T(8,128)(2,1)S(1)} %get-tuple-element.66.grads.grads_0, bf16[16,2048]{1,0:T(8,128)(2,1)S(1)} %get-tuple-element.61.prefix_kv), custom_call_target="tpu_custom_call" | custom-call | flops 1000 | bytes 1000 | tf_op jit(solution)/shard_map/prefix/pallas_call | solution.py:951
  44.9 0.0 collective-permute-start.12
  44.9 1.6 %collective-permute-start.11 = (bf16[16,2048]{1,0:T(8,128)(2,1)S(1)}, bf16[16,2048]{1,0:T(8,128)(2,1)S(1)}, u32[]{:S(2)}, u32[]{:S(2)}) collective-permute-start(bf16[16,2048]{1,0:T(8,128)(2,1)S(1)} %prefix.1.order.own), channel_id=1, source_target_pairs={{0,8},{8,0},{16,24},{24,16},{1,9},{9,1},{17,25},{25,17},{2,10},{10... | collective-permute-start | bytes 196616 | tf_op jit(solution)/shard_map/ppermute | solution.py:1209
  46.5 0.3 collective-permute-start.10
  46.8 0.3 collective-permute-start.15
  47.1 3.7 %query.1 = (f32[128,1024]{1,0:T(8,128)S(1)}, bf16[256,3072]{1,0:T(8,128)(2,1)S(1)}) custom-call(bf16[256,3072]{1,0:T(8,128)(2,1)S(1)} %get-tuple-element.57.qkv_a.queries, bf16[256,3072]{1,0:T(8,128)(2,1)S(1)} %get-tuple-element.58.qkv_b, bf16[256,128]{1,0:T(8,128)(2,1)S(1)} %get-tuple-element.59.marks_a, ...), custom_call_target="tpu_custom_call", output_to_operand_aliasing={{1}: (1, {})} | custom-call | flops 2147483648 | bytes 1000 | tf_op jit(solution)/shard_map/query/pallas_call | solution.py:1065
  50.8 0.0 collective-permute-done.12.part_2
  50.8 0.0 collective-permute-done.11.part_1
  50.8 0.0 collective-permute-done.10.part_0
  50.8 0.1 pack.1
  50.9 0.0 collective-permute-done.16.grads_2
  50.9 0.3 collective-permute-start.17
  51.2 2.1 %collective-permute-start.13 = (bf16[96,1024]{1,0:T(8,128)(2,1)S(1)}, bf16[96,1024]{1,0:T(8,128)(2,1)S(1)}, u32[]{:S(2)}, u32[]{:S(2)}) collective-permute-start(bf16[96,1024]{1,0:T(8,128)(2,1)S(1)} %get-tuple-element.75), channel_id=1, source_target_pairs={{2,0},{3,1},{0,2},{1,3},{10,4},{11,5},{8,6},{9,7},{6,8},{7,9},{4,1... | collective-permute-start | bytes 589832 | tf_op jit(solution)/shard_map/ppermute | solution.py:1214
  53.3 2.1 %collective-permute-start.14 = (bf16[96,1024]{1,0:T(8,128)(2,1)S(1)}, bf16[96,1024]{1,0:T(8,128)(2,1)S(1)}, u32[]{:S(2)}, u32[]{:S(2)}) collective-permute-start(bf16[96,1024]{1,0:T(8,128)(2,1)S(1)} %get-tuple-element.76), channel_id=1, source_target_pairs={{0,0},{1,1},{2,2},{3,3},{8,4},{9,5},{10,6},{11,7},{4,8},{5,9},{6,1... | collective-permute-start | bytes 589832 | tf_op jit(solution)/shard_map/ppermute | solution.py:1214
  55.4 0.0 collective-permute-done.15.grads_1
  55.5 0.0 collective-permute-done.17.grads_3
  55.5 3.8 %final.1 = (bf16[64,1024]{1,0:T(8,128)(2,1)S(1)}, bf16[64,1024]{1,0:T(8,128)(2,1)S(1)}) custom-call(bf16[256,3072]{1,0:T(8,128)(2,1)S(1)} %get-tuple-element.57.qkv_a.queries, bf16[256,3072]{1,0:T(8,128)(2,1)S(1)} %get-tuple-element.80.qkv_b, bf16[256,128]{1,0:T(8,128)(2,1)S(1)} %get-tuple-element.59.marks_a, ...), custom_call_target="tpu_custom_call" | custom-call | flops 1000 | bytes 1000 | tf_op jit(solution)/shard_map/final/pallas_call | solution.py:1135
  59.3 1.7 %collective-permute-start.18 = (bf16[64,1024]{1,0:T(8,128)(2,1)S(1)}, bf16[64,1024]{1,0:T(8,128)(2,1)S(1)}, u32[]{:S(2)}, u32[]{:S(2)}) collective-permute-start(bf16[64,1024]{1,0:T(8,128)(2,1)S(1)} %get-tuple-element.83), channel_id=1, source_target_pairs={{2,0},{3,1},{0,2},{1,3},{10,4},{11,5},{8,6},{9,7},{6,8},{7,9},{4,1... | collective-permute-start | bytes 393224 | tf_op jit(solution)/shard_map/ppermute | solution.py:1228
  61.0 3.4 %collective-permute-start.19 = (bf16[64,1024]{1,0:T(8,128)(2,1)S(1)}, bf16[64,1024]{1,0:T(8,128)(2,1)S(1)}, u32[]{:S(2)}, u32[]{:S(2)}) collective-permute-start(bf16[64,1024]{1,0:T(8,128)(2,1)S(1)} %get-tuple-element.84), channel_id=1, source_target_pairs={{0,0},{1,1},{2,2},{3,3},{8,4},{9,5},{10,6},{11,7},{4,8},{5,9},{6,1... | collective-permute-start | bytes 393224 | tf_op jit(solution)/shard_map/ppermute | solution.py:1228
  64.4 0.0 collective-permute-done.13.home_0.msg_0
  64.4 0.0 collective-permute-done.14.home_1.msg_1
  64.5 0.1 collective-permute-start.22
  64.6 0.3 collective-permute-start.21
  64.9 1.8 %collective-permute-start.20 = (bf16[16,2048]{1,0:T(8,128)(2,1)S(1)}, bf16[16,2048]{1,0:T(8,128)(2,1)S(1)}, u32[]{:S(2)}, u32[]{:S(2)}) collective-permute-start(bf16[16,2048]{1,0:T(8,128)(2,1)S(1)} %unpack.1.part_0), channel_id=1, source_target_pairs={{0,8},{8,0},{16,24},{24,16},{1,9},{9,1},{17,25},{25,17},{2,10},{10... | collective-permute-start | bytes 196616 | tf_op jit(solution)/shard_map/ppermute | solution.py:1230
  66.7 1.0 %land.1 = (bf16[64,16,128]{2,1,0:T(8,128)(2,1)}, f32[2,16,64]{2,1,0:T(8,128)}) custom-call(bf16[96,1024]{1,0:T(8,128)(2,1)S(1)} %collective-permute-done.13.home_0.msg_0, bf16[96,1024]{1,0:T(8,128)(2,1)S(1)} %collective-permute-done.14.home_1.msg_1), custom_call_target="tpu_custom_call" | custom-call | flops 1000 | bytes 1000 | tf_op jit(solution)/shard_map/land/pallas_call | solution.py:421
  67.7 0.8 %collective-permute-done.22.part_3 = bf16[16,2048]{1,0:T(8,128)(2,1)S(1)} collective-permute-done((bf16[16,2048]{1,0:T(8,128)(2,1)S(1)}, bf16[16,2048]{1,0:T(8,128)(2,1)S(1)}, u32[]{:S(2)}, u32[]{:S(2)}) %collective-permute-start.22) | collective-permute-done | bytes 65568 | tf_op jit(solution)/shard_map/ppermute | solution.py:1231
  68.4 0.0 collective-permute-done.21.part_2
  68.5 0.0 collective-permute-done.20.part_1
  68.5 0.0 collective-permute-done.18.home_0
  68.5 1.1 %collective-permute-done.19.home_1 = bf16[64,1024]{1,0:T(8,128)(2,1)S(1)} collective-permute-done((bf16[64,1024]{1,0:T(8,128)(2,1)S(1)}, bf16[64,1024]{1,0:T(8,128)(2,1)S(1)}, u32[]{:S(2)}, u32[]{:S(2)}) %collective-permute-start.19) | collective-permute-done | bytes 131104 | tf_op jit(solution)/shard_map/ppermute | solution.py:1228
  69.6 3.9 %finish.1 = (f32[1024,128]{1,0:T(8,128)}, f32[10,1024]{1,0:T(8,128)}, f32[1024,512]{1,0:T(8,128)}, f32[1,512]{1,0:T(1,128)}, f32[512,2048]{1,0:T(8,128)}, /*index=5*/f32[1,2048]{1,0:T(1,128)}) custom-call(bf16[64,1024]{1,0:T(8,128)(2,1)S(1)} %collective-permute-done.18.home_0, bf16[64,1024]{1,0:T(8,128)(2,1)S(1)} %collective-permute-done.19.home_1, ...), custom_call_target="tpu_custom_call" | custom-call | flops 1000 | bytes 1000 | tf_op jit(solution)/shard_map/finish/pallas_call | solution.py:654
  (3 shorter events, 0.0 us)
Async XLA Ops:
  1.8 12.3 %collective-permute-start = (bf16[64,1152]{1,0:T(8,128)(2,1)S(1)}, bf16[64,1152]{1,0:T(8,128)(2,1)S(1)}, u32[]{:S(2)}, u32[]{:S(2)}) collective-permute-start(bf16[64,1152]{1,0:T(8,128)(2,1)S(1)} %get-tuple-element.51), channel_id=1, source_target_pairs={{0,2},{1,3},{2,0},{3,1},{4,10},{5,11},{6,8},{7,9},{8,6},{9,7},{10,... | collective-permute-start | bytes 442376 | tf_op jit(solution)/shard_map/ppermute | solution.py:1190
  6.6 7.9 %collective-permute-start.1 = (bf16[64,1152]{1,0:T(8,128)(2,1)S(1)}, bf16[64,1152]{1,0:T(8,128)(2,1)S(1)}, u32[]{:S(2)}, u32[]{:S(2)}) collective-permute-start(bf16[64,1152]{1,0:T(8,128)(2,1)S(1)} %get-tuple-element.52), channel_id=1, source_target_pairs={{0,0},{1,1},{2,2},{3,3},{4,8},{5,9},{6,10},{7,11},{8,4},{9,5},{10,... | collective-permute-start | bytes 442376 | tf_op jit(solution)/shard_map/ppermute | solution.py:1190
  14.1 8.8 %copy-start = (f32[1024]{0:T(1024)S(1)}, f32[1024]{0:T(1024)}, u32[]{:S(2)}) copy-start(f32[1024]{0:T(1024)} %param.18) | copy-start | bytes 12292
  14.1 8.8 %copy-start.1 = (f32[1024]{0:T(1024)S(1)}, f32[1024]{0:T(1024)}, u32[]{:S(2)}) copy-start(f32[1024]{0:T(1024)} %param.19) | copy-start | bytes 12292
  14.5 7.8 %collective-permute-start.4 = (bf16[64,1152]{1,0:T(8,128)(2,1)S(1)}, bf16[64,1152]{1,0:T(8,128)(2,1)S(1)}, u32[]{:S(2)}, u32[]{:S(2)}) collective-permute-start(bf16[64,1152]{1,0:T(8,128)(2,1)S(1)} %collective-permute-done.refs_0_.own_0), channel_id=1, source_target_pairs={{0,1},{1,0},{2,3},{3,2},{4,5},{5,4},{6,7},{7,6},{8,9},{9,8},{10,11... | collective-permute-start | bytes 442376 | tf_op jit(solution)/shard_map/ppermute | solution.py:1196
  15.7 2.2 %collective-permute-start.2 = (bf16[64,1152]{1,0:T(8,128)(2,1)S(1)}, bf16[64,1152]{1,0:T(8,128)(2,1)S(1)}, u32[]{:S(2)}, u32[]{:S(2)}) collective-permute-start(bf16[64,1152]{1,0:T(8,128)(2,1)S(1)} %collective-permute-done.refs_0_.own_0), channel_id=1, source_target_pairs={{0,8},{8,0},{16,24},{24,16},{1,9},{9,1},{17,25},{25,17},{2,10},{10... | collective-permute-start | bytes 442376 | tf_op jit(solution)/shard_map/ppermute | solution.py:1197
  15.7 6.6 %collective-permute-start.5 = (bf16[64,1152]{1,0:T(8,128)(2,1)S(1)}, bf16[64,1152]{1,0:T(8,128)(2,1)S(1)}, u32[]{:S(2)}, u32[]{:S(2)}) collective-permute-start(bf16[64,1152]{1,0:T(8,128)(2,1)S(1)} %collective-permute-done.1.refs_1_.own_1), channel_id=1, source_target_pairs={{0,1},{1,0},{2,3},{3,2},{4,5},{5,4},{6,7},{7,6},{8,9},{9,8},{10,11... | collective-permute-start | bytes 442376 | tf_op jit(solution)/shard_map/ppermute | solution.py:1196
  16.0 2.0 %collective-permute-start.3 = (bf16[64,1152]{1,0:T(8,128)(2,1)S(1)}, bf16[64,1152]{1,0:T(8,128)(2,1)S(1)}, u32[]{:S(2)}, u32[]{:S(2)}) collective-permute-start(bf16[64,1152]{1,0:T(8,128)(2,1)S(1)} %collective-permute-done.1.refs_1_.own_1), channel_id=1, source_target_pairs={{0,8},{8,0},{16,24},{24,16},{1,9},{9,1},{17,25},{25,17},{2,10},{10... | collective-permute-start | bytes 442376 | tf_op jit(solution)/shard_map/ppermute | solution.py:1197
  17.9 8.6 %collective-permute-start.8 = (bf16[64,1024]{1,0:T(8,128)(2,1)S(1)}, bf16[64,1024]{1,0:T(8,128)(2,1)S(1)}, u32[]{:S(2)}, u32[]{:S(2)}) collective-permute-start(bf16[64,1024]{1,0:T(8,128)(2,1)S(1)} %get-tuple-element.64), channel_id=1, source_target_pairs={{0,2},{1,3},{2,0},{3,1},{4,10},{5,11},{6,8},{7,9},{8,6},{9,7},{10,... | collective-permute-start | bytes 393224 | tf_op jit(solution)/shard_map/ppermute | solution.py:1198
  19.7 8.6 %collective-permute-start.9 = (bf16[64,1024]{1,0:T(8,128)(2,1)S(1)}, bf16[64,1024]{1,0:T(8,128)(2,1)S(1)}, u32[]{:S(2)}, u32[]{:S(2)}) collective-permute-start(bf16[64,1024]{1,0:T(8,128)(2,1)S(1)} %get-tuple-element.65), channel_id=1, source_target_pairs={{0,0},{1,1},{2,2},{3,3},{4,8},{5,9},{6,10},{7,11},{8,4},{9,5},{10,... | collective-permute-start | bytes 393224 | tf_op jit(solution)/shard_map/ppermute | solution.py:1198
  22.3 2.7 %collective-permute-start.6 = (bf16[64,1152]{1,0:T(8,128)(2,1)S(1)}, bf16[64,1152]{1,0:T(8,128)(2,1)S(1)}, u32[]{:S(2)}, u32[]{:S(2)}) collective-permute-start(bf16[64,1152]{1,0:T(8,128)(2,1)S(1)} %collective-permute-done.4.refs_0_), channel_id=1, source_target_pairs={{0,8},{8,0},{16,24},{24,16},{1,9},{9,1},{17,25},{25,17},{2,10},{10... | collective-permute-start | bytes 442376 | tf_op jit(solution)/shard_map/ppermute | solution.py:1199
  22.4 2.6 %collective-permute-start.7 = (bf16[64,1152]{1,0:T(8,128)(2,1)S(1)}, bf16[64,1152]{1,0:T(8,128)(2,1)S(1)}, u32[]{:S(2)}, u32[]{:S(2)}) collective-permute-start(bf16[64,1152]{1,0:T(8,128)(2,1)S(1)} %collective-permute-done.5.refs_1_), channel_id=1, source_target_pairs={{0,8},{8,0},{16,24},{24,16},{1,9},{9,1},{17,25},{25,17},{2,10},{10... | collective-permute-start | bytes 442376 | tf_op jit(solution)/shard_map/ppermute | solution.py:1199
  25.0 3.3 %copy-start.2 = (f32[1024]{0:T(1024)S(1)}, f32[1024]{0:T(1024)}, u32[]{:S(2)}) copy-start(f32[1024]{0:T(1024)} %param.22) | copy-start | bytes 12292
  25.0 3.3 %copy-start.3 = (f32[1024]{0:T(1024)S(1)}, f32[1024]{0:T(1024)}, u32[]{:S(2)}) copy-start(f32[1024]{0:T(1024)} %param.23) | copy-start | bytes 12292
  42.3 8.7 %collective-permute-start.16 = (bf16[128,1152]{1,0:T(8,128)(2,1)S(1)}, bf16[128,1152]{1,0:T(8,128)(2,1)S(1)}, u32[]{:S(2)}, u32[]{:S(2)}) collective-permute-start(bf16[128,1152]{1,0:T(8,128)(2,1)S(1)} %get-tuple-element.66.grads.grads_0), channel_id=1, source_target_pairs={{0,1},{1,0},{2,3},{3,2},{4,5},{5,4},{6,7},{7,6},{8,9},{9,8},{10,11... | collective-permute-start | bytes 884744 | tf_op jit(solution)/shard_map/ppermute | solution.py:1206
  44.9 5.9 %collective-permute-start.12 = (bf16[16,2048]{1,0:T(8,128)(2,1)S(1)}, bf16[16,2048]{1,0:T(8,128)(2,1)S(1)}, u32[]{:S(2)}, u32[]{:S(2)}) collective-permute-start(bf16[16,2048]{1,0:T(8,128)(2,1)S(1)} %prefix.1.order.own), channel_id=1, source_target_pairs={{0,24},{8,16},{16,8},{24,0},{1,25},{9,17},{17,9},{25,1},{2,26},{10... | collective-permute-start | bytes 196616 | tf_op jit(solution)/shard_map/ppermute | solution.py:1209
  44.9 5.9 %collective-permute-start.11 = (bf16[16,2048]{1,0:T(8,128)(2,1)S(1)}, bf16[16,2048]{1,0:T(8,128)(2,1)S(1)}, u32[]{:S(2)}, u32[]{:S(2)}) collective-permute-start(bf16[16,2048]{1,0:T(8,128)(2,1)S(1)} %prefix.1.order.own), channel_id=1, source_target_pairs={{0,8},{8,0},{16,24},{24,16},{1,9},{9,1},{17,25},{25,17},{2,10},{10... | collective-permute-start | bytes 196616 | tf_op jit(solution)/shard_map/ppermute | solution.py:1209
  46.5 4.3 %collective-permute-start.10 = (bf16[16,2048]{1,0:T(8,128)(2,1)S(1)}, bf16[16,2048]{1,0:T(8,128)(2,1)S(1)}, u32[]{:S(2)}, u32[]{:S(2)}) collective-permute-start(bf16[16,2048]{1,0:T(8,128)(2,1)S(1)} %prefix.1.order.own), channel_id=1, source_target_pairs={{0,16},{8,24},{16,0},{24,8},{1,17},{9,25},{17,1},{25,9},{2,18},{10... | collective-permute-start | bytes 196616 | tf_op jit(solution)/shard_map/ppermute | solution.py:1209
  46.8 8.6 %collective-permute-start.15 = (bf16[128,1152]{1,0:T(8,128)(2,1)S(1)}, bf16[128,1152]{1,0:T(8,128)(2,1)S(1)}, u32[]{:S(2)}, u32[]{:S(2)}) collective-permute-start(bf16[128,1152]{1,0:T(8,128)(2,1)S(1)} %get-tuple-element.66.grads.grads_0), channel_id=1, source_target_pairs={{0,8},{8,0},{16,24},{24,16},{1,9},{9,1},{17,25},{25,17},{2,10},{10... | collective-permute-start | bytes 884744 | tf_op jit(solution)/shard_map/ppermute | solution.py:1207
  50.9 4.5 %collective-permute-start.17 = (bf16[128,1152]{1,0:T(8,128)(2,1)S(1)}, bf16[128,1152]{1,0:T(8,128)(2,1)S(1)}, u32[]{:S(2)}, u32[]{:S(2)}) collective-permute-start(bf16[128,1152]{1,0:T(8,128)(2,1)S(1)} %collective-permute-done.16.grads_2), channel_id=1, source_target_pairs={{0,8},{8,0},{16,24},{24,16},{1,9},{9,1},{17,25},{25,17},{2,10},{10... | collective-permute-start | bytes 884744 | tf_op jit(solution)/shard_map/ppermute | solution.py:1215
  51.2 13.2 %collective-permute-start.13 = (bf16[96,1024]{1,0:T(8,128)(2,1)S(1)}, bf16[96,1024]{1,0:T(8,128)(2,1)S(1)}, u32[]{:S(2)}, u32[]{:S(2)}) collective-permute-start(bf16[96,1024]{1,0:T(8,128)(2,1)S(1)} %get-tuple-element.75), channel_id=1, source_target_pairs={{2,0},{3,1},{0,2},{1,3},{10,4},{11,5},{8,6},{9,7},{6,8},{7,9},{4,1... | collective-permute-start | bytes 589832 | tf_op jit(solution)/shard_map/ppermute | solution.py:1214
  53.3 11.1 %collective-permute-start.14 = (bf16[96,1024]{1,0:T(8,128)(2,1)S(1)}, bf16[96,1024]{1,0:T(8,128)(2,1)S(1)}, u32[]{:S(2)}, u32[]{:S(2)}) collective-permute-start(bf16[96,1024]{1,0:T(8,128)(2,1)S(1)} %get-tuple-element.76), channel_id=1, source_target_pairs={{0,0},{1,1},{2,2},{3,3},{8,4},{9,5},{10,6},{11,7},{4,8},{5,9},{6,1... | collective-permute-start | bytes 589832 | tf_op jit(solution)/shard_map/ppermute | solution.py:1214
  59.3 9.2 %collective-permute-start.18 = (bf16[64,1024]{1,0:T(8,128)(2,1)S(1)}, bf16[64,1024]{1,0:T(8,128)(2,1)S(1)}, u32[]{:S(2)}, u32[]{:S(2)}) collective-permute-start(bf16[64,1024]{1,0:T(8,128)(2,1)S(1)} %get-tuple-element.83), channel_id=1, source_target_pairs={{2,0},{3,1},{0,2},{1,3},{10,4},{11,5},{8,6},{9,7},{6,8},{7,9},{4,1... | collective-permute-start | bytes 393224 | tf_op jit(solution)/shard_map/ppermute | solution.py:1228
  61.0 8.6 %collective-permute-start.19 = (bf16[64,1024]{1,0:T(8,128)(2,1)S(1)}, bf16[64,1024]{1,0:T(8,128)(2,1)S(1)}, u32[]{:S(2)}, u32[]{:S(2)}) collective-permute-start(bf16[64,1024]{1,0:T(8,128)(2,1)S(1)} %get-tuple-element.84), channel_id=1, source_target_pairs={{0,0},{1,1},{2,2},{3,3},{8,4},{9,5},{10,6},{11,7},{4,8},{5,9},{6,1... | collective-permute-start | bytes 393224 | tf_op jit(solution)/shard_map/ppermute | solution.py:1228
  64.5 4.0 %collective-permute-start.22 = (bf16[16,2048]{1,0:T(8,128)(2,1)S(1)}, bf16[16,2048]{1,0:T(8,128)(2,1)S(1)}, u32[]{:S(2)}, u32[]{:S(2)}) collective-permute-start(bf16[16,2048]{1,0:T(8,128)(2,1)S(1)} %unpack.1.part_0), channel_id=1, source_target_pairs={{0,9},{1,8},{2,11},{3,10},{4,13},{5,12},{6,15},{7,14},{8,1},{9,0},... | collective-permute-start | bytes 196616 | tf_op jit(solution)/shard_map/ppermute | solution.py:1231
  64.6 3.9 %collective-permute-start.21 = (bf16[16,2048]{1,0:T(8,128)(2,1)S(1)}, bf16[16,2048]{1,0:T(8,128)(2,1)S(1)}, u32[]{:S(2)}, u32[]{:S(2)}) collective-permute-start(bf16[16,2048]{1,0:T(8,128)(2,1)S(1)} %unpack.1.part_0), channel_id=1, source_target_pairs={{0,1},{1,0},{2,3},{3,2},{4,5},{5,4},{6,7},{7,6},{8,9},{9,8},{10,11... | collective-permute-start | bytes 196616 | tf_op jit(solution)/shard_map/ppermute | solution.py:1230
  64.9 3.6 %collective-permute-start.20 = (bf16[16,2048]{1,0:T(8,128)(2,1)S(1)}, bf16[16,2048]{1,0:T(8,128)(2,1)S(1)}, u32[]{:S(2)}, u32[]{:S(2)}) collective-permute-start(bf16[16,2048]{1,0:T(8,128)(2,1)S(1)} %unpack.1.part_0), channel_id=1, source_target_pairs={{0,8},{8,0},{16,24},{24,16},{1,9},{9,1},{17,25},{25,17},{2,10},{10... | collective-permute-start | bytes 196616 | tf_op jit(solution)/shard_map/ppermute | solution.py:1230

commit v9 on v8

--- a/solution.py
+++ b/solution.py
@@ -357,7 +357,7 @@
     tokens, ids, (out_0, out_1, work) = refs[0], refs[1], refs[-3:]
     half, count, _ = tokens.shape
     odd = odd_place()
-    work[...] = tokens[...].astype(F32).reshape(half * count, LANES)
+    work[pl.ds(0, half * count)] = tokens[...].astype(F32).reshape(half * count, LANES)
     for i in range(count // 2):
         at = pl.ds(i * LANES, LANES)
         first, second = (work[pl.ds(2 * i + r, half, stride=count)] for r in range(2))
@@ -382,7 +382,7 @@
         in_specs=[vmem()] * (1 + len(extra)),
         out_specs=[vmem()] * 2,
         out_shape=[jax.ShapeDtypeStruct((half, width), BF16)] * 2,
-        scratch_shapes=[pltpu.VMEM((half * count, LANES), F32)],
+        scratch_shapes=[pltpu.VMEM(((half + 1) * count, LANES), F32)],
         compiler_params=pltpu.CompilerParams(vmem_limit_bytes=4 * MIB),
         cost_estimate=pl.CostEstimate(flops=1 << 31, bytes_accessed=1000, transcendentals=0),
         name="split",
@@ -391,7 +391,7 @@
 
 def place_rows(msg_0, msg_1, work):
     count = 2 * msg_0.shape[1] // LANES
-    half = work.shape[0] // count
+    half = work.shape[0] // count - 1
     odd = odd_place()
     for i in range(count // 2):
         at = pl.ds(i * LANES, LANES)
@@ -404,7 +404,7 @@
     half = out.shape[0]
     heads = logs.shape[1]
     place_rows(msg_0, msg_1, work)
-    out[...] = work[...].reshape(out.shape).astype(out.dtype)
+    out[...] = work[pl.ds(0, half * out.shape[1])].reshape(out.shape).astype(out.dtype)
     odd = odd_place()
     found = []
     for k, message in enumerate((msg_0, msg_1)):
@@ -426,7 +426,7 @@
             jax.ShapeDtypeStruct((half, count, LANES), BF16),
             jax.ShapeDtypeStruct((2, HEADS, half), F32),
         ],
-        scratch_shapes=[pltpu.VMEM((half * count, LANES), F32)],
+        scratch_shapes=[pltpu.VMEM(((half + 1) * count, LANES), F32)],
         compiler_params=pltpu.CompilerParams(vmem_limit_bytes=4 * MIB),
         cost_estimate=pl.CostEstimate(flops=1000, bytes_accessed=1000, transcendentals=0),
         name="land",
@@ -631,7 +631,7 @@
         stores[-1].start()
     columns, (width, hidden) = steps * step, o_mlp1.shape
     place_rows(home_0, home_1, o_block)
-    stores.append(pltpu.make_async_copy(o_block, block, sems.at[steps + 1]))
+    stores.append(pltpu.make_async_copy(o_block.at[pl.ds(0, block.shape[0])], block, sems.at[steps + 1]))
     stores[-1].start()
     back = two_products(grads, turned[:columns]) * (1.0 - act * act)
     grad_bias1[...] = jnp.sum(back, 0, keepdims=True)
@@ -664,7 +664,7 @@
             jax.ShapeDtypeStruct((1, columns), F32),
         ],
         scratch_shapes=[
-            pltpu.VMEM((half * tiles, LANES), F32),
+            pltpu.VMEM(((half + 1) * tiles, LANES), F32),
             pltpu.VMEM((width, hidden), F32),
             pltpu.VMEM((steps, hidden, columns // steps), F32),
             pltpu.SemaphoreType.DMA((steps + 2,)),

time: 74.2 us -> 74.2 us (level)
  no operation moved by 1% of the time
where the time goes in v9:
time: 74.2 us; the launch traced here: 73.7 us
  Pallas kernels  39.4 us (53%)
  starting transfers between devices  29.1 us (39%)
  waiting for transfers between devices  4.05 us (5%)
  between operations  1.09 us (1%)
    pallas_call x1, Pallas kernels, middle_part(): pl.pallas_call(partial(middle_kernel, count), in_specs=[vmem()] * 11 + [h...  13.9 us
    ppermute x2, starting transfers between devices, body_rows(): own = [lax.ppermute(m, everyone, there[k]) for k, m in enumerate(out_msgs)]  6.68 us
    pallas_call x1, Pallas kernels, adapter_forward(): pl.pallas_call(adapter_kernel, in_specs=[hbm()] * 6, out_specs=[vmem()] *...  5.59 us
    ppermute x2, starting transfers between devices, body_rows(): lax.ppermute(m, everyone, back[k])  5.15 us
    ppermute x2, starting transfers between devices, body_rows(): lax.ppermute(m, everyone, there[k])  4.32 us
    ppermute x2, starting transfers between devices, body_rows(): home = [lax.ppermute(m, everyone, back[k]) for k, m in enumerate(packed)]  4.22 us
    pallas_call x1, Pallas kernels, finish(): pl.pallas_call(adapter_back_kernel, in_specs=[vmem()] * 9, out_specs=[hbm...  3.95 us
    pallas_call x1, Pallas kernels, final_part(): pl.pallas_call(final_kernel, in_specs=[vmem()] * 14, out_specs=[vmem()] *...  3.81 us
  transfers between devices with their start and end apart: 23, of which 4 were waited for; matrix products, arithmetic and copies ran while one was open for 0% of the time, Pallas kernels for 28%

profile of v9, /device:TPU:1, one launch (start us, length us, event | category | flops | bytes accessed | tf_op | source)
XLA Modules:
  0.0 73.7 jit_solution(10312394032216355334)
XLA Ops:
  0.6 1.2 %split.2 = (bf16[64,1152]{1,0:T(8,128)(2,1)S(1)}, bf16[64,1152]{1,0:T(8,128)(2,1)S(1)}) custom-call(bf16[64,16,128]{2,1,0:T(8,128)(2,1)} %bitcast.37, s32[2,64]{1,0:T(2,128)} %bitcast.44), custom_call_target="tpu_custom_call" | custom-call | flops 2147483648 | bytes 1000 | tf_op jit(solution)/shard_map/split/pallas_call | solution.py:380
  1.8 4.8 %collective-permute-start = (bf16[64,1152]{1,0:T(8,128)(2,1)S(1)}, bf16[64,1152]{1,0:T(8,128)(2,1)S(1)}, u32[]{:S(2)}, u32[]{:S(2)}) collective-permute-start(bf16[64,1152]{1,0:T(8,128)(2,1)S(1)} %get-tuple-element.51), channel_id=1, source_target_pairs={{0,2},{1,3},{2,0},{3,1},{4,10},{5,11},{6,8},{7,9},{8,6},{9,7},{10,... | collective-permute-start | bytes 442376 | tf_op jit(solution)/shard_map/ppermute | solution.py:1190
  6.6 1.9 %collective-permute-start.1 = (bf16[64,1152]{1,0:T(8,128)(2,1)S(1)}, bf16[64,1152]{1,0:T(8,128)(2,1)S(1)}, u32[]{:S(2)}, u32[]{:S(2)}) collective-permute-start(bf16[64,1152]{1,0:T(8,128)(2,1)S(1)} %get-tuple-element.52), channel_id=1, source_target_pairs={{0,0},{1,1},{2,2},{3,3},{4,8},{5,9},{6,10},{7,11},{8,4},{9,5},{10,... | collective-permute-start | bytes 442376 | tf_op jit(solution)/shard_map/ppermute | solution.py:1190
  8.5 5.6 %adapter.1 = (bf16[16,2048]{1,0:T(8,128)(2,1)S(1)}, f32[16,512]{1,0:T(8,128)S(1)}, bf16[1024,3072]{1,0:T(8,128)(2,1)S(1)}, bf16[3072,1024]{1,0:T(8,128)(2,1)S(1)...) custom-call(f32[10,1024]{1,0:T(8,128)} %h_embed.1, f32[1024,512]{1,0:T(8,128)} %w_mlp1.1, f32[1,512]{1,0:T(1,128)} %bitcast.42, ...), custom_call_target="tpu_custom_call" | custom-call | flops 4294967296 | bytes 6291456 | tf_op jit(solution)/shard_map/adapter/pallas_call | solution.py:557
  14.1 0.0 copy-start
  14.1 0.0 copy-start.1
  14.1 0.0 collective-permute-done.refs_0_.own_0
  14.1 0.4 collective-permute-done.1.refs_1_.own_1
  14.5 1.2 %collective-permute-start.4 = (bf16[64,1152]{1,0:T(8,128)(2,1)S(1)}, bf16[64,1152]{1,0:T(8,128)(2,1)S(1)}, u32[]{:S(2)}, u32[]{:S(2)}) collective-permute-start(bf16[64,1152]{1,0:T(8,128)(2,1)S(1)} %collective-permute-done.refs_0_.own_0), channel_id=1, source_target_pairs={{0,1},{1,0},{2,3},{3,2},{4,5},{5,4},{6,7},{7,6},{8,9},{9,8},{10,11... | collective-permute-start | bytes 442376 | tf_op jit(solution)/shard_map/ppermute | solution.py:1196
  15.7 0.0 collective-permute-start.2
  15.7 0.2 collective-permute-start.5
  16.0 0.8 %collective-permute-start.3 = (bf16[64,1152]{1,0:T(8,128)(2,1)S(1)}, bf16[64,1152]{1,0:T(8,128)(2,1)S(1)}, u32[]{:S(2)}, u32[]{:S(2)}) collective-permute-start(bf16[64,1152]{1,0:T(8,128)(2,1)S(1)} %collective-permute-done.1.refs_1_.own_1), channel_id=1, source_target_pairs={{0,8},{8,0},{16,24},{24,16},{1,9},{9,1},{17,25},{25,17},{2,10},{10... | collective-permute-start | bytes 442376 | tf_op jit(solution)/shard_map/ppermute | solution.py:1197
  16.8 1.2 %split.3 = (bf16[64,1024]{1,0:T(8,128)(2,1)S(1)}, bf16[64,1024]{1,0:T(8,128)(2,1)S(1)}) custom-call(bf16[64,16,128]{2,1,0:T(8,128)(2,1)} %bitcast.38), custom_call_target="tpu_custom_call" | custom-call | flops 2147483648 | bytes 1000 | tf_op jit(solution)/shard_map/split/pallas_call | solution.py:380
  17.9 0.0 collective-permute-done.2.refs_2_
  17.9 0.0 collective-permute-done.3.refs_3_
  17.9 1.8 %collective-permute-start.8 = (bf16[64,1024]{1,0:T(8,128)(2,1)S(1)}, bf16[64,1024]{1,0:T(8,128)(2,1)S(1)}, u32[]{:S(2)}, u32[]{:S(2)}) collective-permute-start(bf16[64,1024]{1,0:T(8,128)(2,1)S(1)} %get-tuple-element.64), channel_id=1, source_target_pairs={{0,2},{1,3},{2,0},{3,1},{4,10},{5,11},{6,8},{7,9},{8,6},{9,7},{10,... | collective-permute-start | bytes 393224 | tf_op jit(solution)/shard_map/ppermute | solution.py:1198
  19.7 2.5 %collective-permute-start.9 = (bf16[64,1024]{1,0:T(8,128)(2,1)S(1)}, bf16[64,1024]{1,0:T(8,128)(2,1)S(1)}, u32[]{:S(2)}, u32[]{:S(2)}) collective-permute-start(bf16[64,1024]{1,0:T(8,128)(2,1)S(1)} %get-tuple-element.65), channel_id=1, source_target_pairs={{0,0},{1,1},{2,2},{3,3},{4,8},{5,9},{6,10},{7,11},{8,4},{9,5},{10,... | collective-permute-start | bytes 393224 | tf_op jit(solution)/shard_map/ppermute | solution.py:1198
  22.3 0.0 collective-permute-done.4.refs_0_
  22.3 0.1 collective-permute-start.6
  22.4 0.0 collective-permute-done.5.refs_1_
  22.4 0.5 collective-permute-start.7
  22.9 0.0 copy-done
  22.9 0.0 copy-done.1
  22.9 2.1 %project.2 = (bf16[256,3072]{1,0:T(8,128)(2,1)S(1)}, bf16[256,128]{1,0:T(8,128)(2,1)S(1)}) custom-call(bf16[64,1152]{1,0:T(8,128)(2,1)S(1)} %collective-permute-done.refs_0_.own_0, bf16[64,1152]{1,0:T(8,128)(2,1)S(1)} %collective-permute-done.1.refs_1_.own_1, bf16[64,1152]{1,0:T(8,128)(2,1)S(1)} %collective-permute-done.2.refs_2_, ...), custom_call_target="tpu_custom_call" | custom-call | flops 1610612736 | bytes 6291456 | tf_op jit(solution)/shard_map/project/pallas_call | solution.py:454
  25.0 0.0 copy-start.2
  25.0 0.0 copy-start.3
  25.0 0.0 collective-permute-done.6.refs_2_
  25.0 0.0 collective-permute-done.7.refs_3_
  25.0 1.6 %project.3 = (bf16[256,3072]{1,0:T(8,128)(2,1)S(1)}, bf16[256,128]{1,0:T(8,128)(2,1)S(1)}, bf16[256,1024]{1,0:T(8,128)(2,1)S(1)}) custom-call(bf16[64,1152]{1,0:T(8,128)(2,1)S(1)} %collective-permute-done.4.refs_0_, bf16[64,1152]{1,0:T(8,128)(2,1)S(1)} %collective-permute-done.5.refs_1_, bf16[64,1152]{1,0:T(8,128)(2,1)S(1)} %collective-permute-done.6.refs_2_, ...), custom_call_target="tpu_custom_call" | custom-call | flops 1610612736 | bytes 6291456 | tf_op jit(solution)/shard_map/project/pallas_call | solution.py:454
  26.6 0.0 collective-permute-done.8.cot_0
  26.6 1.7 %collective-permute-done.9.cot_1 = bf16[64,1024]{1,0:T(8,128)(2,1)S(1)} collective-permute-done((bf16[64,1024]{1,0:T(8,128)(2,1)S(1)}, bf16[64,1024]{1,0:T(8,128)(2,1)S(1)}, u32[]{:S(2)}, u32[]{:S(2)}) %collective-permute-start.9) | collective-permute-done | bytes 131104 | tf_op jit(solution)/shard_map/ppermute | solution.py:1198
  28.3 13.9 %middle.1 = (bf16[96,1024]{1,0:T(8,128)(2,1)S(1)}, bf16[96,1024]{1,0:T(8,128)(2,1)S(1)}, bf16[128,1152]{1,0:T(8,128)(2,1)S(1)}, f32[128,1024]{1,0:T(8,128)S(1)}) custom-call(bf16[256,3072]{1,0:T(8,128)(2,1)S(1)} %get-tuple-element.57.qkv_a.queries, bf16[256,3072]{1,0:T(8,128)(2,1)S(1)} %get-tuple-element.58.qkv_b, ...), custom_call_target="tpu_custom_call" | custom-call | flops 2147483648 | bytes 1000 | tf_op jit(solution)/shard_map/middle/pallas_call | solution.py:871
  42.3 1.3 %collective-permute-start.16 = (bf16[128,1152]{1,0:T(8,128)(2,1)S(1)}, bf16[128,1152]{1,0:T(8,128)(2,1)S(1)}, u32[]{:S(2)}, u32[]{:S(2)}) collective-permute-start(bf16[128,1152]{1,0:T(8,128)(2,1)S(1)} %get-tuple-element.66.grads.grads_0), channel_id=1, source_target_pairs={{0,1},{1,0},{2,3},{3,2},{4,5},{5,4},{6,7},{7,6},{8,9},{9,8},{10,11... | collective-permute-start | bytes 884744 | tf_op jit(solution)/shard_map/ppermute | solution.py:1206
  43.6 1.4 %prefix.1.order.own = bf16[16,2048]{1,0:T(8,128)(2,1)S(1)} custom-call(bf16[256,3072]{1,0:T(8,128)(2,1)S(1)} %get-tuple-element.57.qkv_a.queries, bf16[128,1152]{1,0:T(8,128)(2,1)S(1)} %get-tuple-element.66.grads.grads_0, bf16[16,2048]{1,0:T(8,128)(2,1)S(1)} %get-tuple-element.61.prefix_kv), custom_call_target="tpu_custom_call" | custom-call | flops 1000 | bytes 1000 | tf_op jit(solution)/shard_map/prefix/pallas_call | solution.py:951
  44.9 0.0 collective-permute-start.12
  44.9 1.6 %collective-permute-start.11 = (bf16[16,2048]{1,0:T(8,128)(2,1)S(1)}, bf16[16,2048]{1,0:T(8,128)(2,1)S(1)}, u32[]{:S(2)}, u32[]{:S(2)}) collective-permute-start(bf16[16,2048]{1,0:T(8,128)(2,1)S(1)} %prefix.1.order.own), channel_id=1, source_target_pairs={{0,8},{8,0},{16,24},{24,16},{1,9},{9,1},{17,25},{25,17},{2,10},{10... | collective-permute-start | bytes 196616 | tf_op jit(solution)/shard_map/ppermute | solution.py:1209
  46.5 0.3 collective-permute-start.10
  46.8 0.3 collective-permute-start.15
  47.1 3.7 %query.1 = (f32[128,1024]{1,0:T(8,128)S(1)}, bf16[256,3072]{1,0:T(8,128)(2,1)S(1)}) custom-call(bf16[256,3072]{1,0:T(8,128)(2,1)S(1)} %get-tuple-element.57.qkv_a.queries, bf16[256,3072]{1,0:T(8,128)(2,1)S(1)} %get-tuple-element.58.qkv_b, bf16[256,128]{1,0:T(8,128)(2,1)S(1)} %get-tuple-element.59.marks_a, ...), custom_call_target="tpu_custom_call", output_to_operand_aliasing={{1}: (1, {})} | custom-call | flops 2147483648 | bytes 1000 | tf_op jit(solution)/shard_map/query/pallas_call | solution.py:1065
  50.8 0.0 collective-permute-done.12.part_2
  50.8 0.0 collective-permute-done.11.part_1
  50.8 0.0 collective-permute-done.10.part_0
  50.8 0.1 pack.1
  50.9 0.0 collective-permute-done.16.grads_2
  50.9 0.3 collective-permute-start.17
  51.2 2.1 %collective-permute-start.13 = (bf16[96,1024]{1,0:T(8,128)(2,1)S(1)}, bf16[96,1024]{1,0:T(8,128)(2,1)S(1)}, u32[]{:S(2)}, u32[]{:S(2)}) collective-permute-start(bf16[96,1024]{1,0:T(8,128)(2,1)S(1)} %get-tuple-element.75), channel_id=1, source_target_pairs={{2,0},{3,1},{0,2},{1,3},{10,4},{11,5},{8,6},{9,7},{6,8},{7,9},{4,1... | collective-permute-start | bytes 589832 | tf_op jit(solution)/shard_map/ppermute | solution.py:1214
  53.3 2.1 %collective-permute-start.14 = (bf16[96,1024]{1,0:T(8,128)(2,1)S(1)}, bf16[96,1024]{1,0:T(8,128)(2,1)S(1)}, u32[]{:S(2)}, u32[]{:S(2)}) collective-permute-start(bf16[96,1024]{1,0:T(8,128)(2,1)S(1)} %get-tuple-element.76), channel_id=1, source_target_pairs={{0,0},{1,1},{2,2},{3,3},{8,4},{9,5},{10,6},{11,7},{4,8},{5,9},{6,1... | collective-permute-start | bytes 589832 | tf_op jit(solution)/shard_map/ppermute | solution.py:1214
  55.4 0.0 collective-permute-done.15.grads_1
  55.5 0.0 collective-permute-done.17.grads_3
  55.5 3.8 %final.1 = (bf16[64,1024]{1,0:T(8,128)(2,1)S(1)}, bf16[64,1024]{1,0:T(8,128)(2,1)S(1)}) custom-call(bf16[256,3072]{1,0:T(8,128)(2,1)S(1)} %get-tuple-element.57.qkv_a.queries, bf16[256,3072]{1,0:T(8,128)(2,1)S(1)} %get-tuple-element.80.qkv_b, bf16[256,128]{1,0:T(8,128)(2,1)S(1)} %get-tuple-element.59.marks_a, ...), custom_call_target="tpu_custom_call" | custom-call | flops 1000 | bytes 1000 | tf_op jit(solution)/shard_map/final/pallas_call | solution.py:1135
  59.3 1.7 %collective-permute-start.18 = (bf16[64,1024]{1,0:T(8,128)(2,1)S(1)}, bf16[64,1024]{1,0:T(8,128)(2,1)S(1)}, u32[]{:S(2)}, u32[]{:S(2)}) collective-permute-start(bf16[64,1024]{1,0:T(8,128)(2,1)S(1)} %get-tuple-element.83), channel_id=1, source_target_pairs={{2,0},{3,1},{0,2},{1,3},{10,4},{11,5},{8,6},{9,7},{6,8},{7,9},{4,1... | collective-permute-start | bytes 393224 | tf_op jit(solution)/shard_map/ppermute | solution.py:1228
  61.0 3.4 %collective-permute-start.19 = (bf16[64,1024]{1,0:T(8,128)(2,1)S(1)}, bf16[64,1024]{1,0:T(8,128)(2,1)S(1)}, u32[]{:S(2)}, u32[]{:S(2)}) collective-permute-start(bf16[64,1024]{1,0:T(8,128)(2,1)S(1)} %get-tuple-element.84), channel_id=1, source_target_pairs={{0,0},{1,1},{2,2},{3,3},{8,4},{9,5},{10,6},{11,7},{4,8},{5,9},{6,1... | collective-permute-start | bytes 393224 | tf_op jit(solution)/shard_map/ppermute | solution.py:1228
  64.4 0.0 collective-permute-done.13.home_0.msg_0
  64.4 0.0 collective-permute-done.14.home_1.msg_1
  64.5 0.1 collective-permute-start.22
  64.6 0.3 collective-permute-start.21
  64.9 1.8 %collective-permute-start.20 = (bf16[16,2048]{1,0:T(8,128)(2,1)S(1)}, bf16[16,2048]{1,0:T(8,128)(2,1)S(1)}, u32[]{:S(2)}, u32[]{:S(2)}) collective-permute-start(bf16[16,2048]{1,0:T(8,128)(2,1)S(1)} %unpack.1.part_0), channel_id=1, source_target_pairs={{0,8},{8,0},{16,24},{24,16},{1,9},{9,1},{17,25},{25,17},{2,10},{10... | collective-permute-start | bytes 196616 | tf_op jit(solution)/shard_map/ppermute | solution.py:1230
  66.7 1.0 %land.1 = (bf16[64,16,128]{2,1,0:T(8,128)(2,1)}, f32[2,16,64]{2,1,0:T(8,128)}) custom-call(bf16[96,1024]{1,0:T(8,128)(2,1)S(1)} %collective-permute-done.13.home_0.msg_0, bf16[96,1024]{1,0:T(8,128)(2,1)S(1)} %collective-permute-done.14.home_1.msg_1), custom_call_target="tpu_custom_call" | custom-call | flops 1000 | bytes 1000 | tf_op jit(solution)/shard_map/land/pallas_call | solution.py:421
  67.7 0.8 %collective-permute-done.22.part_3 = bf16[16,2048]{1,0:T(8,128)(2,1)S(1)} collective-permute-done((bf16[16,2048]{1,0:T(8,128)(2,1)S(1)}, bf16[16,2048]{1,0:T(8,128)(2,1)S(1)}, u32[]{:S(2)}, u32[]{:S(2)}) %collective-permute-start.22) | collective-permute-done | bytes 65568 | tf_op jit(solution)/shard_map/ppermute | solution.py:1231
  68.4 0.0 collective-permute-done.21.part_2
  68.5 0.0 collective-permute-done.20.part_1
  68.5 0.0 collective-permute-done.18.home_0
  68.5 1.1 %collective-permute-done.19.home_1 = bf16[64,1024]{1,0:T(8,128)(2,1)S(1)} collective-permute-done((bf16[64,1024]{1,0:T(8,128)(2,1)S(1)}, bf16[64,1024]{1,0:T(8,128)(2,1)S(1)}, u32[]{:S(2)}, u32[]{:S(2)}) %collective-permute-start.19) | collective-permute-done | bytes 131104 | tf_op jit(solution)/shard_map/ppermute | solution.py:1228
  69.6 3.9 %finish.1 = (f32[1024,128]{1,0:T(8,128)}, f32[10,1024]{1,0:T(8,128)}, f32[1024,512]{1,0:T(8,128)}, f32[1,512]{1,0:T(1,128)}, f32[512,2048]{1,0:T(8,128)}, /*index=5*/f32[1,2048]{1,0:T(1,128)}) custom-call(bf16[64,1024]{1,0:T(8,128)(2,1)S(1)} %collective-permute-done.18.home_0, bf16[64,1024]{1,0:T(8,128)(2,1)S(1)} %collective-permute-done.19.home_1, ...), custom_call_target="tpu_custom_call" | custom-call | flops 1000 | bytes 1000 | tf_op jit(solution)/shard_map/finish/pallas_call | solution.py:654
  (3 shorter events, 0.0 us)
Async XLA Ops:
  1.8 12.3 %collective-permute-start = (bf16[64,1152]{1,0:T(8,128)(2,1)S(1)}, bf16[64,1152]{1,0:T(8,128)(2,1)S(1)}, u32[]{:S(2)}, u32[]{:S(2)}) collective-permute-start(bf16[64,1152]{1,0:T(8,128)(2,1)S(1)} %get-tuple-element.51), channel_id=1, source_target_pairs={{0,2},{1,3},{2,0},{3,1},{4,10},{5,11},{6,8},{7,9},{8,6},{9,7},{10,... | collective-permute-start | bytes 442376 | tf_op jit(solution)/shard_map/ppermute | solution.py:1190
  6.6 7.9 %collective-permute-start.1 = (bf16[64,1152]{1,0:T(8,128)(2,1)S(1)}, bf16[64,1152]{1,0:T(8,128)(2,1)S(1)}, u32[]{:S(2)}, u32[]{:S(2)}) collective-permute-start(bf16[64,1152]{1,0:T(8,128)(2,1)S(1)} %get-tuple-element.52), channel_id=1, source_target_pairs={{0,0},{1,1},{2,2},{3,3},{4,8},{5,9},{6,10},{7,11},{8,4},{9,5},{10,... | collective-permute-start | bytes 442376 | tf_op jit(solution)/shard_map/ppermute | solution.py:1190
  14.1 8.8 %copy-start = (f32[1024]{0:T(1024)S(1)}, f32[1024]{0:T(1024)}, u32[]{:S(2)}) copy-start(f32[1024]{0:T(1024)} %param.18) | copy-start | bytes 12292
  14.1 8.8 %copy-start.1 = (f32[1024]{0:T(1024)S(1)}, f32[1024]{0:T(1024)}, u32[]{:S(2)}) copy-start(f32[1024]{0:T(1024)} %param.19) | copy-start | bytes 12292
  14.5 7.8 %collective-permute-start.4 = (bf16[64,1152]{1,0:T(8,128)(2,1)S(1)}, bf16[64,1152]{1,0:T(8,128)(2,1)S(1)}, u32[]{:S(2)}, u32[]{:S(2)}) collective-permute-start(bf16[64,1152]{1,0:T(8,128)(2,1)S(1)} %collective-permute-done.refs_0_.own_0), channel_id=1, source_target_pairs={{0,1},{1,0},{2,3},{3,2},{4,5},{5,4},{6,7},{7,6},{8,9},{9,8},{10,11... | collective-permute-start | bytes 442376 | tf_op jit(solution)/shard_map/ppermute | solution.py:1196
  15.7 2.2 %collective-permute-start.2 = (bf16[64,1152]{1,0:T(8,128)(2,1)S(1)}, bf16[64,1152]{1,0:T(8,128)(2,1)S(1)}, u32[]{:S(2)}, u32[]{:S(2)}) collective-permute-start(bf16[64,1152]{1,0:T(8,128)(2,1)S(1)} %collective-permute-done.refs_0_.own_0), channel_id=1, source_target_pairs={{0,8},{8,0},{16,24},{24,16},{1,9},{9,1},{17,25},{25,17},{2,10},{10... | collective-permute-start | bytes 442376 | tf_op jit(solution)/shard_map/ppermute | solution.py:1197
  15.7 6.6 %collective-permute-start.5 = (bf16[64,1152]{1,0:T(8,128)(2,1)S(1)}, bf16[64,1152]{1,0:T(8,128)(2,1)S(1)}, u32[]{:S(2)}, u32[]{:S(2)}) collective-permute-start(bf16[64,1152]{1,0:T(8,128)(2,1)S(1)} %collective-permute-done.1.refs_1_.own_1), channel_id=1, source_target_pairs={{0,1},{1,0},{2,3},{3,2},{4,5},{5,4},{6,7},{7,6},{8,9},{9,8},{10,11... | collective-permute-start | bytes 442376 | tf_op jit(solution)/shard_map/ppermute | solution.py:1196
  16.0 2.0 %collective-permute-start.3 = (bf16[64,1152]{1,0:T(8,128)(2,1)S(1)}, bf16[64,1152]{1,0:T(8,128)(2,1)S(1)}, u32[]{:S(2)}, u32[]{:S(2)}) collective-permute-start(bf16[64,1152]{1,0:T(8,128)(2,1)S(1)} %collective-permute-done.1.refs_1_.own_1), channel_id=1, source_target_pairs={{0,8},{8,0},{16,24},{24,16},{1,9},{9,1},{17,25},{25,17},{2,10},{10... | collective-permute-start | bytes 442376 | tf_op jit(solution)/shard_map/ppermute | solution.py:1197
  17.9 8.6 %collective-permute-start.8 = (bf16[64,1024]{1,0:T(8,128)(2,1)S(1)}, bf16[64,1024]{1,0:T(8,128)(2,1)S(1)}, u32[]{:S(2)}, u32[]{:S(2)}) collective-permute-start(bf16[64,1024]{1,0:T(8,128)(2,1)S(1)} %get-tuple-element.64), channel_id=1, source_target_pairs={{0,2},{1,3},{2,0},{3,1},{4,10},{5,11},{6,8},{7,9},{8,6},{9,7},{10,... | collective-permute-start | bytes 393224 | tf_op jit(solution)/shard_map/ppermute | solution.py:1198
  19.7 8.6 %collective-permute-start.9 = (bf16[64,1024]{1,0:T(8,128)(2,1)S(1)}, bf16[64,1024]{1,0:T(8,128)(2,1)S(1)}, u32[]{:S(2)}, u32[]{:S(2)}) collective-permute-start(bf16[64,1024]{1,0:T(8,128)(2,1)S(1)} %get-tuple-element.65), channel_id=1, source_target_pairs={{0,0},{1,1},{2,2},{3,3},{4,8},{5,9},{6,10},{7,11},{8,4},{9,5},{10,... | collective-permute-start | bytes 393224 | tf_op jit(solution)/shard_map/ppermute | solution.py:1198
  22.3 2.7 %collective-permute-start.6 = (bf16[64,1152]{1,0:T(8,128)(2,1)S(1)}, bf16[64,1152]{1,0:T(8,128)(2,1)S(1)}, u32[]{:S(2)}, u32[]{:S(2)}) collective-permute-start(bf16[64,1152]{1,0:T(8,128)(2,1)S(1)} %collective-permute-done.4.refs_0_), channel_id=1, source_target_pairs={{0,8},{8,0},{16,24},{24,16},{1,9},{9,1},{17,25},{25,17},{2,10},{10... | collective-permute-start | bytes 442376 | tf_op jit(solution)/shard_map/ppermute | solution.py:1199
  22.4 2.6 %collective-permute-start.7 = (bf16[64,1152]{1,0:T(8,128)(2,1)S(1)}, bf16[64,1152]{1,0:T(8,128)(2,1)S(1)}, u32[]{:S(2)}, u32[]{:S(2)}) collective-permute-start(bf16[64,1152]{1,0:T(8,128)(2,1)S(1)} %collective-permute-done.5.refs_1_), channel_id=1, source_target_pairs={{0,8},{8,0},{16,24},{24,16},{1,9},{9,1},{17,25},{25,17},{2,10},{10... | collective-permute-start | bytes 442376 | tf_op jit(solution)/shard_map/ppermute | solution.py:1199
  25.0 3.3 %copy-start.2 = (f32[1024]{0:T(1024)S(1)}, f32[1024]{0:T(1024)}, u32[]{:S(2)}) copy-start(f32[1024]{0:T(1024)} %param.22) | copy-start | bytes 12292
  25.0 3.3 %copy-start.3 = (f32[1024]{0:T(1024)S(1)}, f32[1024]{0:T(1024)}, u32[]{:S(2)}) copy-start(f32[1024]{0:T(1024)} %param.23) | copy-start | bytes 12292
  42.3 8.7 %collective-permute-start.16 = (bf16[128,1152]{1,0:T(8,128)(2,1)S(1)}, bf16[128,1152]{1,0:T(8,128)(2,1)S(1)}, u32[]{:S(2)}, u32[]{:S(2)}) collective-permute-start(bf16[128,1152]{1,0:T(8,128)(2,1)S(1)} %get-tuple-element.66.grads.grads_0), channel_id=1, source_target_pairs={{0,1},{1,0},{2,3},{3,2},{4,5},{5,4},{6,7},{7,6},{8,9},{9,8},{10,11... | collective-permute-start | bytes 884744 | tf_op jit(solution)/shard_map/ppermute | solution.py:1206
  44.9 5.9 %collective-permute-start.12 = (bf16[16,2048]{1,0:T(8,128)(2,1)S(1)}, bf16[16,2048]{1,0:T(8,128)(2,1)S(1)}, u32[]{:S(2)}, u32[]{:S(2)}) collective-permute-start(bf16[16,2048]{1,0:T(8,128)(2,1)S(1)} %prefix.1.order.own), channel_id=1, source_target_pairs={{0,24},{8,16},{16,8},{24,0},{1,25},{9,17},{17,9},{25,1},{2,26},{10... | collective-permute-start | bytes 196616 | tf_op jit(solution)/shard_map/ppermute | solution.py:1209
  44.9 5.9 %collective-permute-start.11 = (bf16[16,2048]{1,0:T(8,128)(2,1)S(1)}, bf16[16,2048]{1,0:T(8,128)(2,1)S(1)}, u32[]{:S(2)}, u32[]{:S(2)}) collective-permute-start(bf16[16,2048]{1,0:T(8,128)(2,1)S(1)} %prefix.1.order.own), channel_id=1, source_target_pairs={{0,8},{8,0},{16,24},{24,16},{1,9},{9,1},{17,25},{25,17},{2,10},{10... | collective-permute-start | bytes 196616 | tf_op jit(solution)/shard_map/ppermute | solution.py:1209
  46.5 4.3 %collective-permute-start.10 = (bf16[16,2048]{1,0:T(8,128)(2,1)S(1)}, bf16[16,2048]{1,0:T(8,128)(2,1)S(1)}, u32[]{:S(2)}, u32[]{:S(2)}) collective-permute-start(bf16[16,2048]{1,0:T(8,128)(2,1)S(1)} %prefix.1.order.own), channel_id=1, source_target_pairs={{0,16},{8,24},{16,0},{24,8},{1,17},{9,25},{17,1},{25,9},{2,18},{10... | collective-permute-start | bytes 196616 | tf_op jit(solution)/shard_map/ppermute | solution.py:1209
  46.8 8.6 %collective-permute-start.15 = (bf16[128,1152]{1,0:T(8,128)(2,1)S(1)}, bf16[128,1152]{1,0:T(8,128)(2,1)S(1)}, u32[]{:S(2)}, u32[]{:S(2)}) collective-permute-start(bf16[128,1152]{1,0:T(8,128)(2,1)S(1)} %get-tuple-element.66.grads.grads_0), channel_id=1, source_target_pairs={{0,8},{8,0},{16,24},{24,16},{1,9},{9,1},{17,25},{25,17},{2,10},{10... | collective-permute-start | bytes 884744 | tf_op jit(solution)/shard_map/ppermute | solution.py:1207
  50.9 4.5 %collective-permute-start.17 = (bf16[128,1152]{1,0:T(8,128)(2,1)S(1)}, bf16[128,1152]{1,0:T(8,128)(2,1)S(1)}, u32[]{:S(2)}, u32[]{:S(2)}) collective-permute-start(bf16[128,1152]{1,0:T(8,128)(2,1)S(1)} %collective-permute-done.16.grads_2), channel_id=1, source_target_pairs={{0,8},{8,0},{16,24},{24,16},{1,9},{9,1},{17,25},{25,17},{2,10},{10... | collective-permute-start | bytes 884744 | tf_op jit(solution)/shard_map/ppermute | solution.py:1215
  51.2 13.2 %collective-permute-start.13 = (bf16[96,1024]{1,0:T(8,128)(2,1)S(1)}, bf16[96,1024]{1,0:T(8,128)(2,1)S(1)}, u32[]{:S(2)}, u32[]{:S(2)}) collective-permute-start(bf16[96,1024]{1,0:T(8,128)(2,1)S(1)} %get-tuple-element.75), channel_id=1, source_target_pairs={{2,0},{3,1},{0,2},{1,3},{10,4},{11,5},{8,6},{9,7},{6,8},{7,9},{4,1... | collective-permute-start | bytes 589832 | tf_op jit(solution)/shard_map/ppermute | solution.py:1214
  53.3 11.1 %collective-permute-start.14 = (bf16[96,1024]{1,0:T(8,128)(2,1)S(1)}, bf16[96,1024]{1,0:T(8,128)(2,1)S(1)}, u32[]{:S(2)}, u32[]{:S(2)}) collective-permute-start(bf16[96,1024]{1,0:T(8,128)(2,1)S(1)} %get-tuple-element.76), channel_id=1, source_target_pairs={{0,0},{1,1},{2,2},{3,3},{8,4},{9,5},{10,6},{11,7},{4,8},{5,9},{6,1... | collective-permute-start | bytes 589832 | tf_op jit(solution)/shard_map/ppermute | solution.py:1214
  59.3 9.2 %collective-permute-start.18 = (bf16[64,1024]{1,0:T(8,128)(2,1)S(1)}, bf16[64,1024]{1,0:T(8,128)(2,1)S(1)}, u32[]{:S(2)}, u32[]{:S(2)}) collective-permute-start(bf16[64,1024]{1,0:T(8,128)(2,1)S(1)} %get-tuple-element.83), channel_id=1, source_target_pairs={{2,0},{3,1},{0,2},{1,3},{10,4},{11,5},{8,6},{9,7},{6,8},{7,9},{4,1... | collective-permute-start | bytes 393224 | tf_op jit(solution)/shard_map/ppermute | solution.py:1228
  61.0 8.6 %collective-permute-start.19 = (bf16[64,1024]{1,0:T(8,128)(2,1)S(1)}, bf16[64,1024]{1,0:T(8,128)(2,1)S(1)}, u32[]{:S(2)}, u32[]{:S(2)}) collective-permute-start(bf16[64,1024]{1,0:T(8,128)(2,1)S(1)} %get-tuple-element.84), channel_id=1, source_target_pairs={{0,0},{1,1},{2,2},{3,3},{8,4},{9,5},{10,6},{11,7},{4,8},{5,9},{6,1... | collective-permute-start | bytes 393224 | tf_op jit(solution)/shard_map/ppermute | solution.py:1228
  64.5 4.0 %collective-permute-start.22 = (bf16[16,2048]{1,0:T(8,128)(2,1)S(1)}, bf16[16,2048]{1,0:T(8,128)(2,1)S(1)}, u32[]{:S(2)}, u32[]{:S(2)}) collective-permute-start(bf16[16,2048]{1,0:T(8,128)(2,1)S(1)} %unpack.1.part_0), channel_id=1, source_target_pairs={{0,9},{1,8},{2,11},{3,10},{4,13},{5,12},{6,15},{7,14},{8,1},{9,0},... | collective-permute-start | bytes 196616 | tf_op jit(solution)/shard_map/ppermute | solution.py:1231
  64.6 3.9 %collective-permute-start.21 = (bf16[16,2048]{1,0:T(8,128)(2,1)S(1)}, bf16[16,2048]{1,0:T(8,128)(2,1)S(1)}, u32[]{:S(2)}, u32[]{:S(2)}) collective-permute-start(bf16[16,2048]{1,0:T(8,128)(2,1)S(1)} %unpack.1.part_0), channel_id=1, source_target_pairs={{0,1},{1,0},{2,3},{3,2},{4,5},{5,4},{6,7},{7,6},{8,9},{9,8},{10,11... | collective-permute-start | bytes 196616 | tf_op jit(solution)/shard_map/ppermute | solution.py:1230
  64.9 3.6 %collective-permute-start.20 = (bf16[16,2048]{1,0:T(8,128)(2,1)S(1)}, bf16[16,2048]{1,0:T(8,128)(2,1)S(1)}, u32[]{:S(2)}, u32[]{:S(2)}) collective-permute-start(bf16[16,2048]{1,0:T(8,128)(2,1)S(1)} %unpack.1.part_0), channel_id=1, source_target_pairs={{0,8},{8,0},{16,24},{24,16},{1,9},{9,1},{17,25},{25,17},{2,10},{10... | collective-permute-start | bytes 196616 | tf_op jit(solution)/shard_map/ppermute | solution.py:1230

commit v10 on v9

--- a/solution.py
+++ b/solution.py
@@ -617,19 +617,19 @@
     o_mlp2,
     sems,
 ):
-    steps, step = o_mlp2.shape[0], o_mlp2.shape[2]
+    steps, step = o_mlp2.shape[0], o_mlp2.shape[1]
     first, second, third, fourth = (p[...].astype(F32) for p in (part_0, part_1, part_2, part_3))
     grads = (first + second) + (third + fourth)
     act = inner[...]
     stores = []
     grad_bias2[...] = jnp.sum(grads, 0, keepdims=True)
     for i in range(steps):
-        o_mlp2[i] = outer(act, grads[:, i * step : (i + 1) * step])
+        o_mlp2[i] = outer(act[:, i * step : (i + 1) * step], grads)
         stores.append(
-            pltpu.make_async_copy(o_mlp2.at[i], grad_mlp2.at[:, pl.ds(i * step, step)], sems.at[i])
+            pltpu.make_async_copy(o_mlp2.at[i], grad_mlp2.at[pl.ds(i * step, step)], sems.at[i])
         )
         stores[-1].start()
-    columns, (width, hidden) = steps * step, o_mlp1.shape
+    columns, (width, hidden) = o_mlp2.shape[2], o_mlp1.shape
     place_rows(home_0, home_1, o_block)
     stores.append(pltpu.make_async_copy(o_block.at[pl.ds(0, block.shape[0])], block, sems.at[steps + 1]))
     stores[-1].start()
@@ -666,7 +666,7 @@
         scratch_shapes=[
             pltpu.VMEM(((half + 1) * tiles, LANES), F32),
             pltpu.VMEM((width, hidden), F32),
-            pltpu.VMEM((steps, hidden, columns // steps), F32),
+            pltpu.VMEM((steps, hidden // steps, columns), F32),
             pltpu.SemaphoreType.DMA((steps + 2,)),
         ],
         compiler_params=pltpu.CompilerParams(vmem_limit_bytes=16 * MIB),
@@ -1211,7 +1211,7 @@
         count, qkv_a, kv_b, marks_a, marks_b, prefix_kv, grads, w_back, normed_b, w_near, grad_prefix_kv
     )
     packed = pack(count, grads, (grad_prefix_kv, *after(parts, grad_partial)), back_0, back_1)
-    home = [lax.ppermute(m, everyone, back[k]) for k, m in enumerate(packed)]
+    home = [lax.ppermute(packed[k], everyone, back[k]) for k in (1, 0)][::-1]
     grads_yc = lax.ppermute(after(grads_y, packed), "seq", swap_core)
     final_0, final_1 = final_part(
         qkv_a,

time: 74.2 us -> 74.2 us (level)
  no operation moved by 1% of the time
where the time goes in v10:
time: 74.2 us; the launch traced here: 73.7 us
  Pallas kernels  39.4 us (53%)
  starting transfers between devices  29.1 us (39%)
  waiting for transfers between devices  4.05 us (5%)
  between operations  1.09 us (1%)
    pallas_call x1, Pallas kernels, middle_part(): pl.pallas_call(partial(middle_kernel, count), in_specs=[vmem()] * 11 + [h...  13.9 us
    ppermute x2, starting transfers between devices, body_rows(): own = [lax.ppermute(m, everyone, there[k]) for k, m in enumerate(out_msgs)]  6.68 us
    pallas_call x1, Pallas kernels, adapter_forward(): pl.pallas_call(adapter_kernel, in_specs=[hbm()] * 6, out_specs=[vmem()] *...  5.59 us
    ppermute x2, starting transfers between devices, body_rows(): lax.ppermute(m, everyone, back[k])  5.15 us
    ppermute x2, starting transfers between devices, body_rows(): lax.ppermute(m, everyone, there[k])  4.32 us
    ppermute x2, starting transfers between devices, body_rows(): home = [lax.ppermute(packed[k], everyone, back[k]) for k in (1, 0)][::-1]  4.22 us
    pallas_call x1, Pallas kernels, finish(): pl.pallas_call(adapter_back_kernel, in_specs=[vmem()] * 9, out_specs=[hbm...  3.95 us
    pallas_call x1, Pallas kernels, final_part(): pl.pallas_call(final_kernel, in_specs=[vmem()] * 14, out_specs=[vmem()] *...  3.81 us
  transfers between devices with their start and end apart: 23, of which 4 were waited for; matrix products, arithmetic and copies ran while one was open for 0% of the time, Pallas kernels for 28%

profile of v10, /device:TPU:1, one launch (start us, length us, event | category | flops | bytes accessed | tf_op | source)
XLA Modules:
  0.0 73.7 jit_solution(2220565610748749850)
XLA Ops:
  0.6 1.2 %split.2 = (bf16[64,1152]{1,0:T(8,128)(2,1)S(1)}, bf16[64,1152]{1,0:T(8,128)(2,1)S(1)}) custom-call(bf16[64,16,128]{2,1,0:T(8,128)(2,1)} %bitcast.37, s32[2,64]{1,0:T(2,128)} %bitcast.44), custom_call_target="tpu_custom_call" | custom-call | flops 2147483648 | bytes 1000 | tf_op jit(solution)/shard_map/split/pallas_call | solution.py:380
  1.8 4.8 %collective-permute-start = (bf16[64,1152]{1,0:T(8,128)(2,1)S(1)}, bf16[64,1152]{1,0:T(8,128)(2,1)S(1)}, u32[]{:S(2)}, u32[]{:S(2)}) collective-permute-start(bf16[64,1152]{1,0:T(8,128)(2,1)S(1)} %get-tuple-element.51), channel_id=1, source_target_pairs={{0,2},{1,3},{2,0},{3,1},{4,10},{5,11},{6,8},{7,9},{8,6},{9,7},{10,... | collective-permute-start | bytes 442376 | tf_op jit(solution)/shard_map/ppermute | solution.py:1190
  6.6 1.9 %collective-permute-start.1 = (bf16[64,1152]{1,0:T(8,128)(2,1)S(1)}, bf16[64,1152]{1,0:T(8,128)(2,1)S(1)}, u32[]{:S(2)}, u32[]{:S(2)}) collective-permute-start(bf16[64,1152]{1,0:T(8,128)(2,1)S(1)} %get-tuple-element.52), channel_id=1, source_target_pairs={{0,0},{1,1},{2,2},{3,3},{4,8},{5,9},{6,10},{7,11},{8,4},{9,5},{10,... | collective-permute-start | bytes 442376 | tf_op jit(solution)/shard_map/ppermute | solution.py:1190
  8.5 5.6 %adapter.1 = (bf16[16,2048]{1,0:T(8,128)(2,1)S(1)}, f32[16,512]{1,0:T(8,128)S(1)}, bf16[1024,3072]{1,0:T(8,128)(2,1)S(1)}, bf16[3072,1024]{1,0:T(8,128)(2,1)S(1)...) custom-call(f32[10,1024]{1,0:T(8,128)} %h_embed.1, f32[1024,512]{1,0:T(8,128)} %w_mlp1.1, f32[1,512]{1,0:T(1,128)} %bitcast.42, ...), custom_call_target="tpu_custom_call" | custom-call | flops 4294967296 | bytes 6291456 | tf_op jit(solution)/shard_map/adapter/pallas_call | solution.py:557
  14.1 0.0 copy-start
  14.1 0.0 copy-start.1
  14.1 0.0 collective-permute-done.refs_0_.own_0
  14.1 0.4 collective-permute-done.1.refs_1_.own_1
  14.5 1.2 %collective-permute-start.4 = (bf16[64,1152]{1,0:T(8,128)(2,1)S(1)}, bf16[64,1152]{1,0:T(8,128)(2,1)S(1)}, u32[]{:S(2)}, u32[]{:S(2)}) collective-permute-start(bf16[64,1152]{1,0:T(8,128)(2,1)S(1)} %collective-permute-done.refs_0_.own_0), channel_id=1, source_target_pairs={{0,1},{1,0},{2,3},{3,2},{4,5},{5,4},{6,7},{7,6},{8,9},{9,8},{10,11... | collective-permute-start | bytes 442376 | tf_op jit(solution)/shard_map/ppermute | solution.py:1196
  15.7 0.0 collective-permute-start.2
  15.7 0.2 collective-permute-start.5
  16.0 0.8 %collective-permute-start.3 = (bf16[64,1152]{1,0:T(8,128)(2,1)S(1)}, bf16[64,1152]{1,0:T(8,128)(2,1)S(1)}, u32[]{:S(2)}, u32[]{:S(2)}) collective-permute-start(bf16[64,1152]{1,0:T(8,128)(2,1)S(1)} %collective-permute-done.1.refs_1_.own_1), channel_id=1, source_target_pairs={{0,8},{8,0},{16,24},{24,16},{1,9},{9,1},{17,25},{25,17},{2,10},{10... | collective-permute-start | bytes 442376 | tf_op jit(solution)/shard_map/ppermute | solution.py:1197
  16.8 1.2 %split.3 = (bf16[64,1024]{1,0:T(8,128)(2,1)S(1)}, bf16[64,1024]{1,0:T(8,128)(2,1)S(1)}) custom-call(bf16[64,16,128]{2,1,0:T(8,128)(2,1)} %bitcast.38), custom_call_target="tpu_custom_call" | custom-call | flops 2147483648 | bytes 1000 | tf_op jit(solution)/shard_map/split/pallas_call | solution.py:380
  17.9 0.0 collective-permute-done.2.refs_2_
  17.9 0.0 collective-permute-done.3.refs_3_
  17.9 1.8 %collective-permute-start.8 = (bf16[64,1024]{1,0:T(8,128)(2,1)S(1)}, bf16[64,1024]{1,0:T(8,128)(2,1)S(1)}, u32[]{:S(2)}, u32[]{:S(2)}) collective-permute-start(bf16[64,1024]{1,0:T(8,128)(2,1)S(1)} %get-tuple-element.64), channel_id=1, source_target_pairs={{0,2},{1,3},{2,0},{3,1},{4,10},{5,11},{6,8},{7,9},{8,6},{9,7},{10,... | collective-permute-start | bytes 393224 | tf_op jit(solution)/shard_map/ppermute | solution.py:1198
  19.7 2.5 %collective-permute-start.9 = (bf16[64,1024]{1,0:T(8,128)(2,1)S(1)}, bf16[64,1024]{1,0:T(8,128)(2,1)S(1)}, u32[]{:S(2)}, u32[]{:S(2)}) collective-permute-start(bf16[64,1024]{1,0:T(8,128)(2,1)S(1)} %get-tuple-element.65), channel_id=1, source_target_pairs={{0,0},{1,1},{2,2},{3,3},{4,8},{5,9},{6,10},{7,11},{8,4},{9,5},{10,... | collective-permute-start | bytes 393224 | tf_op jit(solution)/shard_map/ppermute | solution.py:1198
  22.3 0.0 collective-permute-done.4.refs_0_
  22.3 0.1 collective-permute-start.6
  22.4 0.0 collective-permute-done.5.refs_1_
  22.4 0.5 collective-permute-start.7
  22.9 0.0 copy-done
  22.9 0.0 copy-done.1
  22.9 2.1 %project.2 = (bf16[256,3072]{1,0:T(8,128)(2,1)S(1)}, bf16[256,128]{1,0:T(8,128)(2,1)S(1)}) custom-call(bf16[64,1152]{1,0:T(8,128)(2,1)S(1)} %collective-permute-done.refs_0_.own_0, bf16[64,1152]{1,0:T(8,128)(2,1)S(1)} %collective-permute-done.1.refs_1_.own_1, bf16[64,1152]{1,0:T(8,128)(2,1)S(1)} %collective-permute-done.2.refs_2_, ...), custom_call_target="tpu_custom_call" | custom-call | flops 1610612736 | bytes 6291456 | tf_op jit(solution)/shard_map/project/pallas_call | solution.py:454
  25.0 0.0 copy-start.2
  25.0 0.0 copy-start.3
  25.0 0.0 collective-permute-done.6.refs_2_
  25.0 0.0 collective-permute-done.7.refs_3_
  25.0 1.6 %project.3 = (bf16[256,3072]{1,0:T(8,128)(2,1)S(1)}, bf16[256,128]{1,0:T(8,128)(2,1)S(1)}, bf16[256,1024]{1,0:T(8,128)(2,1)S(1)}) custom-call(bf16[64,1152]{1,0:T(8,128)(2,1)S(1)} %collective-permute-done.4.refs_0_, bf16[64,1152]{1,0:T(8,128)(2,1)S(1)} %collective-permute-done.5.refs_1_, bf16[64,1152]{1,0:T(8,128)(2,1)S(1)} %collective-permute-done.6.refs_2_, ...), custom_call_target="tpu_custom_call" | custom-call | flops 1610612736 | bytes 6291456 | tf_op jit(solution)/shard_map/project/pallas_call | solution.py:454
  26.6 0.0 collective-permute-done.8.cot_0
  26.6 1.7 %collective-permute-done.9.cot_1 = bf16[64,1024]{1,0:T(8,128)(2,1)S(1)} collective-permute-done((bf16[64,1024]{1,0:T(8,128)(2,1)S(1)}, bf16[64,1024]{1,0:T(8,128)(2,1)S(1)}, u32[]{:S(2)}, u32[]{:S(2)}) %collective-permute-start.9) | collective-permute-done | bytes 131104 | tf_op jit(solution)/shard_map/ppermute | solution.py:1198
  28.3 13.9 %middle.1 = (bf16[96,1024]{1,0:T(8,128)(2,1)S(1)}, bf16[96,1024]{1,0:T(8,128)(2,1)S(1)}, bf16[128,1152]{1,0:T(8,128)(2,1)S(1)}, f32[128,1024]{1,0:T(8,128)S(1)}) custom-call(bf16[256,3072]{1,0:T(8,128)(2,1)S(1)} %get-tuple-element.57.qkv_a.queries, bf16[256,3072]{1,0:T(8,128)(2,1)S(1)} %get-tuple-element.58.qkv_b, ...), custom_call_target="tpu_custom_call" | custom-call | flops 2147483648 | bytes 1000 | tf_op jit(solution)/shard_map/middle/pallas_call | solution.py:871
  42.3 1.3 %collective-permute-start.16 = (bf16[128,1152]{1,0:T(8,128)(2,1)S(1)}, bf16[128,1152]{1,0:T(8,128)(2,1)S(1)}, u32[]{:S(2)}, u32[]{:S(2)}) collective-permute-start(bf16[128,1152]{1,0:T(8,128)(2,1)S(1)} %get-tuple-element.66.grads.grads_0), channel_id=1, source_target_pairs={{0,1},{1,0},{2,3},{3,2},{4,5},{5,4},{6,7},{7,6},{8,9},{9,8},{10,11... | collective-permute-start | bytes 884744 | tf_op jit(solution)/shard_map/ppermute | solution.py:1206
  43.6 1.4 %prefix.1.order.own = bf16[16,2048]{1,0:T(8,128)(2,1)S(1)} custom-call(bf16[256,3072]{1,0:T(8,128)(2,1)S(1)} %get-tuple-element.57.qkv_a.queries, bf16[128,1152]{1,0:T(8,128)(2,1)S(1)} %get-tuple-element.66.grads.grads_0, bf16[16,2048]{1,0:T(8,128)(2,1)S(1)} %get-tuple-element.61.prefix_kv), custom_call_target="tpu_custom_call" | custom-call | flops 1000 | bytes 1000 | tf_op jit(solution)/shard_map/prefix/pallas_call | solution.py:951
  44.9 0.0 collective-permute-start.12
  44.9 1.6 %collective-permute-start.11 = (bf16[16,2048]{1,0:T(8,128)(2,1)S(1)}, bf16[16,2048]{1,0:T(8,128)(2,1)S(1)}, u32[]{:S(2)}, u32[]{:S(2)}) collective-permute-start(bf16[16,2048]{1,0:T(8,128)(2,1)S(1)} %prefix.1.order.own), channel_id=1, source_target_pairs={{0,8},{8,0},{16,24},{24,16},{1,9},{9,1},{17,25},{25,17},{2,10},{10... | collective-permute-start | bytes 196616 | tf_op jit(solution)/shard_map/ppermute | solution.py:1209
  46.5 0.3 collective-permute-start.10
  46.8 0.3 collective-permute-start.15
  47.1 3.7 %query.1 = (f32[128,1024]{1,0:T(8,128)S(1)}, bf16[256,3072]{1,0:T(8,128)(2,1)S(1)}) custom-call(bf16[256,3072]{1,0:T(8,128)(2,1)S(1)} %get-tuple-element.57.qkv_a.queries, bf16[256,3072]{1,0:T(8,128)(2,1)S(1)} %get-tuple-element.58.qkv_b, bf16[256,128]{1,0:T(8,128)(2,1)S(1)} %get-tuple-element.59.marks_a, ...), custom_call_target="tpu_custom_call", output_to_operand_aliasing={{1}: (1, {})} | custom-call | flops 2147483648 | bytes 1000 | tf_op jit(solution)/shard_map/query/pallas_call | solution.py:1065
  50.8 0.0 collective-permute-done.12.part_2
  50.8 0.0 collective-permute-done.11.part_1
  50.8 0.0 collective-permute-done.10.part_0
  50.8 0.1 pack.1
  50.9 0.0 collective-permute-done.16.grads_2
  50.9 0.3 collective-permute-start.17
  51.2 2.1 %collective-permute-start.13 = (bf16[96,1024]{1,0:T(8,128)(2,1)S(1)}, bf16[96,1024]{1,0:T(8,128)(2,1)S(1)}, u32[]{:S(2)}, u32[]{:S(2)}) collective-permute-start(bf16[96,1024]{1,0:T(8,128)(2,1)S(1)} %get-tuple-element.75), channel_id=1, source_target_pairs={{2,0},{3,1},{0,2},{1,3},{10,4},{11,5},{8,6},{9,7},{6,8},{7,9},{4,1... | collective-permute-start | bytes 589832 | tf_op jit(solution)/shard_map/ppermute | solution.py:1214
  53.3 2.1 %collective-permute-start.14 = (bf16[96,1024]{1,0:T(8,128)(2,1)S(1)}, bf16[96,1024]{1,0:T(8,128)(2,1)S(1)}, u32[]{:S(2)}, u32[]{:S(2)}) collective-permute-start(bf16[96,1024]{1,0:T(8,128)(2,1)S(1)} %get-tuple-element.76), channel_id=1, source_target_pairs={{0,0},{1,1},{2,2},{3,3},{8,4},{9,5},{10,6},{11,7},{4,8},{5,9},{6,1... | collective-permute-start | bytes 589832 | tf_op jit(solution)/shard_map/ppermute | solution.py:1214
  55.4 0.0 collective-permute-done.15.grads_1
  55.5 0.0 collective-permute-done.17.grads_3
  55.5 3.8 %final.1 = (bf16[64,1024]{1,0:T(8,128)(2,1)S(1)}, bf16[64,1024]{1,0:T(8,128)(2,1)S(1)}) custom-call(bf16[256,3072]{1,0:T(8,128)(2,1)S(1)} %get-tuple-element.57.qkv_a.queries, bf16[256,3072]{1,0:T(8,128)(2,1)S(1)} %get-tuple-element.80.qkv_b, bf16[256,128]{1,0:T(8,128)(2,1)S(1)} %get-tuple-element.59.marks_a, ...), custom_call_target="tpu_custom_call" | custom-call | flops 1000 | bytes 1000 | tf_op jit(solution)/shard_map/final/pallas_call | solution.py:1135
  59.3 1.7 %collective-permute-start.18 = (bf16[64,1024]{1,0:T(8,128)(2,1)S(1)}, bf16[64,1024]{1,0:T(8,128)(2,1)S(1)}, u32[]{:S(2)}, u32[]{:S(2)}) collective-permute-start(bf16[64,1024]{1,0:T(8,128)(2,1)S(1)} %get-tuple-element.83), channel_id=1, source_target_pairs={{2,0},{3,1},{0,2},{1,3},{10,4},{11,5},{8,6},{9,7},{6,8},{7,9},{4,1... | collective-permute-start | bytes 393224 | tf_op jit(solution)/shard_map/ppermute | solution.py:1228
  61.0 3.4 %collective-permute-start.19 = (bf16[64,1024]{1,0:T(8,128)(2,1)S(1)}, bf16[64,1024]{1,0:T(8,128)(2,1)S(1)}, u32[]{:S(2)}, u32[]{:S(2)}) collective-permute-start(bf16[64,1024]{1,0:T(8,128)(2,1)S(1)} %get-tuple-element.84), channel_id=1, source_target_pairs={{0,0},{1,1},{2,2},{3,3},{8,4},{9,5},{10,6},{11,7},{4,8},{5,9},{6,1... | collective-permute-start | bytes 393224 | tf_op jit(solution)/shard_map/ppermute | solution.py:1228
  64.4 0.0 collective-permute-done.13.home_0.msg_0
  64.4 0.0 collective-permute-done.14.home_1.msg_1
  64.5 0.1 collective-permute-start.22
  64.6 0.3 collective-permute-start.21
  64.9 1.8 %collective-permute-start.20 = (bf16[16,2048]{1,0:T(8,128)(2,1)S(1)}, bf16[16,2048]{1,0:T(8,128)(2,1)S(1)}, u32[]{:S(2)}, u32[]{:S(2)}) collective-permute-start(bf16[16,2048]{1,0:T(8,128)(2,1)S(1)} %unpack.1.part_0), channel_id=1, source_target_pairs={{0,8},{8,0},{16,24},{24,16},{1,9},{9,1},{17,25},{25,17},{2,10},{10... | collective-permute-start | bytes 196616 | tf_op jit(solution)/shard_map/ppermute | solution.py:1230
  66.7 1.0 %land.1 = (bf16[64,16,128]{2,1,0:T(8,128)(2,1)}, f32[2,16,64]{2,1,0:T(8,128)}) custom-call(bf16[96,1024]{1,0:T(8,128)(2,1)S(1)} %collective-permute-done.13.home_0.msg_0, bf16[96,1024]{1,0:T(8,128)(2,1)S(1)} %collective-permute-done.14.home_1.msg_1), custom_call_target="tpu_custom_call" | custom-call | flops 1000 | bytes 1000 | tf_op jit(solution)/shard_map/land/pallas_call | solution.py:421
  67.7 0.8 %collective-permute-done.22.part_3 = bf16[16,2048]{1,0:T(8,128)(2,1)S(1)} collective-permute-done((bf16[16,2048]{1,0:T(8,128)(2,1)S(1)}, bf16[16,2048]{1,0:T(8,128)(2,1)S(1)}, u32[]{:S(2)}, u32[]{:S(2)}) %collective-permute-start.22) | collective-permute-done | bytes 65568 | tf_op jit(solution)/shard_map/ppermute | solution.py:1231
  68.4 0.0 collective-permute-done.21.part_2
  68.5 0.0 collective-permute-done.20.part_1
  68.5 0.0 collective-permute-done.18.home_0
  68.5 1.1 %collective-permute-done.19.home_1 = bf16[64,1024]{1,0:T(8,128)(2,1)S(1)} collective-permute-done((bf16[64,1024]{1,0:T(8,128)(2,1)S(1)}, bf16[64,1024]{1,0:T(8,128)(2,1)S(1)}, u32[]{:S(2)}, u32[]{:S(2)}) %collective-permute-start.19) | collective-permute-done | bytes 131104 | tf_op jit(solution)/shard_map/ppermute | solution.py:1228
  69.6 3.9 %finish.1 = (f32[1024,128]{1,0:T(8,128)}, f32[10,1024]{1,0:T(8,128)}, f32[1024,512]{1,0:T(8,128)}, f32[1,512]{1,0:T(1,128)}, f32[512,2048]{1,0:T(8,128)}, /*index=5*/f32[1,2048]{1,0:T(1,128)}) custom-call(bf16[64,1024]{1,0:T(8,128)(2,1)S(1)} %collective-permute-done.18.home_0, bf16[64,1024]{1,0:T(8,128)(2,1)S(1)} %collective-permute-done.19.home_1, ...), custom_call_target="tpu_custom_call" | custom-call | flops 1000 | bytes 1000 | tf_op jit(solution)/shard_map/finish/pallas_call | solution.py:654
  (3 shorter events, 0.0 us)
Async XLA Ops:
  1.8 12.3 %collective-permute-start = (bf16[64,1152]{1,0:T(8,128)(2,1)S(1)}, bf16[64,1152]{1,0:T(8,128)(2,1)S(1)}, u32[]{:S(2)}, u32[]{:S(2)}) collective-permute-start(bf16[64,1152]{1,0:T(8,128)(2,1)S(1)} %get-tuple-element.51), channel_id=1, source_target_pairs={{0,2},{1,3},{2,0},{3,1},{4,10},{5,11},{6,8},{7,9},{8,6},{9,7},{10,... | collective-permute-start | bytes 442376 | tf_op jit(solution)/shard_map/ppermute | solution.py:1190
  6.6 7.9 %collective-permute-start.1 = (bf16[64,1152]{1,0:T(8,128)(2,1)S(1)}, bf16[64,1152]{1,0:T(8,128)(2,1)S(1)}, u32[]{:S(2)}, u32[]{:S(2)}) collective-permute-start(bf16[64,1152]{1,0:T(8,128)(2,1)S(1)} %get-tuple-element.52), channel_id=1, source_target_pairs={{0,0},{1,1},{2,2},{3,3},{4,8},{5,9},{6,10},{7,11},{8,4},{9,5},{10,... | collective-permute-start | bytes 442376 | tf_op jit(solution)/shard_map/ppermute | solution.py:1190
  14.1 8.8 %copy-start = (f32[1024]{0:T(1024)S(1)}, f32[1024]{0:T(1024)}, u32[]{:S(2)}) copy-start(f32[1024]{0:T(1024)} %param.18) | copy-start | bytes 12292
  14.1 8.8 %copy-start.1 = (f32[1024]{0:T(1024)S(1)}, f32[1024]{0:T(1024)}, u32[]{:S(2)}) copy-start(f32[1024]{0:T(1024)} %param.19) | copy-start | bytes 12292
  14.5 7.8 %collective-permute-start.4 = (bf16[64,1152]{1,0:T(8,128)(2,1)S(1)}, bf16[64,1152]{1,0:T(8,128)(2,1)S(1)}, u32[]{:S(2)}, u32[]{:S(2)}) collective-permute-start(bf16[64,1152]{1,0:T(8,128)(2,1)S(1)} %collective-permute-done.refs_0_.own_0), channel_id=1, source_target_pairs={{0,1},{1,0},{2,3},{3,2},{4,5},{5,4},{6,7},{7,6},{8,9},{9,8},{10,11... | collective-permute-start | bytes 442376 | tf_op jit(solution)/shard_map/ppermute | solution.py:1196
  15.7 2.2 %collective-permute-start.2 = (bf16[64,1152]{1,0:T(8,128)(2,1)S(1)}, bf16[64,1152]{1,0:T(8,128)(2,1)S(1)}, u32[]{:S(2)}, u32[]{:S(2)}) collective-permute-start(bf16[64,1152]{1,0:T(8,128)(2,1)S(1)} %collective-permute-done.refs_0_.own_0), channel_id=1, source_target_pairs={{0,8},{8,0},{16,24},{24,16},{1,9},{9,1},{17,25},{25,17},{2,10},{10... | collective-permute-start | bytes 442376 | tf_op jit(solution)/shard_map/ppermute | solution.py:1197
  15.7 6.6 %collective-permute-start.5 = (bf16[64,1152]{1,0:T(8,128)(2,1)S(1)}, bf16[64,1152]{1,0:T(8,128)(2,1)S(1)}, u32[]{:S(2)}, u32[]{:S(2)}) collective-permute-start(bf16[64,1152]{1,0:T(8,128)(2,1)S(1)} %collective-permute-done.1.refs_1_.own_1), channel_id=1, source_target_pairs={{0,1},{1,0},{2,3},{3,2},{4,5},{5,4},{6,7},{7,6},{8,9},{9,8},{10,11... | collective-permute-start | bytes 442376 | tf_op jit(solution)/shard_map/ppermute | solution.py:1196
  16.0 2.0 %collective-permute-start.3 = (bf16[64,1152]{1,0:T(8,128)(2,1)S(1)}, bf16[64,1152]{1,0:T(8,128)(2,1)S(1)}, u32[]{:S(2)}, u32[]{:S(2)}) collective-permute-start(bf16[64,1152]{1,0:T(8,128)(2,1)S(1)} %collective-permute-done.1.refs_1_.own_1), channel_id=1, source_target_pairs={{0,8},{8,0},{16,24},{24,16},{1,9},{9,1},{17,25},{25,17},{2,10},{10... | collective-permute-start | bytes 442376 | tf_op jit(solution)/shard_map/ppermute | solution.py:1197
  17.9 8.6 %collective-permute-start.8 = (bf16[64,1024]{1,0:T(8,128)(2,1)S(1)}, bf16[64,1024]{1,0:T(8,128)(2,1)S(1)}, u32[]{:S(2)}, u32[]{:S(2)}) collective-permute-start(bf16[64,1024]{1,0:T(8,128)(2,1)S(1)} %get-tuple-element.64), channel_id=1, source_target_pairs={{0,2},{1,3},{2,0},{3,1},{4,10},{5,11},{6,8},{7,9},{8,6},{9,7},{10,... | collective-permute-start | bytes 393224 | tf_op jit(solution)/shard_map/ppermute | solution.py:1198
  19.7 8.6 %collective-permute-start.9 = (bf16[64,1024]{1,0:T(8,128)(2,1)S(1)}, bf16[64,1024]{1,0:T(8,128)(2,1)S(1)}, u32[]{:S(2)}, u32[]{:S(2)}) collective-permute-start(bf16[64,1024]{1,0:T(8,128)(2,1)S(1)} %get-tuple-element.65), channel_id=1, source_target_pairs={{0,0},{1,1},{2,2},{3,3},{4,8},{5,9},{6,10},{7,11},{8,4},{9,5},{10,... | collective-permute-start | bytes 393224 | tf_op jit(solution)/shard_map/ppermute | solution.py:1198
  22.3 2.7 %collective-permute-start.6 = (bf16[64,1152]{1,0:T(8,128)(2,1)S(1)}, bf16[64,1152]{1,0:T(8,128)(2,1)S(1)}, u32[]{:S(2)}, u32[]{:S(2)}) collective-permute-start(bf16[64,1152]{1,0:T(8,128)(2,1)S(1)} %collective-permute-done.4.refs_0_), channel_id=1, source_target_pairs={{0,8},{8,0},{16,24},{24,16},{1,9},{9,1},{17,25},{25,17},{2,10},{10... | collective-permute-start | bytes 442376 | tf_op jit(solution)/shard_map/ppermute | solution.py:1199
  22.4 2.6 %collective-permute-start.7 = (bf16[64,1152]{1,0:T(8,128)(2,1)S(1)}, bf16[64,1152]{1,0:T(8,128)(2,1)S(1)}, u32[]{:S(2)}, u32[]{:S(2)}) collective-permute-start(bf16[64,1152]{1,0:T(8,128)(2,1)S(1)} %collective-permute-done.5.refs_1_), channel_id=1, source_target_pairs={{0,8},{8,0},{16,24},{24,16},{1,9},{9,1},{17,25},{25,17},{2,10},{10... | collective-permute-start | bytes 442376 | tf_op jit(solution)/shard_map/ppermute | solution.py:1199
  25.0 3.3 %copy-start.2 = (f32[1024]{0:T(1024)S(1)}, f32[1024]{0:T(1024)}, u32[]{:S(2)}) copy-start(f32[1024]{0:T(1024)} %param.22) | copy-start | bytes 12292
  25.0 3.3 %copy-start.3 = (f32[1024]{0:T(1024)S(1)}, f32[1024]{0:T(1024)}, u32[]{:S(2)}) copy-start(f32[1024]{0:T(1024)} %param.23) | copy-start | bytes 12292
  42.3 8.7 %collective-permute-start.16 = (bf16[128,1152]{1,0:T(8,128)(2,1)S(1)}, bf16[128,1152]{1,0:T(8,128)(2,1)S(1)}, u32[]{:S(2)}, u32[]{:S(2)}) collective-permute-start(bf16[128,1152]{1,0:T(8,128)(2,1)S(1)} %get-tuple-element.66.grads.grads_0), channel_id=1, source_target_pairs={{0,1},{1,0},{2,3},{3,2},{4,5},{5,4},{6,7},{7,6},{8,9},{9,8},{10,11... | collective-permute-start | bytes 884744 | tf_op jit(solution)/shard_map/ppermute | solution.py:1206
  44.9 5.9 %collective-permute-start.12 = (bf16[16,2048]{1,0:T(8,128)(2,1)S(1)}, bf16[16,2048]{1,0:T(8,128)(2,1)S(1)}, u32[]{:S(2)}, u32[]{:S(2)}) collective-permute-start(bf16[16,2048]{1,0:T(8,128)(2,1)S(1)} %prefix.1.order.own), channel_id=1, source_target_pairs={{0,24},{8,16},{16,8},{24,0},{1,25},{9,17},{17,9},{25,1},{2,26},{10... | collective-permute-start | bytes 196616 | tf_op jit(solution)/shard_map/ppermute | solution.py:1209
  44.9 5.9 %collective-permute-start.11 = (bf16[16,2048]{1,0:T(8,128)(2,1)S(1)}, bf16[16,2048]{1,0:T(8,128)(2,1)S(1)}, u32[]{:S(2)}, u32[]{:S(2)}) collective-permute-start(bf16[16,2048]{1,0:T(8,128)(2,1)S(1)} %prefix.1.order.own), channel_id=1, source_target_pairs={{0,8},{8,0},{16,24},{24,16},{1,9},{9,1},{17,25},{25,17},{2,10},{10... | collective-permute-start | bytes 196616 | tf_op jit(solution)/shard_map/ppermute | solution.py:1209
  46.5 4.3 %collective-permute-start.10 = (bf16[16,2048]{1,0:T(8,128)(2,1)S(1)}, bf16[16,2048]{1,0:T(8,128)(2,1)S(1)}, u32[]{:S(2)}, u32[]{:S(2)}) collective-permute-start(bf16[16,2048]{1,0:T(8,128)(2,1)S(1)} %prefix.1.order.own), channel_id=1, source_target_pairs={{0,16},{8,24},{16,0},{24,8},{1,17},{9,25},{17,1},{25,9},{2,18},{10... | collective-permute-start | bytes 196616 | tf_op jit(solution)/shard_map/ppermute | solution.py:1209
  46.8 8.6 %collective-permute-start.15 = (bf16[128,1152]{1,0:T(8,128)(2,1)S(1)}, bf16[128,1152]{1,0:T(8,128)(2,1)S(1)}, u32[]{:S(2)}, u32[]{:S(2)}) collective-permute-start(bf16[128,1152]{1,0:T(8,128)(2,1)S(1)} %get-tuple-element.66.grads.grads_0), channel_id=1, source_target_pairs={{0,8},{8,0},{16,24},{24,16},{1,9},{9,1},{17,25},{25,17},{2,10},{10... | collective-permute-start | bytes 884744 | tf_op jit(solution)/shard_map/ppermute | solution.py:1207
  50.9 4.5 %collective-permute-start.17 = (bf16[128,1152]{1,0:T(8,128)(2,1)S(1)}, bf16[128,1152]{1,0:T(8,128)(2,1)S(1)}, u32[]{:S(2)}, u32[]{:S(2)}) collective-permute-start(bf16[128,1152]{1,0:T(8,128)(2,1)S(1)} %collective-permute-done.16.grads_2), channel_id=1, source_target_pairs={{0,8},{8,0},{16,24},{24,16},{1,9},{9,1},{17,25},{25,17},{2,10},{10... | collective-permute-start | bytes 884744 | tf_op jit(solution)/shard_map/ppermute | solution.py:1215
  51.2 13.2 %collective-permute-start.13 = (bf16[96,1024]{1,0:T(8,128)(2,1)S(1)}, bf16[96,1024]{1,0:T(8,128)(2,1)S(1)}, u32[]{:S(2)}, u32[]{:S(2)}) collective-permute-start(bf16[96,1024]{1,0:T(8,128)(2,1)S(1)} %get-tuple-element.75), channel_id=1, source_target_pairs={{2,0},{3,1},{0,2},{1,3},{10,4},{11,5},{8,6},{9,7},{6,8},{7,9},{4,1... | collective-permute-start | bytes 589832 | tf_op jit(solution)/shard_map/ppermute | solution.py:1214
  53.3 11.1 %collective-permute-start.14 = (bf16[96,1024]{1,0:T(8,128)(2,1)S(1)}, bf16[96,1024]{1,0:T(8,128)(2,1)S(1)}, u32[]{:S(2)}, u32[]{:S(2)}) collective-permute-start(bf16[96,1024]{1,0:T(8,128)(2,1)S(1)} %get-tuple-element.76), channel_id=1, source_target_pairs={{0,0},{1,1},{2,2},{3,3},{8,4},{9,5},{10,6},{11,7},{4,8},{5,9},{6,1... | collective-permute-start | bytes 589832 | tf_op jit(solution)/shard_map/ppermute | solution.py:1214
  59.3 9.2 %collective-permute-start.18 = (bf16[64,1024]{1,0:T(8,128)(2,1)S(1)}, bf16[64,1024]{1,0:T(8,128)(2,1)S(1)}, u32[]{:S(2)}, u32[]{:S(2)}) collective-permute-start(bf16[64,1024]{1,0:T(8,128)(2,1)S(1)} %get-tuple-element.83), channel_id=1, source_target_pairs={{2,0},{3,1},{0,2},{1,3},{10,4},{11,5},{8,6},{9,7},{6,8},{7,9},{4,1... | collective-permute-start | bytes 393224 | tf_op jit(solution)/shard_map/ppermute | solution.py:1228
  61.0 8.6 %collective-permute-start.19 = (bf16[64,1024]{1,0:T(8,128)(2,1)S(1)}, bf16[64,1024]{1,0:T(8,128)(2,1)S(1)}, u32[]{:S(2)}, u32[]{:S(2)}) collective-permute-start(bf16[64,1024]{1,0:T(8,128)(2,1)S(1)} %get-tuple-element.84), channel_id=1, source_target_pairs={{0,0},{1,1},{2,2},{3,3},{8,4},{9,5},{10,6},{11,7},{4,8},{5,9},{6,1... | collective-permute-start | bytes 393224 | tf_op jit(solution)/shard_map/ppermute | solution.py:1228
  64.5 4.0 %collective-permute-start.22 = (bf16[16,2048]{1,0:T(8,128)(2,1)S(1)}, bf16[16,2048]{1,0:T(8,128)(2,1)S(1)}, u32[]{:S(2)}, u32[]{:S(2)}) collective-permute-start(bf16[16,2048]{1,0:T(8,128)(2,1)S(1)} %unpack.1.part_0), channel_id=1, source_target_pairs={{0,9},{1,8},{2,11},{3,10},{4,13},{5,12},{6,15},{7,14},{8,1},{9,0},... | collective-permute-start | bytes 196616 | tf_op jit(solution)/shard_map/ppermute | solution.py:1231
  64.6 3.9 %collective-permute-start.21 = (bf16[16,2048]{1,0:T(8,128)(2,1)S(1)}, bf16[16,2048]{1,0:T(8,128)(2,1)S(1)}, u32[]{:S(2)}, u32[]{:S(2)}) collective-permute-start(bf16[16,2048]{1,0:T(8,128)(2,1)S(1)} %unpack.1.part_0), channel_id=1, source_target_pairs={{0,1},{1,0},{2,3},{3,2},{4,5},{5,4},{6,7},{7,6},{8,9},{9,8},{10,11... | collective-permute-start | bytes 196616 | tf_op jit(solution)/shard_map/ppermute | solution.py:1230
  64.9 3.6 %collective-permute-start.20 = (bf16[16,2048]{1,0:T(8,128)(2,1)S(1)}, bf16[16,2048]{1,0:T(8,128)(2,1)S(1)}, u32[]{:S(2)}, u32[]{:S(2)}) collective-permute-start(bf16[16,2048]{1,0:T(8,128)(2,1)S(1)} %unpack.1.part_0), channel_id=1, source_target_pairs={{0,8},{8,0},{16,24},{24,16},{1,9},{9,1},{17,25},{25,17},{2,10},{10... | collective-permute-start | bytes 196616 | tf_op jit(solution)/shard_map/ppermute | solution.py:1230

commit v11 on v9

--- a/solution.py
+++ b/solution.py
@@ -516,19 +516,19 @@
     ):
         small.append(pltpu.make_async_copy(source, target, sems.at[steps + i]))
         small[-1].start()
+    rest = []
+    for i in range(steps):
+        copy = pltpu.make_async_copy(w_mlp2.at[:, pl.ds(i * step, step)], v_mlp2.at[i], sems.at[i])
+        copy.start()
+        rest.append(copy)
     width = w_qkv.shape[0]
     weights = []
-    for i in range(3):
+    for i in (1, 2, 0):
         at = pl.ds(i * width, width)
         weights.append(
             pltpu.make_async_copy(w_qkv.at[:, at], v_qkv.at[:, at], sems.at[steps + len(small) + i])
         )
         weights[-1].start()
-    rest = []
-    for i in range(steps):
-        copy = pltpu.make_async_copy(w_mlp2.at[:, pl.ds(i * step, step)], v_mlp2.at[i], sems.at[i])
-        copy.start()
-        rest.append(copy)
     for copy in small:
         copy.wait()
     source = pad_rows(embed[...], PRE_ROWS)
@@ -538,16 +538,16 @@
     for i in range(v_mlp1.shape[0] // hidden):
         part = v_mlp1[pl.ds(i * hidden, hidden)].astype(BF16)
         turned[pl.ds(columns + i * hidden, hidden)] = part.T
-    for i, copy in enumerate(weights):
-        at = pl.ds(i * width, width)
-        copy.wait()
-        w_back[at] = v_qkv[:, at].T
     for i, copy in enumerate(rest):
         copy.wait()
         turned[pl.ds(i * step, step)] = v_mlp2[i].astype(BF16).T
         span = pl.ds(i * step, step)
         part = three_products(nn, act, v_mlp2[i]) + b_mlp2[:, span]
         out[:, span] = jnp.where(iota(part.shape, 0) < embed.shape[0], part, 0.0).astype(BF16)
+    for i, copy in zip((1, 2, 0), weights):
+        at = pl.ds(i * width, width)
+        copy.wait()
+        w_back[at] = v_qkv[:, at].T
 
 
 def adapter_forward(embed, w_mlp1, b_mlp1, w_mlp2, b_mlp2, w_qkv):
@@ -1195,7 +1195,7 @@
     own = after(own, inner)
     across = [lax.ppermute(m, "blk", swap_y) for m in own]
     beside = [lax.ppermute(m, "seq", swap_core) for m in own]
-    cots = [lax.ppermute(m, everyone, there[k]) for k, m in enumerate(after(cot_msgs, beside))]
+    cots = [lax.ppermute(m, everyone, there[k]) for k, m in enumerate([after(m, b) for m, b in zip(cot_msgs, beside)])]
     beyond = [lax.ppermute(m, "seq", swap_core) for m in across]
 
     qkv_a, marks_a = project(own + beside, ln1_gain, ln1_bias, w_near)

time: 74.2 us -> 74.1 us (level)
  no operation moved by 1% of the time
where the time goes in v11:
time: 74.1 us; the launch traced here: 73.7 us
  Pallas kernels  39.4 us (53%)
  starting transfers between devices  29.2 us (39%)
  waiting for transfers between devices  4.06 us (5%)
  between operations  1.09 us (1%)
    pallas_call x1, Pallas kernels, middle_part(): pl.pallas_call(partial(middle_kernel, count), in_specs=[vmem()] * 11 + [h...  13.9 us
    ppermute x2, starting transfers between devices, body_rows(): own = [lax.ppermute(m, everyone, there[k]) for k, m in enumerate(out_msgs)]  6.68 us
    pallas_call x1, Pallas kernels, adapter_forward(): pl.pallas_call(adapter_kernel, in_specs=[hbm()] * 6, out_specs=[vmem()] *...  5.6 us
    ppermute x2, starting transfers between devices, body_rows(): lax.ppermute(m, everyone, back[k])  5.14 us
    ppermute x2, starting transfers between devices, body_rows(): lax.ppermute(m, everyone, there[k])  4.34 us
    ppermute x2, starting transfers between devices, body_rows(): home = [lax.ppermute(m, everyone, back[k]) for k, m in enumerate(packed)]  4.23 us
    pallas_call x1, Pallas kernels, finish(): pl.pallas_call(adapter_back_kernel, in_specs=[vmem()] * 9, out_specs=[hbm...  3.95 us
    pallas_call x1, Pallas kernels, final_part(): pl.pallas_call(final_kernel, in_specs=[vmem()] * 14, out_specs=[vmem()] *...  3.81 us
  transfers between devices with their start and end apart: 23, of which 4 were waited for; matrix products, arithmetic and copies ran while one was open for 0% of the time, Pallas kernels for 28%

profile of v11, /device:TPU:1, one launch (start us, length us, event | category | flops | bytes accessed | tf_op | source)
XLA Modules:
  0.0 73.7 jit_solution(10904832071604587913)
XLA Ops:
  0.6 1.2 %split.2 = (bf16[64,1152]{1,0:T(8,128)(2,1)S(1)}, bf16[64,1152]{1,0:T(8,128)(2,1)S(1)}) custom-call(bf16[64,16,128]{2,1,0:T(8,128)(2,1)} %bitcast.37, s32[2,64]{1,0:T(2,128)} %bitcast.44), custom_call_target="tpu_custom_call" | custom-call | flops 2147483648 | bytes 1000 | tf_op jit(solution)/shard_map/split/pallas_call | solution.py:380
  1.8 4.8 %collective-permute-start = (bf16[64,1152]{1,0:T(8,128)(2,1)S(1)}, bf16[64,1152]{1,0:T(8,128)(2,1)S(1)}, u32[]{:S(2)}, u32[]{:S(2)}) collective-permute-start(bf16[64,1152]{1,0:T(8,128)(2,1)S(1)} %get-tuple-element.51), channel_id=1, source_target_pairs={{0,2},{1,3},{2,0},{3,1},{4,10},{5,11},{6,8},{7,9},{8,6},{9,7},{10,... | collective-permute-start | bytes 442376 | tf_op jit(solution)/shard_map/ppermute | solution.py:1190
  6.6 1.9 %collective-permute-start.1 = (bf16[64,1152]{1,0:T(8,128)(2,1)S(1)}, bf16[64,1152]{1,0:T(8,128)(2,1)S(1)}, u32[]{:S(2)}, u32[]{:S(2)}) collective-permute-start(bf16[64,1152]{1,0:T(8,128)(2,1)S(1)} %get-tuple-element.52), channel_id=1, source_target_pairs={{0,0},{1,1},{2,2},{3,3},{4,8},{5,9},{6,10},{7,11},{8,4},{9,5},{10,... | collective-permute-start | bytes 442376 | tf_op jit(solution)/shard_map/ppermute | solution.py:1190
  8.5 5.6 %adapter.1 = (bf16[16,2048]{1,0:T(8,128)(2,1)S(1)}, f32[16,512]{1,0:T(8,128)S(1)}, bf16[1024,3072]{1,0:T(8,128)(2,1)S(1)}, bf16[3072,1024]{1,0:T(8,128)(2,1)S(1)...) custom-call(f32[10,1024]{1,0:T(8,128)} %h_embed.1, f32[1024,512]{1,0:T(8,128)} %w_mlp1.1, f32[1,512]{1,0:T(1,128)} %bitcast.42, ...), custom_call_target="tpu_custom_call" | custom-call | flops 4294967296 | bytes 6291456 | tf_op jit(solution)/shard_map/adapter/pallas_call | solution.py:557
  14.1 0.0 copy-start
  14.1 0.0 copy-start.1
  14.1 0.0 collective-permute-done.refs_0_.own_0
  14.1 0.4 collective-permute-done.1.refs_1_.own_1
  14.5 1.2 %collective-permute-start.4 = (bf16[64,1152]{1,0:T(8,128)(2,1)S(1)}, bf16[64,1152]{1,0:T(8,128)(2,1)S(1)}, u32[]{:S(2)}, u32[]{:S(2)}) collective-permute-start(bf16[64,1152]{1,0:T(8,128)(2,1)S(1)} %collective-permute-done.refs_0_.own_0), channel_id=1, source_target_pairs={{0,1},{1,0},{2,3},{3,2},{4,5},{5,4},{6,7},{7,6},{8,9},{9,8},{10,11... | collective-permute-start | bytes 442376 | tf_op jit(solution)/shard_map/ppermute | solution.py:1196
  15.7 0.0 collective-permute-start.2
  15.7 0.2 collective-permute-start.5
  16.0 0.8 %collective-permute-start.3 = (bf16[64,1152]{1,0:T(8,128)(2,1)S(1)}, bf16[64,1152]{1,0:T(8,128)(2,1)S(1)}, u32[]{:S(2)}, u32[]{:S(2)}) collective-permute-start(bf16[64,1152]{1,0:T(8,128)(2,1)S(1)} %collective-permute-done.1.refs_1_.own_1), channel_id=1, source_target_pairs={{0,8},{8,0},{16,24},{24,16},{1,9},{9,1},{17,25},{25,17},{2,10},{10... | collective-permute-start | bytes 442376 | tf_op jit(solution)/shard_map/ppermute | solution.py:1197
  16.8 1.2 %split.3 = (bf16[64,1024]{1,0:T(8,128)(2,1)S(1)}, bf16[64,1024]{1,0:T(8,128)(2,1)S(1)}) custom-call(bf16[64,16,128]{2,1,0:T(8,128)(2,1)} %bitcast.38), custom_call_target="tpu_custom_call" | custom-call | flops 2147483648 | bytes 1000 | tf_op jit(solution)/shard_map/split/pallas_call | solution.py:380
  17.9 0.0 collective-permute-done.2.refs_2_
  17.9 1.8 %collective-permute-start.8 = (bf16[64,1024]{1,0:T(8,128)(2,1)S(1)}, bf16[64,1024]{1,0:T(8,128)(2,1)S(1)}, u32[]{:S(2)}, u32[]{:S(2)}) collective-permute-start(bf16[64,1024]{1,0:T(8,128)(2,1)S(1)} %get-tuple-element.63), channel_id=1, source_target_pairs={{0,2},{1,3},{2,0},{3,1},{4,10},{5,11},{6,8},{7,9},{8,6},{9,7},{10,... | collective-permute-start | bytes 393224 | tf_op jit(solution)/shard_map/ppermute | solution.py:1198
  19.7 0.0 collective-permute-done.3.refs_3_
  19.7 2.5 %collective-permute-start.9 = (bf16[64,1024]{1,0:T(8,128)(2,1)S(1)}, bf16[64,1024]{1,0:T(8,128)(2,1)S(1)}, u32[]{:S(2)}, u32[]{:S(2)}) collective-permute-start(bf16[64,1024]{1,0:T(8,128)(2,1)S(1)} %get-tuple-element.65), channel_id=1, source_target_pairs={{0,0},{1,1},{2,2},{3,3},{4,8},{5,9},{6,10},{7,11},{8,4},{9,5},{10,... | collective-permute-start | bytes 393224 | tf_op jit(solution)/shard_map/ppermute | solution.py:1198
  22.3 0.0 collective-permute-done.4.refs_0_
  22.3 0.1 collective-permute-start.6
  22.4 0.0 collective-permute-done.5.refs_1_
  22.4 0.5 collective-permute-start.7
  22.9 0.0 copy-done
  22.9 2.1 %project.2 = (bf16[256,3072]{1,0:T(8,128)(2,1)S(1)}, bf16[256,128]{1,0:T(8,128)(2,1)S(1)}) custom-call(bf16[64,1152]{1,0:T(8,128)(2,1)S(1)} %collective-permute-done.refs_0_.own_0, bf16[64,1152]{1,0:T(8,128)(2,1)S(1)} %collective-permute-done.1.refs_1_.own_1, bf16[64,1152]{1,0:T(8,128)(2,1)S(1)} %collective-permute-done.2.refs_2_, ...), custom_call_target="tpu_custom_call" | custom-call | flops 1610612736 | bytes 6291456 | tf_op jit(solution)/shard_map/project/pallas_call | solution.py:454
  25.0 0.0 copy-start.2
  25.0 0.0 copy-start.3
  25.0 0.0 collective-permute-done.6.refs_2_
  25.0 0.0 collective-permute-done.7.refs_3_
  25.0 1.5 %project.3 = (bf16[256,3072]{1,0:T(8,128)(2,1)S(1)}, bf16[256,128]{1,0:T(8,128)(2,1)S(1)}, bf16[256,1024]{1,0:T(8,128)(2,1)S(1)}) custom-call(bf16[64,1152]{1,0:T(8,128)(2,1)S(1)} %collective-permute-done.4.refs_0_, bf16[64,1152]{1,0:T(8,128)(2,1)S(1)} %collective-permute-done.5.refs_1_, bf16[64,1152]{1,0:T(8,128)(2,1)S(1)} %collective-permute-done.6.refs_2_, ...), custom_call_target="tpu_custom_call" | custom-call | flops 1610612736 | bytes 6291456 | tf_op jit(solution)/shard_map/project/pallas_call | solution.py:454
  26.6 0.0 collective-permute-done.8.cot_0
  26.6 1.7 %collective-permute-done.9.cot_1 = bf16[64,1024]{1,0:T(8,128)(2,1)S(1)} collective-permute-done((bf16[64,1024]{1,0:T(8,128)(2,1)S(1)}, bf16[64,1024]{1,0:T(8,128)(2,1)S(1)}, u32[]{:S(2)}, u32[]{:S(2)}) %collective-permute-start.9) | collective-permute-done | bytes 131104 | tf_op jit(solution)/shard_map/ppermute | solution.py:1198
  28.3 0.0 copy-done.2
  28.3 13.9 %middle.1 = (bf16[96,1024]{1,0:T(8,128)(2,1)S(1)}, bf16[96,1024]{1,0:T(8,128)(2,1)S(1)}, bf16[128,1152]{1,0:T(8,128)(2,1)S(1)}, f32[128,1024]{1,0:T(8,128)S(1)}) custom-call(bf16[256,3072]{1,0:T(8,128)(2,1)S(1)} %get-tuple-element.57.qkv_a.queries, bf16[256,3072]{1,0:T(8,128)(2,1)S(1)} %get-tuple-element.58.qkv_b, ...), custom_call_target="tpu_custom_call" | custom-call | flops 2147483648 | bytes 1000 | tf_op jit(solution)/shard_map/middle/pallas_call | solution.py:871
  42.3 1.3 %collective-permute-start.16 = (bf16[128,1152]{1,0:T(8,128)(2,1)S(1)}, bf16[128,1152]{1,0:T(8,128)(2,1)S(1)}, u32[]{:S(2)}, u32[]{:S(2)}) collective-permute-start(bf16[128,1152]{1,0:T(8,128)(2,1)S(1)} %get-tuple-element.66.grads.grads_0), channel_id=1, source_target_pairs={{0,1},{1,0},{2,3},{3,2},{4,5},{5,4},{6,7},{7,6},{8,9},{9,8},{10,11... | collective-permute-start | bytes 884744 | tf_op jit(solution)/shard_map/ppermute | solution.py:1206
  43.6 1.4 %prefix.1.order.own = bf16[16,2048]{1,0:T(8,128)(2,1)S(1)} custom-call(bf16[256,3072]{1,0:T(8,128)(2,1)S(1)} %get-tuple-element.57.qkv_a.queries, bf16[128,1152]{1,0:T(8,128)(2,1)S(1)} %get-tuple-element.66.grads.grads_0, bf16[16,2048]{1,0:T(8,128)(2,1)S(1)} %get-tuple-element.61.prefix_kv), custom_call_target="tpu_custom_call" | custom-call | flops 1000 | bytes 1000 | tf_op jit(solution)/shard_map/prefix/pallas_call | solution.py:951
  44.9 0.0 collective-permute-start.12
  44.9 1.6 %collective-permute-start.11 = (bf16[16,2048]{1,0:T(8,128)(2,1)S(1)}, bf16[16,2048]{1,0:T(8,128)(2,1)S(1)}, u32[]{:S(2)}, u32[]{:S(2)}) collective-permute-start(bf16[16,2048]{1,0:T(8,128)(2,1)S(1)} %prefix.1.order.own), channel_id=1, source_target_pairs={{0,8},{8,0},{16,24},{24,16},{1,9},{9,1},{17,25},{25,17},{2,10},{10... | collective-permute-start | bytes 196616 | tf_op jit(solution)/shard_map/ppermute | solution.py:1209
  46.5 0.2 collective-permute-start.10
  46.8 0.3 collective-permute-start.15
  47.1 3.7 %query.1 = (f32[128,1024]{1,0:T(8,128)S(1)}, bf16[256,3072]{1,0:T(8,128)(2,1)S(1)}) custom-call(bf16[256,3072]{1,0:T(8,128)(2,1)S(1)} %get-tuple-element.57.qkv_a.queries, bf16[256,3072]{1,0:T(8,128)(2,1)S(1)} %get-tuple-element.58.qkv_b, bf16[256,128]{1,0:T(8,128)(2,1)S(1)} %get-tuple-element.59.marks_a, ...), custom_call_target="tpu_custom_call", output_to_operand_aliasing={{1}: (1, {})} | custom-call | flops 2147483648 | bytes 1000 | tf_op jit(solution)/shard_map/query/pallas_call | solution.py:1065
  50.8 0.0 collective-permute-done.12.part_2
  50.8 0.0 collective-permute-done.11.part_1
  50.8 0.0 collective-permute-done.10.part_0
  50.8 0.1 pack.1
  50.9 0.0 collective-permute-done.16.grads_2
  50.9 0.3 collective-permute-start.17
  51.2 2.1 %collective-permute-start.13 = (bf16[96,1024]{1,0:T(8,128)(2,1)S(1)}, bf16[96,1024]{1,0:T(8,128)(2,1)S(1)}, u32[]{:S(2)}, u32[]{:S(2)}) collective-permute-start(bf16[96,1024]{1,0:T(8,128)(2,1)S(1)} %get-tuple-element.75), channel_id=1, source_target_pairs={{2,0},{3,1},{0,2},{1,3},{10,4},{11,5},{8,6},{9,7},{6,8},{7,9},{4,1... | collective-permute-start | bytes 589832 | tf_op jit(solution)/shard_map/ppermute | solution.py:1214
  53.3 2.1 %collective-permute-start.14 = (bf16[96,1024]{1,0:T(8,128)(2,1)S(1)}, bf16[96,1024]{1,0:T(8,128)(2,1)S(1)}, u32[]{:S(2)}, u32[]{:S(2)}) collective-permute-start(bf16[96,1024]{1,0:T(8,128)(2,1)S(1)} %get-tuple-element.76), channel_id=1, source_target_pairs={{0,0},{1,1},{2,2},{3,3},{8,4},{9,5},{10,6},{11,7},{4,8},{5,9},{6,1... | collective-permute-start | bytes 589832 | tf_op jit(solution)/shard_map/ppermute | solution.py:1214
  55.4 0.0 collective-permute-done.15.grads_1
  55.5 0.0 collective-permute-done.17.grads_3
  55.5 3.8 %final.1 = (bf16[64,1024]{1,0:T(8,128)(2,1)S(1)}, bf16[64,1024]{1,0:T(8,128)(2,1)S(1)}) custom-call(bf16[256,3072]{1,0:T(8,128)(2,1)S(1)} %get-tuple-element.57.qkv_a.queries, bf16[256,3072]{1,0:T(8,128)(2,1)S(1)} %get-tuple-element.80.qkv_b, bf16[256,128]{1,0:T(8,128)(2,1)S(1)} %get-tuple-element.59.marks_a, ...), custom_call_target="tpu_custom_call" | custom-call | flops 1000 | bytes 1000 | tf_op jit(solution)/shard_map/final/pallas_call | solution.py:1135
  59.3 1.8 %collective-permute-start.18 = (bf16[64,1024]{1,0:T(8,128)(2,1)S(1)}, bf16[64,1024]{1,0:T(8,128)(2,1)S(1)}, u32[]{:S(2)}, u32[]{:S(2)}) collective-permute-start(bf16[64,1024]{1,0:T(8,128)(2,1)S(1)} %get-tuple-element.83), channel_id=1, source_target_pairs={{2,0},{3,1},{0,2},{1,3},{10,4},{11,5},{8,6},{9,7},{6,8},{7,9},{4,1... | collective-permute-start | bytes 393224 | tf_op jit(solution)/shard_map/ppermute | solution.py:1228
  61.0 3.4 %collective-permute-start.19 = (bf16[64,1024]{1,0:T(8,128)(2,1)S(1)}, bf16[64,1024]{1,0:T(8,128)(2,1)S(1)}, u32[]{:S(2)}, u32[]{:S(2)}) collective-permute-start(bf16[64,1024]{1,0:T(8,128)(2,1)S(1)} %get-tuple-element.84), channel_id=1, source_target_pairs={{0,0},{1,1},{2,2},{3,3},{8,4},{9,5},{10,6},{11,7},{4,8},{5,9},{6,1... | collective-permute-start | bytes 393224 | tf_op jit(solution)/shard_map/ppermute | solution.py:1228
  64.4 0.0 collective-permute-done.13.home_0.msg_0
  64.4 0.0 collective-permute-done.14.home_1.msg_1
  64.5 0.1 collective-permute-start.22
  64.6 0.3 collective-permute-start.21
  64.8 1.8 %collective-permute-start.20 = (bf16[16,2048]{1,0:T(8,128)(2,1)S(1)}, bf16[16,2048]{1,0:T(8,128)(2,1)S(1)}, u32[]{:S(2)}, u32[]{:S(2)}) collective-permute-start(bf16[16,2048]{1,0:T(8,128)(2,1)S(1)} %unpack.1.part_0), channel_id=1, source_target_pairs={{0,8},{8,0},{16,24},{24,16},{1,9},{9,1},{17,25},{25,17},{2,10},{10... | collective-permute-start | bytes 196616 | tf_op jit(solution)/shard_map/ppermute | solution.py:1230
  66.7 1.0 %land.1 = (bf16[64,16,128]{2,1,0:T(8,128)(2,1)}, f32[2,16,64]{2,1,0:T(8,128)}) custom-call(bf16[96,1024]{1,0:T(8,128)(2,1)S(1)} %collective-permute-done.13.home_0.msg_0, bf16[96,1024]{1,0:T(8,128)(2,1)S(1)} %collective-permute-done.14.home_1.msg_1), custom_call_target="tpu_custom_call" | custom-call | flops 1000 | bytes 1000 | tf_op jit(solution)/shard_map/land/pallas_call | solution.py:421
  67.7 0.8 %collective-permute-done.22.part_3 = bf16[16,2048]{1,0:T(8,128)(2,1)S(1)} collective-permute-done((bf16[16,2048]{1,0:T(8,128)(2,1)S(1)}, bf16[16,2048]{1,0:T(8,128)(2,1)S(1)}, u32[]{:S(2)}, u32[]{:S(2)}) %collective-permute-start.22) | collective-permute-done | bytes 65568 | tf_op jit(solution)/shard_map/ppermute | solution.py:1231
  68.4 0.0 collective-permute-done.21.part_2
  68.4 0.0 collective-permute-done.20.part_1
  68.4 0.0 collective-permute-done.18.home_0
  68.5 1.2 %collective-permute-done.19.home_1 = bf16[64,1024]{1,0:T(8,128)(2,1)S(1)} collective-permute-done((bf16[64,1024]{1,0:T(8,128)(2,1)S(1)}, bf16[64,1024]{1,0:T(8,128)(2,1)S(1)}, u32[]{:S(2)}, u32[]{:S(2)}) %collective-permute-start.19) | collective-permute-done | bytes 131104 | tf_op jit(solution)/shard_map/ppermute | solution.py:1228
  69.6 3.9 %finish.1 = (f32[1024,128]{1,0:T(8,128)}, f32[10,1024]{1,0:T(8,128)}, f32[1024,512]{1,0:T(8,128)}, f32[1,512]{1,0:T(1,128)}, f32[512,2048]{1,0:T(8,128)}, /*index=5*/f32[1,2048]{1,0:T(1,128)}) custom-call(bf16[64,1024]{1,0:T(8,128)(2,1)S(1)} %collective-permute-done.18.home_0, bf16[64,1024]{1,0:T(8,128)(2,1)S(1)} %collective-permute-done.19.home_1, ...), custom_call_target="tpu_custom_call" | custom-call | flops 1000 | bytes 1000 | tf_op jit(solution)/shard_map/finish/pallas_call | solution.py:654
  (3 shorter events, 0.0 us)
Async XLA Ops:
  1.8 12.3 %collective-permute-start = (bf16[64,1152]{1,0:T(8,128)(2,1)S(1)}, bf16[64,1152]{1,0:T(8,128)(2,1)S(1)}, u32[]{:S(2)}, u32[]{:S(2)}) collective-permute-start(bf16[64,1152]{1,0:T(8,128)(2,1)S(1)} %get-tuple-element.51), channel_id=1, source_target_pairs={{0,2},{1,3},{2,0},{3,1},{4,10},{5,11},{6,8},{7,9},{8,6},{9,7},{10,... | collective-permute-start | bytes 442376 | tf_op jit(solution)/shard_map/ppermute | solution.py:1190
  6.6 7.9 %collective-permute-start.1 = (bf16[64,1152]{1,0:T(8,128)(2,1)S(1)}, bf16[64,1152]{1,0:T(8,128)(2,1)S(1)}, u32[]{:S(2)}, u32[]{:S(2)}) collective-permute-start(bf16[64,1152]{1,0:T(8,128)(2,1)S(1)} %get-tuple-element.52), channel_id=1, source_target_pairs={{0,0},{1,1},{2,2},{3,3},{4,8},{5,9},{6,10},{7,11},{8,4},{9,5},{10,... | collective-permute-start | bytes 442376 | tf_op jit(solution)/shard_map/ppermute | solution.py:1190
  14.1 8.8 %copy-start = (f32[1024]{0:T(1024)S(1)}, f32[1024]{0:T(1024)}, u32[]{:S(2)}) copy-start(f32[1024]{0:T(1024)} %param.18) | copy-start | bytes 12292
  14.1 8.8 %copy-start.1 = (f32[1024]{0:T(1024)S(1)}, f32[1024]{0:T(1024)}, u32[]{:S(2)}) copy-start(f32[1024]{0:T(1024)} %param.19) | copy-start | bytes 12292
  14.5 7.8 %collective-permute-start.4 = (bf16[64,1152]{1,0:T(8,128)(2,1)S(1)}, bf16[64,1152]{1,0:T(8,128)(2,1)S(1)}, u32[]{:S(2)}, u32[]{:S(2)}) collective-permute-start(bf16[64,1152]{1,0:T(8,128)(2,1)S(1)} %collective-permute-done.refs_0_.own_0), channel_id=1, source_target_pairs={{0,1},{1,0},{2,3},{3,2},{4,5},{5,4},{6,7},{7,6},{8,9},{9,8},{10,11... | collective-permute-start | bytes 442376 | tf_op jit(solution)/shard_map/ppermute | solution.py:1196
  15.7 2.2 %collective-permute-start.2 = (bf16[64,1152]{1,0:T(8,128)(2,1)S(1)}, bf16[64,1152]{1,0:T(8,128)(2,1)S(1)}, u32[]{:S(2)}, u32[]{:S(2)}) collective-permute-start(bf16[64,1152]{1,0:T(8,128)(2,1)S(1)} %collective-permute-done.refs_0_.own_0), channel_id=1, source_target_pairs={{0,8},{8,0},{16,24},{24,16},{1,9},{9,1},{17,25},{25,17},{2,10},{10... | collective-permute-start | bytes 442376 | tf_op jit(solution)/shard_map/ppermute | solution.py:1197
  15.7 6.6 %collective-permute-start.5 = (bf16[64,1152]{1,0:T(8,128)(2,1)S(1)}, bf16[64,1152]{1,0:T(8,128)(2,1)S(1)}, u32[]{:S(2)}, u32[]{:S(2)}) collective-permute-start(bf16[64,1152]{1,0:T(8,128)(2,1)S(1)} %collective-permute-done.1.refs_1_.own_1), channel_id=1, source_target_pairs={{0,1},{1,0},{2,3},{3,2},{4,5},{5,4},{6,7},{7,6},{8,9},{9,8},{10,11... | collective-permute-start | bytes 442376 | tf_op jit(solution)/shard_map/ppermute | solution.py:1196
  16.0 3.8 %collective-permute-start.3 = (bf16[64,1152]{1,0:T(8,128)(2,1)S(1)}, bf16[64,1152]{1,0:T(8,128)(2,1)S(1)}, u32[]{:S(2)}, u32[]{:S(2)}) collective-permute-start(bf16[64,1152]{1,0:T(8,128)(2,1)S(1)} %collective-permute-done.1.refs_1_.own_1), channel_id=1, source_target_pairs={{0,8},{8,0},{16,24},{24,16},{1,9},{9,1},{17,25},{25,17},{2,10},{10... | collective-permute-start | bytes 442376 | tf_op jit(solution)/shard_map/ppermute | solution.py:1197
  17.9 8.7 %collective-permute-start.8 = (bf16[64,1024]{1,0:T(8,128)(2,1)S(1)}, bf16[64,1024]{1,0:T(8,128)(2,1)S(1)}, u32[]{:S(2)}, u32[]{:S(2)}) collective-permute-start(bf16[64,1024]{1,0:T(8,128)(2,1)S(1)} %get-tuple-element.63), channel_id=1, source_target_pairs={{0,2},{1,3},{2,0},{3,1},{4,10},{5,11},{6,8},{7,9},{8,6},{9,7},{10,... | collective-permute-start | bytes 393224 | tf_op jit(solution)/shard_map/ppermute | solution.py:1198
  19.7 8.6 %collective-permute-start.9 = (bf16[64,1024]{1,0:T(8,128)(2,1)S(1)}, bf16[64,1024]{1,0:T(8,128)(2,1)S(1)}, u32[]{:S(2)}, u32[]{:S(2)}) collective-permute-start(bf16[64,1024]{1,0:T(8,128)(2,1)S(1)} %get-tuple-element.65), channel_id=1, source_target_pairs={{0,0},{1,1},{2,2},{3,3},{4,8},{5,9},{6,10},{7,11},{8,4},{9,5},{10,... | collective-permute-start | bytes 393224 | tf_op jit(solution)/shard_map/ppermute | solution.py:1198
  22.3 2.7 %collective-permute-start.6 = (bf16[64,1152]{1,0:T(8,128)(2,1)S(1)}, bf16[64,1152]{1,0:T(8,128)(2,1)S(1)}, u32[]{:S(2)}, u32[]{:S(2)}) collective-permute-start(bf16[64,1152]{1,0:T(8,128)(2,1)S(1)} %collective-permute-done.4.refs_0_), channel_id=1, source_target_pairs={{0,8},{8,0},{16,24},{24,16},{1,9},{9,1},{17,25},{25,17},{2,10},{10... | collective-permute-start | bytes 442376 | tf_op jit(solution)/shard_map/ppermute | solution.py:1199
  22.4 2.6 %collective-permute-start.7 = (bf16[64,1152]{1,0:T(8,128)(2,1)S(1)}, bf16[64,1152]{1,0:T(8,128)(2,1)S(1)}, u32[]{:S(2)}, u32[]{:S(2)}) collective-permute-start(bf16[64,1152]{1,0:T(8,128)(2,1)S(1)} %collective-permute-done.5.refs_1_), channel_id=1, source_target_pairs={{0,8},{8,0},{16,24},{24,16},{1,9},{9,1},{17,25},{25,17},{2,10},{10... | collective-permute-start | bytes 442376 | tf_op jit(solution)/shard_map/ppermute | solution.py:1199
  25.0 3.3 %copy-start.2 = (f32[1024]{0:T(1024)S(1)}, f32[1024]{0:T(1024)}, u32[]{:S(2)}) copy-start(f32[1024]{0:T(1024)} %param.22) | copy-start | bytes 12292
  25.0 3.3 %copy-start.3 = (f32[1024]{0:T(1024)S(1)}, f32[1024]{0:T(1024)}, u32[]{:S(2)}) copy-start(f32[1024]{0:T(1024)} %param.23) | copy-start | bytes 12292
  42.3 8.7 %collective-permute-start.16 = (bf16[128,1152]{1,0:T(8,128)(2,1)S(1)}, bf16[128,1152]{1,0:T(8,128)(2,1)S(1)}, u32[]{:S(2)}, u32[]{:S(2)}) collective-permute-start(bf16[128,1152]{1,0:T(8,128)(2,1)S(1)} %get-tuple-element.66.grads.grads_0), channel_id=1, source_target_pairs={{0,1},{1,0},{2,3},{3,2},{4,5},{5,4},{6,7},{7,6},{8,9},{9,8},{10,11... | collective-permute-start | bytes 884744 | tf_op jit(solution)/shard_map/ppermute | solution.py:1206
  44.9 5.9 %collective-permute-start.12 = (bf16[16,2048]{1,0:T(8,128)(2,1)S(1)}, bf16[16,2048]{1,0:T(8,128)(2,1)S(1)}, u32[]{:S(2)}, u32[]{:S(2)}) collective-permute-start(bf16[16,2048]{1,0:T(8,128)(2,1)S(1)} %prefix.1.order.own), channel_id=1, source_target_pairs={{0,24},{8,16},{16,8},{24,0},{1,25},{9,17},{17,9},{25,1},{2,26},{10... | collective-permute-start | bytes 196616 | tf_op jit(solution)/shard_map/ppermute | solution.py:1209
  44.9 5.9 %collective-permute-start.11 = (bf16[16,2048]{1,0:T(8,128)(2,1)S(1)}, bf16[16,2048]{1,0:T(8,128)(2,1)S(1)}, u32[]{:S(2)}, u32[]{:S(2)}) collective-permute-start(bf16[16,2048]{1,0:T(8,128)(2,1)S(1)} %prefix.1.order.own), channel_id=1, source_target_pairs={{0,8},{8,0},{16,24},{24,16},{1,9},{9,1},{17,25},{25,17},{2,10},{10... | collective-permute-start | bytes 196616 | tf_op jit(solution)/shard_map/ppermute | solution.py:1209
  46.5 4.3 %collective-permute-start.10 = (bf16[16,2048]{1,0:T(8,128)(2,1)S(1)}, bf16[16,2048]{1,0:T(8,128)(2,1)S(1)}, u32[]{:S(2)}, u32[]{:S(2)}) collective-permute-start(bf16[16,2048]{1,0:T(8,128)(2,1)S(1)} %prefix.1.order.own), channel_id=1, source_target_pairs={{0,16},{8,24},{16,0},{24,8},{1,17},{9,25},{17,1},{25,9},{2,18},{10... | collective-permute-start | bytes 196616 | tf_op jit(solution)/shard_map/ppermute | solution.py:1209
  46.8 8.7 %collective-permute-start.15 = (bf16[128,1152]{1,0:T(8,128)(2,1)S(1)}, bf16[128,1152]{1,0:T(8,128)(2,1)S(1)}, u32[]{:S(2)}, u32[]{:S(2)}) collective-permute-start(bf16[128,1152]{1,0:T(8,128)(2,1)S(1)} %get-tuple-element.66.grads.grads_0), channel_id=1, source_target_pairs={{0,8},{8,0},{16,24},{24,16},{1,9},{9,1},{17,25},{25,17},{2,10},{10... | collective-permute-start | bytes 884744 | tf_op jit(solution)/shard_map/ppermute | solution.py:1207
  50.9 4.5 %collective-permute-start.17 = (bf16[128,1152]{1,0:T(8,128)(2,1)S(1)}, bf16[128,1152]{1,0:T(8,128)(2,1)S(1)}, u32[]{:S(2)}, u32[]{:S(2)}) collective-permute-start(bf16[128,1152]{1,0:T(8,128)(2,1)S(1)} %collective-permute-done.16.grads_2), channel_id=1, source_target_pairs={{0,8},{8,0},{16,24},{24,16},{1,9},{9,1},{17,25},{25,17},{2,10},{10... | collective-permute-start | bytes 884744 | tf_op jit(solution)/shard_map/ppermute | solution.py:1215
  51.2 13.2 %collective-permute-start.13 = (bf16[96,1024]{1,0:T(8,128)(2,1)S(1)}, bf16[96,1024]{1,0:T(8,128)(2,1)S(1)}, u32[]{:S(2)}, u32[]{:S(2)}) collective-permute-start(bf16[96,1024]{1,0:T(8,128)(2,1)S(1)} %get-tuple-element.75), channel_id=1, source_target_pairs={{2,0},{3,1},{0,2},{1,3},{10,4},{11,5},{8,6},{9,7},{6,8},{7,9},{4,1... | collective-permute-start | bytes 589832 | tf_op jit(solution)/shard_map/ppermute | solution.py:1214
  53.3 11.1 %collective-permute-start.14 = (bf16[96,1024]{1,0:T(8,128)(2,1)S(1)}, bf16[96,1024]{1,0:T(8,128)(2,1)S(1)}, u32[]{:S(2)}, u32[]{:S(2)}) collective-permute-start(bf16[96,1024]{1,0:T(8,128)(2,1)S(1)} %get-tuple-element.76), channel_id=1, source_target_pairs={{0,0},{1,1},{2,2},{3,3},{8,4},{9,5},{10,6},{11,7},{4,8},{5,9},{6,1... | collective-permute-start | bytes 589832 | tf_op jit(solution)/shard_map/ppermute | solution.py:1214
  59.3 9.2 %collective-permute-start.18 = (bf16[64,1024]{1,0:T(8,128)(2,1)S(1)}, bf16[64,1024]{1,0:T(8,128)(2,1)S(1)}, u32[]{:S(2)}, u32[]{:S(2)}) collective-permute-start(bf16[64,1024]{1,0:T(8,128)(2,1)S(1)} %get-tuple-element.83), channel_id=1, source_target_pairs={{2,0},{3,1},{0,2},{1,3},{10,4},{11,5},{8,6},{9,7},{6,8},{7,9},{4,1... | collective-permute-start | bytes 393224 | tf_op jit(solution)/shard_map/ppermute | solution.py:1228
  61.0 8.6 %collective-permute-start.19 = (bf16[64,1024]{1,0:T(8,128)(2,1)S(1)}, bf16[64,1024]{1,0:T(8,128)(2,1)S(1)}, u32[]{:S(2)}, u32[]{:S(2)}) collective-permute-start(bf16[64,1024]{1,0:T(8,128)(2,1)S(1)} %get-tuple-element.84), channel_id=1, source_target_pairs={{0,0},{1,1},{2,2},{3,3},{8,4},{9,5},{10,6},{11,7},{4,8},{5,9},{6,1... | collective-permute-start | bytes 393224 | tf_op jit(solution)/shard_map/ppermute | solution.py:1228
  64.5 4.0 %collective-permute-start.22 = (bf16[16,2048]{1,0:T(8,128)(2,1)S(1)}, bf16[16,2048]{1,0:T(8,128)(2,1)S(1)}, u32[]{:S(2)}, u32[]{:S(2)}) collective-permute-start(bf16[16,2048]{1,0:T(8,128)(2,1)S(1)} %unpack.1.part_0), channel_id=1, source_target_pairs={{0,9},{1,8},{2,11},{3,10},{4,13},{5,12},{6,15},{7,14},{8,1},{9,0},... | collective-permute-start | bytes 196616 | tf_op jit(solution)/shard_map/ppermute | solution.py:1231
  64.6 3.9 %collective-permute-start.21 = (bf16[16,2048]{1,0:T(8,128)(2,1)S(1)}, bf16[16,2048]{1,0:T(8,128)(2,1)S(1)}, u32[]{:S(2)}, u32[]{:S(2)}) collective-permute-start(bf16[16,2048]{1,0:T(8,128)(2,1)S(1)} %unpack.1.part_0), channel_id=1, source_target_pairs={{0,1},{1,0},{2,3},{3,2},{4,5},{5,4},{6,7},{7,6},{8,9},{9,8},{10,11... | collective-permute-start | bytes 196616 | tf_op jit(solution)/shard_map/ppermute | solution.py:1230
  64.8 3.6 %collective-permute-start.20 = (bf16[16,2048]{1,0:T(8,128)(2,1)S(1)}, bf16[16,2048]{1,0:T(8,128)(2,1)S(1)}, u32[]{:S(2)}, u32[]{:S(2)}) collective-permute-start(bf16[16,2048]{1,0:T(8,128)(2,1)S(1)} %unpack.1.part_0), channel_id=1, source_target_pairs={{0,8},{8,0},{16,24},{24,16},{1,9},{9,1},{17,25},{25,17},{2,10},{10... | collective-permute-start | bytes 196616 | tf_op jit(solution)/shard_map/ppermute | solution.py:1230
